TPU v7x, 32 devices: a whole 2x2x4 slice. The times are simulated.
32 devices in a mesh: leaf: 4 (over x, core), row: 8 (over z, y).
Axes of the slice: x: 2, y: 2, z: 4, core: 2. Of those that a mesh axis runs over, the one named last changes fastest.
Arguments:
- loc_rhs: float32 [4, 8, 512, 128], P('leaf', 'row'), may hold values from -6 to 6
- loc_inverse: float32 [4, 8, 512, 512], P('leaf', 'row'), may hold values from -0.25 to 0.25
- loc_coupling: float32 [4, 8, 512, 512], P('leaf', 'row'), may hold values from -0.09375 to 0.09375
- loc_pivots: float32 [4, 8, 512], P('leaf', 'row'), may hold values from 0.5 to 4
- pattern: int32 [4, 8, 4], P('leaf', 'row'), may hold values from 0 to 13, as said below
- win_rhs: float32 [3, 1024, 128], P(None, ('leaf', 'row')), may hold values from -6 to 6
- win_pivots: float32 [3, 1024], P(None, ('leaf', 'row')), may hold values from 0.5 to 4
- win_inverse: float32 [8, 224, 1024], P('row', None, 'leaf'), may hold values from -0.1875 to 0.1875
- win_coupling: float32 [8, 192, 1024], P('row', None, 'leaf'), may hold values from -0.1875 to 0.1875
Outputs:
- loc_solution: float32 [4, 8, 512, 128], P('leaf', 'row')
- win_solution: float32 [3, 1024, 128], P(None, ('leaf', 'row'))
Inputs may be any that keep to these rules, and one draw needn't show every extreme that they name: `pattern`: on each device the 4 tile numbers are distinct; number p stands for rows p * 128 to (p + 1) * 128 - 1 of the path of the device's leaf index.
All inputs are finite; a program needn't handle non-finite values.
Results may differ from a plain program's by a relative error of at most 0.0001.
Values sent between devices are 32-bit elements; how exact they have to be, the bound alone decides.
No kernel may reach another device: no remote copies, remote signals or barrier semaphores. Data moves between devices by JAX's collectives and lax.ppermute only.
A program may use at most 64 MiB of HBM per device.

v0:
```python
import jax
import jax.numpy as jnp
from jax import lax
from jax.sharding import PartitionSpec as P

BASE = 256
TILE = 128


PRECISE = lax.Precision.HIGHEST


def contract_first(left, right):
    return lax.dot_general(left, right, (((0,), (0,)), ((), ())), precision=PRECISE)


def group_sum(partial_value, height, leaf_id, leaf_count):
    group_span = 2**height
    if group_span == 1:
        return partial_value[0]
    padded = jnp.zeros((leaf_count,) + partial_value.shape[1:], jnp.float32)
    padded = lax.dynamic_update_slice_in_dim(
        padded, partial_value, leaf_id // group_span * group_span, 0
    )
    return lax.psum_scatter(padded, "leaf", scatter_dimension=0, tiled=True)[0]


def group_gather(piece, height, leaf_id):
    group_span = 2**height
    if group_span == 1:
        return piece[None]
    whole_set = lax.all_gather(piece[None], "leaf", axis=0, tiled=True)
    return lax.dynamic_slice_in_dim(whole_set, leaf_id // group_span * group_span, group_span, 0)


def masked_block(diag_block, group_span, piece_rows, rank_id, leaf_id):
    row_ids = (
        jnp.arange(group_span)[:, None] * BASE
        + rank_id * piece_rows
        + jnp.arange(piece_rows)[None, :]
    ).reshape(-1)
    col_ids = leaf_id % group_span * BASE + jnp.arange(BASE)
    return jnp.where(col_ids[None, :] < row_ids[:, None], diag_block, 0.0)


def shards(
    loc_rhs,
    loc_inverse,
    loc_coupling,
    loc_pivots,
    pattern,
    win_rhs,
    win_pivots,
    win_inverse,
    win_coupling,
):
    leaf_count = lax.axis_size("leaf")
    rank_count = lax.axis_size("row")
    leaf_id = lax.axis_index("leaf")
    rank_id = lax.axis_index("row")
    levels = win_rhs.shape[0]
    piece_rows = win_rhs.shape[1]
    columns = win_rhs.shape[2]
    groups_total = 2 * leaf_count - 1
    tile_groups = BASE // TILE
    tile_pieces = TILE // piece_rows
    inverse = loc_inverse[0, 0]
    coupling = loc_coupling[0, 0]
    tile_count = coupling.shape[0] // TILE
    own_tiles = pattern[0, 0]
    positions = jnp.arange(inverse.shape[0])
    strict_low = jnp.where(positions[None, :] < positions[:, None], inverse, 0.0)
    solved_loc = loc_rhs[0, 0] + jnp.dot(strict_low, loc_rhs[0, 0], precision=PRECISE)
    loc_terms = jnp.dot(coupling, solved_loc, precision=PRECISE).reshape(
        tile_count, tile_pieces, piece_rows, columns
    )
    local_sums = []
    route_ids = jnp.arange(rank_count)
    tile_place = own_tiles % tile_groups
    place_hit = tile_place[None, :, None] == (route_ids // tile_pieces)[:, None, None]
    part_hit = jnp.arange(tile_pieces)[None, None, :] == (route_ids % tile_pieces)[:, None, None]
    send_mask = (place_hit & part_hit).astype(jnp.float32)
    outgoing = jnp.einsum("rts,tsix->rtix", send_mask, loc_terms, precision=PRECISE)
    known = lax.all_gather(own_tiles[None], "row", axis=0, tiled=True)
    incoming = lax.all_to_all(outgoing, "row", split_axis=0, concat_axis=0, tiled=True)
    receive_mask = (
        (known // tile_groups)[None, :, :] == jnp.arange(groups_total)[:, None, None]
    ).astype(jnp.float32)
    arrived = jnp.einsum("gut,utix->gix", receive_mask, incoming, precision=PRECISE)
    for height in range(levels):
        group_span = 2**height
        local_sums.append(
            group_sum(arrived[group_span - 1 : 2 * group_span - 1], height, leaf_id, leaf_count)
        )
    from_children = jnp.zeros((piece_rows, columns), jnp.float32)
    solved = []
    diagonals = []
    for height in range(levels):
        group_span = 2**height
        diag_block = win_inverse[
            0, (group_span - 1) * piece_rows : (2 * group_span - 1) * piece_rows
        ]
        strict = masked_block(diag_block, group_span, piece_rows, rank_id, leaf_id)
        diagonals.append(strict)
        residual = win_rhs[height] - local_sums[height] - from_children
        gathered = lax.all_gather(residual, "row", axis=0, tiled=True)
        partial_value = jnp.dot(strict, gathered, precision=PRECISE).reshape(
            group_span, piece_rows, columns
        )
        current = residual + group_sum(partial_value, height, leaf_id, leaf_count)
        solved.append(current)
        if height + 1 < levels:
            spread = lax.all_gather(current, "row", axis=0, tiled=True)
            link_block = win_coupling[
                0, (2 * group_span - 2) * piece_rows : (4 * group_span - 2) * piece_rows
            ]
            coupled = jnp.dot(link_block, spread, precision=PRECISE).reshape(
                2 * group_span, piece_rows, columns
            )
            from_children = group_sum(coupled, height + 1, leaf_id, leaf_count)
    from_parent = jnp.zeros((piece_rows, columns), jnp.float32)
    results = [None] * levels
    spreads = [None] * levels
    for height in reversed(range(levels)):
        group_span = 2**height
        wanted = solved[height] / win_pivots[height][:, None] - from_parent
        rows_in = group_gather(wanted, height, leaf_id)
        partial_value = contract_first(
            diagonals[height], rows_in.reshape(group_span * piece_rows, columns)
        )
        current = wanted + lax.psum_scatter(partial_value, "row", scatter_dimension=0, tiled=True)
        results[height] = current
        spreads[height] = group_gather(current, height, leaf_id)
        if height > 0:
            child_span = group_span // 2
            link_block = win_coupling[
                0, (2 * child_span - 2) * piece_rows : (4 * child_span - 2) * piece_rows
            ]
            partial_value = contract_first(
                link_block, spreads[height].reshape(group_span * piece_rows, columns)
            )
            from_parent = lax.psum_scatter(partial_value, "row", scatter_dimension=0, tiled=True)
    joined = jnp.concatenate(spreads, 0)
    reply = jnp.einsum("gut,gix->utix", receive_mask, joined, precision=PRECISE)
    returned = lax.all_to_all(reply, "row", split_axis=0, concat_axis=0, tiled=True)
    picked = jnp.einsum("rts,rtix->tsix", send_mask, returned, precision=PRECISE).reshape(
        tile_count * TILE, columns
    )
    scaled_loc = solved_loc / loc_pivots[0, 0][:, None]
    remainder = scaled_loc - contract_first(coupling, picked)
    answer = remainder + contract_first(strict_low, remainder)
    return (answer[None, None], jnp.stack(results))


def solution(mesh):
    return jax.shard_map(
        shards,
        mesh=mesh,
        in_specs=(
            P("leaf", "row", None, None),
            P("leaf", "row", None, None),
            P("leaf", "row", None, None),
            P("leaf", "row", None),
            P("leaf", "row", None),
            P(None, ("leaf", "row"), None),
            P(None, ("leaf", "row")),
            P("row", None, "leaf"),
            P("row", None, "leaf"),
        ),
        out_specs=(P("leaf", "row", None, None), P(None, ("leaf", "row"), None)),
        check_vma=False,
    )
```

profile of v0, /device:TPU:0, one launch (start us, length us, event | category | flops | bytes accessed | tf_op | source)
XLA Modules:
  0.0 666.4 jit_solution(2858498283063403207)
XLA Ops:
  7.9 2.3 convolution_add_fusion.1
  10.2 1.3 convolution_bitcast_fusion.2
  13.1 7.3 %all-to-all-start = ((f32[8,4,32,128]{3,1,2,0:T(4,128)}), f32[8,4,32,128]{3,1,2,0:T(4,128)S(1)}, u32[]{:S(2)}, u32[]{:S(2)}) async-start(f32[8,4,32,128]{3,1,2,0:T(4,128)} %copy.73), calls=%async_computation | async-start | bytes 1048576 | tf_op jit(solution)/shard_map/all_to_all | solution.py:85
  20.5 22.9 %all-gather = s32[8,1,4]{2,1,0:T(1,128)S(1)} all-gather(s32[1,1,4]{2,1,0:T(1,128)S(1)} %copy-done.13), channel_id=2, replica_groups=mesh['leaf'=4,'row'=8] {'row'}, dimensions={0}, use_global_device_ids=true | all-gather | bytes 144 | tf_op jit(solution)/shard_map/all_gather | solution.py:84
  44.3 30.5 %all-gather.1 = f32[1,256,128]{2,0,1:T(1,128)S(1)} all-gather(f32[1,32,128]{2,0,1:T(1,128)S(1)} %slice_subtract_fusion), channel_id=3, replica_groups=mesh['leaf'=4,'row'=8] {'row'}, dimensions={1}, use_global_device_ids=true | all-gather | bytes 147456 | tf_op jit(solution)/shard_map/all_gather | solution.py:106
  75.1 30.5 %all_gather.32 = f32[256,128]{1,0:T(8,128)S(1)} all-gather(f32[32,128]{1,0:T(8,128)S(1)} %convolution_add_fusion.2), channel_id=1, replica_groups=mesh['leaf'=4,'row'=8] {'row'}, dimensions={0}, use_global_device_ids=true | all-gather | bytes 147456 | tf_op jit(solution)/shard_map/all_gather | solution.py:113
  107.4 17.2 %reduce-scatter.14.cloned.1.call-done = f32[1,32,128]{2,1,0:T(8,128)} async-done(((f32[4,32,128]{2,1,0:T(8,128)}), f32[1,32,128]{2,1,0:T(8,128)}) %reduce-scatter.14.cloned.1.call-update) | async-done | bytes 16400 | tf_op jit(solution)/shard_map/reduce_scatter | solution.py:25
  124.6 22.0 %reduce-scatter.12.cloned.1.call-done = f32[1,32,128]{2,1,0:T(8,128)} async-done(((f32[4,32,128]{2,1,0:T(8,128)}), f32[1,32,128]{2,1,0:T(8,128)}) %reduce-scatter.12.cloned.1.call-update) | async-done | bytes 16400 | tf_op jit(solution)/shard_map/reduce_scatter | solution.py:25
  147.4 30.6 %all-gather.2 = f32[1,256,128]{2,1,0:T(8,128)S(1)} all-gather(f32[1,32,128]{2,1,0:T(8,128)S(1)} %subtract_subtract_fusion.1), channel_id=4, replica_groups=mesh['leaf'=4,'row'=8] {'row'}, dimensions={1}, use_global_device_ids=true | all-gather | bytes 147456 | tf_op jit(solution)/shard_map/all_gather | solution.py:106
  180.5 18.8 %reduce-scatter.16.cloned.1.call-done = f32[1,32,128]{2,1,0:T(8,128)} async-done(((f32[4,32,128]{2,1,0:T(8,128)}), f32[1,32,128]{2,1,0:T(8,128)}) %reduce-scatter.16.cloned.1.call-update) | async-done | bytes 16400 | tf_op jit(solution)/shard_map/reduce_scatter | solution.py:25
  200.0 30.6 %all-gather.7 = f32[1,256,128]{2,1,0:T(8,128)S(1)} all-gather(f32[1,32,128]{2,1,0:T(8,128)S(1)} %add.231), channel_id=9, replica_groups=mesh['leaf'=4,'row'=8] {'row'}, dimensions={1}, use_global_device_ids=true | all-gather | bytes 147456 | tf_op jit(solution)/shard_map/all_gather | solution.py:113
  231.7 19.4 %reduce-scatter.20.cloned.1.call-done = f32[1,32,128]{2,1,0:T(8,128)} async-done(((f32[4,32,128]{2,1,0:T(8,128)}), f32[1,32,128]{2,1,0:T(8,128)}) %reduce-scatter.20.cloned.1.call-update) | async-done | bytes 16400 | tf_op jit(solution)/shard_map/reduce_scatter | solution.py:25
  251.8 30.6 %all-gather.3 = f32[1,256,128]{2,0,1:T(1,128)S(1)} all-gather(f32[1,32,128]{2,0,1:T(1,128)S(1)} %bitcast.156), channel_id=5, replica_groups=mesh['leaf'=4,'row'=8] {'row'}, dimensions={1}, use_global_device_ids=true | all-gather | bytes 147456 | tf_op jit(solution)/shard_map/all_gather | solution.py:106
  284.0 18.9 %reduce-scatter.22.cloned.1.call-done = f32[1,32,128]{2,1,0:T(8,128)} async-done(((f32[4,32,128]{2,1,0:T(8,128)}), f32[1,32,128]{2,1,0:T(8,128)}) %reduce-scatter.22.cloned.1.call-update) | async-done | bytes 16400 | tf_op jit(solution)/shard_map/reduce_scatter | solution.py:25
  303.7 5.2 all_gather.36
  308.9 1.1 fusion.18
  310.1 61.0 %reduce-scatter.24.cloned.1.call-done = f32[32,128]{1,0:T(8,128)} async-done(((f32[256,128]{1,0:T(8,128)}), f32[32,128]{1,0:T(8,128)}) %reduce-scatter.24.cloned.1.call-update) | async-done | bytes 16400 | tf_op jit(solution)/shard_map/reduce_scatter | solution.py:131
  371.9 5.2 all-gather.4
  377.2 1.0 convolution_bitcast_fusion.4
  378.4 59.9 %reduce-scatter.26.cloned.1.call-done = f32[32,128]{1,0:T(8,128)} async-done(((f32[256,128]{1,0:T(8,128)}), f32[32,128]{1,0:T(8,128)}) %reduce-scatter.26.cloned.1.call-update) | async-done | bytes 16400 | tf_op jit(solution)/shard_map/reduce_scatter | solution.py:142
  439.0 5.2 all-gather.5
  444.3 1.1 fusion.32
  445.5 60.0 %reduce-scatter.28.cloned.1.call-done = f32[32,128]{1,0:T(8,128)} async-done(((f32[256,128]{1,0:T(8,128)}), f32[32,128]{1,0:T(8,128)}) %reduce-scatter.28.cloned.1.call-update) | async-done | bytes 16400 | tf_op jit(solution)/shard_map/reduce_scatter | solution.py:131
  506.2 5.2 all-gather.6
  511.4 1.1 convolution_bitcast_fusion.5
  512.6 60.0 %reduce-scatter.30.cloned.1.call-done = f32[32,128]{1,0:T(8,128)} async-done(((f32[256,128]{1,0:T(8,128)}), f32[32,128]{1,0:T(8,128)}) %reduce-scatter.30.cloned.1.call-update) | async-done | bytes 16400 | tf_op jit(solution)/shard_map/reduce_scatter | solution.py:142
  572.5 1.8 fusion.55
  574.5 61.9 %reduce-scatter.32.cloned.1.call-done = f32[32,128]{1,0:T(8,128)} async-done(((f32[256,128]{1,0:T(8,128)}), f32[32,128]{1,0:T(8,128)}) %reduce-scatter.32.cloned.1.call-update) | async-done | bytes 16400 | tf_op jit(solution)/shard_map/reduce_scatter | solution.py:131
  638.5 3.7 all-to-all-start.1
  642.8 12.0 %all-to-all-done.1 = f32[8,4,32,128]{3,2,1,0:T(8,128)S(1)} async-done(((f32[8,4,32,128]{3,2,1,0:T(8,128)}), f32[8,4,32,128]{3,2,1,0:T(8,128)S(1)}, u32[]{:S(2)}, u32[]{:S(2)}) %all-to-all-start.1) | async-done | bytes 524320 | tf_op jit(solution)/shard_map/all_to_all | solution.py:145
  656.1 1.8 fusion.1
  657.9 1.9 fusion
  (109 shorter events, 20.2 us)
Async XLA Ops:
  7.2 3.0 copy-start
  7.2 0.7 copy-start.13
  13.1 30.4 %all-to-all-start = ((f32[8,4,32,128]{3,1,2,0:T(4,128)}), f32[8,4,32,128]{3,1,2,0:T(4,128)S(1)}, u32[]{:S(2)}, u32[]{:S(2)}) async-start(f32[8,4,32,128]{3,1,2,0:T(4,128)} %copy.73), calls=%async_computation | async-start | bytes 1048576 | tf_op jit(solution)/shard_map/all_to_all | solution.py:85
  20.4 104.2 %reduce-scatter.14.cloned.1.call-start = ((), (), s32[]{:S(2)}) async-start(), calls=%async_computation.14 | async-start | bytes 81920 | tf_op jit(solution)/shard_map/reduce_scatter | solution.py:25
  43.5 0.7 slice-start.2
  44.2 30.7 %copy-start.2 = (f32[1,224,256]{2,1,0:T(8,128)S(1)}, f32[1,224,256]{2,1,0:T(8,128)}, u32[]{:S(2)}) copy-start(f32[1,224,256]{2,1,0:T(8,128)} %param.16) | copy-start | bytes 688132
  74.8 30.8 %copy-start.4 = (f32[1,192,256]{2,1,0:T(8,128)S(1)}, f32[1,192,256]{2,1,0:T(8,128)}, u32[]{:S(2)}) copy-start(f32[1,192,256]{2,1,0:T(8,128)} %param.17) | copy-start | bytes 589828
  105.8 0.6 copy-start.6
  106.5 40.1 %reduce-scatter.12.cloned.1.call-start = ((), (), s32[]{:S(2)}) async-start(), calls=%async_computation.13 | async-start | bytes 81920 | tf_op jit(solution)/shard_map/reduce_scatter | solution.py:25
  106.6 0.6 copy-start.7
  107.2 92.0 %reduce-scatter.16.cloned.1.call-start = ((), (), s32[]{:S(2)}) async-start(), calls=%async_computation.15 | async-start | bytes 81920 | tf_op jit(solution)/shard_map/reduce_scatter | solution.py:25
  107.4 39.2 %copy-start.8 = (f32[3,32,128]{2,1,0:T(8,128)S(1)}, f32[3,32,128]{2,1,0:T(8,128)}, u32[]{:S(2)}) copy-start(f32[3,32,128]{2,1,0:T(8,128)} %param.14) | copy-start | bytes 147460
  177.9 0.8 slice-start
  179.0 0.6 copy-start.5
  179.7 52.0 %reduce-scatter.18.cloned.1.call-start = ((), (), s32[]{:S(2)}) async-start(), calls=%async_computation.16 | async-start | bytes 81920 | tf_op jit(solution)/shard_map/reduce_scatter | solution.py:25
  180.4 70.6 %reduce-scatter.20.cloned.1.call-start = ((), (), s32[]{:S(2)}) async-start(), calls=%async_computation.17 | async-start | bytes 81920 | tf_op jit(solution)/shard_map/reduce_scatter | solution.py:25
  231.5 71.4 %reduce-scatter.22.cloned.1.call-start = ((), (), s32[]{:S(2)}) async-start(), calls=%async_computation.18 | async-start | bytes 81920 | tf_op jit(solution)/shard_map/reduce_scatter | solution.py:25
  231.6 50.8 %slice-start.1 = ((f32[1,224,256]{2,1,0:T(8,128)}), f32[1,128,256]{2,1,0:T(8,128)S(1)}, s32[]{:S(2)}) async-start(f32[1,224,256]{2,1,0:T(8,128)} %param.16), calls=%async_computation.25 | async-start | bytes 262144 | tf_op jit(solution)/shard_map/slice | solution.py:100
  282.4 26.5 %copy-start.3 = (f32[1,224,256]{2,1,0:T(8,128)S(1)}, f32[1,224,256]{2,1,0:T(8,128)}, u32[]{:S(2)}) copy-start(f32[1,224,256]{2,1,0:T(8,128)} %param.16) | copy-start | bytes 688132
  283.4 0.7 copy-start.12
  283.4 87.7 %reduce-scatter.24.cloned.1.call-start = ((), (), s32[]{:S(2)}) async-start(), calls=%async_computation.19 | async-start | bytes 147456 | tf_op jit(solution)/shard_map/reduce_scatter | solution.py:131
  310.1 61.1 %copy-start.9 = (f32[1,32,128]{2,1,0:T(8,128)S(1)}, f32[1,32,128]{2,1,0:T(8,128)}, u32[]{:S(2)}) copy-start(f32[1,32,128]{2,1,0:T(8,128)} %reduce-scatter.22.cloned.1.call-done) | copy-start | bytes 49156
  310.1 128.2 %reduce-scatter.26.cloned.1.call-start = ((), (), s32[]{:S(2)}) async-start(), calls=%async_computation.20 | async-start | bytes 147456 | tf_op jit(solution)/shard_map/reduce_scatter | solution.py:142
  378.2 127.2 %reduce-scatter.28.cloned.1.call-start = ((), (), s32[]{:S(2)}) async-start(), calls=%async_computation.21 | async-start | bytes 147456 | tf_op jit(solution)/shard_map/reduce_scatter | solution.py:131
  445.4 127.1 %reduce-scatter.30.cloned.1.call-start = ((), (), s32[]{:S(2)}) async-start(), calls=%async_computation.22 | async-start | bytes 147456 | tf_op jit(solution)/shard_map/reduce_scatter | solution.py:142
  512.5 123.9 %reduce-scatter.32.cloned.1.call-start = ((), (), s32[]{:S(2)}) async-start(), calls=%async_computation.23 | async-start | bytes 147456 | tf_op jit(solution)/shard_map/reduce_scatter | solution.py:131
  574.5 61.9 %copy-start.10 = (f32[32,128]{1,0:T(8,128)S(1)}, f32[32,128]{1,0:T(8,128)}, u32[]{:S(2)}) copy-start(f32[32,128]{1,0:T(8,128)} %reduce-scatter.30.cloned.1.call-done) | copy-start | bytes 49156
  638.5 16.3 %all-to-all-start.1 = ((f32[8,4,32,128]{3,2,1,0:T(8,128)}), f32[8,4,32,128]{3,2,1,0:T(8,128)S(1)}, u32[]{:S(2)}, u32[]{:S(2)}) async-start(f32[8,4,32,128]{3,2,1,0:T(8,128)} %copy.86), calls=%async_computation.12 | async-start | bytes 1048576 | tf_op jit(solution)/shard_map/all_to_all | solution.py:145
  655.4 0.7 copy-start.11
  655.5 2.5 copy-start.1
Sparse Core Ops, SparseCore 0:
  106.6 17.9 reduce-scatter.13
  127.1 19.4 reduce-scatter.11
  179.8 19.3 reduce-scatter.15
  201.7 19.4 reduce-scatter.17
  231.6 19.4 reduce-scatter.19
  283.5 19.3 reduce-scatter.21
  310.2 60.8 reduce-scatter.23
  378.4 59.8 reduce-scatter.25
  445.6 59.8 reduce-scatter.27
  512.6 59.8 reduce-scatter.29
  576.4 59.8 reduce-scatter.31
where the time goes:
time: 668 us; the launch traced here: 666 us
  waiting for transfers between devices  411 us (62%)
  blocking collectives  197 us (29%)
  matrix products  18.1 us (3%)
  between operations  14.2 us (2%)
  starting transfers between devices  11.4 us (2%)
  local copies, waits for them, and re-layouts  7.8 us (1%)
  other arithmetic  7 us (1%)
    reduce_scatter x5, waiting for transfers between devices, shards(): lax.psum_scatter(partial_value, 'row', scatter_dimension=0, tiled=True)  303 us
    reduce_scatter x6, waiting for transfers between devices, group_sum(): return lax.psum_scatter(padded, 'leaf', scatter_dimension=0, tiled=True)[0]  96.3 us
    all_gather x3, blocking collectives, shards(): gathered = lax.all_gather(residual, 'row', axis=0, tiled=True)  91.7 us
    all_gather x2, blocking collectives, shards(): spread = lax.all_gather(current, 'row', axis=0, tiled=True)  61.1 us
    all_gather x1, blocking collectives, shards(): known = lax.all_gather(own_tiles[None], 'row', axis=0, tiled=True)  22.9 us
    all_gather x4, blocking collectives, group_gather(): whole_set = lax.all_gather(piece[None], 'leaf', axis=0, tiled=True)  20.9 us
  transfers between devices with their start and end apart: 13, of which 11 were waited for; matrix products, arithmetic and copies ran while one was open for 1% of the time, Pallas kernels for 0%

commit v1 on v0

v1 whole, which is shorter than its diff:
```python
import jax
import jax.numpy as jnp
from jax import lax
from jax.sharding import PartitionSpec as P

TILE = 128
NEAR = lax.Precision.HIGH


def dot(left, right, left_dim, right_dim):
    return lax.dot_general(left, right, (((left_dim,), (right_dim,)), ((), ())), precision=NEAR)


def swap(value, axis, count, offset):
    return lax.ppermute(value, axis, [(i, i ^ offset) for i in range(count)])


def gather_rows(block, count, me):
    parts = [(0, block)]
    step = count // 2
    while step:
        stacked = jnp.stack([p for _, p in parts])
        other = swap(stacked, "row", count, step)
        parts = parts + [(o ^ step, other[i]) for i, (o, _) in enumerate(parts)]
        step //= 2
    parts.sort(key=lambda pair: pair[0])
    stacked = jnp.stack([p for _, p in parts])
    return jnp.stack(
        [lax.dynamic_index_in_dim(stacked, me ^ r, 0, keepdims=False) for r in range(count)]
    )


def shards(
    loc_rhs,
    loc_inverse,
    loc_coupling,
    loc_pivots,
    pattern,
    win_rhs,
    win_pivots,
    win_inverse,
    win_coupling,
):
    leaves = lax.axis_size("leaf")
    ranks = lax.axis_size("row")
    leaf = lax.axis_index("leaf")
    rank = lax.axis_index("row")
    levels, piece, columns = win_rhs.shape
    base = piece * ranks
    share = columns // ranks
    path_tiles = (2 * leaves - 1) * base // TILE
    tiles = pattern.shape[2]
    local = loc_rhs.shape[2]

    def group_swaps(value, height):
        return [value] + [swap(value, "leaf", leaves, j) for j in range(1, 2**height)]

    def group_sum(value, height):
        return sum(group_swaps(value, height))

    def group_gather(value, height):
        span = 2**height
        stacked = jnp.stack(group_swaps(value, height))
        return jnp.concatenate(
            [
                lax.dynamic_index_in_dim(stacked, leaf % span ^ q, 0, keepdims=False)
                for q in range(span)
            ],
            -1,
        )

    def own(value, height):
        start = leaf % 2**height * base
        return lax.dynamic_slice_in_dim(value, start, base, 1)

    early = jnp.concatenate(
        [
            win_rhs.transpose(2, 0, 1).reshape(ranks, share, levels * piece),
            jnp.broadcast_to(win_pivots.reshape(1, 1, -1), (ranks, 1, levels * piece)),
            jnp.broadcast_to(
                jnp.pad(pattern[0].astype(jnp.float32), ((0, 0), (0, levels * piece - tiles))),
                (ranks, 1, levels * piece),
            ),
        ],
        1,
    )
    early = lax.all_to_all(early, "row", 0, 0, tiled=True)
    known = early[:, share + 1, :tiles].astype(jnp.int32)
    early = early[:, : share + 1].reshape(ranks, share + 1, levels, piece)
    early = early.transpose(2, 1, 0, 3).reshape(levels, share + 1, base)
    rhs, pivots = early[:, :share], early[:, share:]

    def stacked_rows(block, span):
        block = gather_rows(block, ranks, rank).reshape(ranks, span, piece, base)
        return block.transpose(1, 0, 2, 3).reshape(span * base, base)

    diagonals, links = [], []
    for height in range(levels):
        span = 2**height
        block = stacked_rows(win_inverse[0, (span - 1) * piece : (2 * span - 1) * piece], span)
        row_ids = jnp.arange(span * base)[:, None]
        col_ids = leaf % span * base + jnp.arange(base)[None, :]
        diagonals.append(jnp.where(col_ids < row_ids, block, 0.0))
        if height + 1 < levels:
            links.append(
                stacked_rows(
                    win_coupling[0, (2 * span - 2) * piece : (4 * span - 2) * piece], 2 * span
                )
            )

    rhs_loc = loc_rhs[0, 0]
    inverse = loc_inverse[0, 0]
    coupling = loc_coupling[0, 0]
    positions = jnp.arange(local)
    strict = jnp.where(positions[None, :] < positions[:, None], inverse, 0.0)
    solved_loc = rhs_loc.T + dot(rhs_loc, strict, 0, 1)
    terms = dot(solved_loc, coupling, 1, 1).reshape(ranks, share, tiles * TILE)
    terms = lax.all_to_all(terms, "row", 0, 0, tiled=True)
    hits = (known[:, :, None] == jnp.arange(path_tiles)).astype(jnp.float32)
    path = jnp.einsum(
        "bcti,btp->cpi",
        terms.reshape(ranks, share, tiles, TILE),
        hits,
        precision=lax.Precision.HIGHEST,
    ).reshape(share, path_tiles * TILE)

    ahead = jnp.zeros((share, base), jnp.float32)
    solved = []
    for height in range(levels):
        span = 2**height
        partial = -path[:, (span - 1) * base : (2 * span - 1) * base] - ahead
        partial = partial.reshape(share, span, base)
        mine = (jnp.arange(span) == leaf % span)[None, :, None]
        partial = (partial + jnp.where(mine, rhs[height][:, None], 0.0)).reshape(share, span * base)
        residual = group_sum(partial, height)
        product = dot(own(residual, height), diagonals[height], 1, 1)
        current = own(residual + group_sum(product, height), height)
        solved.append(current)
        if height + 1 < levels:
            ahead = dot(current, links[height], 1, 1)

    above = jnp.zeros((share, base), jnp.float32)
    results = [None] * levels
    wholes = [None] * levels
    for height in reversed(range(levels)):
        wanted = solved[height] / pivots[height] - above
        full = group_gather(wanted, height)
        results[height] = wanted + dot(full, diagonals[height], 1, 0)
        wholes[height] = group_gather(results[height], height)
        if height > 0:
            above = dot(wholes[height], links[height - 1], 1, 0)
    whole = jnp.concatenate(wholes, 1).reshape(share, path_tiles, TILE)

    reply = jnp.einsum(
        "cpi,btp->bcti", whole, hits, precision=lax.Precision.HIGHEST
    ).reshape(ranks, share, tiles * TILE)
    final = jnp.stack(results).reshape(levels, share, ranks, piece)
    final = final.transpose(2, 1, 0, 3).reshape(ranks, share, levels * piece)
    back = lax.all_to_all(jnp.concatenate([reply, final], 2), "row", 0, 0, tiled=True)
    back = back.reshape(columns, tiles * TILE + levels * piece)
    picked = back[:, : tiles * TILE]
    final = back[:, tiles * TILE :].reshape(columns, levels, piece).transpose(1, 2, 0)

    remainder = solved_loc / loc_pivots[0] - dot(picked, coupling, 1, 0)
    answer = remainder.T + dot(strict, remainder, 0, 1)
    return answer[None, None], final


def solution(mesh):
    return jax.shard_map(
        shards,
        mesh=mesh,
        in_specs=(
            P("leaf", "row", None, None),
            P("leaf", "row", None, None),
            P("leaf", "row", None, None),
            P("leaf", "row", None),
            P("leaf", "row", None),
            P(None, ("leaf", "row"), None),
            P(None, ("leaf", "row")),
            P("row", None, "leaf"),
            P("row", None, "leaf"),
        ),
        out_specs=(P("leaf", "row", None, None), P(None, ("leaf", "row"), None)),
        check_vma=False,
    )
```

time: 668 us -> 143 us (0.21)
  waiting for transfers between devices: 411 us -> 30.7 us
  blocking collectives: 197 us -> 15.7 us
  local copies, waits for them, and re-layouts: 7.8 us -> 35.9 us
  starting transfers between devices: 11.4 us -> 36.5 us
  between operations: 14.2 us -> 1.85 us
  matrix products: 18.1 us -> 9.4 us
    reduce_scatter x11 -> x0, waiting for transfers between devices: 399 us -> none  [the longest x5 303 us: shards(): lax.psum_scatter(partial_value, 'row', scatter_dimension=0, tiled=True)]
    all_gather x10 -> x0, blocking collectives: 197 us -> none  [the longest x3 91.7 us: shards(): gathered = lax.all_gather(residual, 'row', axis=0, tiled=True)]
    ppermute x0 -> x31, waiting for transfers between devices: none -> 30.7 us  [swap(): return lax.ppermute(value, axis, [(i, i ^ offset) for i in range(count)])]
    ppermute x0 -> x31, starting transfers between devices: none -> 27.7 us  [swap(): return lax.ppermute(value, axis, [(i, i ^ offset) for i in range(count)])]
    unnamed x29 -> x155, local copies, waits for them, and re-layouts: 3.91 us -> 22.5 us
    all_to_all x0 -> x1, blocking collectives: none -> 15.7 us  [shards(): lax.all_to_all(jnp.concatenate([reply, final], 2), 'row', 0, 0, tiled=True)]
    all_to_all x2, waiting for transfers between devices: 12 us -> 0.01 us  [the longest x1 0.01 us: shards(): early = lax.all_to_all(early, 'row', 0, 0, tiled=True)]
    dot_general x18 -> x16, matrix products: 18.1 us -> 9.4 us  [the longest x14 7.97 us: dot(): lax.dot_general(left, right, (((left_dim,), (right_dim,)), ((), ())), pre...]
  transfers between devices with their start and end apart: 13 -> 33, of which waited for: 11 -> 15; matrix products, arithmetic and copies ran while one was open for 1% -> 29% of each run, Pallas kernels for 0% -> 0%
where the time goes in v1:
time: 143 us; the launch traced here: 141 us
  starting transfers between devices  36.5 us (26%)
  local copies, waits for them, and re-layouts  35.9 us (25%)
  waiting for transfers between devices  30.7 us (21%)
  blocking collectives  15.7 us (11%)
  other arithmetic  11 us (8%)
  matrix products  9.4 us (7%)
  between operations  1.85 us (1%)
    ppermute x31, waiting for transfers between devices, swap(): return lax.ppermute(value, axis, [(i, i ^ offset) for i in range(count)])  30.7 us
    ppermute x31, starting transfers between devices, swap(): return lax.ppermute(value, axis, [(i, i ^ offset) for i in range(count)])  27.7 us
    unnamed x155, local copies, waits for them, and re-layouts  22.5 us
    all_to_all x1, blocking collectives, shards(): lax.all_to_all(jnp.concatenate([reply, final], 2), 'row', 0, 0, tiled=True)  15.7 us
    another operation x10, other arithmetic, gather_rows(): stacked = jnp.stack([p for _, p in parts])  8.01 us
    dot_general x14, matrix products, dot(): lax.dot_general(left, right, (((left_dim,), (right_dim,)), ((), ())), pre...  7.97 us
    all_to_all x1, starting transfers between devices, shards(): terms = lax.all_to_all(terms, 'row', 0, 0, tiled=True)  4.96 us
    all_to_all x1, starting transfers between devices, shards(): early = lax.all_to_all(early, 'row', 0, 0, tiled=True)  3.91 us
  transfers between devices with their start and end apart: 33, of which 15 were waited for; matrix products, arithmetic and copies ran while one was open for 29% of the time, Pallas kernels for 0%

profile of v1, /device:TPU:0, one launch (start us, length us, event | category | flops | bytes accessed | tf_op | source)
XLA Modules:
  0.0 141.1 jit_solution(9455361713439045099)
XLA Ops:
  0.7 1.7 %fusion.70 = (f32[1,128,256]{2,1,0:T(8,128)S(1)}, f32[8,128,256]{2,1,0:T(8,128)}) fusion(f32[1,192,256]{2,1,0:T(8,128)} %param.17), kind=kLoop, calls=%fused_computation.220 | loop fusion | bytes 393216 | tf_op jit(solution)/shard_map/slice | solution.py:107
  2.3 4.0 %collective-permute-start.11 = (f32[1,128,256]{2,1,0:T(8,128)S(1)}, f32[1,128,256]{2,1,0:T(8,128)S(1)}, u32[]{:S(2)}, u32[]{:S(2)}) collective-permute-start(f32[1,128,256]{2,1,0:T(8,128)S(1)} %get-tuple-element.20), channel_id=1, source_target_pairs={{0,4},{1,5},{2,6},{3,7},{4,0},{5,1},{6,2},{7,3},{8,12},{9,13},{10,... | collective-permute-start | bytes 393224 | tf_op jit(solution)/shard_map/ppermute | solution.py:15
  6.5 1.5 %fusion.71 = (f32[1,64,256]{2,1,0:T(8,128)S(1)}, f32[8,64,256]{2,1,0:T(8,128)}) fusion(f32[1,192,256]{2,1,0:T(8,128)} %param.17), kind=kLoop, calls=%fused_computation.221 | loop fusion | bytes 196608 | tf_op jit(solution)/shard_map/slice | solution.py:107
  7.9 2.9 %collective-permute-start.3 = (f32[1,64,256]{2,1,0:T(8,128)S(1)}, f32[1,64,256]{2,1,0:T(8,128)S(1)}, u32[]{:S(2)}, u32[]{:S(2)}) collective-permute-start(f32[1,64,256]{2,1,0:T(8,128)S(1)} %get-tuple-element.22), channel_id=1, source_target_pairs={{0,4},{1,5},{2,6},{3,7},{4,0},{5,1},{6,2},{7,3},{8,12},{9,13},{10,... | collective-permute-start | bytes 196616 | tf_op jit(solution)/shard_map/ppermute | solution.py:15
  12.1 2.9 %collective-permute-start = (f32[1,32,256]{2,1,0:T(8,128)S(1)}, f32[1,32,256]{2,1,0:T(8,128)}, u32[]{:S(2)}, u32[]{:S(2)}) collective-permute-start(f32[1,32,256]{2,1,0:T(8,128)S(1)} %get-tuple-element.14), channel_id=1, source_target_pairs={{0,4},{1,5},{2,6},{3,7},{4,0},{5,1},{6,2},{7,3},{8,12},{9,13},{10,... | collective-permute-start | bytes 98312 | tf_op jit(solution)/shard_map/ppermute | solution.py:15
  16.1 3.9 %all-to-all-start = ((f32[8,18,96]{2,1,0:T(8,128)}), f32[8,18,96]{2,1,0:T(8,128)S(1)}, u32[]{:S(2)}, u32[]{:S(2)}) async-start(f32[8,18,96]{2,1,0:T(8,128)} %pad_maximum_fusion.10), calls=%async_computation | async-start | bytes 196608 | tf_op jit(solution)/shard_map/all_to_all | solution.py:87
  21.4 1.8 %convolution_add_fusion.1 = f32[512,128]{0,1:T(8,128)S(1)} fusion(f32[1,1,512,512]{3,2,1,0:T(8,128)} %param.10, f32[1,1,512,128]{3,2,1,0:T(8,128)S(1)} %copy-done.11, f32[1,1,512,128]{2,3,1,0:T(8,128)S(1)} %copy.82), kind=kOutput, calls=%fused_computation.3 | convolution fusion | flops 201916416 | bytes 1835008 | tf_op jit(solution)/shard_map/dot_general | solution.py:11
  23.2 1.4 fusion.3
  25.9 1.1 collective-permute-done
  27.0 1.4 pad_maximum_fusion.11
  30.0 1.1 collective-permute-start.4
  32.7 5.0 %all-to-all-start.1 = ((f32[8,16,512]{2,1,0:T(8,128)}), f32[8,16,512]{2,1,0:T(8,128)S(1)}, u32[]{:S(2)}, u32[]{:S(2)}) async-start(f32[8,16,512]{2,1,0:T(8,128)} %fusion.3), calls=%async_computation.1 | async-start | bytes 524288 | tf_op jit(solution)/shard_map/all_to_all | solution.py:118
  41.6 2.1 %collective-permute-start.2 = (f32[4,32,256]{2,1,0:T(8,128)S(1)}, f32[4,32,256]{2,1,0:T(8,128)S(1)}, u32[]{:S(2)}, u32[]{:S(2)}) collective-permute-start(f32[4,32,256]{2,1,0:T(8,128)S(1)} %pad_maximum_fusion.7), channel_id=1, source_target_pairs={{0,1},{1,0},{2,3},{3,2},{4,5},{5,4},{6,7},{7,6},{8,9},{9,8},{10,11... | collective-permute-start | bytes 393224 | tf_op jit(solution)/shard_map/ppermute | solution.py:15
  43.8 1.5 %collective-permute-start.12 = (f32[2,128,256]{2,1,0:T(8,128)S(1)}, f32[2,128,256]{2,1,0:T(8,128)S(1)}, u32[]{:S(2)}, u32[]{:S(2)}) collective-permute-start(f32[2,128,256]{2,1,0:T(8,128)S(1)} %pad_maximum_fusion.5), channel_id=1, source_target_pairs={{0,2},{1,3},{2,0},{3,1},{4,6},{5,7},{6,4},{7,5},{8,10},{9,11},{10,... | collective-permute-start | bytes 786440 | tf_op jit(solution)/shard_map/ppermute | solution.py:15
  48.6 2.0 %collective-permute-start.9 = (f32[4,64,256]{2,1,0:T(8,128)S(1)}, f32[4,64,256]{2,1,0:T(8,128)S(1)}, u32[]{:S(2)}, u32[]{:S(2)}) collective-permute-start(f32[4,64,256]{2,1,0:T(8,128)S(1)} %pad_maximum_fusion.4), channel_id=1, source_target_pairs={{0,1},{1,0},{2,3},{3,2},{4,5},{5,4},{6,7},{7,6},{8,9},{9,8},{10,11... | collective-permute-start | bytes 786440 | tf_op jit(solution)/shard_map/ppermute | solution.py:15
  54.2 2.7 %collective-permute-done.5 = f32[4,64,256]{2,1,0:T(8,128)S(1)} collective-permute-done((f32[4,64,256]{2,1,0:T(8,128)S(1)}, f32[4,64,256]{2,1,0:T(8,128)S(1)}, u32[]{:S(2)}, u32[]{:S(2)}) %collective-permute-start.5) | collective-permute-done | bytes 262176 | tf_op jit(solution)/shard_map/ppermute | solution.py:15
  58.6 3.9 %collective-permute-done.9 = f32[4,64,256]{2,1,0:T(8,128)S(1)} collective-permute-done((f32[4,64,256]{2,1,0:T(8,128)S(1)}, f32[4,64,256]{2,1,0:T(8,128)S(1)}, u32[]{:S(2)}, u32[]{:S(2)}) %collective-permute-start.9) | collective-permute-done | bytes 262176 | tf_op jit(solution)/shard_map/ppermute | solution.py:15
  65.2 1.1 fusion.15
  70.8 1.1 copy.88
  75.7 1.0 pad_maximum_fusion.1
  80.6 10.3 %collective-permute-done.19 = f32[4,128,256]{2,1,0:T(8,128)S(1)} collective-permute-done((f32[4,128,256]{2,1,0:T(8,128)S(1)}, f32[4,128,256]{2,1,0:T(8,128)S(1)}, u32[]{:S(2)}, u32[]{:S(2)}) %collective-permute-start.19) | collective-permute-done | bytes 524320 | tf_op jit(solution)/shard_map/ppermute | solution.py:15
  97.3 1.5 %collective-permute-done.16 = f32[16,1024]{1,0:T(8,128)S(1)} collective-permute-done((f32[16,1024]{1,0:T(8,128)S(1)}, f32[16,1024]{1,0:T(8,128)S(1)}, u32[]{:S(2)}, u32[]{:S(2)}) %collective-permute-start.16) | collective-permute-done | bytes 65568 | tf_op jit(solution)/shard_map/ppermute | solution.py:15
  98.8 1.5 %collective-permute-done.15 = f32[16,1024]{1,0:T(8,128)S(1)} collective-permute-done((f32[16,1024]{1,0:T(8,128)S(1)}, f32[16,1024]{1,0:T(8,128)S(1)}, u32[]{:S(2)}, u32[]{:S(2)}) %collective-permute-start.15) | collective-permute-done | bytes 65568 | tf_op jit(solution)/shard_map/ppermute | solution.py:15
  101.5 1.0 collective-permute-start.21
  102.7 1.3 fusion.72
  104.0 1.0 collective-permute-done.22
  105.0 1.7 %collective-permute-done.21 = f32[16,1024]{1,0:T(8,128)S(1)} collective-permute-done((f32[16,1024]{1,0:T(8,128)S(1)}, f32[16,1024]{1,0:T(8,128)S(1)}, u32[]{:S(2)}, u32[]{:S(2)}) %collective-permute-start.21) | collective-permute-done | bytes 65568 | tf_op jit(solution)/shard_map/ppermute | solution.py:15
  107.1 1.1 collective-permute-start.24
  108.6 1.4 %collective-permute-done.25 = f32[16,256]{1,0:T(8,128)S(1)} collective-permute-done((f32[16,256]{1,0:T(8,128)S(1)}, f32[16,256]{1,0:T(8,128)S(1)}, u32[]{:S(2)}, u32[]{:S(2)}) %collective-permute-start.25) | collective-permute-done | bytes 16416 | tf_op jit(solution)/shard_map/ppermute | solution.py:15
  113.1 1.3 collective-permute-done.28
  116.6 1.1 collective-permute-done.29
  122.2 15.7 %all_to_all.15 = f32[8,16,608]{2,1,0:T(8,128)S(1)} all-to-all(f32[8,16,608]{2,1,0:T(8,128)S(1)} %pad_maximum_fusion.2), channel_id=1, replica_groups=mesh['leaf'=4,'row'=8] {'row'}, dimensions={0} | all-to-all | bytes 622592 | tf_op jit(solution)/shard_map/all_to_all | solution.py:159
  (298 shorter events, 56.3 us)
Async XLA Ops:
  2.3 41.4 %collective-permute-start.11 = (f32[1,128,256]{2,1,0:T(8,128)S(1)}, f32[1,128,256]{2,1,0:T(8,128)S(1)}, u32[]{:S(2)}, u32[]{:S(2)}) collective-permute-start(f32[1,128,256]{2,1,0:T(8,128)S(1)} %get-tuple-element.20), channel_id=1, source_target_pairs={{0,4},{1,5},{2,6},{3,7},{4,0},{5,1},{6,2},{7,3},{8,12},{9,13},{10,... | collective-permute-start | bytes 393224 | tf_op jit(solution)/shard_map/ppermute | solution.py:15
  6.4 38.9 %collective-permute-start.17 = (f32[1,128,256]{2,1,0:T(8,128)S(1)}, f32[1,128,256]{2,1,0:T(8,128)S(1)}, u32[]{:S(2)}, u32[]{:S(2)}) collective-permute-start(f32[1,128,256]{2,1,0:T(8,128)S(1)} %get-tuple-element.18), channel_id=1, source_target_pairs={{0,4},{1,5},{2,6},{3,7},{4,0},{5,1},{6,2},{7,3},{8,12},{9,13},{10,... | collective-permute-start | bytes 393224 | tf_op jit(solution)/shard_map/ppermute | solution.py:15
  7.9 21.4 %collective-permute-start.3 = (f32[1,64,256]{2,1,0:T(8,128)S(1)}, f32[1,64,256]{2,1,0:T(8,128)S(1)}, u32[]{:S(2)}, u32[]{:S(2)}) collective-permute-start(f32[1,64,256]{2,1,0:T(8,128)S(1)} %get-tuple-element.22), channel_id=1, source_target_pairs={{0,4},{1,5},{2,6},{3,7},{4,0},{5,1},{6,2},{7,3},{8,12},{9,13},{10,... | collective-permute-start | bytes 196616 | tf_op jit(solution)/shard_map/ppermute | solution.py:15
  11.5 19.7 %collective-permute-start.7 = (f32[1,64,256]{2,1,0:T(8,128)S(1)}, f32[1,64,256]{2,1,0:T(8,128)S(1)}, u32[]{:S(2)}, u32[]{:S(2)}) collective-permute-start(f32[1,64,256]{2,1,0:T(8,128)S(1)} %get-tuple-element.16), channel_id=1, source_target_pairs={{0,4},{1,5},{2,6},{3,7},{4,0},{5,1},{6,2},{7,3},{8,12},{9,13},{10,... | collective-permute-start | bytes 196616 | tf_op jit(solution)/shard_map/ppermute | solution.py:15
  12.1 14.9 %collective-permute-start = (f32[1,32,256]{2,1,0:T(8,128)S(1)}, f32[1,32,256]{2,1,0:T(8,128)}, u32[]{:S(2)}, u32[]{:S(2)}) collective-permute-start(f32[1,32,256]{2,1,0:T(8,128)S(1)} %get-tuple-element.14), channel_id=1, source_target_pairs={{0,4},{1,5},{2,6},{3,7},{4,0},{5,1},{6,2},{7,3},{8,12},{9,13},{10,... | collective-permute-start | bytes 98312 | tf_op jit(solution)/shard_map/ppermute | solution.py:15
  16.1 16.6 %all-to-all-start = ((f32[8,18,96]{2,1,0:T(8,128)}), f32[8,18,96]{2,1,0:T(8,128)S(1)}, u32[]{:S(2)}, u32[]{:S(2)}) async-start(f32[8,18,96]{2,1,0:T(8,128)} %pad_maximum_fusion.10), calls=%async_computation | async-start | bytes 196608 | tf_op jit(solution)/shard_map/all_to_all | solution.py:87
  28.4 12.4 %collective-permute-start.1 = (f32[2,32,256]{2,1,0:T(8,128)}, f32[2,32,256]{2,1,0:T(8,128)}, u32[]{:S(2)}, u32[]{:S(2)}) collective-permute-start(f32[2,32,256]{2,1,0:T(8,128)} %pad_maximum_fusion.11), channel_id=1, source_target_pairs={{0,2},{1,3},{2,0},{3,1},{4,6},{5,7},{6,4},{7,5},{8,10},{9,11},{10,... | collective-permute-start | bytes 196616 | tf_op jit(solution)/shard_map/ppermute | solution.py:15
  30.0 16.6 %collective-permute-start.4 = (f32[2,64,256]{2,1,0:T(8,128)}, f32[2,64,256]{2,1,0:T(8,128)}, u32[]{:S(2)}, u32[]{:S(2)}) collective-permute-start(f32[2,64,256]{2,1,0:T(8,128)} %pad_maximum_fusion.8), channel_id=1, source_target_pairs={{0,2},{1,3},{2,0},{3,1},{4,6},{5,7},{6,4},{7,5},{8,10},{9,11},{10,... | collective-permute-start | bytes 393224 | tf_op jit(solution)/shard_map/ppermute | solution.py:15
  31.8 15.9 %collective-permute-start.8 = (f32[2,64,256]{2,1,0:T(8,128)}, f32[2,64,256]{2,1,0:T(8,128)}, u32[]{:S(2)}, u32[]{:S(2)}) collective-permute-start(f32[2,64,256]{2,1,0:T(8,128)} %pad_maximum_fusion.9), channel_id=1, source_target_pairs={{0,2},{1,3},{2,0},{3,1},{4,6},{5,7},{6,4},{7,5},{8,10},{9,11},{10,... | collective-permute-start | bytes 393224 | tf_op jit(solution)/shard_map/ppermute | solution.py:15
  32.7 32.3 %all-to-all-start.1 = ((f32[8,16,512]{2,1,0:T(8,128)}), f32[8,16,512]{2,1,0:T(8,128)S(1)}, u32[]{:S(2)}, u32[]{:S(2)}) async-start(f32[8,16,512]{2,1,0:T(8,128)} %fusion.3), calls=%async_computation.1 | async-start | bytes 524288 | tf_op jit(solution)/shard_map/all_to_all | solution.py:118
  41.6 9.0 %collective-permute-start.2 = (f32[4,32,256]{2,1,0:T(8,128)S(1)}, f32[4,32,256]{2,1,0:T(8,128)S(1)}, u32[]{:S(2)}, u32[]{:S(2)}) collective-permute-start(f32[4,32,256]{2,1,0:T(8,128)S(1)} %pad_maximum_fusion.7), channel_id=1, source_target_pairs={{0,1},{1,0},{2,3},{3,2},{4,5},{5,4},{6,7},{7,6},{8,9},{9,8},{10,11... | collective-permute-start | bytes 393224 | tf_op jit(solution)/shard_map/ppermute | solution.py:15
  43.8 9.5 %collective-permute-start.12 = (f32[2,128,256]{2,1,0:T(8,128)S(1)}, f32[2,128,256]{2,1,0:T(8,128)S(1)}, u32[]{:S(2)}, u32[]{:S(2)}) collective-permute-start(f32[2,128,256]{2,1,0:T(8,128)S(1)} %pad_maximum_fusion.5), channel_id=1, source_target_pairs={{0,2},{1,3},{2,0},{3,1},{4,6},{5,7},{6,4},{7,5},{8,10},{9,11},{10,... | collective-permute-start | bytes 786440 | tf_op jit(solution)/shard_map/ppermute | solution.py:15
  46.0 29.6 %collective-permute-start.18 = (f32[2,128,256]{2,1,0:T(8,128)}, f32[2,128,256]{2,1,0:T(8,128)}, u32[]{:S(2)}, u32[]{:S(2)}) collective-permute-start(f32[2,128,256]{2,1,0:T(8,128)} %pad_maximum_fusion.6), channel_id=1, source_target_pairs={{0,2},{1,3},{2,0},{3,1},{4,6},{5,7},{6,4},{7,5},{8,10},{9,11},{10,... | collective-permute-start | bytes 786440 | tf_op jit(solution)/shard_map/ppermute | solution.py:15
  47.6 9.3 %collective-permute-start.5 = (f32[4,64,256]{2,1,0:T(8,128)S(1)}, f32[4,64,256]{2,1,0:T(8,128)S(1)}, u32[]{:S(2)}, u32[]{:S(2)}) collective-permute-start(f32[4,64,256]{2,1,0:T(8,128)S(1)} %pad_maximum_fusion.3), channel_id=1, source_target_pairs={{0,1},{1,0},{2,3},{3,2},{4,5},{5,4},{6,7},{7,6},{8,9},{9,8},{10,11... | collective-permute-start | bytes 786440 | tf_op jit(solution)/shard_map/ppermute | solution.py:15
  48.6 13.9 %collective-permute-start.9 = (f32[4,64,256]{2,1,0:T(8,128)S(1)}, f32[4,64,256]{2,1,0:T(8,128)S(1)}, u32[]{:S(2)}, u32[]{:S(2)}) collective-permute-start(f32[4,64,256]{2,1,0:T(8,128)S(1)} %pad_maximum_fusion.4), channel_id=1, source_target_pairs={{0,1},{1,0},{2,3},{3,2},{4,5},{5,4},{6,7},{7,6},{8,9},{9,8},{10,11... | collective-permute-start | bytes 786440 | tf_op jit(solution)/shard_map/ppermute | solution.py:15
  54.1 22.7 %collective-permute-start.13 = (f32[4,128,256]{2,1,0:T(8,128)}, f32[4,128,256]{2,1,0:T(8,128)}, u32[]{:S(2)}, u32[]{:S(2)}) collective-permute-start(f32[4,128,256]{2,1,0:T(8,128)} %pad_maximum_fusion), channel_id=1, source_target_pairs={{0,1},{1,0},{2,3},{3,2},{4,5},{5,4},{6,7},{7,6},{8,9},{9,8},{10,11... | collective-permute-start | bytes 1572872 | tf_op jit(solution)/shard_map/ppermute | solution.py:15
  73.9 1.3 collective-permute-start.6
  75.5 1.3 collective-permute-start.10
  76.7 14.2 %collective-permute-start.19 = (f32[4,128,256]{2,1,0:T(8,128)S(1)}, f32[4,128,256]{2,1,0:T(8,128)S(1)}, u32[]{:S(2)}, u32[]{:S(2)}) collective-permute-start(f32[4,128,256]{2,1,0:T(8,128)S(1)} %pad_maximum_fusion.1), channel_id=1, source_target_pairs={{0,1},{1,0},{2,3},{3,2},{4,5},{5,4},{6,7},{7,6},{8,9},{9,8},{10,11... | collective-permute-start | bytes 1572872 | tf_op jit(solution)/shard_map/ppermute | solution.py:15
  94.4 4.4 %collective-permute-start.16 = (f32[16,1024]{1,0:T(8,128)S(1)}, f32[16,1024]{1,0:T(8,128)S(1)}, u32[]{:S(2)}, u32[]{:S(2)}) collective-permute-start(f32[16,1024]{1,0:T(8,128)S(1)} %fusion.1), channel_id=1, source_target_pairs={{0,24},{8,16},{16,8},{24,0},{1,25},{9,17},{17,9},{25,1},{2,26},{10... | collective-permute-start | bytes 196616 | tf_op jit(solution)/shard_map/ppermute | solution.py:15
  95.1 5.2 %collective-permute-start.15 = (f32[16,1024]{1,0:T(8,128)S(1)}, f32[16,1024]{1,0:T(8,128)S(1)}, u32[]{:S(2)}, u32[]{:S(2)}) collective-permute-start(f32[16,1024]{1,0:T(8,128)S(1)} %fusion.1), channel_id=1, source_target_pairs={{0,16},{8,24},{16,0},{24,8},{1,17},{9,25},{17,1},{25,9},{2,18},{10... | collective-permute-start | bytes 196616 | tf_op jit(solution)/shard_map/ppermute | solution.py:15
  96.1 4.2 %collective-permute-start.14 = (f32[16,1024]{1,0:T(8,128)S(1)}, f32[16,1024]{1,0:T(8,128)S(1)}, u32[]{:S(2)}, u32[]{:S(2)}) collective-permute-start(f32[16,1024]{1,0:T(8,128)S(1)} %fusion.1), channel_id=1, source_target_pairs={{0,8},{8,0},{16,24},{24,16},{1,9},{9,1},{17,25},{25,17},{2,10},{10... | collective-permute-start | bytes 196616 | tf_op jit(solution)/shard_map/ppermute | solution.py:15
  100.8 4.2 %collective-permute-start.22 = (f32[16,1024]{1,0:T(8,128)S(1)}, f32[16,1024]{1,0:T(8,128)S(1)}, u32[]{:S(2)}, u32[]{:S(2)}) collective-permute-start(f32[16,1024]{1,0:T(8,128)S(1)} %fusion.56), channel_id=1, source_target_pairs={{0,24},{8,16},{16,8},{24,0},{1,25},{9,17},{17,9},{25,1},{2,26},{10... | collective-permute-start | bytes 196616 | tf_op jit(solution)/shard_map/ppermute | solution.py:15
  101.5 5.1 %collective-permute-start.21 = (f32[16,1024]{1,0:T(8,128)S(1)}, f32[16,1024]{1,0:T(8,128)S(1)}, u32[]{:S(2)}, u32[]{:S(2)}) collective-permute-start(f32[16,1024]{1,0:T(8,128)S(1)} %fusion.56), channel_id=1, source_target_pairs={{0,16},{8,24},{16,0},{24,8},{1,17},{9,25},{17,1},{25,9},{2,18},{10... | collective-permute-start | bytes 196616 | tf_op jit(solution)/shard_map/ppermute | solution.py:15
  102.6 4.1 %collective-permute-start.20 = (f32[16,1024]{1,0:T(8,128)S(1)}, f32[16,1024]{1,0:T(8,128)S(1)}, u32[]{:S(2)}, u32[]{:S(2)}) collective-permute-start(f32[16,1024]{1,0:T(8,128)S(1)} %fusion.56), channel_id=1, source_target_pairs={{0,8},{8,0},{16,24},{24,16},{1,9},{9,1},{17,25},{25,17},{2,10},{10... | collective-permute-start | bytes 196616 | tf_op jit(solution)/shard_map/ppermute | solution.py:15
  106.7 3.4 %collective-permute-start.25 = (f32[16,256]{1,0:T(8,128)S(1)}, f32[16,256]{1,0:T(8,128)S(1)}, u32[]{:S(2)}, u32[]{:S(2)}) collective-permute-start(f32[16,256]{1,0:T(8,128)S(1)} %fusion.47), channel_id=1, source_target_pairs={{0,24},{8,16},{16,8},{24,0},{1,25},{9,17},{17,9},{25,1},{2,26},{10... | collective-permute-start | bytes 49160 | tf_op jit(solution)/shard_map/ppermute | solution.py:15
  107.1 3.7 %collective-permute-start.24 = (f32[16,256]{1,0:T(8,128)S(1)}, f32[16,256]{1,0:T(8,128)S(1)}, u32[]{:S(2)}, u32[]{:S(2)}) collective-permute-start(f32[16,256]{1,0:T(8,128)S(1)} %fusion.47), channel_id=1, source_target_pairs={{0,16},{8,24},{16,0},{24,8},{1,17},{9,25},{17,1},{25,9},{2,18},{10... | collective-permute-start | bytes 49160 | tf_op jit(solution)/shard_map/ppermute | solution.py:15
  108.2 2.6 %collective-permute-start.23 = (f32[16,256]{1,0:T(8,128)S(1)}, f32[16,256]{1,0:T(8,128)S(1)}, u32[]{:S(2)}, u32[]{:S(2)}) collective-permute-start(f32[16,256]{1,0:T(8,128)S(1)} %fusion.47), channel_id=1, source_target_pairs={{0,8},{8,0},{16,24},{24,16},{1,9},{9,1},{17,25},{25,17},{2,10},{10... | collective-permute-start | bytes 49160 | tf_op jit(solution)/shard_map/ppermute | solution.py:15
  111.2 3.2 %collective-permute-start.28 = (f32[16,256]{1,0:T(8,128)S(1)}, f32[16,256]{1,0:T(8,128)S(1)}, u32[]{:S(2)}, u32[]{:S(2)}) collective-permute-start(f32[16,256]{1,0:T(8,128)S(1)} %convolution_add_fusion.4), channel_id=1, source_target_pairs={{0,24},{8,16},{16,8},{24,0},{1,25},{9,17},{17,9},{25,1},{2,26},{10... | collective-permute-start | bytes 49160 | tf_op jit(solution)/shard_map/ppermute | solution.py:15
  111.5 3.9 %collective-permute-start.27 = (f32[16,256]{1,0:T(8,128)S(1)}, f32[16,256]{1,0:T(8,128)S(1)}, u32[]{:S(2)}, u32[]{:S(2)}) collective-permute-start(f32[16,256]{1,0:T(8,128)S(1)} %convolution_add_fusion.4), channel_id=1, source_target_pairs={{0,16},{8,24},{16,0},{24,8},{1,17},{9,25},{17,1},{25,9},{2,18},{10... | collective-permute-start | bytes 49160 | tf_op jit(solution)/shard_map/ppermute | solution.py:15
  112.5 2.9 %collective-permute-start.26 = (f32[16,256]{1,0:T(8,128)S(1)}, f32[16,256]{1,0:T(8,128)S(1)}, u32[]{:S(2)}, u32[]{:S(2)}) collective-permute-start(f32[16,256]{1,0:T(8,128)S(1)} %convolution_add_fusion.4), channel_id=1, source_target_pairs={{0,8},{8,0},{16,24},{24,16},{1,9},{9,1},{17,25},{25,17},{2,10},{10... | collective-permute-start | bytes 49160 | tf_op jit(solution)/shard_map/ppermute | solution.py:15
  117.9 1.3 collective-permute-start.30
  (44 other events, 148.2 us)

commit v2 on v1

v2 whole, which is shorter than its diff:
```python
import jax
import jax.numpy as jnp
from jax import lax
from jax.experimental import pallas as pl
from jax.experimental.pallas import tpu as pltpu
from jax.sharding import PartitionSpec as P

TILE = 128
EXACT = lax.Precision.HIGHEST
F32 = jnp.float32
BF16 = jnp.bfloat16


def swap(value, axis, count, offset):
    return lax.ppermute(value, axis, [(i, i ^ offset) for i in range(count)])


def gather_parts(block, count):
    parts = {0: block}
    step = count // 2
    while step:
        for offset in list(parts):
            parts[offset ^ step] = swap(parts[offset], "row", count, step)
        step //= 2
    return [parts[offset] for offset in range(count)]


def call(body, outs, arrays, scalars=(), scratch=()):
    return pl.pallas_call(
        body,
        out_shape=[jax.ShapeDtypeStruct(*o) for o in outs],
        in_specs=[pl.BlockSpec(memory_space=pltpu.SMEM)] * len(scalars)
        + [pl.BlockSpec(memory_space=pltpu.VMEM)] * len(arrays),
        out_specs=[pl.BlockSpec(memory_space=pltpu.VMEM)] * len(outs),
        scratch_shapes=list(scratch),
        compiler_params=pltpu.CompilerParams(vmem_limit_bytes=40 << 20),
    )(*scalars, *arrays)


def split(value):
    high = value.astype(BF16).astype(F32)
    return high, value - high


def times(value, high, low, right_dim):
    rows = value.shape[0]
    dims = (((1,), (right_dim,)), ((), ()))

    def product(part):
        return lax.dot_general(part, high, dims, preferred_element_type=F32) + lax.dot_general(
            part, low, dims, preferred_element_type=F32
        )

    first, second = split(value)
    if rows % 8:
        return product(first.astype(BF16)) + product(second.astype(BF16))
    both = product(jnp.concatenate([first, second], 0).astype(BF16))
    return both[:rows] + both[rows:]


def strict_lower(block):
    row_ids = lax.broadcasted_iota(jnp.int32, block.shape, 0)
    col_ids = lax.broadcasted_iota(jnp.int32, block.shape, 1)
    return jnp.where(col_ids < row_ids, block, 0.0)


def shards(
    loc_rhs,
    loc_inverse,
    loc_coupling,
    loc_pivots,
    pattern,
    win_rhs,
    win_pivots,
    win_inverse,
    win_coupling,
):
    leaves = lax.axis_size("leaf")
    ranks = lax.axis_size("row")
    leaf = lax.axis_index("leaf")
    rank = lax.axis_index("row")
    levels, piece, columns = win_rhs.shape
    base = piece * ranks
    share = columns // ranks
    halves = base // TILE
    path_tiles = (2 * leaves - 1) * halves
    tiles = pattern.shape[2]
    local = loc_rhs.shape[2]
    top = levels - 1
    ids = jnp.stack([leaf, rank]).astype(jnp.int32)
    wide = (share, base)

    def leaf_swaps(values):
        return [values[0]] + [swap(v, "leaf", leaves, j) for j, v in enumerate(values) if j]

    def inverse_rows(level):
        return (2**level - 1) * piece, (2 ** (level + 1) - 1) * piece

    def coupling_rows(level):
        return (2 ** (level + 1) - 2) * piece, (2 ** (level + 2) - 2) * piece

    def gathered(names):
        rows = []
        for kind, level in names:
            source = win_inverse if kind == "A" else win_coupling
            low, high = inverse_rows(level) if kind == "A" else coupling_rows(level)
            rows.append(source[0, low:high])
        return gather_parts(jnp.concatenate(rows, 0), ranks)

    def assemble(parts, names):
        spans = [2**level if kind == "A" else 2 ** (level + 1) for kind, level in names]

        def body(ids_ref, *refs):
            parts_refs, outs = refs[:ranks], refs[ranks:-1]
            natural = refs[-1]
            me, group = ids_ref[1], ids_ref[0]
            for offset, ref in enumerate(parts_refs):
                start = pl.multiple_of((me ^ offset) * piece, 8)
                for slot in range(sum(spans)):
                    natural[slot, pl.ds(start, piece), :] = ref[
                        slot * piece : (slot + 1) * piece, :
                    ]
            first = 0
            for index, ((kind, level), span) in enumerate(zip(names, spans)):
                for slot in range(span):
                    block = natural[first + slot]
                    if kind == "A":
                        row_ids = lax.broadcasted_iota(jnp.int32, block.shape, 0) + slot * base
                        col_ids = lax.broadcasted_iota(jnp.int32, block.shape, 1)
                        col_ids = col_ids + group % span * base
                        block = jnp.where(col_ids < row_ids, block, 0.0)
                    high, low = split(block)
                    outs[2 * index][slot] = high.astype(BF16)
                    outs[2 * index + 1][slot] = low.astype(BF16)
                first += span

        outs = [((span, base, base), BF16) for span in spans for _ in range(2)]
        made = call(
            body, outs, parts, (ids,), [pltpu.VMEM((sum(spans), base, base), F32)]
        )
        return {name: made[2 * i : 2 * i + 2] for i, name in enumerate(names)}

    lower_names = [("A", level) for level in range(top)]
    lower_names += [("B", level) for level in range(top - 1)]
    upper_names = [("B", top - 1), ("A", top)]
    lower_parts = gathered(lower_names)
    upper_parts = gathered(upper_names)

    def local_forward(rhs_ref, inverse_ref, coupling_ref, solved_ref, terms_ref):
        rhs = rhs_ref[...]
        solved = rhs + jnp.dot(strict_lower(inverse_ref[...]), rhs, precision=EXACT)
        solved_ref[...] = solved.T
        terms_ref[...] = jnp.dot(coupling_ref[...], solved, precision=EXACT).T

    solved_loc, terms = call(
        local_forward,
        [((columns, local), F32), ((columns, tiles * TILE), F32)],
        (loc_rhs[0, 0], loc_inverse[0, 0], loc_coupling[0, 0]),
    )
    terms = lax.all_to_all(
        terms.reshape(ranks, share, tiles * TILE), "row", 0, 0, tiled=True
    )

    extra = jnp.pad(pattern[0].astype(F32), ((0, 0), (0, levels * piece - tiles)))
    early = jnp.concatenate(
        [
            win_rhs.transpose(2, 0, 1).reshape(ranks, share, levels * piece),
            jnp.broadcast_to(win_pivots.reshape(1, 1, -1), (ranks, 1, levels * piece)),
            jnp.broadcast_to(extra, (ranks, 1, levels * piece)),
        ],
        1,
    )
    early = lax.all_to_all(early, "row", 0, 0, tiled=True)
    known = early[:, share + 1, :tiles].astype(jnp.int32).reshape(-1)
    early = early[:, : share + 1].reshape(ranks, share + 1, levels, piece)
    early = early.transpose(2, 1, 0, 3).reshape(levels, share + 1, base)
    rhs, pivots = early[:, :share], early[:, share:]
    top_pivots = leaf_swaps([pivots[top]] * leaves)

    lower = assemble(lower_parts, lower_names)
    upper = assemble(upper_parts, upper_names)
    blocks = {**lower, **upper}

    def scatter(ids_ref, known_ref, terms_ref, rhs_ref, *refs):
        outs, path = refs[:-1], refs[-1]
        path[...] = jnp.zeros_like(path)
        for source in range(ranks):
            for tile in range(tiles):
                place = known_ref[source * tiles + tile]
                path[place] = path[place] - terms_ref[source, :, tile * TILE : (tile + 1) * TILE]
        for level in range(levels):
            span = 2**level
            for slot in range(span):
                first = (span - 1 + slot) * halves
                outs[level][slot] = jnp.concatenate([path[first + h] for h in range(halves)], 1)
            own = ids_ref[0] % span
            outs[level][own] = outs[level][own] + rhs_ref[level]

    rest = call(
        scatter,
        [((2**level, *wide), F32) for level in range(levels)],
        (terms, rhs),
        (ids, known),
        [pltpu.VMEM((path_tiles, share, TILE), F32)],
    )

    def total(refs):
        value = refs[0][...]
        for ref in refs[1:]:
            value = value + ref[...]
        return value

    def diagonal(level, chunks):
        span = 2**level
        high, low = blocks["A", level]

        def body(ids_ref, *refs):
            chunk_refs, (high_ref, low_ref) = refs[:span], refs[span : span + 2]
            outs, parts = refs[span + 2 : -1], refs[-1]
            own = ids_ref[0] % span
            value = total(chunk_refs)
            for slot in range(span):
                parts[slot] = times(value, high_ref[slot], low_ref[slot], 1)
            parts[own] = parts[own] + value
            if level == top:
                outs[0][...] = parts[...]
            else:
                for offset, out in enumerate(outs):
                    out[...] = parts[own ^ offset]

        outs = [((span, *wide), F32)] if level == top else [(wide, F32)] * span
        return call(
            body, outs, (*chunks, high, low), (ids,), [pltpu.VMEM((span, *wide), F32)]
        )

    def link(level, chunks):
        span, above = 2**level, 2 ** (level + 1)
        high, low = blocks["B", level]

        def body(ids_ref, *refs):
            chunk_refs = refs[:span]
            high_ref, low_ref, rest_ref, solved_ref = refs[span : span + 4]
            outs, parts = refs[span + 4 : -1], refs[-1]
            value = total(chunk_refs)
            solved_ref[...] = value
            for slot in range(above):
                parts[slot] = rest_ref[slot] - times(value, high_ref[slot], low_ref[slot], 1)
            own = ids_ref[0] % above
            for offset, out in enumerate(outs):
                out[...] = parts[own ^ offset]

        made = call(
            body,
            [(wide, F32)] * (above + 1),
            (*chunks, high, low, rest[level + 1]),
            (ids,),
            [pltpu.VMEM((above, *wide), F32)],
        )
        return made[0], made[1:]

    chunks = [rest[0][0]]
    solved = []
    for level in range(top):
        chunks = leaf_swaps(diagonal(level, chunks))
        value, chunks = link(level, chunks)
        solved.append(value)
        chunks = leaf_swaps(chunks)
    sums = leaf_swaps(diagonal(top, chunks) * leaves)

    def peak(ids_ref, *refs):
        sum_refs, pivot_refs = refs[:leaves], refs[leaves : 2 * leaves]
        high_ref, low_ref, out, wanted = refs[2 * leaves :]
        own = ids_ref[0] % leaves
        wanted[...] = total(sum_refs)
        for offset, ref in enumerate(pivot_refs):
            wanted[own ^ offset] = wanted[own ^ offset] / ref[...]
        value = wanted[own]
        for slot in range(leaves):
            value = value + times(wanted[slot], high_ref[slot], low_ref[slot], 0)
        out[...] = value

    current = call(
        peak,
        [(wide, F32)],
        (*sums, *top_pivots, *blocks["A", top]),
        (ids,),
        [pltpu.VMEM((leaves, *wide), F32)],
    )

    def ordered(own, refs, held):
        for offset, ref in enumerate(refs):
            held[own ^ offset] = ref[...]

    def against(held, high_ref, low_ref, span):
        value = times(held[0], high_ref[0], low_ref[0], 0)
        for slot in range(1, span):
            value = value + times(held[slot], high_ref[slot], low_ref[slot], 0)
        return value

    def descend(level, parts):
        span = 2**level

        def body(ids_ref, *refs):
            part_refs = refs[:span]
            high_ref, low_ref, solved_ref, pivot_ref, out, held = refs[span:]
            ordered(ids_ref[0] % span, part_refs, held)
            above = against(held, high_ref, low_ref, span)
            out[...] = solved_ref[...] / pivot_ref[...] - above

        return call(
            body,
            [(wide, F32)],
            (*parts, *blocks["B", level - 1], solved[level - 1], pivots[level - 1]),
            (ids,),
            [pltpu.VMEM((span, *wide), F32)],
        )

    def transposed(level, parts):
        span = 2**level

        def body(ids_ref, *refs):
            part_refs = refs[:span]
            high_ref, low_ref, out, held = refs[span:]
            ordered(ids_ref[0] % span, part_refs, held)
            out[...] = part_refs[0][...] + against(held, high_ref, low_ref, span)

        return call(
            body,
            [(wide, F32)],
            (*parts, *blocks["A", level]),
            (ids,),
            [pltpu.VMEM((span, *wide), F32)],
        )

    everything = {top: leaf_swaps(current * leaves)}
    for level in range(top, 1, -1):
        wanted = leaf_swaps(descend(level, everything[level]) * 2 ** (level - 1))
        everything[level - 1] = leaf_swaps(transposed(level - 1, wanted) * 2 ** (level - 1))

    packed = tiles * TILE + TILE

    def finish(ids_ref, known_ref, *refs):
        refs = list(refs)
        parts = {level: [refs.pop(0) for _ in range(2**level)] for level in range(1, levels)}
        link_high, link_low, solved_ref, pivot_ref, high_ref, low_ref = refs[:6]
        outs, path, held = refs[6:-2], refs[-2], refs[-1]
        group, me = ids_ref[0], ids_ref[1]
        ordered(group % 2, parts[1], held)
        wanted = solved_ref[...] / pivot_ref[...] - against(held, link_high, link_low, 2)
        lowest = wanted + times(wanted, high_ref[0], low_ref[0], 0)
        owned = [lowest]
        for half in range(halves):
            path[half] = lowest[:, half * TILE : (half + 1) * TILE]
        for level in range(1, levels):
            span = 2**level
            owned.append(parts[level][0][...])
            for offset, ref in enumerate(parts[level]):
                first = (span - 1 + (group % span ^ offset)) * halves
                for half in range(halves):
                    path[first + half] = ref[:, half * TILE : (half + 1) * TILE]
        lane = lax.broadcasted_iota(jnp.int32, (share, TILE), 1)
        for offset, out in enumerate(outs):
            target = me ^ offset
            for tile in range(tiles):
                out[:, tile * TILE : (tile + 1) * TILE] = path[known_ref[target * tiles + tile]]
            pieces = jnp.zeros((share, TILE), F32)
            for level in range(levels):
                shift = (base + level * piece - target * piece) % base
                turned = pltpu.roll(owned[level], shift, 1)[:, :TILE]
                mine = (lane >= level * piece) & (lane < (level + 1) * piece)
                pieces = jnp.where(mine, turned, pieces)
            out[:, tiles * TILE :] = pieces

    replies = call(
        finish,
        [((share, packed), F32)] * ranks,
        (
            *[part for level in range(1, levels) for part in everything[level]],
            *blocks["B", 0],
            solved[0],
            pivots[0],
            *blocks["A", 0],
        ),
        (ids, known),
        [pltpu.VMEM((path_tiles, share, TILE), F32), pltpu.VMEM((2, *wide), F32)],
    )
    replies = [replies[0]] + [swap(v, "row", ranks, j) for j, v in enumerate(replies) if j]
    if share % 8:
        stacked = jnp.stack(replies)[rank ^ jnp.arange(ranks)]
        replies = [stacked.reshape(columns, packed)]

    def local_backward(ids_ref, *refs):
        refs = list(refs)
        reply_refs = [refs.pop(0) for _ in replies]
        solved_ref, pivot_ref, inverse_ref, coupling_ref, out, window_ref, back = refs
        me = ids_ref[1]
        if len(reply_refs) == 1:
            back[...] = reply_refs[0][...]
        else:
            for offset, ref in enumerate(reply_refs):
                start = pl.multiple_of((me ^ offset) * share, 8)
                back[pl.ds(start, share), :] = ref[...]
        remainder = solved_ref[...] / pivot_ref[...] - jnp.dot(
            back[:, : tiles * TILE], coupling_ref[...], precision=EXACT
        )
        answer = remainder + jnp.dot(
            remainder, strict_lower(inverse_ref[...]), precision=EXACT
        )
        out[...] = answer.T
        final = back[:, tiles * TILE :].T
        for level in range(levels):
            window_ref[level] = final[level * piece : (level + 1) * piece]

    answer, window = call(
        local_backward,
        [((local, columns), F32), ((levels, piece, columns), F32)],
        (*replies, solved_loc, loc_pivots[0], loc_inverse[0, 0], loc_coupling[0, 0]),
        (ids,),
        [pltpu.VMEM((columns, packed), F32)],
    )
    return answer[None, None], window


def solution(mesh):
    return jax.shard_map(
        shards,
        mesh=mesh,
        in_specs=(
            P("leaf", "row", None, None),
            P("leaf", "row", None, None),
            P("leaf", "row", None, None),
            P("leaf", "row", None),
            P("leaf", "row", None),
            P(None, ("leaf", "row"), None),
            P(None, ("leaf", "row")),
            P("row", None, "leaf"),
            P("row", None, "leaf"),
        ),
        out_specs=(P("leaf", "row", None, None), P(None, ("leaf", "row"), None)),
        check_vma=False,
    )
```

time: 143 us -> 128 us (0.90); the launches traced: 141 us -> 128 us
  local copies, waits for them, and re-layouts: 35.9 us -> 12.8 us
  Pallas kernels: 0 us -> 18 us
  blocking collectives: 15.7 us -> 0 us
  waiting for transfers between devices: 30.7 us -> 44.6 us
  starting transfers between devices: 36.5 us -> 50 us
  other arithmetic: 11 us -> 1.55 us
  matrix products: 9.4 us -> 0 us
    unnamed x155 -> x26, local copies, waits for them, and re-layouts: 22.5 us -> 3.02 us
    pallas_call x0 -> x14, Pallas kernels: none -> 18 us  [call(): pl.pallas_call(body, out_shape=[jax.ShapeDtypeStruct(*o) for o in outs],...]
    all_to_all x1 -> x0, blocking collectives: 15.7 us -> none  [shards(): lax.all_to_all(jnp.concatenate([reply, final], 2), 'row', 0, 0, tiled=True)]
    ppermute x31 -> x37, waiting for transfers between devices: 30.7 us -> 44.5 us  [swap(): return lax.ppermute(value, axis, [(i, i ^ offset) for i in range(count)])]
    ppermute x31 -> x37, starting transfers between devices: 27.7 us -> 39.5 us  [swap(): return lax.ppermute(value, axis, [(i, i ^ offset) for i in range(count)])]
    dot_general x16 -> x0, matrix products: 9.4 us -> none  [the longest x14 7.97 us: dot(): lax.dot_general(left, right, (((left_dim,), (right_dim,)), ((), ())), pre...]
    another operation x13 -> x1, other arithmetic: 8.03 us -> 0.07 us  [shards(): ids = jnp.stack([leaf, rank]).astype(jnp.int32)]
    slice x9 -> x1, local copies, waits for them, and re-layouts: 7.22 us -> 0.8 us  [shards(): rhs, pivots = (early[:, :share], early[:, share:])]
  transfers between devices with their start and end apart: 33 -> 39, of which waited for: 15 -> 17; matrix products, arithmetic and copies ran while one was open for 29% -> 8% of each run, Pallas kernels for 0% -> 8%
where the time goes in v2:
time: 128 us
  starting transfers between devices  50 us (39%)
  waiting for transfers between devices  44.6 us (35%)
  Pallas kernels  18 us (14%)
  local copies, waits for them, and re-layouts  12.8 us (10%)
  other arithmetic  1.55 us (1%)
    ppermute x37, waiting for transfers between devices, swap(): return lax.ppermute(value, axis, [(i, i ^ offset) for i in range(count)])  44.5 us
    ppermute x37, starting transfers between devices, swap(): return lax.ppermute(value, axis, [(i, i ^ offset) for i in range(count)])  39.5 us
    pallas_call x14, Pallas kernels, call(): pl.pallas_call(body, out_shape=[jax.ShapeDtypeStruct(*o) for o in outs],...  18 us
    all_to_all x1, starting transfers between devices, shards(): lax.all_to_all(terms.reshape(ranks, share, tiles * TILE), 'row', 0, 0, ti...  5.66 us
    all_to_all x1, starting transfers between devices, shards(): early = lax.all_to_all(early, 'row', 0, 0, tiled=True)  4.82 us
    unnamed x26, local copies, waits for them, and re-layouts  3.02 us
    squeeze x3, local copies, waits for them, and re-layouts, gathered(): rows.append(source[0, low:high])  2.61 us
  transfers between devices with their start and end apart: 39, of which 17 were waited for; matrix products, arithmetic and copies ran while one was open for 8% of the time, Pallas kernels for 8%

profile of v2, /device:TPU:0, one launch (start us, length us, event | category | flops | bytes accessed | tf_op | source)
XLA Modules:
  0.0 127.7 jit_solution(13084337653127795735)
XLA Ops:
  2.4 4.1 %collective-permute-start.3 = (f32[160,256]{1,0:T(8,128)S(1)}, f32[160,256]{1,0:T(8,128)S(1)}, u32[]{:S(2)}, u32[]{:S(2)}) collective-permute-start(f32[160,256]{1,0:T(8,128)S(1)} %pad_maximum_fusion.1.refs_0_), channel_id=1, source_target_pairs={{0,4},{1,5},{2,6},{3,7},{4,0},{5,1},{6,2},{7,3},{8,12},{9,13},{10,... | collective-permute-start | bytes 491528 | tf_op jit(solution)/shard_map/ppermute | solution.py:15
  6.5 1.6 %collective-permute-start.1 = (f32[160,256]{1,0:T(8,128)S(1)}, f32[160,256]{1,0:T(8,128)}, u32[]{:S(2)}, u32[]{:S(2)}) collective-permute-start(f32[160,256]{1,0:T(8,128)S(1)} %pad_maximum_fusion.1.refs_0_), channel_id=1, source_target_pairs={{0,2},{1,3},{2,0},{3,1},{4,6},{5,7},{6,4},{7,5},{8,10},{9,11},{10,... | collective-permute-start | bytes 491528 | tf_op jit(solution)/shard_map/ppermute | solution.py:15
  10.5 4.8 %all-to-all-start = ((f32[8,18,96]{2,1,0:T(8,128)}), f32[8,18,96]{2,1,0:T(8,128)}, u32[]{:S(2)}, u32[]{:S(2)}) async-start(f32[8,18,96]{2,1,0:T(8,128)} %pad_maximum_fusion.2), calls=%async_computation | async-start | bytes 196608 | tf_op jit(solution)/shard_map/all_to_all | solution.py:173
  15.4 2.0 %collective-permute-start = (f32[160,256]{1,0:T(8,128)S(1)}, f32[160,256]{1,0:T(8,128)}, u32[]{:S(2)}, u32[]{:S(2)}) collective-permute-start(f32[160,256]{1,0:T(8,128)S(1)} %pad_maximum_fusion.1.refs_0_), channel_id=1, source_target_pairs={{0,1},{1,0},{2,3},{3,2},{4,5},{5,4},{6,7},{7,6},{8,9},{9,8},{10,11... | collective-permute-start | bytes 491528 | tf_op jit(solution)/shard_map/ppermute | solution.py:15
  17.4 1.5 %collective-permute-start.10 = (f32[256,256]{1,0:T(8,128)S(1)}, f32[256,256]{1,0:T(8,128)}, u32[]{:S(2)}, u32[]{:S(2)}) collective-permute-start(f32[256,256]{1,0:T(8,128)S(1)} %pad_maximum_fusion.refs_0_), channel_id=1, source_target_pairs={{0,2},{1,3},{2,0},{3,1},{4,6},{5,7},{6,4},{7,5},{8,10},{9,11},{10,... | collective-permute-start | bytes 786440 | tf_op jit(solution)/shard_map/ppermute | solution.py:15
  18.8 8.3 %collective-permute-done.12.refs_4_ = f32[256,256]{1,0:T(8,128)S(1)} collective-permute-done((f32[256,256]{1,0:T(8,128)S(1)}, f32[256,256]{1,0:T(8,128)S(1)}, u32[]{:S(2)}, u32[]{:S(2)}) %collective-permute-start.12) | collective-permute-done | bytes 262176 | tf_op jit(solution)/shard_map/ppermute | solution.py:15
  27.4 3.5 %shard_map.104 = (f32[128,512]{1,0:T(8,128)S(1)}, f32[128,512]{1,0:T(8,128)S(1)}) custom-call(f32[512,128]{1,0:T(8,128)S(1)} %bitcast.40, f32[512,512]{1,0:T(8,128)S(1)} %bitcast.36, f32[512,512]{1,0:T(8,128)S(1)} %bitcast.38), custom_call_target="tpu_custom_call" | custom-call | tf_op jit(solution)/shard_map/pallas_call | solution.py:29
  31.6 5.7 %all-to-all-start.1 = ((f32[8,16,512]{2,1,0:T(8,128)}), f32[8,16,512]{2,1,0:T(8,128)S(1)}, u32[]{:S(2)}, u32[]{:S(2)}) async-start(f32[8,16,512]{2,1,0:T(8,128)} %bitcast.41), calls=%async_computation.1 | async-start | bytes 524288 | tf_op jit(solution)/shard_map/all_to_all | solution.py:160
  37.3 2.0 %collective-permute-start.5 = (f32[160,256]{1,0:T(8,128)S(1)}, f32[160,256]{1,0:T(8,128)S(1)}, u32[]{:S(2)}, u32[]{:S(2)}) collective-permute-start(f32[160,256]{1,0:T(8,128)S(1)} %collective-permute-done.3.refs_4_), channel_id=1, source_target_pairs={{0,2},{1,3},{2,0},{3,1},{4,6},{5,7},{6,4},{7,5},{8,10},{9,11},{10,... | collective-permute-start | bytes 491528 | tf_op jit(solution)/shard_map/ppermute | solution.py:15
  39.3 1.5 %collective-permute-start.4 = (f32[160,256]{1,0:T(8,128)S(1)}, f32[160,256]{1,0:T(8,128)S(1)}, u32[]{:S(2)}, u32[]{:S(2)}) collective-permute-start(f32[160,256]{1,0:T(8,128)S(1)} %collective-permute-done.3.refs_4_), channel_id=1, source_target_pairs={{0,1},{1,0},{2,3},{3,2},{4,5},{5,4},{6,7},{7,6},{8,9},{9,8},{10,11... | collective-permute-start | bytes 491528 | tf_op jit(solution)/shard_map/ppermute | solution.py:15
  41.3 1.5 %collective-permute-start.9 = (f32[256,256]{1,0:T(8,128)S(1)}, f32[256,256]{1,0:T(8,128)}, u32[]{:S(2)}, u32[]{:S(2)}) collective-permute-start(f32[256,256]{1,0:T(8,128)S(1)} %pad_maximum_fusion.refs_0_), channel_id=1, source_target_pairs={{0,1},{1,0},{2,3},{3,2},{4,5},{5,4},{6,7},{7,6},{8,9},{9,8},{10,11... | collective-permute-start | bytes 786440 | tf_op jit(solution)/shard_map/ppermute | solution.py:15
  42.8 4.3 %collective-permute-done.5.refs_6_ = f32[160,256]{1,0:T(8,128)S(1)} collective-permute-done((f32[160,256]{1,0:T(8,128)S(1)}, f32[160,256]{1,0:T(8,128)S(1)}, u32[]{:S(2)}, u32[]{:S(2)}) %collective-permute-start.5) | collective-permute-done | bytes 163872 | tf_op jit(solution)/shard_map/ppermute | solution.py:15
  47.1 1.5 %collective-permute-start.13 = (f32[256,256]{1,0:T(8,128)S(1)}, f32[256,256]{1,0:T(8,128)}, u32[]{:S(2)}, u32[]{:S(2)}) collective-permute-start(f32[256,256]{1,0:T(8,128)S(1)} %collective-permute-done.12.refs_4_), channel_id=1, source_target_pairs={{0,1},{1,0},{2,3},{3,2},{4,5},{5,4},{6,7},{7,6},{8,9},{9,8},{10,11... | collective-permute-start | bytes 786440 | tf_op jit(solution)/shard_map/ppermute | solution.py:15
  49.8 1.5 %collective-permute-start.15 = (f32[256,256]{1,0:T(8,128)}, f32[256,256]{1,0:T(8,128)}, u32[]{:S(2)}, u32[]{:S(2)}) collective-permute-start(f32[256,256]{1,0:T(8,128)} %collective-permute-done.14.refs_6_), channel_id=1, source_target_pairs={{0,1},{1,0},{2,3},{3,2},{4,5},{5,4},{6,7},{7,6},{8,9},{9,8},{10,11... | collective-permute-start | bytes 786440 | tf_op jit(solution)/shard_map/ppermute | solution.py:15
  55.1 1.6 %copy.15 = f32[3,17,8,32]{3,2,1,0:T(8,128)} copy(f32[3,17,8,32]{3,0,2,1:T(4,128)} %bitcast.44) | data formatting | bytes 104448 | tf_op jit(solution)/shard_map/transpose | solution.py:176
  56.7 1.7 %reshape.40 = f32[3,17,256]{2,1,0:T(8,128)} reshape(f32[3,17,8,32]{3,2,1,0:T(8,128)} %copy.15) | data formatting | bytes 104448 | tf_op jit(solution)/shard_map/reshape | solution.py:176
  59.9 16.3 %collective-permute-done.6.refs_7_ = f32[160,256]{1,0:T(8,128)} collective-permute-done((f32[160,256]{1,0:T(8,128)}, f32[160,256]{1,0:T(8,128)}, u32[]{:S(2)}, u32[]{:S(2)}) %collective-permute-start.6) | collective-permute-done | bytes 163872 | tf_op jit(solution)/shard_map/ppermute | solution.py:15
  77.1 1.6 %shard_map.106 = (bf16[1,256,256]{2,1,0:T(8,128)(2,1)S(1)}, bf16[1,256,256]{2,1,0:T(8,128)(2,1)S(1)}, bf16[2,256,256]{2,1,0:T(8,128)(2,1)S(1)}, bf16[2,256,256]{...) custom-call(s32[2]{0:T(128)S(1)} %pad_add_fusion.ids_ref, ...), custom_call_target="tpu_custom_call" | custom-call | tf_op jit(solution)/shard_map/pallas_call | solution.py:29
  82.4 2.0 %shard_map.110 = (bf16[4,256,256]{2,1,0:T(8,128)(2,1)S(1)}, bf16[4,256,256]{2,1,0:T(8,128)(2,1)S(1)}, bf16[4,256,256]{2,1,0:T(8,128)(2,1)S(1)}, bf16[4,256,256]{2,1,0:T(8,128)(2,1)S(1)}) custom-call(s32[2]{0:T(128)S(1)} %pad_add_fusion.ids_ref, f32[256,256]{1,0:T(8,128)S(1)} %pad_maximum_fusion.refs_0_, f32[256,256]{1,0:T(8,128)} %collective-permute-done.9.refs_1_, ...), custom_call_target="tpu_custom_call" | custom-call | tf_op jit(solution)/shard_map/pallas_call | solution.py:29
  85.8 1.5 %collective-permute-start.17 = (f32[16,256]{1,0:T(8,128)S(1)}, f32[16,256]{1,0:T(8,128)S(1)}, u32[]{:S(2)}, u32[]{:S(2)}) collective-permute-start(f32[16,256]{1,0:T(8,128)S(1)} %get-tuple-element.55), channel_id=1, source_target_pairs={{0,16},{8,24},{16,0},{24,8},{1,17},{9,25},{17,1},{25,9},{2,18},{10... | collective-permute-start | bytes 49160 | tf_op jit(solution)/shard_map/ppermute | solution.py:15
  87.4 2.2 %collective-permute-done.17.refs_2_ = f32[16,256]{1,0:T(8,128)S(1)} collective-permute-done((f32[16,256]{1,0:T(8,128)S(1)}, f32[16,256]{1,0:T(8,128)S(1)}, u32[]{:S(2)}, u32[]{:S(2)}) %collective-permute-start.17) | collective-permute-done | bytes 16416 | tf_op jit(solution)/shard_map/ppermute | solution.py:15
  92.0 1.4 %collective-permute-start.20 = (f32[4,16,256]{2,1,0:T(8,128)S(1)}, f32[4,16,256]{2,1,0:T(8,128)S(1)}, u32[]{:S(2)}, u32[]{:S(2)}) collective-permute-start(f32[4,16,256]{2,1,0:T(8,128)S(1)} %shard_map.112.refs_0_), channel_id=1, source_target_pairs={{0,16},{8,24},{16,0},{24,8},{1,17},{9,25},{17,1},{25,9},{2,18},{10... | collective-permute-start | bytes 196616 | tf_op jit(solution)/shard_map/ppermute | solution.py:15
  94.8 1.4 %collective-permute-start.23 = (f32[1,256]{1,0:T(1,128)S(1)}, f32[1,256]{1,0:T(1,128)S(1)}, u32[]{:S(2)}, u32[]{:S(2)}) collective-permute-start(f32[1,256]{1,0:T(1,128)S(1)} %get-tuple-element.74.refs_4_), channel_id=1, source_target_pairs={{0,16},{8,24},{16,0},{24,8},{1,17},{9,25},{17,1},{25,9},{2,18},{10... | collective-permute-start | bytes 3080 | tf_op jit(solution)/shard_map/ppermute | solution.py:15
  99.8 1.4 %collective-permute-start.26 = (f32[16,256]{1,0:T(8,128)S(1)}, f32[16,256]{1,0:T(8,128)S(1)}, u32[]{:S(2)}, u32[]{:S(2)}) collective-permute-start(f32[16,256]{1,0:T(8,128)S(1)} %shard_map.113.refs_0_.refs_2_), channel_id=1, source_target_pairs={{0,16},{8,24},{16,0},{24,8},{1,17},{9,25},{17,1},{25,9},{2,18},{10... | collective-permute-start | bytes 49160 | tf_op jit(solution)/shard_map/ppermute | solution.py:15
  101.3 1.3 collective-permute-done.27.refs_3_.refs_5_
  102.5 1.2 collective-permute-done.26.refs_2_.refs_4_
  110.1 2.1 %collective-permute-start.32 = (f32[16,640]{1,0:T(8,128)S(1)}, f32[16,640]{1,0:T(8,128)S(1)}, u32[]{:S(2)}, u32[]{:S(2)}) collective-permute-start(f32[16,640]{1,0:T(8,128)S(1)} %get-tuple-element.64), channel_id=1, source_target_pairs={{0,3},{1,2},{2,1},{3,0},{4,7},{5,6},{6,5},{7,4},{8,11},{9,10},{10,... | collective-permute-start | bytes 122888 | tf_op jit(solution)/shard_map/ppermute | solution.py:15
  112.3 2.0 %collective-permute-start.33 = (f32[16,640]{1,0:T(8,128)S(1)}, f32[16,640]{1,0:T(8,128)S(1)}, u32[]{:S(2)}, u32[]{:S(2)}) collective-permute-start(f32[16,640]{1,0:T(8,128)S(1)} %get-tuple-element.65), channel_id=1, source_target_pairs={{0,4},{1,5},{2,6},{3,7},{4,0},{5,1},{6,2},{7,3},{8,12},{9,13},{10,... | collective-permute-start | bytes 122888 | tf_op jit(solution)/shard_map/ppermute | solution.py:15
  115.4 2.3 %collective-permute-start.35 = (f32[16,640]{1,0:T(8,128)S(1)}, f32[16,640]{1,0:T(8,128)S(1)}, u32[]{:S(2)}, u32[]{:S(2)}) collective-permute-start(f32[16,640]{1,0:T(8,128)S(1)} %get-tuple-element.67), channel_id=1, source_target_pairs={{0,6},{1,7},{2,4},{3,5},{4,2},{5,3},{6,0},{7,1},{8,14},{9,15},{10,... | collective-permute-start | bytes 122888 | tf_op jit(solution)/shard_map/ppermute | solution.py:15
  117.7 2.2 %collective-permute-start.36 = (f32[16,640]{1,0:T(8,128)S(1)}, f32[16,640]{1,0:T(8,128)S(1)}, u32[]{:S(2)}, u32[]{:S(2)}) collective-permute-start(f32[16,640]{1,0:T(8,128)S(1)} %get-tuple-element.68), channel_id=1, source_target_pairs={{0,7},{1,6},{2,5},{3,4},{4,3},{5,2},{6,1},{7,0},{8,15},{9,14},{10,... | collective-permute-start | bytes 122888 | tf_op jit(solution)/shard_map/ppermute | solution.py:15
  121.3 3.1 %collective-permute-done.36.refs_7_ = f32[16,640]{1,0:T(8,128)S(1)} collective-permute-done((f32[16,640]{1,0:T(8,128)S(1)}, f32[16,640]{1,0:T(8,128)S(1)}, u32[]{:S(2)}, u32[]{:S(2)}) %collective-permute-start.36) | collective-permute-done | bytes 40992 | tf_op jit(solution)/shard_map/ppermute | solution.py:15
  125.1 2.6 %shard_map.117 = (f32[512,128]{1,0:T(8,128)}, f32[3,32,128]{2,1,0:T(8,128)}) custom-call(s32[2]{0:T(128)S(1)} %pad_add_fusion.ids_ref, f32[16,640]{1,0:T(8,128)S(1)} %get-tuple-element.61.refs_0_, f32[16,640]{1,0:T(8,128)S(1)} %collective-permute-done.30.refs_1_, f32[16,640]{1,0:T(8,128)S(1)} %collective-permute-done.31.refs_2_, ...), custom_call_target="tpu_custom_call" | custom-call | tf_op jit(solution)/shard_map/pallas_call | solution.py:29
  (108 shorter events, 35.1 us)
Async XLA Ops:
  2.4 34.9 %collective-permute-start.3 = (f32[160,256]{1,0:T(8,128)S(1)}, f32[160,256]{1,0:T(8,128)S(1)}, u32[]{:S(2)}, u32[]{:S(2)}) collective-permute-start(f32[160,256]{1,0:T(8,128)S(1)} %pad_maximum_fusion.1.refs_0_), channel_id=1, source_target_pairs={{0,4},{1,5},{2,6},{3,7},{4,0},{5,1},{6,2},{7,3},{8,12},{9,13},{10,... | collective-permute-start | bytes 491528 | tf_op jit(solution)/shard_map/ppermute | solution.py:15
  6.5 32.8 %collective-permute-start.1 = (f32[160,256]{1,0:T(8,128)S(1)}, f32[160,256]{1,0:T(8,128)}, u32[]{:S(2)}, u32[]{:S(2)}) collective-permute-start(f32[160,256]{1,0:T(8,128)S(1)} %pad_maximum_fusion.1.refs_0_), channel_id=1, source_target_pairs={{0,2},{1,3},{2,0},{3,1},{4,6},{5,7},{6,4},{7,5},{8,10},{9,11},{10,... | collective-permute-start | bytes 491528 | tf_op jit(solution)/shard_map/ppermute | solution.py:15
  9.0 18.1 %collective-permute-start.12 = (f32[256,256]{1,0:T(8,128)S(1)}, f32[256,256]{1,0:T(8,128)S(1)}, u32[]{:S(2)}, u32[]{:S(2)}) collective-permute-start(f32[256,256]{1,0:T(8,128)S(1)} %pad_maximum_fusion.refs_0_), channel_id=1, source_target_pairs={{0,4},{1,5},{2,6},{3,7},{4,0},{5,1},{6,2},{7,3},{8,12},{9,13},{10,... | collective-permute-start | bytes 786440 | tf_op jit(solution)/shard_map/ppermute | solution.py:15
  10.5 21.1 %all-to-all-start = ((f32[8,18,96]{2,1,0:T(8,128)}), f32[8,18,96]{2,1,0:T(8,128)}, u32[]{:S(2)}, u32[]{:S(2)}) async-start(f32[8,18,96]{2,1,0:T(8,128)} %pad_maximum_fusion.2), calls=%async_computation | async-start | bytes 196608 | tf_op jit(solution)/shard_map/all_to_all | solution.py:173
  15.4 25.4 %collective-permute-start = (f32[160,256]{1,0:T(8,128)S(1)}, f32[160,256]{1,0:T(8,128)}, u32[]{:S(2)}, u32[]{:S(2)}) collective-permute-start(f32[160,256]{1,0:T(8,128)S(1)} %pad_maximum_fusion.1.refs_0_), channel_id=1, source_target_pairs={{0,1},{1,0},{2,3},{3,2},{4,5},{5,4},{6,7},{7,6},{8,9},{9,8},{10,11... | collective-permute-start | bytes 491528 | tf_op jit(solution)/shard_map/ppermute | solution.py:15
  17.4 23.9 %collective-permute-start.10 = (f32[256,256]{1,0:T(8,128)S(1)}, f32[256,256]{1,0:T(8,128)}, u32[]{:S(2)}, u32[]{:S(2)}) collective-permute-start(f32[256,256]{1,0:T(8,128)S(1)} %pad_maximum_fusion.refs_0_), channel_id=1, source_target_pairs={{0,2},{1,3},{2,0},{3,1},{4,6},{5,7},{6,4},{7,5},{8,10},{9,11},{10,... | collective-permute-start | bytes 786440 | tf_op jit(solution)/shard_map/ppermute | solution.py:15
  27.2 22.6 %collective-permute-start.14 = (f32[256,256]{1,0:T(8,128)S(1)}, f32[256,256]{1,0:T(8,128)}, u32[]{:S(2)}, u32[]{:S(2)}) collective-permute-start(f32[256,256]{1,0:T(8,128)S(1)} %collective-permute-done.12.refs_4_), channel_id=1, source_target_pairs={{0,2},{1,3},{2,0},{3,1},{4,6},{5,7},{6,4},{7,5},{8,10},{9,11},{10,... | collective-permute-start | bytes 786440 | tf_op jit(solution)/shard_map/ppermute | solution.py:15
  31.6 27.6 %all-to-all-start.1 = ((f32[8,16,512]{2,1,0:T(8,128)}), f32[8,16,512]{2,1,0:T(8,128)S(1)}, u32[]{:S(2)}, u32[]{:S(2)}) async-start(f32[8,16,512]{2,1,0:T(8,128)} %bitcast.41), calls=%async_computation.1 | async-start | bytes 524288 | tf_op jit(solution)/shard_map/all_to_all | solution.py:160
  37.3 9.8 %collective-permute-start.5 = (f32[160,256]{1,0:T(8,128)S(1)}, f32[160,256]{1,0:T(8,128)S(1)}, u32[]{:S(2)}, u32[]{:S(2)}) collective-permute-start(f32[160,256]{1,0:T(8,128)S(1)} %collective-permute-done.3.refs_4_), channel_id=1, source_target_pairs={{0,2},{1,3},{2,0},{3,1},{4,6},{5,7},{6,4},{7,5},{8,10},{9,11},{10,... | collective-permute-start | bytes 491528 | tf_op jit(solution)/shard_map/ppermute | solution.py:15
  39.3 9.3 %collective-permute-start.4 = (f32[160,256]{1,0:T(8,128)S(1)}, f32[160,256]{1,0:T(8,128)S(1)}, u32[]{:S(2)}, u32[]{:S(2)}) collective-permute-start(f32[160,256]{1,0:T(8,128)S(1)} %collective-permute-done.3.refs_4_), channel_id=1, source_target_pairs={{0,1},{1,0},{2,3},{3,2},{4,5},{5,4},{6,7},{7,6},{8,9},{9,8},{10,11... | collective-permute-start | bytes 491528 | tf_op jit(solution)/shard_map/ppermute | solution.py:15
  40.8 10.7 %collective-permute-start.2 = (f32[160,256]{1,0:T(8,128)}, f32[160,256]{1,0:T(8,128)}, u32[]{:S(2)}, u32[]{:S(2)}) collective-permute-start(f32[160,256]{1,0:T(8,128)} %collective-permute-done.1.refs_2_), channel_id=1, source_target_pairs={{0,1},{1,0},{2,3},{3,2},{4,5},{5,4},{6,7},{7,6},{8,9},{9,8},{10,11... | collective-permute-start | bytes 491528 | tf_op jit(solution)/shard_map/ppermute | solution.py:15
  41.3 41.1 %collective-permute-start.9 = (f32[256,256]{1,0:T(8,128)S(1)}, f32[256,256]{1,0:T(8,128)}, u32[]{:S(2)}, u32[]{:S(2)}) collective-permute-start(f32[256,256]{1,0:T(8,128)S(1)} %pad_maximum_fusion.refs_0_), channel_id=1, source_target_pairs={{0,1},{1,0},{2,3},{3,2},{4,5},{5,4},{6,7},{7,6},{8,9},{9,8},{10,11... | collective-permute-start | bytes 786440 | tf_op jit(solution)/shard_map/ppermute | solution.py:15
  47.1 35.3 %collective-permute-start.13 = (f32[256,256]{1,0:T(8,128)S(1)}, f32[256,256]{1,0:T(8,128)}, u32[]{:S(2)}, u32[]{:S(2)}) collective-permute-start(f32[256,256]{1,0:T(8,128)S(1)} %collective-permute-done.12.refs_4_), channel_id=1, source_target_pairs={{0,1},{1,0},{2,3},{3,2},{4,5},{5,4},{6,7},{7,6},{8,9},{9,8},{10,11... | collective-permute-start | bytes 786440 | tf_op jit(solution)/shard_map/ppermute | solution.py:15
  49.2 33.2 %collective-permute-start.11 = (f32[256,256]{1,0:T(8,128)}, f32[256,256]{1,0:T(8,128)}, u32[]{:S(2)}, u32[]{:S(2)}) collective-permute-start(f32[256,256]{1,0:T(8,128)} %collective-permute-done.10.refs_2_), channel_id=1, source_target_pairs={{0,1},{1,0},{2,3},{3,2},{4,5},{5,4},{6,7},{7,6},{8,9},{9,8},{10,11... | collective-permute-start | bytes 786440 | tf_op jit(solution)/shard_map/ppermute | solution.py:15
  49.8 32.6 %collective-permute-start.15 = (f32[256,256]{1,0:T(8,128)}, f32[256,256]{1,0:T(8,128)}, u32[]{:S(2)}, u32[]{:S(2)}) collective-permute-start(f32[256,256]{1,0:T(8,128)} %collective-permute-done.14.refs_6_), channel_id=1, source_target_pairs={{0,1},{1,0},{2,3},{3,2},{4,5},{5,4},{6,7},{7,6},{8,9},{9,8},{10,11... | collective-permute-start | bytes 786440 | tf_op jit(solution)/shard_map/ppermute | solution.py:15
  51.4 24.7 %collective-permute-start.6 = (f32[160,256]{1,0:T(8,128)}, f32[160,256]{1,0:T(8,128)}, u32[]{:S(2)}, u32[]{:S(2)}) collective-permute-start(f32[160,256]{1,0:T(8,128)} %copy-done.4), channel_id=1, source_target_pairs={{0,1},{1,0},{2,3},{3,2},{4,5},{5,4},{6,7},{7,6},{8,9},{9,8},{10,11... | collective-permute-start | bytes 491528 | tf_op jit(solution)/shard_map/ppermute | solution.py:15
  85.8 3.7 %collective-permute-start.17 = (f32[16,256]{1,0:T(8,128)S(1)}, f32[16,256]{1,0:T(8,128)S(1)}, u32[]{:S(2)}, u32[]{:S(2)}) collective-permute-start(f32[16,256]{1,0:T(8,128)S(1)} %get-tuple-element.55), channel_id=1, source_target_pairs={{0,16},{8,24},{16,0},{24,8},{1,17},{9,25},{17,1},{25,9},{2,18},{10... | collective-permute-start | bytes 49160 | tf_op jit(solution)/shard_map/ppermute | solution.py:15
  87.3 3.3 %collective-permute-start.18 = (f32[16,256]{1,0:T(8,128)S(1)}, f32[16,256]{1,0:T(8,128)S(1)}, u32[]{:S(2)}, u32[]{:S(2)}) collective-permute-start(f32[16,256]{1,0:T(8,128)S(1)} %get-tuple-element.56), channel_id=1, source_target_pairs={{0,24},{8,16},{16,8},{24,0},{1,25},{9,17},{17,9},{25,1},{2,26},{10... | collective-permute-start | bytes 49160 | tf_op jit(solution)/shard_map/ppermute | solution.py:15
  91.6 6.9 %collective-permute-start.21 = (f32[4,16,256]{2,1,0:T(8,128)S(1)}, f32[4,16,256]{2,1,0:T(8,128)S(1)}, u32[]{:S(2)}, u32[]{:S(2)}) collective-permute-start(f32[4,16,256]{2,1,0:T(8,128)S(1)} %shard_map.112.refs_0_), channel_id=1, source_target_pairs={{0,24},{8,16},{16,8},{24,0},{1,25},{9,17},{17,9},{25,1},{2,26},{10... | collective-permute-start | bytes 196616 | tf_op jit(solution)/shard_map/ppermute | solution.py:15
  92.0 6.5 %collective-permute-start.20 = (f32[4,16,256]{2,1,0:T(8,128)S(1)}, f32[4,16,256]{2,1,0:T(8,128)S(1)}, u32[]{:S(2)}, u32[]{:S(2)}) collective-permute-start(f32[4,16,256]{2,1,0:T(8,128)S(1)} %shard_map.112.refs_0_), channel_id=1, source_target_pairs={{0,16},{8,24},{16,0},{24,8},{1,17},{9,25},{17,1},{25,9},{2,18},{10... | collective-permute-start | bytes 196616 | tf_op jit(solution)/shard_map/ppermute | solution.py:15
  93.4 5.1 %collective-permute-start.19 = (f32[4,16,256]{2,1,0:T(8,128)S(1)}, f32[4,16,256]{2,1,0:T(8,128)S(1)}, u32[]{:S(2)}, u32[]{:S(2)}) collective-permute-start(f32[4,16,256]{2,1,0:T(8,128)S(1)} %shard_map.112.refs_0_), channel_id=1, source_target_pairs={{0,8},{8,0},{16,24},{24,16},{1,9},{9,1},{17,25},{25,17},{2,10},{10... | collective-permute-start | bytes 196616 | tf_op jit(solution)/shard_map/ppermute | solution.py:15
  94.3 3.1 %collective-permute-start.24 = (f32[1,256]{1,0:T(1,128)S(1)}, f32[1,256]{1,0:T(1,128)S(1)}, u32[]{:S(2)}, u32[]{:S(2)}) collective-permute-start(f32[1,256]{1,0:T(1,128)S(1)} %get-tuple-element.74.refs_4_), channel_id=1, source_target_pairs={{0,24},{8,16},{16,8},{24,0},{1,25},{9,17},{17,9},{25,1},{2,26},{10... | collective-permute-start | bytes 3080 | tf_op jit(solution)/shard_map/ppermute | solution.py:15
  94.8 3.6 %collective-permute-start.23 = (f32[1,256]{1,0:T(1,128)S(1)}, f32[1,256]{1,0:T(1,128)S(1)}, u32[]{:S(2)}, u32[]{:S(2)}) collective-permute-start(f32[1,256]{1,0:T(1,128)S(1)} %get-tuple-element.74.refs_4_), channel_id=1, source_target_pairs={{0,16},{8,24},{16,0},{24,8},{1,17},{9,25},{17,1},{25,9},{2,18},{10... | collective-permute-start | bytes 3080 | tf_op jit(solution)/shard_map/ppermute | solution.py:15
  99.3 3.2 %collective-permute-start.27 = (f32[16,256]{1,0:T(8,128)S(1)}, f32[16,256]{1,0:T(8,128)S(1)}, u32[]{:S(2)}, u32[]{:S(2)}) collective-permute-start(f32[16,256]{1,0:T(8,128)S(1)} %shard_map.113.refs_0_.refs_2_), channel_id=1, source_target_pairs={{0,24},{8,16},{16,8},{24,0},{1,25},{9,17},{17,9},{25,1},{2,26},{10... | collective-permute-start | bytes 49160 | tf_op jit(solution)/shard_map/ppermute | solution.py:15
  99.8 3.9 %collective-permute-start.26 = (f32[16,256]{1,0:T(8,128)S(1)}, f32[16,256]{1,0:T(8,128)S(1)}, u32[]{:S(2)}, u32[]{:S(2)}) collective-permute-start(f32[16,256]{1,0:T(8,128)S(1)} %shard_map.113.refs_0_.refs_2_), channel_id=1, source_target_pairs={{0,16},{8,24},{16,0},{24,8},{1,17},{9,25},{17,1},{25,9},{2,18},{10... | collective-permute-start | bytes 49160 | tf_op jit(solution)/shard_map/ppermute | solution.py:15
  108.7 6.7 %collective-permute-start.30 = (f32[16,640]{1,0:T(8,128)S(1)}, f32[16,640]{1,0:T(8,128)S(1)}, u32[]{:S(2)}, u32[]{:S(2)}) collective-permute-start(f32[16,640]{1,0:T(8,128)S(1)} %get-tuple-element.62), channel_id=1, source_target_pairs={{0,1},{1,0},{2,3},{3,2},{4,5},{5,4},{6,7},{7,6},{8,9},{9,8},{10,11... | collective-permute-start | bytes 122888 | tf_op jit(solution)/shard_map/ppermute | solution.py:15
  109.6 8.2 %collective-permute-start.31 = (f32[16,640]{1,0:T(8,128)S(1)}, f32[16,640]{1,0:T(8,128)S(1)}, u32[]{:S(2)}, u32[]{:S(2)}) collective-permute-start(f32[16,640]{1,0:T(8,128)S(1)} %get-tuple-element.63), channel_id=1, source_target_pairs={{0,2},{1,3},{2,0},{3,1},{4,6},{5,7},{6,4},{7,5},{8,10},{9,11},{10,... | collective-permute-start | bytes 122888 | tf_op jit(solution)/shard_map/ppermute | solution.py:15
  110.1 9.8 %collective-permute-start.32 = (f32[16,640]{1,0:T(8,128)S(1)}, f32[16,640]{1,0:T(8,128)S(1)}, u32[]{:S(2)}, u32[]{:S(2)}) collective-permute-start(f32[16,640]{1,0:T(8,128)S(1)} %get-tuple-element.64), channel_id=1, source_target_pairs={{0,3},{1,2},{2,1},{3,0},{4,7},{5,6},{6,5},{7,4},{8,11},{9,10},{10,... | collective-permute-start | bytes 122888 | tf_op jit(solution)/shard_map/ppermute | solution.py:15
  112.3 7.7 %collective-permute-start.33 = (f32[16,640]{1,0:T(8,128)S(1)}, f32[16,640]{1,0:T(8,128)S(1)}, u32[]{:S(2)}, u32[]{:S(2)}) collective-permute-start(f32[16,640]{1,0:T(8,128)S(1)} %get-tuple-element.65), channel_id=1, source_target_pairs={{0,4},{1,5},{2,6},{3,7},{4,0},{5,1},{6,2},{7,3},{8,12},{9,13},{10,... | collective-permute-start | bytes 122888 | tf_op jit(solution)/shard_map/ppermute | solution.py:15
  114.3 6.6 %collective-permute-start.34 = (f32[16,640]{1,0:T(8,128)S(1)}, f32[16,640]{1,0:T(8,128)S(1)}, u32[]{:S(2)}, u32[]{:S(2)}) collective-permute-start(f32[16,640]{1,0:T(8,128)S(1)} %get-tuple-element.66), channel_id=1, source_target_pairs={{0,5},{1,4},{2,7},{3,6},{4,1},{5,0},{6,3},{7,2},{8,13},{9,12},{10,... | collective-permute-start | bytes 122888 | tf_op jit(solution)/shard_map/ppermute | solution.py:15
  115.4 5.9 %collective-permute-start.35 = (f32[16,640]{1,0:T(8,128)S(1)}, f32[16,640]{1,0:T(8,128)S(1)}, u32[]{:S(2)}, u32[]{:S(2)}) collective-permute-start(f32[16,640]{1,0:T(8,128)S(1)} %get-tuple-element.67), channel_id=1, source_target_pairs={{0,6},{1,7},{2,4},{3,5},{4,2},{5,3},{6,0},{7,1},{8,14},{9,15},{10,... | collective-permute-start | bytes 122888 | tf_op jit(solution)/shard_map/ppermute | solution.py:15
  117.7 6.7 %collective-permute-start.36 = (f32[16,640]{1,0:T(8,128)S(1)}, f32[16,640]{1,0:T(8,128)S(1)}, u32[]{:S(2)}, u32[]{:S(2)}) collective-permute-start(f32[16,640]{1,0:T(8,128)S(1)} %get-tuple-element.68), channel_id=1, source_target_pairs={{0,7},{1,6},{2,5},{3,4},{4,3},{5,2},{6,1},{7,0},{8,15},{9,14},{10,... | collective-permute-start | bytes 122888 | tf_op jit(solution)/shard_map/ppermute | solution.py:15
  (20 other events, 129.7 us)

commit v3 on v2

--- a/solution.py
+++ b/solution.py
@@ -1,3 +1,5 @@
+import math
+
 import jax
 import jax.numpy as jnp
 from jax import lax
@@ -25,7 +27,9 @@
     return [parts[offset] for offset in range(count)]
 
 
-def call(body, outs, arrays, scalars=(), scratch=()):
+def call(body, outs, arrays, scalars=(), scratch=(), work=0):
+    moved = sum(a.size * a.dtype.itemsize for a in arrays)
+    moved += sum(math.prod(shape) * jnp.dtype(kind).itemsize for shape, kind in outs)
     return pl.pallas_call(
         body,
         out_shape=[jax.ShapeDtypeStruct(*o) for o in outs],
@@ -34,6 +38,7 @@
         out_specs=[pl.BlockSpec(memory_space=pltpu.VMEM)] * len(outs),
         scratch_shapes=list(scratch),
         compiler_params=pltpu.CompilerParams(vmem_limit_bytes=40 << 20),
+        cost_estimate=pl.CostEstimate(flops=work, bytes_accessed=moved, transcendentals=0),
     )(*scalars, *arrays)
 
 
@@ -146,43 +151,44 @@
     lower_parts = gathered(lower_names)
     upper_parts = gathered(upper_names)
 
-    def local_forward(rhs_ref, inverse_ref, coupling_ref, solved_ref, terms_ref):
+    narrow = TILE - levels * piece
+    aux = jnp.concatenate([win_pivots.reshape(-1), pattern[0, 0].astype(F32)])
+    aux = jnp.pad(aux, (0, share * narrow - aux.size)).reshape(share, narrow)
+    aux = jnp.tile(jnp.pad(aux, ((0, 0), (levels * piece, 0))), (ranks, 1))
+    packed = tiles * TILE + TILE
+
+    def local_forward(rhs_ref, inverse_ref, coupling_ref, window_ref, aux_ref, *outs):
+        solved_ref, terms_ref, held = outs
         rhs = rhs_ref[...]
         solved = rhs + jnp.dot(strict_lower(inverse_ref[...]), rhs, precision=EXACT)
         solved_ref[...] = solved.T
-        terms_ref[...] = jnp.dot(coupling_ref[...], solved, precision=EXACT).T
+        terms_ref[:, : tiles * TILE] = jnp.dot(coupling_ref[...], solved, precision=EXACT).T
+        held[...] = jnp.zeros_like(held)
+        for level in range(levels):
+            held[level * piece : (level + 1) * piece, :] = window_ref[level]
+        terms_ref[:, tiles * TILE :] = held[...].T + aux_ref[...]
 
     solved_loc, terms = call(
         local_forward,
-        [((columns, local), F32), ((columns, tiles * TILE), F32)],
-        (loc_rhs[0, 0], loc_inverse[0, 0], loc_coupling[0, 0]),
-    )
-    terms = lax.all_to_all(
-        terms.reshape(ranks, share, tiles * TILE), "row", 0, 0, tiled=True
-    )
-
-    extra = jnp.pad(pattern[0].astype(F32), ((0, 0), (0, levels * piece - tiles)))
-    early = jnp.concatenate(
-        [
-            win_rhs.transpose(2, 0, 1).reshape(ranks, share, levels * piece),
-            jnp.broadcast_to(win_pivots.reshape(1, 1, -1), (ranks, 1, levels * piece)),
-            jnp.broadcast_to(extra, (ranks, 1, levels * piece)),
-        ],
-        1,
-    )
-    early = lax.all_to_all(early, "row", 0, 0, tiled=True)
-    known = early[:, share + 1, :tiles].astype(jnp.int32).reshape(-1)
-    early = early[:, : share + 1].reshape(ranks, share + 1, levels, piece)
-    early = early.transpose(2, 1, 0, 3).reshape(levels, share + 1, base)
-    rhs, pivots = early[:, :share], early[:, share:]
+        [((columns, local), F32), ((columns, packed), F32)],
+        (loc_rhs[0, 0], loc_inverse[0, 0], loc_coupling[0, 0], win_rhs, aux),
+        scratch=[pltpu.VMEM((TILE, columns), F32)],
+        work=24 * local * local * columns,
+    )
+    terms = lax.all_to_all(terms.reshape(ranks, share, packed), "row", 0, 0, tiled=True)
+    aux = terms[:, :, tiles * TILE + levels * piece :].reshape(ranks, -1)
+    known = aux[:, levels * piece : levels * piece + tiles].astype(jnp.int32).reshape(-1)
+    pivots = aux[:, : levels * piece].reshape(ranks, levels, piece)
+    pivots = pivots.transpose(1, 0, 2).reshape(levels, 1, base)
     top_pivots = leaf_swaps([pivots[top]] * leaves)
 
     lower = assemble(lower_parts, lower_names)
     upper = assemble(upper_parts, upper_names)
     blocks = {**lower, **upper}
 
-    def scatter(ids_ref, known_ref, terms_ref, rhs_ref, *refs):
+    def scatter(ids_ref, known_ref, terms_ref, *refs):
         outs, path = refs[:-1], refs[-1]
+        lane = lax.broadcasted_iota(jnp.int32, (share, TILE), 1)
         path[...] = jnp.zeros_like(path)
         for source in range(ranks):
             for tile in range(tiles):
@@ -194,12 +200,21 @@
                 first = (span - 1 + slot) * halves
                 outs[level][slot] = jnp.concatenate([path[first + h] for h in range(halves)], 1)
             own = ids_ref[0] % span
-            outs[level][own] = outs[level][own] + rhs_ref[level]
+            rows = []
+            for half in range(halves):
+                row = jnp.zeros((share, TILE), F32)
+                for source in range(half * TILE // piece, (half + 1) * TILE // piece):
+                    place = source * piece % TILE
+                    shift = (TILE + place - level * piece) % TILE
+                    turned = pltpu.roll(terms_ref[source, :, tiles * TILE :], shift, 1)
+                    row = jnp.where((lane >= place) & (lane < place + piece), turned, row)
+                rows.append(row)
+            outs[level][own] = outs[level][own] + jnp.concatenate(rows, 1)
 
     rest = call(
         scatter,
         [((2**level, *wide), F32) for level in range(levels)],
-        (terms, rhs),
+        (terms,),
         (ids, known),
         [pltpu.VMEM((path_tiles, share, TILE), F32)],
     )
@@ -337,14 +352,12 @@
         wanted = leaf_swaps(descend(level, everything[level]) * 2 ** (level - 1))
         everything[level - 1] = leaf_swaps(transposed(level - 1, wanted) * 2 ** (level - 1))
 
-    packed = tiles * TILE + TILE
-
     def finish(ids_ref, known_ref, *refs):
         refs = list(refs)
         parts = {level: [refs.pop(0) for _ in range(2**level)] for level in range(1, levels)}
         link_high, link_low, solved_ref, pivot_ref, high_ref, low_ref = refs[:6]
-        outs, path, held = refs[6:-2], refs[-2], refs[-1]
-        group, me = ids_ref[0], ids_ref[1]
+        out, path, held = refs[6:]
+        group = ids_ref[0]
         ordered(group % 2, parts[1], held)
         wanted = solved_ref[...] / pivot_ref[...] - against(held, link_high, link_low, 2)
         lowest = wanted + times(wanted, high_ref[0], low_ref[0], 0)
@@ -359,21 +372,22 @@
                 for half in range(halves):
                     path[first + half] = ref[:, half * TILE : (half + 1) * TILE]
         lane = lax.broadcasted_iota(jnp.int32, (share, TILE), 1)
-        for offset, out in enumerate(outs):
-            target = me ^ offset
+        for target in range(ranks):
             for tile in range(tiles):
-                out[:, tile * TILE : (tile + 1) * TILE] = path[known_ref[target * tiles + tile]]
+                out[target, :, tile * TILE : (tile + 1) * TILE] = path[
+                    known_ref[target * tiles + tile]
+                ]
             pieces = jnp.zeros((share, TILE), F32)
             for level in range(levels):
                 shift = (base + level * piece - target * piece) % base
                 turned = pltpu.roll(owned[level], shift, 1)[:, :TILE]
                 mine = (lane >= level * piece) & (lane < (level + 1) * piece)
                 pieces = jnp.where(mine, turned, pieces)
-            out[:, tiles * TILE :] = pieces
+            out[target, :, tiles * TILE :] = pieces
 
     replies = call(
         finish,
-        [((share, packed), F32)] * ranks,
+        [((ranks, share, packed), F32)],
         (
             *[part for level in range(1, levels) for part in everything[level]],
             *blocks["B", 0],
@@ -384,22 +398,9 @@
         (ids, known),
         [pltpu.VMEM((path_tiles, share, TILE), F32), pltpu.VMEM((2, *wide), F32)],
     )
-    replies = [replies[0]] + [swap(v, "row", ranks, j) for j, v in enumerate(replies) if j]
-    if share % 8:
-        stacked = jnp.stack(replies)[rank ^ jnp.arange(ranks)]
-        replies = [stacked.reshape(columns, packed)]
-
-    def local_backward(ids_ref, *refs):
-        refs = list(refs)
-        reply_refs = [refs.pop(0) for _ in replies]
-        solved_ref, pivot_ref, inverse_ref, coupling_ref, out, window_ref, back = refs
-        me = ids_ref[1]
-        if len(reply_refs) == 1:
-            back[...] = reply_refs[0][...]
-        else:
-            for offset, ref in enumerate(reply_refs):
-                start = pl.multiple_of((me ^ offset) * share, 8)
-                back[pl.ds(start, share), :] = ref[...]
+    back = lax.all_to_all(replies[0], "row", 0, 0, tiled=True).reshape(columns, packed)
+
+    def local_backward(back, solved_ref, pivot_ref, inverse_ref, coupling_ref, out, window_ref):
         remainder = solved_ref[...] / pivot_ref[...] - jnp.dot(
             back[:, : tiles * TILE], coupling_ref[...], precision=EXACT
         )
@@ -414,9 +415,8 @@
     answer, window = call(
         local_backward,
         [((local, columns), F32), ((levels, piece, columns), F32)],
-        (*replies, solved_loc, loc_pivots[0], loc_inverse[0, 0], loc_coupling[0, 0]),
-        (ids,),
-        [pltpu.VMEM((columns, packed), F32)],
+        (back, solved_loc, loc_pivots[0], loc_inverse[0, 0], loc_coupling[0, 0]),
+        work=24 * local * local * columns,
     )
     return answer[None, None], window
 

time: 128 us -> 124 us (0.969)
  starting transfers between devices: 50 us -> 32.5 us
  blocking collectives: 0 us -> 15.4 us
  waiting for transfers between devices: 44.6 us -> 33.3 us
  local copies, waits for them, and re-layouts: 12.8 us -> 22.9 us
  other arithmetic: 1.55 us -> 0.26 us
    all_to_all x0 -> x1, blocking collectives: none -> 15.4 us  [shards(): lax.all_to_all(replies[0], 'row', 0, 0, tiled=True).reshape(columns, packed)]
    unnamed x26 -> x78, local copies, waits for them, and re-layouts: 3.02 us -> 18.3 us
    ppermute x37 -> x30, waiting for transfers between devices: 44.5 us -> 33.3 us  [swap(): return lax.ppermute(value, axis, [(i, i ^ offset) for i in range(count)])]
    ppermute x37 -> x30, starting transfers between devices: 39.5 us -> 28.7 us  [swap(): return lax.ppermute(value, axis, [(i, i ^ offset) for i in range(count)])]
    all_to_all x2 -> x1, starting transfers between devices: 10.5 us -> 3.82 us  [shards(): lax.all_to_all(terms.reshape(ranks, share, packed), 'row', 0, 0, tiled=True)]
    transpose x2 -> x0, local copies, waits for them, and re-layouts: 1.79 us -> none  [the longest x1 1.64 us: shards(): early = early.transpose(2, 1, 0, 3).reshape(levels, share + 1, base)]
    reshape x3 -> x5, local copies, waits for them, and re-layouts: 2.72 us -> 1.02 us  [the longest x1 0.68 us: shards(): pivots = aux[:, :levels * piece].reshape(ranks, levels, piece)]
  transfers between devices with their start and end apart: 39 -> 31, of which waited for: 17 -> 14; matrix products, arithmetic and copies ran while one was open for 8% -> 3% of each run, Pallas kernels for 8% -> 8%
where the time goes in v3:
time: 124 us; the launch traced here: 123 us
  waiting for transfers between devices  33.3 us (27%)
  starting transfers between devices  32.5 us (26%)
  local copies, waits for them, and re-layouts  22.9 us (18%)
  Pallas kernels  17.6 us (14%)
  blocking collectives  15.4 us (12%)
    ppermute x30, waiting for transfers between devices, swap(): return lax.ppermute(value, axis, [(i, i ^ offset) for i in range(count)])  33.3 us
    ppermute x30, starting transfers between devices, swap(): return lax.ppermute(value, axis, [(i, i ^ offset) for i in range(count)])  28.7 us
    unnamed x78, local copies, waits for them, and re-layouts  18.3 us
    pallas_call x14, Pallas kernels, call(): pl.pallas_call(body, out_shape=[jax.ShapeDtypeStruct(*o) for o in outs],...  17.6 us
    all_to_all x1, blocking collectives, shards(): lax.all_to_all(replies[0], 'row', 0, 0, tiled=True).reshape(columns, packed)  15.4 us
    all_to_all x1, starting transfers between devices, shards(): lax.all_to_all(terms.reshape(ranks, share, packed), 'row', 0, 0, tiled=True)  3.82 us
    squeeze x3, local copies, waits for them, and re-layouts, gathered(): rows.append(source[0, low:high])  2.72 us
  transfers between devices with their start and end apart: 31, of which 14 were waited for; matrix products, arithmetic and copies ran while one was open for 3% of the time, Pallas kernels for 8%

profile of v3, /device:TPU:0, one launch (start us, length us, event | category | flops | bytes accessed | tf_op | source)
XLA Modules:
  0.0 122.8 jit_solution(741335129001144540)
XLA Ops:
  0.6 1.1 slice_bitcast_fusion
  1.8 4.1 %collective-permute-start.12 = (f32[256,256]{1,0:T(8,128)S(1)}, f32[256,256]{1,0:T(8,128)S(1)}, u32[]{:S(2)}, u32[]{:S(2)}) collective-permute-start(f32[256,256]{1,0:T(8,128)S(1)} %pad_maximum_fusion.refs_0_), channel_id=1, source_target_pairs={{0,4},{1,5},{2,6},{3,7},{4,0},{5,1},{6,2},{7,3},{8,12},{9,13},{10,... | collective-permute-start | bytes 786440 | tf_op jit(solution)/shard_map/ppermute | solution.py:17
  6.9 1.2 copy-done.28
  9.1 4.3 %shard_map.104 = (f32[128,512]{1,0:T(8,128)S(1)}, f32[128,640]{1,0:T(8,128)}) custom-call(f32[512,128]{1,0:T(8,128)S(1)} %bitcast.31, f32[512,512]{1,0:T(8,128)S(1)} %bitcast.27, f32[512,512]{1,0:T(8,128)S(1)} %bitcast.29, f32[3,32,128]{2,1,0:T(8,128)S(1)} %copy-done.31, f32[128,128]{1,0:T(8,128)S(1)} %bitcast.25), custom_call_target="tpu_custom_call" | custom-call | flops 805306368 | bytes 3063808 | tf_op jit(solution)/shard_map/pallas_call | solution.py:33
  14.1 3.8 %all-to-all-start = ((f32[8,16,640]{2,1,0:T(8,128)}), f32[8,16,640]{2,1,0:T(8,128)S(1)}, u32[]{:S(2)}, u32[]{:S(2)}) async-start(f32[8,16,640]{2,1,0:T(8,128)} %bitcast.7), calls=%async_computation | async-start | bytes 655360 | tf_op jit(solution)/shard_map/all_to_all | solution.py:178
  19.5 3.0 %collective-permute-start.3 = (f32[160,256]{1,0:T(8,128)S(1)}, f32[160,256]{1,0:T(8,128)S(1)}, u32[]{:S(2)}, u32[]{:S(2)}) collective-permute-start(f32[160,256]{1,0:T(8,128)S(1)} %pad_maximum_fusion.1.refs_0_), channel_id=1, source_target_pairs={{0,4},{1,5},{2,6},{3,7},{4,0},{5,1},{6,2},{7,3},{8,12},{9,13},{10,... | collective-permute-start | bytes 491528 | tf_op jit(solution)/shard_map/ppermute | solution.py:17
  22.5 1.5 %collective-permute-start.1 = (f32[160,256]{1,0:T(8,128)S(1)}, f32[160,256]{1,0:T(8,128)S(1)}, u32[]{:S(2)}, u32[]{:S(2)}) collective-permute-start(f32[160,256]{1,0:T(8,128)S(1)} %pad_maximum_fusion.1.refs_0_), channel_id=1, source_target_pairs={{0,2},{1,3},{2,0},{3,1},{4,6},{5,7},{6,4},{7,5},{8,10},{9,11},{10,... | collective-permute-start | bytes 491528 | tf_op jit(solution)/shard_map/ppermute | solution.py:17
  24.0 1.5 %collective-permute-start = (f32[160,256]{1,0:T(8,128)S(1)}, f32[160,256]{1,0:T(8,128)S(1)}, u32[]{:S(2)}, u32[]{:S(2)}) collective-permute-start(f32[160,256]{1,0:T(8,128)S(1)} %pad_maximum_fusion.1.refs_0_), channel_id=1, source_target_pairs={{0,1},{1,0},{2,3},{3,2},{4,5},{5,4},{6,7},{7,6},{8,9},{9,8},{10,11... | collective-permute-start | bytes 491528 | tf_op jit(solution)/shard_map/ppermute | solution.py:17
  26.0 1.5 %collective-permute-start.14 = (f32[256,256]{1,0:T(8,128)S(1)}, f32[256,256]{1,0:T(8,128)S(1)}, u32[]{:S(2)}, u32[]{:S(2)}) collective-permute-start(f32[256,256]{1,0:T(8,128)S(1)} %collective-permute-done.12.refs_4_), channel_id=1, source_target_pairs={{0,2},{1,3},{2,0},{3,1},{4,6},{5,7},{6,4},{7,5},{8,10},{9,11},{10,... | collective-permute-start | bytes 786440 | tf_op jit(solution)/shard_map/ppermute | solution.py:17
  27.5 7.8 %collective-permute-done.3.refs_4_ = f32[160,256]{1,0:T(8,128)S(1)} collective-permute-done((f32[160,256]{1,0:T(8,128)S(1)}, f32[160,256]{1,0:T(8,128)S(1)}, u32[]{:S(2)}, u32[]{:S(2)}) %collective-permute-start.3) | collective-permute-done | bytes 163872 | tf_op jit(solution)/shard_map/ppermute | solution.py:17
  35.3 1.4 %collective-permute-start.4 = (f32[160,256]{1,0:T(8,128)S(1)}, f32[160,256]{1,0:T(8,128)S(1)}, u32[]{:S(2)}, u32[]{:S(2)}) collective-permute-start(f32[160,256]{1,0:T(8,128)S(1)} %collective-permute-done.3.refs_4_), channel_id=1, source_target_pairs={{0,1},{1,0},{2,3},{3,2},{4,5},{5,4},{6,7},{7,6},{8,9},{9,8},{10,11... | collective-permute-start | bytes 491528 | tf_op jit(solution)/shard_map/ppermute | solution.py:17
  38.7 9.1 %collective-permute-done.5.refs_6_ = f32[160,256]{1,0:T(8,128)S(1)} collective-permute-done((f32[160,256]{1,0:T(8,128)S(1)}, f32[160,256]{1,0:T(8,128)S(1)}, u32[]{:S(2)}, u32[]{:S(2)}) %collective-permute-start.5) | collective-permute-done | bytes 163872 | tf_op jit(solution)/shard_map/ppermute | solution.py:17
  47.8 1.7 %collective-permute-start.6 = (f32[160,256]{1,0:T(8,128)S(1)}, f32[160,256]{1,0:T(8,128)S(1)}, u32[]{:S(2)}, u32[]{:S(2)}) collective-permute-start(f32[160,256]{1,0:T(8,128)S(1)} %collective-permute-done.5.refs_6_), channel_id=1, source_target_pairs={{0,1},{1,0},{2,3},{3,2},{4,5},{5,4},{6,7},{7,6},{8,9},{9,8},{10,11... | collective-permute-start | bytes 491528 | tf_op jit(solution)/shard_map/ppermute | solution.py:17
  51.1 1.7 %collective-permute-start.13 = (f32[256,256]{1,0:T(8,128)S(1)}, f32[256,256]{1,0:T(8,128)S(1)}, u32[]{:S(2)}, u32[]{:S(2)}) collective-permute-start(f32[256,256]{1,0:T(8,128)S(1)} %collective-permute-done.12.refs_4_), channel_id=1, source_target_pairs={{0,1},{1,0},{2,3},{3,2},{4,5},{5,4},{6,7},{7,6},{8,9},{9,8},{10,11... | collective-permute-start | bytes 786440 | tf_op jit(solution)/shard_map/ppermute | solution.py:17
  53.8 1.7 %collective-permute-start.15 = (f32[256,256]{1,0:T(8,128)S(1)}, f32[256,256]{1,0:T(8,128)}, u32[]{:S(2)}, u32[]{:S(2)}) collective-permute-start(f32[256,256]{1,0:T(8,128)S(1)} %collective-permute-done.14.refs_6_), channel_id=1, source_target_pairs={{0,1},{1,0},{2,3},{3,2},{4,5},{5,4},{6,7},{7,6},{8,9},{9,8},{10,11... | collective-permute-start | bytes 786440 | tf_op jit(solution)/shard_map/ppermute | solution.py:17
  65.4 1.2 collective-permute-done.7.refs_1_
  69.1 2.5 %collective-permute-done.11.refs_3_ = f32[256,256]{1,0:T(8,128)} collective-permute-done((f32[256,256]{1,0:T(8,128)S(1)}, f32[256,256]{1,0:T(8,128)}, u32[]{:S(2)}, u32[]{:S(2)}) %collective-permute-start.11) | collective-permute-done | bytes 262176 | tf_op jit(solution)/shard_map/ppermute | solution.py:17
  71.5 4.2 %collective-permute-done.15.refs_7_ = f32[256,256]{1,0:T(8,128)} collective-permute-done((f32[256,256]{1,0:T(8,128)S(1)}, f32[256,256]{1,0:T(8,128)}, u32[]{:S(2)}, u32[]{:S(2)}) %collective-permute-start.15) | collective-permute-done | bytes 262176 | tf_op jit(solution)/shard_map/ppermute | solution.py:17
  77.6 1.7 %shard_map.110 = (bf16[4,256,256]{2,1,0:T(8,128)(2,1)S(1)}, bf16[4,256,256]{2,1,0:T(8,128)(2,1)S(1)}, bf16[4,256,256]{2,1,0:T(8,128)(2,1)S(1)}, bf16[4,256,256]{2,1,0:T(8,128)(2,1)S(1)}) custom-call(s32[2]{0:T(128)S(1)} %pad_add_fusion.ids_ref, f32[256,256]{1,0:T(8,128)S(1)} %pad_maximum_fusion.refs_0_, f32[256,256]{1,0:T(8,128)S(1)} %copy-done.9, ...), custom_call_target="tpu_custom_call" | custom-call | bytes 4194304 | tf_op jit(solution)/shard_map/pallas_call | solution.py:33
  80.4 1.6 %collective-permute-start.17 = (f32[16,256]{1,0:T(8,128)S(1)}, f32[16,256]{1,0:T(8,128)S(1)}, u32[]{:S(2)}, u32[]{:S(2)}) collective-permute-start(f32[16,256]{1,0:T(8,128)S(1)} %get-tuple-element.47), channel_id=1, source_target_pairs={{0,16},{8,24},{16,0},{24,8},{1,17},{9,25},{17,1},{25,9},{2,18},{10... | collective-permute-start | bytes 49160 | tf_op jit(solution)/shard_map/ppermute | solution.py:17
  86.6 1.4 %collective-permute-start.20 = (f32[4,16,256]{2,1,0:T(8,128)S(1)}, f32[4,16,256]{2,1,0:T(8,128)S(1)}, u32[]{:S(2)}, u32[]{:S(2)}) collective-permute-start(f32[4,16,256]{2,1,0:T(8,128)S(1)} %shard_map.112.refs_0_), channel_id=1, source_target_pairs={{0,16},{8,24},{16,0},{24,8},{1,17},{9,25},{17,1},{25,9},{2,18},{10... | collective-permute-start | bytes 196616 | tf_op jit(solution)/shard_map/ppermute | solution.py:17
  88.8 1.4 %collective-permute-start.23 = (f32[1,256]{1,0:T(1,128)S(1)}, f32[1,256]{1,0:T(1,128)S(1)}, u32[]{:S(2)}, u32[]{:S(2)}) collective-permute-start(f32[1,256]{1,0:T(1,128)S(1)} %squeeze.51.refs_4_), channel_id=1, source_target_pairs={{0,16},{8,24},{16,0},{24,8},{1,17},{9,25},{17,1},{25,9},{2,18},{10... | collective-permute-start | bytes 3080 | tf_op jit(solution)/shard_map/ppermute | solution.py:17
  90.2 1.4 %collective-permute-done.24.refs_7_ = f32[1,256]{1,0:T(1,128)S(1)} collective-permute-done((f32[1,256]{1,0:T(1,128)S(1)}, f32[1,256]{1,0:T(1,128)S(1)}, u32[]{:S(2)}, u32[]{:S(2)}) %collective-permute-start.24) | collective-permute-done | bytes 1056 | tf_op jit(solution)/shard_map/ppermute | solution.py:17
  92.9 1.1 shard_map.113.refs_0_.refs_2_
  94.7 1.3 %collective-permute-start.26 = (f32[16,256]{1,0:T(8,128)S(1)}, f32[16,256]{1,0:T(8,128)S(1)}, u32[]{:S(2)}, u32[]{:S(2)}) collective-permute-start(f32[16,256]{1,0:T(8,128)S(1)} %shard_map.113.refs_0_.refs_2_), channel_id=1, source_target_pairs={{0,16},{8,24},{16,0},{24,8},{1,17},{9,25},{17,1},{25,9},{2,18},{10... | collective-permute-start | bytes 49160 | tf_op jit(solution)/shard_map/ppermute | solution.py:17
  96.1 1.1 collective-permute-done.27.refs_3_.refs_5_
  97.2 1.2 collective-permute-done.26.refs_2_.refs_4_
  99.3 1.2 collective-permute-done.28.refs_1_
  102.4 1.0 shard_map.116
  103.4 15.4 %all_to_all.10 = f32[8,16,640]{2,1,0:T(8,128)S(1)} all-to-all(f32[8,16,640]{2,1,0:T(8,128)S(1)} %shard_map.116), channel_id=1, replica_groups=mesh['leaf'=4,'row'=8] {'row'}, dimensions={0} | all-to-all | bytes 655360 | tf_op jit(solution)/shard_map/all_to_all | solution.py:401
  119.5 1.2 copy-done.29
  120.7 2.0 %shard_map.117 = (f32[512,128]{1,0:T(8,128)}, f32[3,32,128]{2,1,0:T(8,128)}) custom-call(f32[128,640]{1,0:T(8,128)S(1)} %bitcast.24, f32[128,512]{1,0:T(8,128)S(1)} %copy-done.34, f32[1,512]{1,0:T(1,128)S(1)} %bitcast.32, f32[512,512]{1,0:T(8,128)S(1)} %bitcast.28, f32[512,512]{1,0:T(8,128)S(1)} %bitcast.30), custom_call_target="tpu_custom_call" | custom-call | flops 805306368 | bytes 3000320 | tf_op jit(solution)/shard_map/pallas_call | solution.py:33
  (146 shorter events, 35.7 us)
Async XLA Ops:
  1.8 24.2 %collective-permute-start.12 = (f32[256,256]{1,0:T(8,128)S(1)}, f32[256,256]{1,0:T(8,128)S(1)}, u32[]{:S(2)}, u32[]{:S(2)}) collective-permute-start(f32[256,256]{1,0:T(8,128)S(1)} %pad_maximum_fusion.refs_0_), channel_id=1, source_target_pairs={{0,4},{1,5},{2,6},{3,7},{4,0},{5,1},{6,2},{7,3},{8,12},{9,13},{10,... | collective-permute-start | bytes 786440 | tf_op jit(solution)/shard_map/ppermute | solution.py:17
  14.1 48.7 %all-to-all-start = ((f32[8,16,640]{2,1,0:T(8,128)}), f32[8,16,640]{2,1,0:T(8,128)S(1)}, u32[]{:S(2)}, u32[]{:S(2)}) async-start(f32[8,16,640]{2,1,0:T(8,128)} %bitcast.7), calls=%async_computation | async-start | bytes 655360 | tf_op jit(solution)/shard_map/all_to_all | solution.py:178
  19.5 15.8 %collective-permute-start.3 = (f32[160,256]{1,0:T(8,128)S(1)}, f32[160,256]{1,0:T(8,128)S(1)}, u32[]{:S(2)}, u32[]{:S(2)}) collective-permute-start(f32[160,256]{1,0:T(8,128)S(1)} %pad_maximum_fusion.1.refs_0_), channel_id=1, source_target_pairs={{0,4},{1,5},{2,6},{3,7},{4,0},{5,1},{6,2},{7,3},{8,12},{9,13},{10,... | collective-permute-start | bytes 491528 | tf_op jit(solution)/shard_map/ppermute | solution.py:17
  22.5 12.8 %collective-permute-start.1 = (f32[160,256]{1,0:T(8,128)S(1)}, f32[160,256]{1,0:T(8,128)S(1)}, u32[]{:S(2)}, u32[]{:S(2)}) collective-permute-start(f32[160,256]{1,0:T(8,128)S(1)} %pad_maximum_fusion.1.refs_0_), channel_id=1, source_target_pairs={{0,2},{1,3},{2,0},{3,1},{4,6},{5,7},{6,4},{7,5},{8,10},{9,11},{10,... | collective-permute-start | bytes 491528 | tf_op jit(solution)/shard_map/ppermute | solution.py:17
  24.0 12.8 %collective-permute-start = (f32[160,256]{1,0:T(8,128)S(1)}, f32[160,256]{1,0:T(8,128)S(1)}, u32[]{:S(2)}, u32[]{:S(2)}) collective-permute-start(f32[160,256]{1,0:T(8,128)S(1)} %pad_maximum_fusion.1.refs_0_), channel_id=1, source_target_pairs={{0,1},{1,0},{2,3},{3,2},{4,5},{5,4},{6,7},{7,6},{8,9},{9,8},{10,11... | collective-permute-start | bytes 491528 | tf_op jit(solution)/shard_map/ppermute | solution.py:17
  25.5 24.7 %collective-permute-start.10 = (f32[256,256]{1,0:T(8,128)S(1)}, f32[256,256]{1,0:T(8,128)S(1)}, u32[]{:S(2)}, u32[]{:S(2)}) collective-permute-start(f32[256,256]{1,0:T(8,128)S(1)} %pad_maximum_fusion.refs_0_), channel_id=1, source_target_pairs={{0,2},{1,3},{2,0},{3,1},{4,6},{5,7},{6,4},{7,5},{8,10},{9,11},{10,... | collective-permute-start | bytes 786440 | tf_op jit(solution)/shard_map/ppermute | solution.py:17
  26.0 36.7 %copy-start.2 = (f32[256,256]{1,0:T(8,128)}, f32[256,256]{1,0:T(8,128)S(1)}, u32[]{:S(2)}) copy-start(f32[256,256]{1,0:T(8,128)S(1)} %collective-permute-done.12.refs_4_) | copy-start | bytes 786436
  26.0 27.8 %collective-permute-start.14 = (f32[256,256]{1,0:T(8,128)S(1)}, f32[256,256]{1,0:T(8,128)S(1)}, u32[]{:S(2)}, u32[]{:S(2)}) collective-permute-start(f32[256,256]{1,0:T(8,128)S(1)} %collective-permute-done.12.refs_4_), channel_id=1, source_target_pairs={{0,2},{1,3},{2,0},{3,1},{4,6},{5,7},{6,4},{7,5},{8,10},{9,11},{10,... | collective-permute-start | bytes 786440 | tf_op jit(solution)/shard_map/ppermute | solution.py:17
  35.3 12.5 %collective-permute-start.5 = (f32[160,256]{1,0:T(8,128)S(1)}, f32[160,256]{1,0:T(8,128)S(1)}, u32[]{:S(2)}, u32[]{:S(2)}) collective-permute-start(f32[160,256]{1,0:T(8,128)S(1)} %collective-permute-done.3.refs_4_), channel_id=1, source_target_pairs={{0,2},{1,3},{2,0},{3,1},{4,6},{5,7},{6,4},{7,5},{8,10},{9,11},{10,... | collective-permute-start | bytes 491528 | tf_op jit(solution)/shard_map/ppermute | solution.py:17
  35.3 15.2 %collective-permute-start.4 = (f32[160,256]{1,0:T(8,128)S(1)}, f32[160,256]{1,0:T(8,128)S(1)}, u32[]{:S(2)}, u32[]{:S(2)}) collective-permute-start(f32[160,256]{1,0:T(8,128)S(1)} %collective-permute-done.3.refs_4_), channel_id=1, source_target_pairs={{0,1},{1,0},{2,3},{3,2},{4,5},{5,4},{6,7},{7,6},{8,9},{9,8},{10,11... | collective-permute-start | bytes 491528 | tf_op jit(solution)/shard_map/ppermute | solution.py:17
  37.4 15.4 %collective-permute-start.2 = (f32[160,256]{1,0:T(8,128)S(1)}, f32[160,256]{1,0:T(8,128)S(1)}, u32[]{:S(2)}, u32[]{:S(2)}) collective-permute-start(f32[160,256]{1,0:T(8,128)S(1)} %collective-permute-done.1.refs_2_), channel_id=1, source_target_pairs={{0,1},{1,0},{2,3},{3,2},{4,5},{5,4},{6,7},{7,6},{8,9},{9,8},{10,11... | collective-permute-start | bytes 491528 | tf_op jit(solution)/shard_map/ppermute | solution.py:17
  47.8 7.8 %collective-permute-start.6 = (f32[160,256]{1,0:T(8,128)S(1)}, f32[160,256]{1,0:T(8,128)S(1)}, u32[]{:S(2)}, u32[]{:S(2)}) collective-permute-start(f32[160,256]{1,0:T(8,128)S(1)} %collective-permute-done.5.refs_6_), channel_id=1, source_target_pairs={{0,1},{1,0},{2,3},{3,2},{4,5},{5,4},{6,7},{7,6},{8,9},{9,8},{10,11... | collective-permute-start | bytes 491528 | tf_op jit(solution)/shard_map/ppermute | solution.py:17
  50.2 17.5 %collective-permute-start.9 = (f32[256,256]{1,0:T(8,128)S(1)}, f32[256,256]{1,0:T(8,128)S(1)}, u32[]{:S(2)}, u32[]{:S(2)}) collective-permute-start(f32[256,256]{1,0:T(8,128)S(1)} %pad_maximum_fusion.refs_0_), channel_id=1, source_target_pairs={{0,1},{1,0},{2,3},{3,2},{4,5},{5,4},{6,7},{7,6},{8,9},{9,8},{10,11... | collective-permute-start | bytes 786440 | tf_op jit(solution)/shard_map/ppermute | solution.py:17
  51.1 17.2 %collective-permute-start.13 = (f32[256,256]{1,0:T(8,128)S(1)}, f32[256,256]{1,0:T(8,128)S(1)}, u32[]{:S(2)}, u32[]{:S(2)}) collective-permute-start(f32[256,256]{1,0:T(8,128)S(1)} %collective-permute-done.12.refs_4_), channel_id=1, source_target_pairs={{0,1},{1,0},{2,3},{3,2},{4,5},{5,4},{6,7},{7,6},{8,9},{9,8},{10,11... | collective-permute-start | bytes 786440 | tf_op jit(solution)/shard_map/ppermute | solution.py:17
  53.5 18.0 %collective-permute-start.11 = (f32[256,256]{1,0:T(8,128)S(1)}, f32[256,256]{1,0:T(8,128)}, u32[]{:S(2)}, u32[]{:S(2)}) collective-permute-start(f32[256,256]{1,0:T(8,128)S(1)} %collective-permute-done.10.refs_2_), channel_id=1, source_target_pairs={{0,1},{1,0},{2,3},{3,2},{4,5},{5,4},{6,7},{7,6},{8,9},{9,8},{10,11... | collective-permute-start | bytes 786440 | tf_op jit(solution)/shard_map/ppermute | solution.py:17
  53.8 21.9 %collective-permute-start.15 = (f32[256,256]{1,0:T(8,128)S(1)}, f32[256,256]{1,0:T(8,128)}, u32[]{:S(2)}, u32[]{:S(2)}) collective-permute-start(f32[256,256]{1,0:T(8,128)S(1)} %collective-permute-done.14.refs_6_), channel_id=1, source_target_pairs={{0,1},{1,0},{2,3},{3,2},{4,5},{5,4},{6,7},{7,6},{8,9},{9,8},{10,11... | collective-permute-start | bytes 786440 | tf_op jit(solution)/shard_map/ppermute | solution.py:17
  65.4 1.2 %collective-permute-start.7 = (f32[16,256]{1,0:T(8,128)S(1)}, f32[16,256]{1,0:T(8,128)S(1)}, u32[]{:S(2)}, u32[]{:S(2)}) collective-permute-start(f32[16,256]{1,0:T(8,128)S(1)} %get-tuple-element.37), channel_id=1, source_target_pairs={{0,8},{8,0},{16,24},{24,16},{1,9},{9,1},{17,25},{25,17},{2,10},{10... | collective-permute-start | bytes 49160 | tf_op jit(solution)/shard_map/ppermute | solution.py:17
  67.4 11.9 %collective-permute-start.8 = (f32[16,256]{1,0:T(8,128)S(1)}, f32[16,256]{1,0:T(8,128)S(1)}, u32[]{:S(2)}, u32[]{:S(2)}) collective-permute-start(f32[16,256]{1,0:T(8,128)S(1)} %get-tuple-element.41), channel_id=1, source_target_pairs={{0,8},{8,0},{16,24},{24,16},{1,9},{9,1},{17,25},{25,17},{2,10},{10... | collective-permute-start | bytes 49160 | tf_op jit(solution)/shard_map/ppermute | solution.py:17
  80.3 3.0 %collective-permute-start.16 = (f32[16,256]{1,0:T(8,128)S(1)}, f32[16,256]{1,0:T(8,128)S(1)}, u32[]{:S(2)}, u32[]{:S(2)}) collective-permute-start(f32[16,256]{1,0:T(8,128)S(1)} %get-tuple-element.46), channel_id=1, source_target_pairs={{0,8},{8,0},{16,24},{24,16},{1,9},{9,1},{17,25},{25,17},{2,10},{10... | collective-permute-start | bytes 49160 | tf_op jit(solution)/shard_map/ppermute | solution.py:17
  80.4 3.8 %collective-permute-start.17 = (f32[16,256]{1,0:T(8,128)S(1)}, f32[16,256]{1,0:T(8,128)S(1)}, u32[]{:S(2)}, u32[]{:S(2)}) collective-permute-start(f32[16,256]{1,0:T(8,128)S(1)} %get-tuple-element.47), channel_id=1, source_target_pairs={{0,16},{8,24},{16,0},{24,8},{1,17},{9,25},{17,1},{25,9},{2,18},{10... | collective-permute-start | bytes 49160 | tf_op jit(solution)/shard_map/ppermute | solution.py:17
  81.9 3.2 %collective-permute-start.18 = (f32[16,256]{1,0:T(8,128)S(1)}, f32[16,256]{1,0:T(8,128)S(1)}, u32[]{:S(2)}, u32[]{:S(2)}) collective-permute-start(f32[16,256]{1,0:T(8,128)S(1)} %get-tuple-element.48), channel_id=1, source_target_pairs={{0,24},{8,16},{16,8},{24,0},{1,25},{9,17},{17,9},{25,1},{2,26},{10... | collective-permute-start | bytes 49160 | tf_op jit(solution)/shard_map/ppermute | solution.py:17
  86.1 6.8 %collective-permute-start.21 = (f32[4,16,256]{2,1,0:T(8,128)S(1)}, f32[4,16,256]{2,1,0:T(8,128)S(1)}, u32[]{:S(2)}, u32[]{:S(2)}) collective-permute-start(f32[4,16,256]{2,1,0:T(8,128)S(1)} %shard_map.112.refs_0_), channel_id=1, source_target_pairs={{0,24},{8,16},{16,8},{24,0},{1,25},{9,17},{17,9},{25,1},{2,26},{10... | collective-permute-start | bytes 196616 | tf_op jit(solution)/shard_map/ppermute | solution.py:17
  86.6 6.3 %collective-permute-start.20 = (f32[4,16,256]{2,1,0:T(8,128)S(1)}, f32[4,16,256]{2,1,0:T(8,128)S(1)}, u32[]{:S(2)}, u32[]{:S(2)}) collective-permute-start(f32[4,16,256]{2,1,0:T(8,128)S(1)} %shard_map.112.refs_0_), channel_id=1, source_target_pairs={{0,16},{8,24},{16,0},{24,8},{1,17},{9,25},{17,1},{25,9},{2,18},{10... | collective-permute-start | bytes 196616 | tf_op jit(solution)/shard_map/ppermute | solution.py:17
  87.9 5.0 %collective-permute-start.19 = (f32[4,16,256]{2,1,0:T(8,128)S(1)}, f32[4,16,256]{2,1,0:T(8,128)}, u32[]{:S(2)}, u32[]{:S(2)}) collective-permute-start(f32[4,16,256]{2,1,0:T(8,128)S(1)} %shard_map.112.refs_0_), channel_id=1, source_target_pairs={{0,8},{8,0},{16,24},{24,16},{1,9},{9,1},{17,25},{25,17},{2,10},{10... | collective-permute-start | bytes 196616 | tf_op jit(solution)/shard_map/ppermute | solution.py:17
  88.1 3.5 %collective-permute-start.24 = (f32[1,256]{1,0:T(1,128)S(1)}, f32[1,256]{1,0:T(1,128)S(1)}, u32[]{:S(2)}, u32[]{:S(2)}) collective-permute-start(f32[1,256]{1,0:T(1,128)S(1)} %squeeze.51.refs_4_), channel_id=1, source_target_pairs={{0,24},{8,16},{16,8},{24,0},{1,25},{9,17},{17,9},{25,1},{2,26},{10... | collective-permute-start | bytes 3080 | tf_op jit(solution)/shard_map/ppermute | solution.py:17
  88.8 3.6 %collective-permute-start.23 = (f32[1,256]{1,0:T(1,128)S(1)}, f32[1,256]{1,0:T(1,128)S(1)}, u32[]{:S(2)}, u32[]{:S(2)}) collective-permute-start(f32[1,256]{1,0:T(1,128)S(1)} %squeeze.51.refs_4_), channel_id=1, source_target_pairs={{0,16},{8,24},{16,0},{24,8},{1,17},{9,25},{17,1},{25,9},{2,18},{10... | collective-permute-start | bytes 3080 | tf_op jit(solution)/shard_map/ppermute | solution.py:17
  91.6 1.3 %collective-permute-start.22 = (f32[1,256]{1,0:T(1,128)S(1)}, f32[1,256]{1,0:T(1,128)S(1)}, u32[]{:S(2)}, u32[]{:S(2)}) collective-permute-start(f32[1,256]{1,0:T(1,128)S(1)} %squeeze.51.refs_4_), channel_id=1, source_target_pairs={{0,8},{8,0},{16,24},{24,16},{1,9},{9,1},{17,25},{25,17},{2,10},{10... | collective-permute-start | bytes 3080 | tf_op jit(solution)/shard_map/ppermute | solution.py:17
  94.0 3.2 %collective-permute-start.27 = (f32[16,256]{1,0:T(8,128)S(1)}, f32[16,256]{1,0:T(8,128)S(1)}, u32[]{:S(2)}, u32[]{:S(2)}) collective-permute-start(f32[16,256]{1,0:T(8,128)S(1)} %shard_map.113.refs_0_.refs_2_), channel_id=1, source_target_pairs={{0,24},{8,16},{16,8},{24,0},{1,25},{9,17},{17,9},{25,1},{2,26},{10... | collective-permute-start | bytes 49160 | tf_op jit(solution)/shard_map/ppermute | solution.py:17
  94.7 3.8 %collective-permute-start.26 = (f32[16,256]{1,0:T(8,128)S(1)}, f32[16,256]{1,0:T(8,128)S(1)}, u32[]{:S(2)}, u32[]{:S(2)}) collective-permute-start(f32[16,256]{1,0:T(8,128)S(1)} %shard_map.113.refs_0_.refs_2_), channel_id=1, source_target_pairs={{0,16},{8,24},{16,0},{24,8},{1,17},{9,25},{17,1},{25,9},{2,18},{10... | collective-permute-start | bytes 49160 | tf_op jit(solution)/shard_map/ppermute | solution.py:17
  96.0 2.4 %collective-permute-start.25 = (f32[16,256]{1,0:T(8,128)S(1)}, f32[16,256]{1,0:T(8,128)S(1)}, u32[]{:S(2)}, u32[]{:S(2)}) collective-permute-start(f32[16,256]{1,0:T(8,128)S(1)} %shard_map.113.refs_0_.refs_2_), channel_id=1, source_target_pairs={{0,8},{8,0},{16,24},{24,16},{1,9},{9,1},{17,25},{25,17},{2,10},{10... | collective-permute-start | bytes 49160 | tf_op jit(solution)/shard_map/ppermute | solution.py:17
  99.3 1.2 collective-permute-start.28
  101.2 1.2 collective-permute-start.29
  (39 other events, 128.8 us)

commit v4 on v3

--- a/solution.py
+++ b/solution.py
@@ -17,24 +17,37 @@
     return lax.ppermute(value, axis, [(i, i ^ offset) for i in range(count)])
 
 
-def gather_parts(block, count):
-    parts = {0: block}
-    step = count // 2
-    while step:
-        for offset in list(parts):
-            parts[offset ^ step] = swap(parts[offset], "row", count, step)
-        step //= 2
-    return [parts[offset] for offset in range(count)]
-
-
-def call(body, outs, arrays, scalars=(), scratch=(), work=0):
+def ring_order(count):
+    return list(range(0, count, 2)) + list(range(count - 1, 0, -2))
+
+
+def ring_gather(groups, count):
+    order = ring_order(count)
+    right = [(order[i], order[(i + 1) % count]) for i in range(count)]
+    left = [(target, source) for source, target in right]
+    parts = [[(0, block)] for block in groups]
+    moving = [[block, block] for block in groups]
+    for step in range(1, count // 2 + 1):
+        for index in range(len(groups)):
+            last = 2 * step == count
+            if not last or index % 2 == 0:
+                moving[index][0] = lax.ppermute(moving[index][0], "row", right)
+                parts[index].append((-step, moving[index][0]))
+            if not last or index % 2 == 1:
+                moving[index][1] = lax.ppermute(moving[index][1], "row", left)
+                parts[index].append((step, moving[index][1]))
+    return parts
+
+
+def call(body, outs, arrays, scalars=(), scratch=(), work=0, remote=0):
     moved = sum(a.size * a.dtype.itemsize for a in arrays)
     moved += sum(math.prod(shape) * jnp.dtype(kind).itemsize for shape, kind in outs)
     return pl.pallas_call(
         body,
         out_shape=[jax.ShapeDtypeStruct(*o) for o in outs],
         in_specs=[pl.BlockSpec(memory_space=pltpu.SMEM)] * len(scalars)
-        + [pl.BlockSpec(memory_space=pltpu.VMEM)] * len(arrays),
+        + [pl.BlockSpec(memory_space=pltpu.VMEM)] * (len(arrays) - remote)
+        + [pl.BlockSpec(memory_space=pl.ANY)] * remote,
         out_specs=[pl.BlockSpec(memory_space=pltpu.VMEM)] * len(outs),
         scratch_shapes=list(scratch),
         compiler_params=pltpu.CompilerParams(vmem_limit_bytes=40 << 20),
@@ -98,33 +111,32 @@
     def leaf_swaps(values):
         return [values[0]] + [swap(v, "leaf", leaves, j) for j, v in enumerate(values) if j]
 
-    def inverse_rows(level):
-        return (2**level - 1) * piece, (2 ** (level + 1) - 1) * piece
-
-    def coupling_rows(level):
-        return (2 ** (level + 1) - 2) * piece, (2 ** (level + 2) - 2) * piece
-
-    def gathered(names):
-        rows = []
-        for kind, level in names:
-            source = win_inverse if kind == "A" else win_coupling
-            low, high = inverse_rows(level) if kind == "A" else coupling_rows(level)
-            rows.append(source[0, low:high])
-        return gather_parts(jnp.concatenate(rows, 0), ranks)
+    def source_row(me, step):
+        place = jnp.where(me % 2 == 0, me // 2, ranks - 1 - me // 2)
+        place = (place + step + ranks) % ranks
+        return jnp.where(2 * place < ranks, 2 * place, 2 * (ranks - 1 - place) + 1)
 
     def assemble(parts, names):
         spans = [2**level if kind == "A" else 2 ** (level + 1) for kind, level in names]
+        steps = [step for step, _ in parts]
+        parts = [part for _, part in parts]
 
         def body(ids_ref, *refs):
-            parts_refs, outs = refs[:ranks], refs[ranks:-1]
-            natural = refs[-1]
-            me, group = ids_ref[1], ids_ref[0]
-            for offset, ref in enumerate(parts_refs):
-                start = pl.multiple_of((me ^ offset) * piece, 8)
-                for slot in range(sum(spans)):
-                    natural[slot, pl.ds(start, piece), :] = ref[
-                        slot * piece : (slot + 1) * piece, :
-                    ]
+            parts_refs, outs = refs[:ranks], refs[ranks:-2]
+            natural, done = refs[-2:]
+            group = ids_ref[0]
+            copies = []
+            for index, ref in enumerate(parts_refs):
+                start = pl.multiple_of(source_row(ids_ref[1], steps[index]) * piece, 8)
+                copies.append(
+                    pltpu.make_async_copy(
+                        ref, natural.at[:, pl.ds(start, piece), :], done.at[index]
+                    )
+                )
+            for copy in copies:
+                copy.start()
+            for copy in copies:
+                copy.wait()
             first = 0
             for index, ((kind, level), span) in enumerate(zip(names, spans)):
                 for slot in range(span):
@@ -141,15 +153,24 @@
 
         outs = [((span, base, base), BF16) for span in spans for _ in range(2)]
         made = call(
-            body, outs, parts, (ids,), [pltpu.VMEM((sum(spans), base, base), F32)]
+            body,
+            outs,
+            parts,
+            (ids,),
+            [pltpu.VMEM((sum(spans), base, base), F32), pltpu.SemaphoreType.DMA((ranks,))],
+            remote=ranks,
         )
         return {name: made[2 * i : 2 * i + 2] for i, name in enumerate(names)}
 
     lower_names = [("A", level) for level in range(top)]
-    lower_names += [("B", level) for level in range(top - 1)]
-    upper_names = [("B", top - 1), ("A", top)]
-    lower_parts = gathered(lower_names)
-    upper_parts = gathered(upper_names)
+    lower_names += [("B", level) for level in range(top)]
+    upper_names = [("A", top)]
+    below = (2**top - 1) * piece
+    own_blocks = [
+        jnp.concatenate([win_inverse[0, :below], win_coupling[0]], 0).reshape(-1, piece, base),
+        win_inverse[0, below:].reshape(-1, piece, base),
+    ]
+    lower_parts, upper_parts = ring_gather(own_blocks, ranks)
 
     narrow = TILE - levels * piece
     aux = jnp.concatenate([win_pivots.reshape(-1), pattern[0, 0].astype(F32)])
@@ -158,7 +179,7 @@
     packed = tiles * TILE + TILE
 
     def local_forward(rhs_ref, inverse_ref, coupling_ref, window_ref, aux_ref, *outs):
-        solved_ref, terms_ref, held = outs
+        solved_ref, terms_ref, held = outs[1:]
         rhs = rhs_ref[...]
         solved = rhs + jnp.dot(strict_lower(inverse_ref[...]), rhs, precision=EXACT)
         solved_ref[...] = solved.T
@@ -171,7 +192,8 @@
     solved_loc, terms = call(
         local_forward,
         [((columns, local), F32), ((columns, packed), F32)],
-        (loc_rhs[0, 0], loc_inverse[0, 0], loc_coupling[0, 0], win_rhs, aux),
+        (loc_rhs[0, 0], loc_inverse[0, 0], loc_coupling[0, 0], win_rhs, aux, lower_parts[1][1]),
+        remote=1,
         scratch=[pltpu.VMEM((TILE, columns), F32)],
         work=24 * local * local * columns,
     )
@@ -400,22 +422,35 @@
     )
     back = lax.all_to_all(replies[0], "row", 0, 0, tiled=True).reshape(columns, packed)
 
-    def local_backward(back, solved_ref, pivot_ref, inverse_ref, coupling_ref, out, window_ref):
-        remainder = solved_ref[...] / pivot_ref[...] - jnp.dot(
-            back[:, : tiles * TILE], coupling_ref[...], precision=EXACT
-        )
-        answer = remainder + jnp.dot(
-            remainder, strict_lower(inverse_ref[...]), precision=EXACT
-        )
-        out[...] = answer.T
+    def local_backward(back, solved_ref, pivot_ref, inverse_any, coupling_any, *refs):
+        out, window_ref, inverse_ref, coupling_ref, done = refs
+        first = pltpu.make_async_copy(coupling_any, coupling_ref, done.at[0])
+        second = pltpu.make_async_copy(inverse_any, inverse_ref, done.at[1])
+        first.start()
+        second.start()
         final = back[:, tiles * TILE :].T
         for level in range(levels):
             window_ref[level] = final[level * piece : (level + 1) * piece]
+        first.wait()
+        remainder = solved_ref[...] / pivot_ref[...] - jnp.dot(
+            back[:, : tiles * TILE], coupling_ref[...], precision=EXACT
+        )
+        second.wait()
+        answer = remainder + jnp.dot(
+            remainder, strict_lower(inverse_ref[...]), precision=EXACT
+        )
+        out[...] = answer.T
 
     answer, window = call(
         local_backward,
         [((local, columns), F32), ((levels, piece, columns), F32)],
         (back, solved_loc, loc_pivots[0], loc_inverse[0, 0], loc_coupling[0, 0]),
+        scratch=[
+            pltpu.VMEM((local, local), F32),
+            pltpu.VMEM((tiles * TILE, local), F32),
+            pltpu.SemaphoreType.DMA((2,)),
+        ],
+        remote=2,
         work=24 * local * local * columns,
     )
     return answer[None, None], window

time: 124 us -> 121 us (0.976)
  waiting for transfers between devices: 33.3 us -> 31.2 us
  starting transfers between devices: 32.5 us -> 30.7 us
  Pallas kernels: 17.6 us -> 19.4 us
  local copies, waits for them, and re-layouts: 22.9 us -> 21.5 us
    ppermute x30 -> x16, waiting for transfers between devices: 33.3 us -> 8.24 us  [swap(): return lax.ppermute(value, axis, [(i, i ^ offset) for i in range(count)])]
    ppermute x0 -> x14, waiting for transfers between devices: none -> 23 us  [the longest x7 16 us: ring_gather(): moving[index][1] = lax.ppermute(moving[index][1], 'row', left)]
    ppermute x30 -> x16, starting transfers between devices: 28.7 us -> 9.14 us  [swap(): return lax.ppermute(value, axis, [(i, i ^ offset) for i in range(count)])]
    ppermute x0 -> x14, starting transfers between devices: none -> 16.6 us  [the longest x7 11 us: ring_gather(): moving[index][0] = lax.ppermute(moving[index][0], 'row', right)]
    pallas_call x14, Pallas kernels: 17.6 us -> 19.4 us  [call(): pl.pallas_call(body, out_shape=[jax.ShapeDtypeStruct(*o) for o in outs],...]
    unnamed x78 -> x82, local copies, waits for them, and re-layouts: 18.3 us -> 16.5 us
    squeeze x3 -> x1, local copies, waits for them, and re-layouts: 2.72 us -> 0.94 us  [shards(): win_inverse[0, :below]]
  transfers between devices with their start and end apart: 31 -> 31, of which waited for: 14 -> 14; matrix products, arithmetic and copies ran while one was open for 3% -> 3% of each run, Pallas kernels for 8% -> 10%
where the time goes in v4:
time: 121 us; the launch traced here: 120 us
  waiting for transfers between devices  31.2 us (26%)
  starting transfers between devices  30.7 us (25%)
  local copies, waits for them, and re-layouts  21.5 us (18%)
  Pallas kernels  19.4 us (16%)
  blocking collectives  15.8 us (13%)
    pallas_call x14, Pallas kernels, call(): pl.pallas_call(body, out_shape=[jax.ShapeDtypeStruct(*o) for o in outs],...  19.4 us
    unnamed x82, local copies, waits for them, and re-layouts  16.5 us
    ppermute x7, waiting for transfers between devices, ring_gather(): moving[index][1] = lax.ppermute(moving[index][1], 'row', left)  16 us
    all_to_all x1, blocking collectives, shards(): lax.all_to_all(replies[0], 'row', 0, 0, tiled=True).reshape(columns, packed)  15.8 us
    ppermute x7, starting transfers between devices, ring_gather(): moving[index][0] = lax.ppermute(moving[index][0], 'row', right)  11 us
    ppermute x16, starting transfers between devices, swap(): return lax.ppermute(value, axis, [(i, i ^ offset) for i in range(count)])  9.14 us
    ppermute x16, waiting for transfers between devices, swap(): return lax.ppermute(value, axis, [(i, i ^ offset) for i in range(count)])  8.24 us
    ppermute x7, waiting for transfers between devices, ring_gather(): moving[index][0] = lax.ppermute(moving[index][0], 'row', right)  6.96 us
  transfers between devices with their start and end apart: 31, of which 14 were waited for; matrix products, arithmetic and copies ran while one was open for 3% of the time, Pallas kernels for 10%

profile of v4, /device:TPU:0, one launch (start us, length us, event | category | flops | bytes accessed | tf_op | source)
XLA Modules:
  0.0 119.9 jit_solution(3011729456440727737)
XLA Ops:
  1.7 3.1 %collective-permute-start = (f32[9,32,256]{2,1,0:T(8,128)S(1)}, f32[9,32,256]{2,1,0:T(8,128)S(1)}, u32[]{:S(2)}, u32[]{:S(2)}) collective-permute-start(f32[9,32,256]{2,1,0:T(8,128)S(1)} %bitcast.19), channel_id=1, source_target_pairs={{0,2},{2,4},{4,6},{6,7},{7,5},{5,3},{3,1},{1,0},{8,10},{10,12},{12... | collective-permute-start | bytes 884744 | tf_op jit(solution)/shard_map/ppermute | solution.py:34
  4.8 6.9 %collective-permute-done.outs_0_.refs_1_ = f32[9,32,256]{2,1,0:T(8,128)S(1)} collective-permute-done((f32[9,32,256]{2,1,0:T(8,128)S(1)}, f32[9,32,256]{2,1,0:T(8,128)S(1)}, u32[]{:S(2)}, u32[]{:S(2)}) %collective-permute-start) | collective-permute-done | bytes 294944 | tf_op jit(solution)/shard_map/ppermute | solution.py:34
  11.7 1.8 %collective-permute-start.2 = (f32[9,32,256]{2,1,0:T(8,128)S(1)}, f32[9,32,256]{2,1,0:T(8,128)S(1)}, u32[]{:S(2)}, u32[]{:S(2)}) collective-permute-start(f32[9,32,256]{2,1,0:T(8,128)S(1)} %collective-permute-done.outs_0_.refs_1_), channel_id=1, source_target_pairs={{0,2},{2,4},{4,6},{6,7},{7,5},{5,3},{3,1},{1,0},{8,10},{10,12},{12... | collective-permute-start | bytes 884744 | tf_op jit(solution)/shard_map/ppermute | solution.py:34
  14.4 1.2 %copy-done.26 = f32[1,1,512,512]{3,2,1,0:T(8,128)S(1)} copy-done((f32[1,1,512,512]{3,2,1,0:T(8,128)S(1)}, f32[1,1,512,512]{3,2,1,0:T(8,128)}, u32[]{:S(2)}) %copy-start.26) | copy-done | bytes 1048600
  15.7 1.2 %copy-done.28 = f32[1,1,512,512]{3,2,1,0:T(8,128)S(1)} copy-done((f32[1,1,512,512]{3,2,1,0:T(8,128)S(1)}, f32[1,1,512,512]{3,2,1,0:T(8,128)}, u32[]{:S(2)}) %copy-start.28) | copy-done | bytes 1048600
  16.9 4.3 %shard_map.104 = (f32[128,512]{1,0:T(8,128)S(1)}, f32[128,640]{1,0:T(8,128)}) custom-call(f32[512,128]{1,0:T(8,128)S(1)} %bitcast.32, f32[512,512]{1,0:T(8,128)S(1)} %bitcast.28, f32[512,512]{1,0:T(8,128)S(1)} %bitcast.30, f32[3,32,128]{2,1,0:T(8,128)S(1)} %copy-done.31, f32[128,128]{1,0:T(8,128)S(1)} %bitcast.26, ...), custom_call_target="tpu_custom_call" | custom-call | flops 805306368 | bytes 3358720 | tf_op jit(solution)/shard_map/pallas_call | solution.py:45
  21.8 5.0 %all-to-all-start = ((f32[8,16,640]{2,1,0:T(8,128)}), f32[8,16,640]{2,1,0:T(8,128)S(1)}, u32[]{:S(2)}, u32[]{:S(2)}) async-start(f32[8,16,640]{2,1,0:T(8,128)} %bitcast.10), calls=%async_computation | async-start | bytes 655360 | tf_op jit(solution)/shard_map/all_to_all | solution.py:200
  26.8 2.1 %collective-permute-start.3 = (f32[9,32,256]{2,1,0:T(8,128)S(1)}, f32[9,32,256]{2,1,0:T(8,128)S(1)}, u32[]{:S(2)}, u32[]{:S(2)}) collective-permute-start(f32[9,32,256]{2,1,0:T(8,128)S(1)} %collective-permute-done.1.refs_2_), channel_id=1, source_target_pairs={{2,0},{4,2},{6,4},{7,6},{5,7},{3,5},{1,3},{0,1},{10,8},{12,10},{14... | collective-permute-start | bytes 884744 | tf_op jit(solution)/shard_map/ppermute | solution.py:37
  29.0 2.0 %collective-permute-start.13 = (f32[4,32,256]{2,1,0:T(8,128)S(1)}, f32[4,32,256]{2,1,0:T(8,128)S(1)}, u32[]{:S(2)}, u32[]{:S(2)}) collective-permute-start(f32[4,32,256]{2,1,0:T(8,128)S(1)} %bitcast.22), channel_id=1, source_target_pairs={{2,0},{4,2},{6,4},{7,6},{5,7},{3,5},{1,3},{0,1},{10,8},{12,10},{14... | collective-permute-start | bytes 393224 | tf_op jit(solution)/shard_map/ppermute | solution.py:37
  31.1 11.3 %collective-permute-done.13.refs_2_ = f32[4,32,256]{2,1,0:T(8,128)S(1)} collective-permute-done((f32[4,32,256]{2,1,0:T(8,128)S(1)}, f32[4,32,256]{2,1,0:T(8,128)S(1)}, u32[]{:S(2)}, u32[]{:S(2)}) %collective-permute-start.13) | collective-permute-done | bytes 131104 | tf_op jit(solution)/shard_map/ppermute | solution.py:37
  43.0 3.3 %collective-permute-start.14 = (f32[4,32,256]{2,1,0:T(8,128)S(1)}, f32[4,32,256]{2,1,0:T(8,128)}, u32[]{:S(2)}, u32[]{:S(2)}) collective-permute-start(f32[4,32,256]{2,1,0:T(8,128)S(1)} %collective-permute-done.12.refs_1_), channel_id=1, source_target_pairs={{0,2},{2,4},{4,6},{6,7},{7,5},{5,3},{3,1},{1,0},{8,10},{10,12},{12... | collective-permute-start | bytes 393224 | tf_op jit(solution)/shard_map/ppermute | solution.py:34
  47.0 1.6 %collective-permute-done.15.refs_4_ = f32[4,32,256]{2,1,0:T(8,128)S(1)} collective-permute-done((f32[4,32,256]{2,1,0:T(8,128)S(1)}, f32[4,32,256]{2,1,0:T(8,128)S(1)}, u32[]{:S(2)}, u32[]{:S(2)}) %collective-permute-start.15) | collective-permute-done | bytes 131104 | tf_op jit(solution)/shard_map/ppermute | solution.py:37
  49.2 1.6 %collective-permute-start.5 = (f32[9,32,256]{2,1,0:T(8,128)S(1)}, f32[9,32,256]{2,1,0:T(8,128)S(1)}, u32[]{:S(2)}, u32[]{:S(2)}) collective-permute-start(f32[9,32,256]{2,1,0:T(8,128)S(1)} %collective-permute-done.3.refs_4_), channel_id=1, source_target_pairs={{2,0},{4,2},{6,4},{7,6},{5,7},{3,5},{1,3},{0,1},{10,8},{12,10},{14... | collective-permute-start | bytes 884744 | tf_op jit(solution)/shard_map/ppermute | solution.py:37
  53.0 2.0 %collective-permute-start.16 = (f32[4,32,256]{2,1,0:T(8,128)}, f32[4,32,256]{2,1,0:T(8,128)}, u32[]{:S(2)}, u32[]{:S(2)}) collective-permute-start(f32[4,32,256]{2,1,0:T(8,128)} %collective-permute-done.14.refs_3_), channel_id=1, source_target_pairs={{0,2},{2,4},{4,6},{6,7},{7,5},{5,3},{3,1},{1,0},{8,10},{10,12},{12... | collective-permute-start | bytes 393224 | tf_op jit(solution)/shard_map/ppermute | solution.py:34
  56.4 2.8 %collective-permute-done.5.refs_6_ = f32[9,32,256]{2,1,0:T(8,128)S(1)} collective-permute-done((f32[9,32,256]{2,1,0:T(8,128)S(1)}, f32[9,32,256]{2,1,0:T(8,128)S(1)}, u32[]{:S(2)}, u32[]{:S(2)}) %collective-permute-start.5) | collective-permute-done | bytes 294944 | tf_op jit(solution)/shard_map/ppermute | solution.py:37
  65.5 1.2 %shard_map.106 = (bf16[1,256,256]{2,1,0:T(8,128)(2,1)S(1)}, bf16[1,256,256]{2,1,0:T(8,128)(2,1)S(1)}, bf16[2,256,256]{2,1,0:T(8,128)(2,1)S(1)}, bf16[2,256,256]{...) custom-call(s32[2]{0:T(128)S(1)} %pad_add_fusion.ids_ref, ...), custom_call_target="tpu_custom_call" | custom-call | bytes 4718592 | tf_op jit(solution)/shard_map/pallas_call | solution.py:45
  68.4 1.2 collective-permute-done.7.refs_1_
  70.6 1.0 collective-permute-done.8.refs_1_
  71.7 1.6 %shard_map.110 = (f32[16,256]{1,0:T(8,128)S(1)}, f32[16,256]{1,0:T(8,128)S(1)}, f32[16,256]{1,0:T(8,128)}, f32[16,256]{1,0:T(8,128)}, f32[16,256]{1,0:T(8,128)}) custom-call(s32[2]{0:T(128)S(1)} %pad_add_fusion.ids_ref, f32[16,256]{1,0:T(8,128)S(1)} %get-tuple-element.40.refs_0_, f32[16,256]{1,0:T(8,128)S(1)} %collective-permute-done.8.refs_1_, ...), custom_call_target="tpu_custom_call" | custom-call | bytes 1228800 | tf_op jit(solution)/shard_map/pallas_call | solution.py:45
  73.2 1.5 %collective-permute-start.10 = (f32[16,256]{1,0:T(8,128)}, f32[16,256]{1,0:T(8,128)}, u32[]{:S(2)}, u32[]{:S(2)}) collective-permute-start(f32[16,256]{1,0:T(8,128)} %get-tuple-element.47), channel_id=1, source_target_pairs={{0,16},{8,24},{16,0},{24,8},{1,17},{9,25},{17,1},{25,9},{2,18},{10... | collective-permute-start | bytes 49160 | tf_op jit(solution)/shard_map/ppermute | solution.py:17
  75.4 2.1 %shard_map.111 = (bf16[4,256,256]{2,1,0:T(8,128)(2,1)S(1)}, bf16[4,256,256]{2,1,0:T(8,128)(2,1)S(1)}) custom-call(s32[2]{0:T(128)S(1)} %pad_add_fusion.ids_ref, f32[4,32,256]{2,1,0:T(8,128)S(1)} %bitcast.24, f32[4,32,256]{2,1,0:T(8,128)S(1)} %copy-done.15, f32[4,32,256]{2,1,0:T(8,128)S(1)} %copy-done.13, f32[4,32,256]{2,1,0:T(8,128)} %collective-permute-done.14.refs_3_, ...), custom_call_target="tpu_custom_call" | custom-call | bytes 2097152 | tf_op jit(solution)/shard_map/pallas_call | solution.py:45
  79.0 1.2 shard_map.112.refs_0_
  80.2 1.6 %collective-permute-start.20 = (f32[4,16,256]{2,1,0:T(8,128)S(1)}, f32[4,16,256]{2,1,0:T(8,128)}, u32[]{:S(2)}, u32[]{:S(2)}) collective-permute-start(f32[4,16,256]{2,1,0:T(8,128)S(1)} %shard_map.112.refs_0_), channel_id=1, source_target_pairs={{0,16},{8,24},{16,0},{24,8},{1,17},{9,25},{17,1},{25,9},{2,18},{10... | collective-permute-start | bytes 196616 | tf_op jit(solution)/shard_map/ppermute | solution.py:17
  83.8 1.5 %collective-permute-start.23 = (f32[1,256]{1,0:T(1,128)S(1)}, f32[1,256]{1,0:T(1,128)S(1)}, u32[]{:S(2)}, u32[]{:S(2)}) collective-permute-start(f32[1,256]{1,0:T(1,128)S(1)} %squeeze.39.refs_4_), channel_id=1, source_target_pairs={{0,16},{8,24},{16,0},{24,8},{1,17},{9,25},{17,1},{25,9},{2,18},{10... | collective-permute-start | bytes 3080 | tf_op jit(solution)/shard_map/ppermute | solution.py:17
  86.1 1.3 %collective-permute-done.23.refs_6_ = f32[1,256]{1,0:T(1,128)S(1)} collective-permute-done((f32[1,256]{1,0:T(1,128)S(1)}, f32[1,256]{1,0:T(1,128)S(1)}, u32[]{:S(2)}, u32[]{:S(2)}) %collective-permute-start.23) | collective-permute-done | bytes 1056 | tf_op jit(solution)/shard_map/ppermute | solution.py:17
  89.8 1.2 shard_map.113.refs_0_.refs_2_
  91.1 1.0 collective-permute-start.26
  93.6 1.3 %collective-permute-done.26.refs_2_.refs_4_ = f32[16,256]{1,0:T(8,128)S(1)} collective-permute-done((f32[16,256]{1,0:T(8,128)S(1)}, f32[16,256]{1,0:T(8,128)S(1)}, u32[]{:S(2)}, u32[]{:S(2)}) %collective-permute-start.26) | collective-permute-done | bytes 16416 | tf_op jit(solution)/shard_map/ppermute | solution.py:17
  97.0 1.1 collective-permute-done.28.refs_1_
  100.0 1.0 shard_map.116
  101.1 15.8 %all_to_all.10 = f32[8,16,640]{2,1,0:T(8,128)S(1)} all-to-all(f32[8,16,640]{2,1,0:T(8,128)S(1)} %shard_map.116), channel_id=1, replica_groups=mesh['leaf'=4,'row'=8] {'row'}, dimensions={0} | all-to-all | bytes 655360 | tf_op jit(solution)/shard_map/all_to_all | solution.py:423
  117.5 2.3 %shard_map.117 = (f32[512,128]{1,0:T(8,128)}, f32[3,32,128]{2,1,0:T(8,128)}) custom-call(f32[128,640]{1,0:T(8,128)S(1)} %bitcast.25, f32[128,512]{1,0:T(8,128)S(1)} %copy-done.34, f32[1,512]{1,0:T(1,128)S(1)} %bitcast.33, f32[512,512]{1,0:T(8,128)S(1)} %bitcast.29, f32[512,512]{1,0:T(8,128)S(1)} %bitcast.31), custom_call_target="tpu_custom_call" | custom-call | flops 805306368 | bytes 3000320 | tf_op jit(solution)/shard_map/pallas_call | solution.py:45
  (148 shorter events, 31.1 us)
Async XLA Ops:
  1.7 10.0 %collective-permute-start = (f32[9,32,256]{2,1,0:T(8,128)S(1)}, f32[9,32,256]{2,1,0:T(8,128)S(1)}, u32[]{:S(2)}, u32[]{:S(2)}) collective-permute-start(f32[9,32,256]{2,1,0:T(8,128)S(1)} %bitcast.19), channel_id=1, source_target_pairs={{0,2},{2,4},{4,6},{6,7},{7,5},{5,3},{3,1},{1,0},{8,10},{10,12},{12... | collective-permute-start | bytes 884744 | tf_op jit(solution)/shard_map/ppermute | solution.py:34
  4.7 22.1 %collective-permute-start.1 = (f32[9,32,256]{2,1,0:T(8,128)S(1)}, f32[9,32,256]{2,1,0:T(8,128)S(1)}, u32[]{:S(2)}, u32[]{:S(2)}) collective-permute-start(f32[9,32,256]{2,1,0:T(8,128)S(1)} %bitcast.20), channel_id=1, source_target_pairs={{2,0},{4,2},{6,4},{7,6},{5,7},{3,5},{1,3},{0,1},{10,8},{12,10},{14... | collective-permute-start | bytes 884744 | tf_op jit(solution)/shard_map/ppermute | solution.py:37
  11.7 17.2 %collective-permute-start.2 = (f32[9,32,256]{2,1,0:T(8,128)S(1)}, f32[9,32,256]{2,1,0:T(8,128)S(1)}, u32[]{:S(2)}, u32[]{:S(2)}) collective-permute-start(f32[9,32,256]{2,1,0:T(8,128)S(1)} %collective-permute-done.outs_0_.refs_1_), channel_id=1, source_target_pairs={{0,2},{2,4},{4,6},{6,7},{7,5},{5,3},{3,1},{1,0},{8,10},{10,12},{12... | collective-permute-start | bytes 884744 | tf_op jit(solution)/shard_map/ppermute | solution.py:34
  21.8 33.5 %all-to-all-start = ((f32[8,16,640]{2,1,0:T(8,128)}), f32[8,16,640]{2,1,0:T(8,128)S(1)}, u32[]{:S(2)}, u32[]{:S(2)}) async-start(f32[8,16,640]{2,1,0:T(8,128)} %bitcast.10), calls=%async_computation | async-start | bytes 655360 | tf_op jit(solution)/shard_map/all_to_all | solution.py:200
  26.8 29.6 %copy-start = (f32[9,32,256]{2,1,0:T(8,128)}, f32[9,32,256]{2,1,0:T(8,128)S(1)}, u32[]{:S(2)}) copy-start(f32[9,32,256]{2,1,0:T(8,128)S(1)} %collective-permute-done.1.refs_2_) | copy-start | bytes 884740
  26.8 22.4 %collective-permute-start.3 = (f32[9,32,256]{2,1,0:T(8,128)S(1)}, f32[9,32,256]{2,1,0:T(8,128)S(1)}, u32[]{:S(2)}, u32[]{:S(2)}) collective-permute-start(f32[9,32,256]{2,1,0:T(8,128)S(1)} %collective-permute-done.1.refs_2_), channel_id=1, source_target_pairs={{2,0},{4,2},{6,4},{7,6},{5,7},{3,5},{1,3},{0,1},{10,8},{12,10},{14... | collective-permute-start | bytes 884744 | tf_op jit(solution)/shard_map/ppermute | solution.py:37
  28.9 22.6 %collective-permute-start.4 = (f32[9,32,256]{2,1,0:T(8,128)S(1)}, f32[9,32,256]{2,1,0:T(8,128)S(1)}, u32[]{:S(2)}, u32[]{:S(2)}) collective-permute-start(f32[9,32,256]{2,1,0:T(8,128)S(1)} %collective-permute-done.2.refs_3_), channel_id=1, source_target_pairs={{0,2},{2,4},{4,6},{6,7},{7,5},{5,3},{3,1},{1,0},{8,10},{10,12},{12... | collective-permute-start | bytes 884744 | tf_op jit(solution)/shard_map/ppermute | solution.py:34
  29.0 13.4 %collective-permute-start.13 = (f32[4,32,256]{2,1,0:T(8,128)S(1)}, f32[4,32,256]{2,1,0:T(8,128)S(1)}, u32[]{:S(2)}, u32[]{:S(2)}) collective-permute-start(f32[4,32,256]{2,1,0:T(8,128)S(1)} %bitcast.22), channel_id=1, source_target_pairs={{2,0},{4,2},{6,4},{7,6},{5,7},{3,5},{1,3},{0,1},{10,8},{12,10},{14... | collective-permute-start | bytes 393224 | tf_op jit(solution)/shard_map/ppermute | solution.py:37
  31.0 12.1 %collective-permute-start.12 = (f32[4,32,256]{2,1,0:T(8,128)S(1)}, f32[4,32,256]{2,1,0:T(8,128)S(1)}, u32[]{:S(2)}, u32[]{:S(2)}) collective-permute-start(f32[4,32,256]{2,1,0:T(8,128)S(1)} %bitcast.23), channel_id=1, source_target_pairs={{0,2},{2,4},{4,6},{6,7},{7,5},{5,3},{3,1},{1,0},{8,10},{10,12},{12... | collective-permute-start | bytes 393224 | tf_op jit(solution)/shard_map/ppermute | solution.py:34
  42.4 6.2 %collective-permute-start.15 = (f32[4,32,256]{2,1,0:T(8,128)S(1)}, f32[4,32,256]{2,1,0:T(8,128)S(1)}, u32[]{:S(2)}, u32[]{:S(2)}) collective-permute-start(f32[4,32,256]{2,1,0:T(8,128)S(1)} %collective-permute-done.13.refs_2_), channel_id=1, source_target_pairs={{2,0},{4,2},{6,4},{7,6},{5,7},{3,5},{1,3},{0,1},{10,8},{12,10},{14... | collective-permute-start | bytes 393224 | tf_op jit(solution)/shard_map/ppermute | solution.py:37
  43.0 10.0 %collective-permute-start.14 = (f32[4,32,256]{2,1,0:T(8,128)S(1)}, f32[4,32,256]{2,1,0:T(8,128)}, u32[]{:S(2)}, u32[]{:S(2)}) collective-permute-start(f32[4,32,256]{2,1,0:T(8,128)S(1)} %collective-permute-done.12.refs_1_), channel_id=1, source_target_pairs={{0,2},{2,4},{4,6},{6,7},{7,5},{5,3},{3,1},{1,0},{8,10},{10,12},{12... | collective-permute-start | bytes 393224 | tf_op jit(solution)/shard_map/ppermute | solution.py:34
  48.6 6.8 %collective-permute-start.17 = (f32[4,32,256]{2,1,0:T(8,128)S(1)}, f32[4,32,256]{2,1,0:T(8,128)}, u32[]{:S(2)}, u32[]{:S(2)}) collective-permute-start(f32[4,32,256]{2,1,0:T(8,128)S(1)} %collective-permute-done.15.refs_4_), channel_id=1, source_target_pairs={{2,0},{4,2},{6,4},{7,6},{5,7},{3,5},{1,3},{0,1},{10,8},{12,10},{14... | collective-permute-start | bytes 393224 | tf_op jit(solution)/shard_map/ppermute | solution.py:37
  49.2 9.9 %collective-permute-start.5 = (f32[9,32,256]{2,1,0:T(8,128)S(1)}, f32[9,32,256]{2,1,0:T(8,128)S(1)}, u32[]{:S(2)}, u32[]{:S(2)}) collective-permute-start(f32[9,32,256]{2,1,0:T(8,128)S(1)} %collective-permute-done.3.refs_4_), channel_id=1, source_target_pairs={{2,0},{4,2},{6,4},{7,6},{5,7},{3,5},{1,3},{0,1},{10,8},{12,10},{14... | collective-permute-start | bytes 884744 | tf_op jit(solution)/shard_map/ppermute | solution.py:37
  51.5 8.5 %collective-permute-start.6 = (f32[9,32,256]{2,1,0:T(8,128)S(1)}, f32[9,32,256]{2,1,0:T(8,128)S(1)}, u32[]{:S(2)}, u32[]{:S(2)}) collective-permute-start(f32[9,32,256]{2,1,0:T(8,128)S(1)} %collective-permute-done.4.refs_5_), channel_id=1, source_target_pairs={{0,2},{2,4},{4,6},{6,7},{7,5},{5,3},{3,1},{1,0},{8,10},{10,12},{12... | collective-permute-start | bytes 884744 | tf_op jit(solution)/shard_map/ppermute | solution.py:34
  53.0 22.4 %collective-permute-start.16 = (f32[4,32,256]{2,1,0:T(8,128)}, f32[4,32,256]{2,1,0:T(8,128)}, u32[]{:S(2)}, u32[]{:S(2)}) collective-permute-start(f32[4,32,256]{2,1,0:T(8,128)} %collective-permute-done.14.refs_3_), channel_id=1, source_target_pairs={{0,2},{2,4},{4,6},{6,7},{7,5},{5,3},{3,1},{1,0},{8,10},{10,12},{12... | collective-permute-start | bytes 393224 | tf_op jit(solution)/shard_map/ppermute | solution.py:34
  55.4 20.0 %collective-permute-start.18 = (f32[4,32,256]{2,1,0:T(8,128)}, f32[4,32,256]{2,1,0:T(8,128)}, u32[]{:S(2)}, u32[]{:S(2)}) collective-permute-start(f32[4,32,256]{2,1,0:T(8,128)} %collective-permute-done.17.refs_6_), channel_id=1, source_target_pairs={{2,0},{4,2},{6,4},{7,6},{5,7},{3,5},{1,3},{0,1},{10,8},{12,10},{14... | collective-permute-start | bytes 393224 | tf_op jit(solution)/shard_map/ppermute | solution.py:37
  68.3 1.2 %collective-permute-start.7 = (f32[16,256]{1,0:T(8,128)S(1)}, f32[16,256]{1,0:T(8,128)S(1)}, u32[]{:S(2)}, u32[]{:S(2)}) collective-permute-start(f32[16,256]{1,0:T(8,128)S(1)} %get-tuple-element.37), channel_id=1, source_target_pairs={{0,8},{8,0},{16,24},{24,16},{1,9},{9,1},{17,25},{25,17},{2,10},{10... | collective-permute-start | bytes 49160 | tf_op jit(solution)/shard_map/ppermute | solution.py:17
  70.4 1.2 %collective-permute-start.8 = (f32[16,256]{1,0:T(8,128)S(1)}, f32[16,256]{1,0:T(8,128)S(1)}, u32[]{:S(2)}, u32[]{:S(2)}) collective-permute-start(f32[16,256]{1,0:T(8,128)S(1)} %get-tuple-element.41), channel_id=1, source_target_pairs={{0,8},{8,0},{16,24},{24,16},{1,9},{9,1},{17,25},{25,17},{2,10},{10... | collective-permute-start | bytes 49160 | tf_op jit(solution)/shard_map/ppermute | solution.py:17
  73.2 5.7 %collective-permute-start.10 = (f32[16,256]{1,0:T(8,128)}, f32[16,256]{1,0:T(8,128)}, u32[]{:S(2)}, u32[]{:S(2)}) collective-permute-start(f32[16,256]{1,0:T(8,128)} %get-tuple-element.47), channel_id=1, source_target_pairs={{0,16},{8,24},{16,0},{24,8},{1,17},{9,25},{17,1},{25,9},{2,18},{10... | collective-permute-start | bytes 49160 | tf_op jit(solution)/shard_map/ppermute | solution.py:17
  74.7 4.2 %collective-permute-start.11 = (f32[16,256]{1,0:T(8,128)}, f32[16,256]{1,0:T(8,128)}, u32[]{:S(2)}, u32[]{:S(2)}) collective-permute-start(f32[16,256]{1,0:T(8,128)} %get-tuple-element.48), channel_id=1, source_target_pairs={{0,24},{8,16},{16,8},{24,0},{1,25},{9,17},{17,9},{25,1},{2,26},{10... | collective-permute-start | bytes 49160 | tf_op jit(solution)/shard_map/ppermute | solution.py:17
  74.8 4.2 %collective-permute-start.9 = (f32[16,256]{1,0:T(8,128)}, f32[16,256]{1,0:T(8,128)}, u32[]{:S(2)}, u32[]{:S(2)}) collective-permute-start(f32[16,256]{1,0:T(8,128)} %get-tuple-element.46), channel_id=1, source_target_pairs={{0,8},{8,0},{16,24},{24,16},{1,9},{9,1},{17,25},{25,17},{2,10},{10... | collective-permute-start | bytes 49160 | tf_op jit(solution)/shard_map/ppermute | solution.py:17
  80.2 8.2 %collective-permute-start.19 = (f32[4,16,256]{2,1,0:T(8,128)S(1)}, f32[4,16,256]{2,1,0:T(8,128)S(1)}, u32[]{:S(2)}, u32[]{:S(2)}) collective-permute-start(f32[4,16,256]{2,1,0:T(8,128)S(1)} %shard_map.112.refs_0_), channel_id=1, source_target_pairs={{0,8},{8,0},{16,24},{24,16},{1,9},{9,1},{17,25},{25,17},{2,10},{10... | collective-permute-start | bytes 196616 | tf_op jit(solution)/shard_map/ppermute | solution.py:17
  80.2 8.7 %collective-permute-start.20 = (f32[4,16,256]{2,1,0:T(8,128)S(1)}, f32[4,16,256]{2,1,0:T(8,128)}, u32[]{:S(2)}, u32[]{:S(2)}) collective-permute-start(f32[4,16,256]{2,1,0:T(8,128)S(1)} %shard_map.112.refs_0_), channel_id=1, source_target_pairs={{0,16},{8,24},{16,0},{24,8},{1,17},{9,25},{17,1},{25,9},{2,18},{10... | collective-permute-start | bytes 196616 | tf_op jit(solution)/shard_map/ppermute | solution.py:17
  81.8 7.1 %collective-permute-start.21 = (f32[4,16,256]{2,1,0:T(8,128)S(1)}, f32[4,16,256]{2,1,0:T(8,128)}, u32[]{:S(2)}, u32[]{:S(2)}) collective-permute-start(f32[4,16,256]{2,1,0:T(8,128)S(1)} %shard_map.112.refs_0_), channel_id=1, source_target_pairs={{0,24},{8,16},{16,8},{24,0},{1,25},{9,17},{17,9},{25,1},{2,26},{10... | collective-permute-start | bytes 196616 | tf_op jit(solution)/shard_map/ppermute | solution.py:17
  83.5 1.8 %collective-permute-start.22 = (f32[1,256]{1,0:T(1,128)S(1)}, f32[1,256]{1,0:T(1,128)S(1)}, u32[]{:S(2)}, u32[]{:S(2)}) collective-permute-start(f32[1,256]{1,0:T(1,128)S(1)} %squeeze.39.refs_4_), channel_id=1, source_target_pairs={{0,8},{8,0},{16,24},{24,16},{1,9},{9,1},{17,25},{25,17},{2,10},{10... | collective-permute-start | bytes 3080 | tf_op jit(solution)/shard_map/ppermute | solution.py:17
  83.8 3.6 %collective-permute-start.23 = (f32[1,256]{1,0:T(1,128)S(1)}, f32[1,256]{1,0:T(1,128)S(1)}, u32[]{:S(2)}, u32[]{:S(2)}) collective-permute-start(f32[1,256]{1,0:T(1,128)S(1)} %squeeze.39.refs_4_), channel_id=1, source_target_pairs={{0,16},{8,24},{16,0},{24,8},{1,17},{9,25},{17,1},{25,9},{2,18},{10... | collective-permute-start | bytes 3080 | tf_op jit(solution)/shard_map/ppermute | solution.py:17
  85.3 3.0 %collective-permute-start.24 = (f32[1,256]{1,0:T(1,128)S(1)}, f32[1,256]{1,0:T(1,128)S(1)}, u32[]{:S(2)}, u32[]{:S(2)}) collective-permute-start(f32[1,256]{1,0:T(1,128)S(1)} %squeeze.39.refs_4_), channel_id=1, source_target_pairs={{0,24},{8,16},{16,8},{24,0},{1,25},{9,17},{17,9},{25,1},{2,26},{10... | collective-permute-start | bytes 3080 | tf_op jit(solution)/shard_map/ppermute | solution.py:17
  90.9 2.6 %collective-permute-start.25 = (f32[16,256]{1,0:T(8,128)S(1)}, f32[16,256]{1,0:T(8,128)S(1)}, u32[]{:S(2)}, u32[]{:S(2)}) collective-permute-start(f32[16,256]{1,0:T(8,128)S(1)} %shard_map.113.refs_0_.refs_2_), channel_id=1, source_target_pairs={{0,8},{8,0},{16,24},{24,16},{1,9},{9,1},{17,25},{25,17},{2,10},{10... | collective-permute-start | bytes 49160 | tf_op jit(solution)/shard_map/ppermute | solution.py:17
  91.1 3.8 %collective-permute-start.26 = (f32[16,256]{1,0:T(8,128)S(1)}, f32[16,256]{1,0:T(8,128)S(1)}, u32[]{:S(2)}, u32[]{:S(2)}) collective-permute-start(f32[16,256]{1,0:T(8,128)S(1)} %shard_map.113.refs_0_.refs_2_), channel_id=1, source_target_pairs={{0,16},{8,24},{16,0},{24,8},{1,17},{9,25},{17,1},{25,9},{2,18},{10... | collective-permute-start | bytes 49160 | tf_op jit(solution)/shard_map/ppermute | solution.py:17
  92.1 3.3 %collective-permute-start.27 = (f32[16,256]{1,0:T(8,128)S(1)}, f32[16,256]{1,0:T(8,128)S(1)}, u32[]{:S(2)}, u32[]{:S(2)}) collective-permute-start(f32[16,256]{1,0:T(8,128)S(1)} %shard_map.113.refs_0_.refs_2_), channel_id=1, source_target_pairs={{0,24},{8,16},{16,8},{24,0},{1,25},{9,17},{17,9},{25,1},{2,26},{10... | collective-permute-start | bytes 49160 | tf_op jit(solution)/shard_map/ppermute | solution.py:17
  96.9 1.2 collective-permute-start.28
  98.8 1.2 collective-permute-start.29
  (41 other events, 157.4 us)

commit v5 on v4

--- a/solution.py
+++ b/solution.py
@@ -39,7 +39,7 @@
     return parts
 
 
-def call(body, outs, arrays, scalars=(), scratch=(), work=0, remote=0):
+def call(body, outs, arrays, scalars=(), scratch=(), work=0, remote=0, room=40):
     moved = sum(a.size * a.dtype.itemsize for a in arrays)
     moved += sum(math.prod(shape) * jnp.dtype(kind).itemsize for shape, kind in outs)
     return pl.pallas_call(
@@ -47,10 +47,10 @@
         out_shape=[jax.ShapeDtypeStruct(*o) for o in outs],
         in_specs=[pl.BlockSpec(memory_space=pltpu.SMEM)] * len(scalars)
         + [pl.BlockSpec(memory_space=pltpu.VMEM)] * (len(arrays) - remote)
-        + [pl.BlockSpec(memory_space=pl.ANY)] * remote,
+        + [pl.BlockSpec(memory_space=pltpu.HBM)] * remote,
         out_specs=[pl.BlockSpec(memory_space=pltpu.VMEM)] * len(outs),
         scratch_shapes=list(scratch),
-        compiler_params=pltpu.CompilerParams(vmem_limit_bytes=40 << 20),
+        compiler_params=pltpu.CompilerParams(vmem_limit_bytes=room << 20),
         cost_estimate=pl.CostEstimate(flops=work, bytes_accessed=moved, transcendentals=0),
     )(*scalars, *arrays)
 
@@ -178,31 +178,45 @@
     aux = jnp.tile(jnp.pad(aux, ((0, 0), (levels * piece, 0))), (ranks, 1))
     packed = tiles * TILE + TILE
 
-    def local_forward(rhs_ref, inverse_ref, coupling_ref, window_ref, aux_ref, *outs):
-        solved_ref, terms_ref, held = outs[1:]
+    firsts = [part for parts in (lower_parts, upper_parts) for step, part in parts if step in (1, -1)]
+
+    def local_forward(rhs_ref, window_ref, aux_ref, inverse_any, coupling_any, *refs):
+        solved_ref, terms_ref, held, inverse_ref, coupling_ref, done = refs[len(firsts) :]
+        first = pltpu.make_async_copy(inverse_any, inverse_ref, done.at[0])
+        second = pltpu.make_async_copy(coupling_any, coupling_ref, done.at[1])
+        first.start()
+        second.start()
         rhs = rhs_ref[...]
-        solved = rhs + jnp.dot(strict_lower(inverse_ref[...]), rhs, precision=EXACT)
-        solved_ref[...] = solved.T
-        terms_ref[:, : tiles * TILE] = jnp.dot(coupling_ref[...], solved, precision=EXACT).T
         held[...] = jnp.zeros_like(held)
         for level in range(levels):
             held[level * piece : (level + 1) * piece, :] = window_ref[level]
         terms_ref[:, tiles * TILE :] = held[...].T + aux_ref[...]
+        first.wait()
+        solved = rhs + jnp.dot(strict_lower(inverse_ref[...]), rhs, precision=EXACT)
+        solved_ref[...] = solved.T
+        second.wait()
+        terms_ref[:, : tiles * TILE] = jnp.dot(coupling_ref[...], solved, precision=EXACT).T
 
     solved_loc, terms = call(
         local_forward,
         [((columns, local), F32), ((columns, packed), F32)],
-        (loc_rhs[0, 0], loc_inverse[0, 0], loc_coupling[0, 0], win_rhs, aux, lower_parts[1][1]),
-        remote=1,
-        scratch=[pltpu.VMEM((TILE, columns), F32)],
+        (loc_rhs[0, 0], win_rhs, aux, loc_inverse[0, 0], loc_coupling[0, 0], *firsts),
+        remote=2 + len(firsts),
+        scratch=[
+            pltpu.VMEM((TILE, columns), F32),
+            pltpu.VMEM((local, local), F32),
+            pltpu.VMEM((tiles * TILE, local), F32),
+            pltpu.SemaphoreType.DMA((2,)),
+        ],
         work=24 * local * local * columns,
+        room=60,
     )
     terms = lax.all_to_all(terms.reshape(ranks, share, packed), "row", 0, 0, tiled=True)
     aux = terms[:, :, tiles * TILE + levels * piece :].reshape(ranks, -1)
     known = aux[:, levels * piece : levels * piece + tiles].astype(jnp.int32).reshape(-1)
     pivots = aux[:, : levels * piece].reshape(ranks, levels, piece)
     pivots = pivots.transpose(1, 0, 2).reshape(levels, 1, base)
-    top_pivots = leaf_swaps([pivots[top]] * leaves)
+    all_pivots = leaf_swaps([pivots] * leaves)
 
     lower = assemble(lower_parts, lower_names)
     upper = assemble(upper_parts, upper_names)
@@ -218,9 +232,11 @@
                 path[place] = path[place] - terms_ref[source, :, tile * TILE : (tile + 1) * TILE]
         for level in range(levels):
             span = 2**level
+            filled = outs[level]
             for slot in range(span):
                 first = (span - 1 + slot) * halves
-                outs[level][slot] = jnp.concatenate([path[first + h] for h in range(halves)], 1)
+                for half in range(halves):
+                    filled[slot, :, half * TILE : (half + 1) * TILE] = path[first + half]
             own = ids_ref[0] % span
             rows = []
             for half in range(halves):
@@ -231,7 +247,7 @@
                     turned = pltpu.roll(terms_ref[source, :, tiles * TILE :], shift, 1)
                     row = jnp.where((lane >= place) & (lane < place + piece), turned, row)
                 rows.append(row)
-            outs[level][own] = outs[level][own] + jnp.concatenate(rows, 1)
+            filled[own] = filled[own] + jnp.concatenate(rows, 1)
 
     rest = call(
         scatter,
@@ -242,18 +258,18 @@
     )
 
     def total(refs):
-        value = refs[0][...]
+        value = refs[0][0] if len(refs[0].shape) > len(wide) and len(refs) == 1 else refs[0][...]
         for ref in refs[1:]:
             value = value + ref[...]
         return value
 
-    def diagonal(level, chunks):
+    def diagonal(level, chunks, ahead=()):
         span = 2**level
         high, low = blocks["A", level]
 
         def body(ids_ref, *refs):
             chunk_refs, (high_ref, low_ref) = refs[:span], refs[span : span + 2]
-            outs, parts = refs[span + 2 : -1], refs[-1]
+            outs, parts = refs[span + 2 + len(ahead) : -1], refs[-1]
             own = ids_ref[0] % span
             value = total(chunk_refs)
             for slot in range(span):
@@ -267,7 +283,11 @@
 
         outs = [((span, *wide), F32)] if level == top else [(wide, F32)] * span
         return call(
-            body, outs, (*chunks, high, low), (ids,), [pltpu.VMEM((span, *wide), F32)]
+            body,
+            outs,
+            (*chunks, high, low, *ahead),
+            (ids,),
+            [pltpu.VMEM((span, *wide), F32)],
         )
 
     def link(level, chunks):
@@ -295,10 +315,10 @@
         )
         return made[0], made[1:]
 
-    chunks = [rest[0][0]]
+    chunks = [rest[0]]
     solved = []
     for level in range(top):
-        chunks = leaf_swaps(diagonal(level, chunks))
+        chunks = leaf_swaps(diagonal(level, chunks, () if level else all_pivots))
         value, chunks = link(level, chunks)
         solved.append(value)
         chunks = leaf_swaps(chunks)
@@ -310,7 +330,7 @@
         own = ids_ref[0] % leaves
         wanted[...] = total(sum_refs)
         for offset, ref in enumerate(pivot_refs):
-            wanted[own ^ offset] = wanted[own ^ offset] / ref[...]
+            wanted[own ^ offset] = wanted[own ^ offset] / ref[top]
         value = wanted[own]
         for slot in range(leaves):
             value = value + times(wanted[slot], high_ref[slot], low_ref[slot], 0)
@@ -319,7 +339,7 @@
     current = call(
         peak,
         [(wide, F32)],
-        (*sums, *top_pivots, *blocks["A", top]),
+        (*sums, *all_pivots, *blocks["A", top]),
         (ids,),
         [pltpu.VMEM((leaves, *wide), F32)],
     )
@@ -342,12 +362,12 @@
             high_ref, low_ref, solved_ref, pivot_ref, out, held = refs[span:]
             ordered(ids_ref[0] % span, part_refs, held)
             above = against(held, high_ref, low_ref, span)
-            out[...] = solved_ref[...] / pivot_ref[...] - above
+            out[...] = solved_ref[...] / pivot_ref[level - 1] - above
 
         return call(
             body,
             [(wide, F32)],
-            (*parts, *blocks["B", level - 1], solved[level - 1], pivots[level - 1]),
+            (*parts, *blocks["B", level - 1], solved[level - 1], pivots),
             (ids,),
             [pltpu.VMEM((span, *wide), F32)],
         )
@@ -381,7 +401,7 @@
         out, path, held = refs[6:]
         group = ids_ref[0]
         ordered(group % 2, parts[1], held)
-        wanted = solved_ref[...] / pivot_ref[...] - against(held, link_high, link_low, 2)
+        wanted = solved_ref[...] / pivot_ref[0] - against(held, link_high, link_low, 2)
         lowest = wanted + times(wanted, high_ref[0], low_ref[0], 0)
         owned = [lowest]
         for half in range(halves):
@@ -414,7 +434,7 @@
             *[part for level in range(1, levels) for part in everything[level]],
             *blocks["B", 0],
             solved[0],
-            pivots[0],
+            pivots,
             *blocks["A", 0],
         ),
         (ids, known),
@@ -452,6 +472,7 @@
         ],
         remote=2,
         work=24 * local * local * columns,
+        room=60,
     )
     return answer[None, None], window
 

time: 121 us -> 110 us (0.909)
  local copies, waits for them, and re-layouts: 21.5 us -> 3.84 us
  waiting for transfers between devices: 31.2 us -> 36.2 us
  Pallas kernels: 19.4 us -> 22.6 us
    unnamed x82 -> x24, local copies, waits for them, and re-layouts: 16.5 us -> 0.08 us
    ppermute x7, waiting for transfers between devices: 6.96 us -> 11.5 us  [ring_gather(): moving[index][0] = lax.ppermute(moving[index][0], 'row', right)]
    pallas_call x14, Pallas kernels: 19.4 us -> 22.6 us  [call(): pl.pallas_call(body, out_shape=[jax.ShapeDtypeStruct(*o) for o in outs],...]
    ppermute x16, waiting for transfers between devices: 8.24 us -> 11.2 us  [swap(): return lax.ppermute(value, axis, [(i, i ^ offset) for i in range(count)])]
    ppermute x7, waiting for transfers between devices: 16 us -> 13.5 us  [ring_gather(): moving[index][1] = lax.ppermute(moving[index][1], 'row', left)]
    ppermute x7, starting transfers between devices: 5.63 us -> 4.01 us  [ring_gather(): moving[index][1] = lax.ppermute(moving[index][1], 'row', left)]
    squeeze x3 -> x0, local copies, waits for them, and re-layouts: 1.59 us -> none  [the longest x1 0.76 us: descend(): pivots[level - 1]]
    ppermute x7, starting transfers between devices: 11 us -> 12.5 us  [ring_gather(): moving[index][0] = lax.ppermute(moving[index][0], 'row', right)]
  transfers between devices with their start and end apart: 31 -> 31, of which waited for: 14 -> 14; matrix products, arithmetic and copies ran while one was open for 3% -> 3% of each run, Pallas kernels for 10% -> 13%
where the time goes in v5:
time: 110 us
  waiting for transfers between devices  36.2 us (33%)
  starting transfers between devices  29.9 us (27%)
  Pallas kernels  22.6 us (21%)
  blocking collectives  16.1 us (15%)
  local copies, waits for them, and re-layouts  3.84 us (3%)
    pallas_call x14, Pallas kernels, call(): pl.pallas_call(body, out_shape=[jax.ShapeDtypeStruct(*o) for o in outs],...  22.6 us
    all_to_all x1, blocking collectives, shards(): lax.all_to_all(replies[0], 'row', 0, 0, tiled=True).reshape(columns, packed)  16.1 us
    ppermute x7, waiting for transfers between devices, ring_gather(): moving[index][1] = lax.ppermute(moving[index][1], 'row', left)  13.5 us
    ppermute x7, starting transfers between devices, ring_gather(): moving[index][0] = lax.ppermute(moving[index][0], 'row', right)  12.5 us
    ppermute x7, waiting for transfers between devices, ring_gather(): moving[index][0] = lax.ppermute(moving[index][0], 'row', right)  11.5 us
    ppermute x16, waiting for transfers between devices, swap(): return lax.ppermute(value, axis, [(i, i ^ offset) for i in range(count)])  11.2 us
    ppermute x16, starting transfers between devices, swap(): return lax.ppermute(value, axis, [(i, i ^ offset) for i in range(count)])  8.4 us
    all_to_all x1, starting transfers between devices, shards(): lax.all_to_all(terms.reshape(ranks, share, packed), 'row', 0, 0, tiled=True)  4.97 us
  transfers between devices with their start and end apart: 31, of which 14 were waited for; matrix products, arithmetic and copies ran while one was open for 3% of the time, Pallas kernels for 13%

profile of v5, /device:TPU:0, one launch (start us, length us, event | category | flops | bytes accessed | tf_op | source)
XLA Modules:
  0.0 109.8 jit_solution(2880751917364319913)
XLA Ops:
  0.6 0.9 slice_bitcast_fusion
  1.6 3.1 %collective-permute-start = (f32[9,32,256]{2,1,0:T(8,128)S(1)}, f32[9,32,256]{2,1,0:T(8,128)S(1)}, u32[]{:S(2)}, u32[]{:S(2)}) collective-permute-start(f32[9,32,256]{2,1,0:T(8,128)S(1)} %bitcast.18), channel_id=1, source_target_pairs={{0,2},{2,4},{4,6},{6,7},{7,5},{5,3},{3,1},{1,0},{8,10},{10,12},{12... | collective-permute-start | bytes 884744 | tf_op jit(solution)/shard_map/ppermute | solution.py:34
  4.7 2.1 %collective-permute-start.2 = (f32[4,32,256]{2,1,0:T(8,128)S(1)}, f32[4,32,256]{2,1,0:T(8,128)S(1)}, u32[]{:S(2)}, u32[]{:S(2)}) collective-permute-start(f32[4,32,256]{2,1,0:T(8,128)S(1)} %bitcast.21), channel_id=1, source_target_pairs={{0,2},{2,4},{4,6},{6,7},{7,5},{5,3},{3,1},{1,0},{8,10},{10,12},{12... | collective-permute-start | bytes 393224 | tf_op jit(solution)/shard_map/ppermute | solution.py:34
  6.8 5.7 %collective-permute-done.refs_0_.refs_1_ = f32[9,32,256]{2,1,0:T(8,128)S(1)} collective-permute-done((f32[9,32,256]{2,1,0:T(8,128)S(1)}, f32[9,32,256]{2,1,0:T(8,128)S(1)}, u32[]{:S(2)}, u32[]{:S(2)}) %collective-permute-start) | collective-permute-done | bytes 294944 | tf_op jit(solution)/shard_map/ppermute | solution.py:34
  12.5 2.1 %collective-permute-start.4 = (f32[9,32,256]{2,1,0:T(8,128)S(1)}, f32[9,32,256]{2,1,0:T(8,128)S(1)}, u32[]{:S(2)}, u32[]{:S(2)}) collective-permute-start(f32[9,32,256]{2,1,0:T(8,128)S(1)} %collective-permute-done.refs_0_.refs_1_), channel_id=1, source_target_pairs={{0,2},{2,4},{4,6},{6,7},{7,5},{5,3},{3,1},{1,0},{8,10},{10,12},{12... | collective-permute-start | bytes 884744 | tf_op jit(solution)/shard_map/ppermute | solution.py:34
  15.0 5.8 %collective-permute-done.4.refs_3_ = f32[9,32,256]{2,1,0:T(8,128)S(1)} collective-permute-done((f32[9,32,256]{2,1,0:T(8,128)S(1)}, f32[9,32,256]{2,1,0:T(8,128)S(1)}, u32[]{:S(2)}, u32[]{:S(2)}) %collective-permute-start.4) | collective-permute-done | bytes 294944 | tf_op jit(solution)/shard_map/ppermute | solution.py:34
  20.8 1.8 %collective-permute-start.6 = (f32[9,32,256]{2,1,0:T(8,128)S(1)}, f32[9,32,256]{2,1,0:T(8,128)S(1)}, u32[]{:S(2)}, u32[]{:S(2)}) collective-permute-start(f32[9,32,256]{2,1,0:T(8,128)S(1)} %collective-permute-done.4.refs_3_), channel_id=1, source_target_pairs={{0,2},{2,4},{4,6},{6,7},{7,5},{5,3},{3,1},{1,0},{8,10},{10,12},{12... | collective-permute-start | bytes 884744 | tf_op jit(solution)/shard_map/ppermute | solution.py:34
  23.3 6.6 %shard_map.104 = (f32[128,512]{1,0:T(8,128)}, f32[128,640]{1,0:T(8,128)}) custom-call(f32[512,128]{1,0:T(8,128)} %bitcast.30, f32[3,32,128]{2,1,0:T(8,128)} %window_ref.1, f32[128,128]{1,0:T(8,128)} %bitcast.31, f32[512,512]{1,0:T(8,128)} %bitcast.24, f32[512,512]{1,0:T(8,128)} %bitcast.26, f32[9,32,256]{2,1,0:T(8,128)} %copy-done, f32[9,32,256]{2,1,0:T(8,128)} %copy-done.2, ...), custom_call_target="tpu_custom_call" | custom-call | flops 805306368 | bytes 3915776 | tf_op jit(solution)/shard_map/pallas_call | solution.py:45
  29.9 5.0 %all-to-all-start = ((f32[8,16,640]{2,1,0:T(8,128)}), f32[8,16,640]{2,1,0:T(8,128)S(1)}, u32[]{:S(2)}, u32[]{:S(2)}) async-start(f32[8,16,640]{2,1,0:T(8,128)} %bitcast.28), calls=%async_computation | async-start | bytes 655360 | tf_op jit(solution)/shard_map/all_to_all | solution.py:214
  34.9 2.0 %collective-permute-start.7 = (f32[9,32,256]{2,1,0:T(8,128)S(1)}, f32[9,32,256]{2,1,0:T(8,128)S(1)}, u32[]{:S(2)}, u32[]{:S(2)}) collective-permute-start(f32[9,32,256]{2,1,0:T(8,128)S(1)} %collective-permute-done.5.refs_4_), channel_id=1, source_target_pairs={{2,0},{4,2},{6,4},{7,6},{5,7},{3,5},{1,3},{0,1},{10,8},{12,10},{14... | collective-permute-start | bytes 884744 | tf_op jit(solution)/shard_map/ppermute | solution.py:37
  37.0 2.0 %collective-permute-start.18 = (f32[4,32,256]{2,1,0:T(8,128)S(1)}, f32[4,32,256]{2,1,0:T(8,128)S(1)}, u32[]{:S(2)}, u32[]{:S(2)}) collective-permute-start(f32[4,32,256]{2,1,0:T(8,128)S(1)} %copy-done.7), channel_id=1, source_target_pairs={{2,0},{4,2},{6,4},{7,6},{5,7},{3,5},{1,3},{0,1},{10,8},{12,10},{14... | collective-permute-start | bytes 393224 | tf_op jit(solution)/shard_map/ppermute | solution.py:37
  39.0 10.6 %collective-permute-done.18.refs_4_ = f32[4,32,256]{2,1,0:T(8,128)S(1)} collective-permute-done((f32[4,32,256]{2,1,0:T(8,128)S(1)}, f32[4,32,256]{2,1,0:T(8,128)S(1)}, u32[]{:S(2)}, u32[]{:S(2)}) %collective-permute-start.18) | collective-permute-done | bytes 131104 | tf_op jit(solution)/shard_map/ppermute | solution.py:37
  49.8 3.3 %collective-permute-start.19 = (f32[4,32,256]{2,1,0:T(8,128)S(1)}, f32[4,32,256]{2,1,0:T(8,128)}, u32[]{:S(2)}, u32[]{:S(2)}) collective-permute-start(f32[4,32,256]{2,1,0:T(8,128)S(1)} %collective-permute-done.17.refs_3_), channel_id=1, source_target_pairs={{0,2},{2,4},{4,6},{6,7},{7,5},{5,3},{3,1},{1,0},{8,10},{10,12},{12... | collective-permute-start | bytes 393224 | tf_op jit(solution)/shard_map/ppermute | solution.py:34
  53.1 2.8 %collective-permute-done.20.refs_6_ = f32[4,32,256]{2,1,0:T(8,128)S(1)} collective-permute-done((f32[4,32,256]{2,1,0:T(8,128)S(1)}, f32[4,32,256]{2,1,0:T(8,128)S(1)}, u32[]{:S(2)}, u32[]{:S(2)}) %collective-permute-start.20) | collective-permute-done | bytes 131104 | tf_op jit(solution)/shard_map/ppermute | solution.py:37
  56.6 0.9 reshape.40
  57.7 1.5 %collective-permute-start.10 = (f32[3,1,256]{2,1,0:T(1,128)S(1)}, f32[3,1,256]{2,1,0:T(1,128)S(1)}, u32[]{:S(2)}, u32[]{:S(2)}) collective-permute-start(f32[3,1,256]{2,1,0:T(1,128)S(1)} %reshape.43.refs_3_.refs_4_.refs_7_.refs_9_), channel_id=1, source_target_pairs={{0,16},{8,24},{16,0},{24,8},{1,17},{9,25},{17,1},{25,9},{2,18},{10... | collective-permute-start | bytes 9224 | tf_op jit(solution)/shard_map/ppermute | solution.py:17
  60.7 1.3 %shard_map.106 = (bf16[1,256,256]{2,1,0:T(8,128)(2,1)S(1)}, bf16[1,256,256]{2,1,0:T(8,128)(2,1)S(1)}, bf16[2,256,256]{2,1,0:T(8,128)(2,1)S(1)}, bf16[2,256,256]{...) custom-call(s32[2]{0:T(128)S(1)} %pad_add_fusion.ids_ref, ...), custom_call_target="tpu_custom_call" | custom-call | bytes 4718592 | tf_op jit(solution)/shard_map/pallas_call | solution.py:45
  63.8 1.2 %collective-permute-done.12.refs_1_ = f32[16,256]{1,0:T(8,128)S(1)} collective-permute-done((f32[16,256]{1,0:T(8,128)S(1)}, f32[16,256]{1,0:T(8,128)S(1)}, u32[]{:S(2)}, u32[]{:S(2)}) %collective-permute-start.12) | collective-permute-done | bytes 16416 | tf_op jit(solution)/shard_map/ppermute | solution.py:17
  66.0 1.0 collective-permute-done.13.refs_1_
  67.0 0.9 shard_map.110
  68.2 1.3 %collective-permute-start.15 = (f32[16,256]{1,0:T(8,128)S(1)}, f32[16,256]{1,0:T(8,128)S(1)}, u32[]{:S(2)}, u32[]{:S(2)}) collective-permute-start(f32[16,256]{1,0:T(8,128)S(1)} %get-tuple-element.47), channel_id=1, source_target_pairs={{0,16},{8,24},{16,0},{24,8},{1,17},{9,25},{17,1},{25,9},{2,18},{10... | collective-permute-start | bytes 49160 | tf_op jit(solution)/shard_map/ppermute | solution.py:17
  69.9 2.1 %shard_map.111 = (bf16[4,256,256]{2,1,0:T(8,128)(2,1)S(1)}, bf16[4,256,256]{2,1,0:T(8,128)(2,1)S(1)}) custom-call(s32[2]{0:T(128)S(1)} %pad_add_fusion.ids_ref, f32[4,32,256]{2,1,0:T(8,128)S(1)} %bitcast.23, f32[4,32,256]{2,1,0:T(8,128)S(1)} %copy-done.5, f32[4,32,256]{2,1,0:T(8,128)S(1)} %copy-done.7, f32[4,32,256]{2,1,0:T(8,128)S(1)} %collective-permute-done.17.refs_3_, ...), custom_call_target="tpu_custom_call" | custom-call | bytes 2097152 | tf_op jit(solution)/shard_map/pallas_call | solution.py:45
  72.6 1.0 shard_map.112.refs_0_
  73.8 1.0 collective-permute-start.23
  75.5 3.1 %collective-permute-done.23.refs_2_ = f32[4,16,256]{2,1,0:T(8,128)S(1)} collective-permute-done((f32[4,16,256]{2,1,0:T(8,128)S(1)}, f32[4,16,256]{2,1,0:T(8,128)S(1)}, u32[]{:S(2)}, u32[]{:S(2)}) %collective-permute-start.23) | collective-permute-done | bytes 65568 | tf_op jit(solution)/shard_map/ppermute | solution.py:17
  80.2 0.9 collective-permute-start.26
  81.9 2.1 %collective-permute-done.26.refs_2_.refs_4_ = f32[16,256]{1,0:T(8,128)S(1)} collective-permute-done((f32[16,256]{1,0:T(8,128)S(1)}, f32[16,256]{1,0:T(8,128)S(1)}, u32[]{:S(2)}, u32[]{:S(2)}) %collective-permute-start.26) | collective-permute-done | bytes 16416 | tf_op jit(solution)/shard_map/ppermute | solution.py:17
  85.3 1.1 collective-permute-done.28.refs_1_
  87.2 1.0 collective-permute-done.29.refs_1_
  88.3 1.0 shard_map.116
  89.3 16.1 %all_to_all.10 = f32[8,16,640]{2,1,0:T(8,128)} all-to-all(f32[8,16,640]{2,1,0:T(8,128)S(1)} %shard_map.116), channel_id=1, replica_groups=mesh['leaf'=4,'row'=8] {'row'}, dimensions={0} | all-to-all | bytes 655360 | tf_op jit(solution)/shard_map/all_to_all | solution.py:443
  105.4 4.4 %shard_map.117 = (f32[512,128]{1,0:T(8,128)}, f32[3,32,128]{2,1,0:T(8,128)}) custom-call(f32[128,640]{1,0:T(8,128)} %bitcast.29, f32[128,512]{1,0:T(8,128)} %get-tuple-element.53.solved_ref, f32[1,512]{1,0:T(1,128)} %bitcast.34, f32[512,512]{1,0:T(8,128)} %bitcast.25, f32[512,512]{1,0:T(8,128)} %bitcast.27), custom_call_target="tpu_custom_call" | custom-call | flops 805306368 | bytes 3000320 | tf_op jit(solution)/shard_map/pallas_call | solution.py:45
  (87 shorter events, 13.3 us)
Async XLA Ops:
  1.6 10.9 %collective-permute-start = (f32[9,32,256]{2,1,0:T(8,128)S(1)}, f32[9,32,256]{2,1,0:T(8,128)S(1)}, u32[]{:S(2)}, u32[]{:S(2)}) collective-permute-start(f32[9,32,256]{2,1,0:T(8,128)S(1)} %bitcast.18), channel_id=1, source_target_pairs={{0,2},{2,4},{4,6},{6,7},{7,5},{5,3},{3,1},{1,0},{8,10},{10,12},{12... | collective-permute-start | bytes 884744 | tf_op jit(solution)/shard_map/ppermute | solution.py:34
  4.7 10.2 %collective-permute-start.1 = (f32[9,32,256]{2,1,0:T(8,128)S(1)}, f32[9,32,256]{2,1,0:T(8,128)S(1)}, u32[]{:S(2)}, u32[]{:S(2)}) collective-permute-start(f32[9,32,256]{2,1,0:T(8,128)S(1)} %bitcast.19), channel_id=1, source_target_pairs={{2,0},{4,2},{6,4},{7,6},{5,7},{3,5},{1,3},{0,1},{10,8},{12,10},{14... | collective-permute-start | bytes 884744 | tf_op jit(solution)/shard_map/ppermute | solution.py:37
  4.7 17.8 %collective-permute-start.2 = (f32[4,32,256]{2,1,0:T(8,128)S(1)}, f32[4,32,256]{2,1,0:T(8,128)S(1)}, u32[]{:S(2)}, u32[]{:S(2)}) collective-permute-start(f32[4,32,256]{2,1,0:T(8,128)S(1)} %bitcast.21), channel_id=1, source_target_pairs={{0,2},{2,4},{4,6},{6,7},{7,5},{5,3},{3,1},{1,0},{8,10},{10,12},{12... | collective-permute-start | bytes 393224 | tf_op jit(solution)/shard_map/ppermute | solution.py:34
  6.8 15.8 %collective-permute-start.3 = (f32[4,32,256]{2,1,0:T(8,128)S(1)}, f32[4,32,256]{2,1,0:T(8,128)S(1)}, u32[]{:S(2)}, u32[]{:S(2)}) collective-permute-start(f32[4,32,256]{2,1,0:T(8,128)S(1)} %bitcast.22), channel_id=1, source_target_pairs={{2,0},{4,2},{6,4},{7,6},{5,7},{3,5},{1,3},{0,1},{10,8},{12,10},{14... | collective-permute-start | bytes 393224 | tf_op jit(solution)/shard_map/ppermute | solution.py:37
  12.5 8.3 %collective-permute-start.4 = (f32[9,32,256]{2,1,0:T(8,128)S(1)}, f32[9,32,256]{2,1,0:T(8,128)S(1)}, u32[]{:S(2)}, u32[]{:S(2)}) collective-permute-start(f32[9,32,256]{2,1,0:T(8,128)S(1)} %collective-permute-done.refs_0_.refs_1_), channel_id=1, source_target_pairs={{0,2},{2,4},{4,6},{6,7},{7,5},{5,3},{3,1},{1,0},{8,10},{10,12},{12... | collective-permute-start | bytes 884744 | tf_op jit(solution)/shard_map/ppermute | solution.py:34
  14.9 20.0 %collective-permute-start.5 = (f32[9,32,256]{2,1,0:T(8,128)S(1)}, f32[9,32,256]{2,1,0:T(8,128)S(1)}, u32[]{:S(2)}, u32[]{:S(2)}) collective-permute-start(f32[9,32,256]{2,1,0:T(8,128)S(1)} %collective-permute-done.1.refs_1_.refs_2_), channel_id=1, source_target_pairs={{2,0},{4,2},{6,4},{7,6},{5,7},{3,5},{1,3},{0,1},{10,8},{12,10},{14... | collective-permute-start | bytes 884744 | tf_op jit(solution)/shard_map/ppermute | solution.py:37
  20.8 16.1 %collective-permute-start.6 = (f32[9,32,256]{2,1,0:T(8,128)S(1)}, f32[9,32,256]{2,1,0:T(8,128)S(1)}, u32[]{:S(2)}, u32[]{:S(2)}) collective-permute-start(f32[9,32,256]{2,1,0:T(8,128)S(1)} %collective-permute-done.4.refs_3_), channel_id=1, source_target_pairs={{0,2},{2,4},{4,6},{6,7},{7,5},{5,3},{3,1},{1,0},{8,10},{10,12},{12... | collective-permute-start | bytes 884744 | tf_op jit(solution)/shard_map/ppermute | solution.py:34
  29.9 26.0 %all-to-all-start = ((f32[8,16,640]{2,1,0:T(8,128)}), f32[8,16,640]{2,1,0:T(8,128)S(1)}, u32[]{:S(2)}, u32[]{:S(2)}) async-start(f32[8,16,640]{2,1,0:T(8,128)} %bitcast.28), calls=%async_computation | async-start | bytes 655360 | tf_op jit(solution)/shard_map/all_to_all | solution.py:214
  34.9 24.3 %collective-permute-start.7 = (f32[9,32,256]{2,1,0:T(8,128)S(1)}, f32[9,32,256]{2,1,0:T(8,128)S(1)}, u32[]{:S(2)}, u32[]{:S(2)}) collective-permute-start(f32[9,32,256]{2,1,0:T(8,128)S(1)} %collective-permute-done.5.refs_4_), channel_id=1, source_target_pairs={{2,0},{4,2},{6,4},{7,6},{5,7},{3,5},{1,3},{0,1},{10,8},{12,10},{14... | collective-permute-start | bytes 884744 | tf_op jit(solution)/shard_map/ppermute | solution.py:37
  36.9 22.3 %collective-permute-start.8 = (f32[9,32,256]{2,1,0:T(8,128)S(1)}, f32[9,32,256]{2,1,0:T(8,128)S(1)}, u32[]{:S(2)}, u32[]{:S(2)}) collective-permute-start(f32[9,32,256]{2,1,0:T(8,128)S(1)} %collective-permute-done.6.refs_5_), channel_id=1, source_target_pairs={{0,2},{2,4},{4,6},{6,7},{7,5},{5,3},{3,1},{1,0},{8,10},{10,12},{12... | collective-permute-start | bytes 884744 | tf_op jit(solution)/shard_map/ppermute | solution.py:34
  37.0 12.7 %collective-permute-start.18 = (f32[4,32,256]{2,1,0:T(8,128)S(1)}, f32[4,32,256]{2,1,0:T(8,128)S(1)}, u32[]{:S(2)}, u32[]{:S(2)}) collective-permute-start(f32[4,32,256]{2,1,0:T(8,128)S(1)} %copy-done.7), channel_id=1, source_target_pairs={{2,0},{4,2},{6,4},{7,6},{5,7},{3,5},{1,3},{0,1},{10,8},{12,10},{14... | collective-permute-start | bytes 393224 | tf_op jit(solution)/shard_map/ppermute | solution.py:37
  39.0 10.8 %collective-permute-start.17 = (f32[4,32,256]{2,1,0:T(8,128)S(1)}, f32[4,32,256]{2,1,0:T(8,128)S(1)}, u32[]{:S(2)}, u32[]{:S(2)}) collective-permute-start(f32[4,32,256]{2,1,0:T(8,128)S(1)} %copy-done.5), channel_id=1, source_target_pairs={{0,2},{2,4},{4,6},{6,7},{7,5},{5,3},{3,1},{1,0},{8,10},{10,12},{12... | collective-permute-start | bytes 393224 | tf_op jit(solution)/shard_map/ppermute | solution.py:34
  49.7 6.2 %collective-permute-start.20 = (f32[4,32,256]{2,1,0:T(8,128)S(1)}, f32[4,32,256]{2,1,0:T(8,128)S(1)}, u32[]{:S(2)}, u32[]{:S(2)}) collective-permute-start(f32[4,32,256]{2,1,0:T(8,128)S(1)} %collective-permute-done.18.refs_4_), channel_id=1, source_target_pairs={{2,0},{4,2},{6,4},{7,6},{5,7},{3,5},{1,3},{0,1},{10,8},{12,10},{14... | collective-permute-start | bytes 393224 | tf_op jit(solution)/shard_map/ppermute | solution.py:37
  49.8 11.0 %copy-start.3 = (f32[9,32,256]{2,1,0:T(8,128)S(1)}, f32[9,32,256]{2,1,0:T(8,128)}, u32[]{:S(2)}) copy-start(f32[9,32,256]{2,1,0:T(8,128)} %copy-done.2) | copy-start | bytes 884740
  49.8 20.1 %collective-permute-start.19 = (f32[4,32,256]{2,1,0:T(8,128)S(1)}, f32[4,32,256]{2,1,0:T(8,128)}, u32[]{:S(2)}, u32[]{:S(2)}) collective-permute-start(f32[4,32,256]{2,1,0:T(8,128)S(1)} %collective-permute-done.17.refs_3_), channel_id=1, source_target_pairs={{0,2},{2,4},{4,6},{6,7},{7,5},{5,3},{3,1},{1,0},{8,10},{10,12},{12... | collective-permute-start | bytes 393224 | tf_op jit(solution)/shard_map/ppermute | solution.py:34
  55.9 14.0 %collective-permute-start.21 = (f32[4,32,256]{2,1,0:T(8,128)S(1)}, f32[4,32,256]{2,1,0:T(8,128)}, u32[]{:S(2)}, u32[]{:S(2)}) collective-permute-start(f32[4,32,256]{2,1,0:T(8,128)S(1)} %collective-permute-done.20.refs_6_), channel_id=1, source_target_pairs={{2,0},{4,2},{6,4},{7,6},{5,7},{3,5},{1,3},{0,1},{10,8},{12,10},{14... | collective-permute-start | bytes 393224 | tf_op jit(solution)/shard_map/ppermute | solution.py:37
  57.7 4.3 %collective-permute-start.10 = (f32[3,1,256]{2,1,0:T(1,128)S(1)}, f32[3,1,256]{2,1,0:T(1,128)S(1)}, u32[]{:S(2)}, u32[]{:S(2)}) collective-permute-start(f32[3,1,256]{2,1,0:T(1,128)S(1)} %reshape.43.refs_3_.refs_4_.refs_7_.refs_9_), channel_id=1, source_target_pairs={{0,16},{8,24},{16,0},{24,8},{1,17},{9,25},{17,1},{25,9},{2,18},{10... | collective-permute-start | bytes 9224 | tf_op jit(solution)/shard_map/ppermute | solution.py:17
  59.2 3.0 %collective-permute-start.11 = (f32[3,1,256]{2,1,0:T(1,128)S(1)}, f32[3,1,256]{2,1,0:T(1,128)S(1)}, u32[]{:S(2)}, u32[]{:S(2)}) collective-permute-start(f32[3,1,256]{2,1,0:T(1,128)S(1)} %reshape.43.refs_3_.refs_4_.refs_7_.refs_9_), channel_id=1, source_target_pairs={{0,24},{8,16},{16,8},{24,0},{1,25},{9,17},{17,9},{25,1},{2,26},{10... | collective-permute-start | bytes 9224 | tf_op jit(solution)/shard_map/ppermute | solution.py:17
  59.2 3.0 %collective-permute-start.9 = (f32[3,1,256]{2,1,0:T(1,128)S(1)}, f32[3,1,256]{2,1,0:T(1,128)S(1)}, u32[]{:S(2)}, u32[]{:S(2)}) collective-permute-start(f32[3,1,256]{2,1,0:T(1,128)S(1)} %reshape.43.refs_3_.refs_4_.refs_7_.refs_9_), channel_id=1, source_target_pairs={{0,8},{8,0},{16,24},{24,16},{1,9},{9,1},{17,25},{25,17},{2,10},{10... | collective-permute-start | bytes 9224 | tf_op jit(solution)/shard_map/ppermute | solution.py:17
  63.8 1.2 %collective-permute-start.12 = (f32[16,256]{1,0:T(8,128)S(1)}, f32[16,256]{1,0:T(8,128)S(1)}, u32[]{:S(2)}, u32[]{:S(2)}) collective-permute-start(f32[16,256]{1,0:T(8,128)S(1)} %get-tuple-element.37), channel_id=1, source_target_pairs={{0,8},{8,0},{16,24},{24,16},{1,9},{9,1},{17,25},{25,17},{2,10},{10... | collective-permute-start | bytes 49160 | tf_op jit(solution)/shard_map/ppermute | solution.py:17
  65.8 1.2 %collective-permute-start.13 = (f32[16,256]{1,0:T(8,128)S(1)}, f32[16,256]{1,0:T(8,128)S(1)}, u32[]{:S(2)}, u32[]{:S(2)}) collective-permute-start(f32[16,256]{1,0:T(8,128)S(1)} %get-tuple-element.41), channel_id=1, source_target_pairs={{0,8},{8,0},{16,24},{24,16},{1,9},{9,1},{17,25},{25,17},{2,10},{10... | collective-permute-start | bytes 49160 | tf_op jit(solution)/shard_map/ppermute | solution.py:17
  68.0 4.0 %collective-permute-start.14 = (f32[16,256]{1,0:T(8,128)S(1)}, f32[16,256]{1,0:T(8,128)S(1)}, u32[]{:S(2)}, u32[]{:S(2)}) collective-permute-start(f32[16,256]{1,0:T(8,128)S(1)} %get-tuple-element.46), channel_id=1, source_target_pairs={{0,8},{8,0},{16,24},{24,16},{1,9},{9,1},{17,25},{25,17},{2,10},{10... | collective-permute-start | bytes 49160 | tf_op jit(solution)/shard_map/ppermute | solution.py:17
  68.2 3.8 %collective-permute-start.15 = (f32[16,256]{1,0:T(8,128)S(1)}, f32[16,256]{1,0:T(8,128)S(1)}, u32[]{:S(2)}, u32[]{:S(2)}) collective-permute-start(f32[16,256]{1,0:T(8,128)S(1)} %get-tuple-element.47), channel_id=1, source_target_pairs={{0,16},{8,24},{16,0},{24,8},{1,17},{9,25},{17,1},{25,9},{2,18},{10... | collective-permute-start | bytes 49160 | tf_op jit(solution)/shard_map/ppermute | solution.py:17
  69.5 3.2 %collective-permute-start.16 = (f32[16,256]{1,0:T(8,128)S(1)}, f32[16,256]{1,0:T(8,128)S(1)}, u32[]{:S(2)}, u32[]{:S(2)}) collective-permute-start(f32[16,256]{1,0:T(8,128)S(1)} %get-tuple-element.48), channel_id=1, source_target_pairs={{0,24},{8,16},{16,8},{24,0},{1,25},{9,17},{17,9},{25,1},{2,26},{10... | collective-permute-start | bytes 49160 | tf_op jit(solution)/shard_map/ppermute | solution.py:17
  73.6 1.9 %collective-permute-start.22 = (f32[4,16,256]{2,1,0:T(8,128)S(1)}, f32[4,16,256]{2,1,0:T(8,128)S(1)}, u32[]{:S(2)}, u32[]{:S(2)}) collective-permute-start(f32[4,16,256]{2,1,0:T(8,128)S(1)} %shard_map.112.refs_0_), channel_id=1, source_target_pairs={{0,8},{8,0},{16,24},{24,16},{1,9},{9,1},{17,25},{25,17},{2,10},{10... | collective-permute-start | bytes 196616 | tf_op jit(solution)/shard_map/ppermute | solution.py:17
  73.8 4.8 %collective-permute-start.23 = (f32[4,16,256]{2,1,0:T(8,128)S(1)}, f32[4,16,256]{2,1,0:T(8,128)S(1)}, u32[]{:S(2)}, u32[]{:S(2)}) collective-permute-start(f32[4,16,256]{2,1,0:T(8,128)S(1)} %shard_map.112.refs_0_), channel_id=1, source_target_pairs={{0,16},{8,24},{16,0},{24,8},{1,17},{9,25},{17,1},{25,9},{2,18},{10... | collective-permute-start | bytes 196616 | tf_op jit(solution)/shard_map/ppermute | solution.py:17
  74.8 4.4 %collective-permute-start.24 = (f32[4,16,256]{2,1,0:T(8,128)S(1)}, f32[4,16,256]{2,1,0:T(8,128)S(1)}, u32[]{:S(2)}, u32[]{:S(2)}) collective-permute-start(f32[4,16,256]{2,1,0:T(8,128)S(1)} %shard_map.112.refs_0_), channel_id=1, source_target_pairs={{0,24},{8,16},{16,8},{24,0},{1,25},{9,17},{17,9},{25,1},{2,26},{10... | collective-permute-start | bytes 196616 | tf_op jit(solution)/shard_map/ppermute | solution.py:17
  80.0 1.9 %collective-permute-start.25 = (f32[16,256]{1,0:T(8,128)S(1)}, f32[16,256]{1,0:T(8,128)S(1)}, u32[]{:S(2)}, u32[]{:S(2)}) collective-permute-start(f32[16,256]{1,0:T(8,128)S(1)} %shard_map.113.refs_0_.refs_2_), channel_id=1, source_target_pairs={{0,8},{8,0},{16,24},{24,16},{1,9},{9,1},{17,25},{25,17},{2,10},{10... | collective-permute-start | bytes 49160 | tf_op jit(solution)/shard_map/ppermute | solution.py:17
  80.2 3.7 %collective-permute-start.26 = (f32[16,256]{1,0:T(8,128)S(1)}, f32[16,256]{1,0:T(8,128)S(1)}, u32[]{:S(2)}, u32[]{:S(2)}) collective-permute-start(f32[16,256]{1,0:T(8,128)S(1)} %shard_map.113.refs_0_.refs_2_), channel_id=1, source_target_pairs={{0,16},{8,24},{16,0},{24,8},{1,17},{9,25},{17,1},{25,9},{2,18},{10... | collective-permute-start | bytes 49160 | tf_op jit(solution)/shard_map/ppermute | solution.py:17
  81.2 3.2 %collective-permute-start.27 = (f32[16,256]{1,0:T(8,128)S(1)}, f32[16,256]{1,0:T(8,128)S(1)}, u32[]{:S(2)}, u32[]{:S(2)}) collective-permute-start(f32[16,256]{1,0:T(8,128)S(1)} %shard_map.113.refs_0_.refs_2_), channel_id=1, source_target_pairs={{0,24},{8,16},{16,8},{24,0},{1,25},{9,17},{17,9},{25,1},{2,26},{10... | collective-permute-start | bytes 49160 | tf_op jit(solution)/shard_map/ppermute | solution.py:17
  85.1 1.2 %collective-permute-start.28 = (f32[16,256]{1,0:T(8,128)S(1)}, f32[16,256]{1,0:T(8,128)S(1)}, u32[]{:S(2)}, u32[]{:S(2)}) collective-permute-start(f32[16,256]{1,0:T(8,128)S(1)} %shard_map.114.refs_0_), channel_id=1, source_target_pairs={{0,8},{8,0},{16,24},{24,16},{1,9},{9,1},{17,25},{25,17},{2,10},{10... | collective-permute-start | bytes 49160 | tf_op jit(solution)/shard_map/ppermute | solution.py:17
  87.1 1.2 %collective-permute-start.29 = (f32[16,256]{1,0:T(8,128)S(1)}, f32[16,256]{1,0:T(8,128)S(1)}, u32[]{:S(2)}, u32[]{:S(2)}) collective-permute-start(f32[16,256]{1,0:T(8,128)S(1)} %shard_map.115.refs_0_), channel_id=1, source_target_pairs={{0,8},{8,0},{16,24},{24,16},{1,9},{9,1},{17,25},{25,17},{2,10},{10... | collective-permute-start | bytes 49160 | tf_op jit(solution)/shard_map/ppermute | solution.py:17
  (11 other events, 71.5 us)

commit v6 on v5

--- a/solution.py
+++ b/solution.py
@@ -39,7 +39,7 @@
     return parts
 
 
-def call(body, outs, arrays, scalars=(), scratch=(), work=0, remote=0, room=40):
+def call(body, outs, arrays, scalars=(), scratch=(), work=0, remote=0, room=16):
     moved = sum(a.size * a.dtype.itemsize for a in arrays)
     moved += sum(math.prod(shape) * jnp.dtype(kind).itemsize for shape, kind in outs)
     return pl.pallas_call(
@@ -159,6 +159,7 @@
             (ids,),
             [pltpu.VMEM((sum(spans), base, base), F32), pltpu.SemaphoreType.DMA((ranks,))],
             remote=ranks,
+            room=24,
         )
         return {name: made[2 * i : 2 * i + 2] for i, name in enumerate(names)}
 
@@ -172,16 +173,21 @@
     ]
     lower_parts, upper_parts = ring_gather(own_blocks, ranks)
 
-    narrow = TILE - levels * piece
-    aux = jnp.concatenate([win_pivots.reshape(-1), pattern[0, 0].astype(F32)])
-    aux = jnp.pad(aux, (0, share * narrow - aux.size)).reshape(share, narrow)
-    aux = jnp.tile(jnp.pad(aux, ((0, 0), (levels * piece, 0))), (ranks, 1))
+    start = levels * piece
+    beside = start + piece + tiles <= TILE
+    number_row, number_lane = (0, start + piece) if beside else (levels, start)
+    aux = jnp.zeros((share, TILE), F32)
+    aux = lax.dynamic_update_slice(aux, win_pivots, (0, start))
+    aux = lax.dynamic_update_slice(aux, pattern[0].astype(F32), (number_row, number_lane))
+    aux = jnp.tile(aux, (ranks, 1))
     packed = tiles * TILE + TILE
 
     firsts = [part for parts in (lower_parts, upper_parts) for step, part in parts if step in (1, -1)]
 
     def local_forward(rhs_ref, window_ref, aux_ref, inverse_any, coupling_any, *refs):
-        solved_ref, terms_ref, held, inverse_ref, coupling_ref, done = refs[len(firsts) :]
+        refs = refs[len(firsts) :]
+        solved_ref, terms_ref, split_refs = refs[0], refs[1], refs[2:6]
+        held, inverse_ref, coupling_ref, done = refs[6:]
         first = pltpu.make_async_copy(inverse_any, inverse_ref, done.at[0])
         second = pltpu.make_async_copy(coupling_any, coupling_ref, done.at[1])
         first.start()
@@ -192,14 +198,18 @@
             held[level * piece : (level + 1) * piece, :] = window_ref[level]
         terms_ref[:, tiles * TILE :] = held[...].T + aux_ref[...]
         first.wait()
-        solved = rhs + jnp.dot(strict_lower(inverse_ref[...]), rhs, precision=EXACT)
+        strict = strict_lower(inverse_ref[...])
+        solved = rhs + jnp.dot(strict, rhs, precision=EXACT)
         solved_ref[...] = solved.T
         second.wait()
         terms_ref[:, : tiles * TILE] = jnp.dot(coupling_ref[...], solved, precision=EXACT).T
-
-    solved_loc, terms = call(
+        for part_ref, part in zip(split_refs, split(coupling_ref[...]) + split(strict)):
+            part_ref[...] = part.astype(BF16)
+
+    square = [((tiles * TILE, local), BF16)] * 2 + [((local, local), BF16)] * 2
+    solved_loc, terms, *local_parts = call(
         local_forward,
-        [((columns, local), F32), ((columns, packed), F32)],
+        [((columns, local), F32), ((columns, packed), F32)] + square,
         (loc_rhs[0, 0], win_rhs, aux, loc_inverse[0, 0], loc_coupling[0, 0], *firsts),
         remote=2 + len(firsts),
         scratch=[
@@ -209,27 +219,38 @@
             pltpu.SemaphoreType.DMA((2,)),
         ],
         work=24 * local * local * columns,
-        room=60,
+        room=24,
     )
     terms = lax.all_to_all(terms.reshape(ranks, share, packed), "row", 0, 0, tiled=True)
-    aux = terms[:, :, tiles * TILE + levels * piece :].reshape(ranks, -1)
-    known = aux[:, levels * piece : levels * piece + tiles].astype(jnp.int32).reshape(-1)
-    pivots = aux[:, : levels * piece].reshape(ranks, levels, piece)
-    pivots = pivots.transpose(1, 0, 2).reshape(levels, 1, base)
-    all_pivots = leaf_swaps([pivots] * leaves)
+    number_lane += tiles * TILE
+    known = terms[:, number_row, number_lane : number_lane + tiles].astype(jnp.int32)
 
     lower = assemble(lower_parts, lower_names)
     upper = assemble(upper_parts, upper_names)
     blocks = {**lower, **upper}
 
     def scatter(ids_ref, known_ref, terms_ref, *refs):
-        outs, path = refs[:-1], refs[-1]
+        outs, pivots_ref, path = refs[:-2], refs[-2], refs[-1]
         lane = lax.broadcasted_iota(jnp.int32, (share, TILE), 1)
         path[...] = jnp.zeros_like(path)
         for source in range(ranks):
             for tile in range(tiles):
-                place = known_ref[source * tiles + tile]
+                place = known_ref[source, tile]
                 path[place] = path[place] - terms_ref[source, :, tile * TILE : (tile + 1) * TILE]
+
+        def spread(first):
+            rows = []
+            for half in range(halves):
+                row = jnp.zeros((share, TILE), F32)
+                for source in range(half * TILE // piece, (half + 1) * TILE // piece):
+                    place = source * piece % TILE
+                    shift = (TILE + place - first) % TILE
+                    turned = pltpu.roll(terms_ref[source, :, tiles * TILE :], shift, 1)
+                    row = jnp.where((lane >= place) & (lane < place + piece), turned, row)
+                rows.append(row)
+            return jnp.concatenate(rows, 1)
+
+        pivots_ref[...] = spread(levels * piece)
         for level in range(levels):
             span = 2**level
             filled = outs[level]
@@ -238,24 +259,17 @@
                 for half in range(halves):
                     filled[slot, :, half * TILE : (half + 1) * TILE] = path[first + half]
             own = ids_ref[0] % span
-            rows = []
-            for half in range(halves):
-                row = jnp.zeros((share, TILE), F32)
-                for source in range(half * TILE // piece, (half + 1) * TILE // piece):
-                    place = source * piece % TILE
-                    shift = (TILE + place - level * piece) % TILE
-                    turned = pltpu.roll(terms_ref[source, :, tiles * TILE :], shift, 1)
-                    row = jnp.where((lane >= place) & (lane < place + piece), turned, row)
-                rows.append(row)
-            filled[own] = filled[own] + jnp.concatenate(rows, 1)
-
-    rest = call(
+            filled[own] = filled[own] + spread(level * piece)
+
+    *rest, pivots = call(
         scatter,
-        [((2**level, *wide), F32) for level in range(levels)],
+        [((2**level, *wide), F32) for level in range(levels)] + [(wide, F32)],
         (terms,),
         (ids, known),
         [pltpu.VMEM((path_tiles, share, TILE), F32)],
     )
+
+    all_pivots = leaf_swaps([pivots] * leaves)
 
     def total(refs):
         value = refs[0][0] if len(refs[0].shape) > len(wide) and len(refs) == 1 else refs[0][...]
@@ -318,7 +332,7 @@
     chunks = [rest[0]]
     solved = []
     for level in range(top):
-        chunks = leaf_swaps(diagonal(level, chunks, () if level else all_pivots))
+        chunks = leaf_swaps(diagonal(level, chunks, all_pivots if level == 1 else ()))
         value, chunks = link(level, chunks)
         solved.append(value)
         chunks = leaf_swaps(chunks)
@@ -330,7 +344,7 @@
         own = ids_ref[0] % leaves
         wanted[...] = total(sum_refs)
         for offset, ref in enumerate(pivot_refs):
-            wanted[own ^ offset] = wanted[own ^ offset] / ref[top]
+            wanted[own ^ offset] = wanted[own ^ offset] / ref[top : top + 1, :]
         value = wanted[own]
         for slot in range(leaves):
             value = value + times(wanted[slot], high_ref[slot], low_ref[slot], 0)
@@ -362,7 +376,7 @@
             high_ref, low_ref, solved_ref, pivot_ref, out, held = refs[span:]
             ordered(ids_ref[0] % span, part_refs, held)
             above = against(held, high_ref, low_ref, span)
-            out[...] = solved_ref[...] / pivot_ref[level - 1] - above
+            out[...] = solved_ref[...] / pivot_ref[level - 1 : level, :] - above
 
         return call(
             body,
@@ -401,7 +415,7 @@
         out, path, held = refs[6:]
         group = ids_ref[0]
         ordered(group % 2, parts[1], held)
-        wanted = solved_ref[...] / pivot_ref[0] - against(held, link_high, link_low, 2)
+        wanted = solved_ref[...] / pivot_ref[0:1, :] - against(held, link_high, link_low, 2)
         lowest = wanted + times(wanted, high_ref[0], low_ref[0], 0)
         owned = [lowest]
         for half in range(halves):
@@ -416,9 +430,7 @@
         lane = lax.broadcasted_iota(jnp.int32, (share, TILE), 1)
         for target in range(ranks):
             for tile in range(tiles):
-                out[target, :, tile * TILE : (tile + 1) * TILE] = path[
-                    known_ref[target * tiles + tile]
-                ]
+                out[target, :, tile * TILE : (tile + 1) * TILE] = path[known_ref[target, tile]]
             pieces = jnp.zeros((share, TILE), F32)
             for level in range(levels):
                 shift = (base + level * piece - target * piece) % base
@@ -442,37 +454,34 @@
     )
     back = lax.all_to_all(replies[0], "row", 0, 0, tiled=True).reshape(columns, packed)
 
-    def local_backward(back, solved_ref, pivot_ref, inverse_any, coupling_any, *refs):
-        out, window_ref, inverse_ref, coupling_ref, done = refs
-        first = pltpu.make_async_copy(coupling_any, coupling_ref, done.at[0])
-        second = pltpu.make_async_copy(inverse_any, inverse_ref, done.at[1])
-        first.start()
-        second.start()
+    def local_backward(back, solved_ref, pivot_ref, *refs):
+        sources, (out, window_ref), held, done = refs[:4], refs[4:6], refs[6:10], refs[10]
+        copies = [
+            pltpu.make_async_copy(source, target, done.at[index])
+            for index, (source, target) in enumerate(zip(sources, held))
+        ]
+        for copy in copies:
+            copy.start()
         final = back[:, tiles * TILE :].T
         for level in range(levels):
             window_ref[level] = final[level * piece : (level + 1) * piece]
-        first.wait()
-        remainder = solved_ref[...] / pivot_ref[...] - jnp.dot(
-            back[:, : tiles * TILE], coupling_ref[...], precision=EXACT
-        )
-        second.wait()
-        answer = remainder + jnp.dot(
-            remainder, strict_lower(inverse_ref[...]), precision=EXACT
-        )
+        scaled = solved_ref[...] / pivot_ref[...]
+        copies[0].wait()
+        copies[1].wait()
+        remainder = scaled - times(back[:, : tiles * TILE], held[0][...], held[1][...], 0)
+        copies[2].wait()
+        copies[3].wait()
+        answer = remainder + times(remainder, held[2][...], held[3][...], 0)
         out[...] = answer.T
 
     answer, window = call(
         local_backward,
         [((local, columns), F32), ((levels, piece, columns), F32)],
-        (back, solved_loc, loc_pivots[0], loc_inverse[0, 0], loc_coupling[0, 0]),
-        scratch=[
-            pltpu.VMEM((local, local), F32),
-            pltpu.VMEM((tiles * TILE, local), F32),
-            pltpu.SemaphoreType.DMA((2,)),
-        ],
-        remote=2,
+        (back, solved_loc, loc_pivots[0], *local_parts),
+        scratch=[pltpu.VMEM(*part) for part in square] + [pltpu.SemaphoreType.DMA((4,))],
+        remote=4,
         work=24 * local * local * columns,
-        room=60,
+        room=24,
     )
     return answer[None, None], window
 

time: 110 us -> 110 us (level)
  local copies, waits for them, and re-layouts: 3.84 us -> 8.99 us
  Pallas kernels: 22.6 us -> 18.8 us
  waiting for transfers between devices: 36.2 us -> 33.7 us
  starting transfers between devices: 29.9 us -> 31.1 us
    ppermute x7, waiting for transfers between devices: 11.5 us -> 4.69 us  [ring_gather(): moving[index][0] = lax.ppermute(moving[index][0], 'row', right)]
    unnamed x24 -> x34, local copies, waits for them, and re-layouts: 0.08 us -> 6.75 us
    ppermute x7, waiting for transfers between devices: 13.5 us -> 18.3 us  [ring_gather(): moving[index][1] = lax.ppermute(moving[index][1], 'row', left)]
    ppermute x7, starting transfers between devices: 4.01 us -> 8.78 us  [ring_gather(): moving[index][1] = lax.ppermute(moving[index][1], 'row', left)]
    ppermute x7, starting transfers between devices: 12.5 us -> 8.02 us  [ring_gather(): moving[index][0] = lax.ppermute(moving[index][0], 'row', right)]
    pallas_call x14, Pallas kernels: 22.6 us -> 18.8 us  [call(): pl.pallas_call(body, out_shape=[jax.ShapeDtypeStruct(*o) for o in outs],...]
    reshape x6 -> x0, local copies, waits for them, and re-layouts: 1.33 us -> none  [the longest x1 0.92 us: shards(): aux = terms[:, :, tiles * TILE + levels * piece:].reshape(ranks, -1)]
  transfers between devices with their start and end apart: 31 -> 31, of which waited for: 14 -> 14; matrix products, arithmetic and copies ran while one was open for 3% -> 1% of each run, Pallas kernels for 13% -> 11%
where the time goes in v6:
time: 110 us
  waiting for transfers between devices  33.7 us (31%)
  starting transfers between devices  31.1 us (28%)
  Pallas kernels  18.8 us (17%)
  blocking collectives  15.1 us (14%)
  local copies, waits for them, and re-layouts  8.99 us (8%)
  other arithmetic  1.1 us (1%)
    pallas_call x14, Pallas kernels, call(): pl.pallas_call(body, out_shape=[jax.ShapeDtypeStruct(*o) for o in outs],...  18.8 us
    ppermute x7, waiting for transfers between devices, ring_gather(): moving[index][1] = lax.ppermute(moving[index][1], 'row', left)  18.3 us
    all_to_all x1, blocking collectives, shards(): lax.all_to_all(replies[0], 'row', 0, 0, tiled=True).reshape(columns, packed)  15.1 us
    ppermute x16, waiting for transfers between devices, swap(): return lax.ppermute(value, axis, [(i, i ^ offset) for i in range(count)])  10.7 us
    ppermute x7, starting transfers between devices, ring_gather(): moving[index][1] = lax.ppermute(moving[index][1], 'row', left)  8.78 us
    ppermute x16, starting transfers between devices, swap(): return lax.ppermute(value, axis, [(i, i ^ offset) for i in range(count)])  8.6 us
    ppermute x7, starting transfers between devices, ring_gather(): moving[index][0] = lax.ppermute(moving[index][0], 'row', right)  8.02 us
    unnamed x34, local copies, waits for them, and re-layouts  6.75 us
  transfers between devices with their start and end apart: 31, of which 14 were waited for; matrix products, arithmetic and copies ran while one was open for 1% of the time, Pallas kernels for 11%

profile of v6, /device:TPU:0, one launch (start us, length us, event | category | flops | bytes accessed | tf_op | source)
XLA Modules:
  0.0 109.5 jit_solution(9242314110879488773)
XLA Ops:
  0.6 1.0 slice_bitcast_fusion
  2.6 3.1 %collective-permute-start = (f32[9,32,256]{2,1,0:T(8,128)S(1)}, f32[9,32,256]{2,1,0:T(8,128)S(1)}, u32[]{:S(2)}, u32[]{:S(2)}) collective-permute-start(f32[9,32,256]{2,1,0:T(8,128)S(1)} %bitcast.18), channel_id=1, source_target_pairs={{0,2},{2,4},{4,6},{6,7},{7,5},{5,3},{3,1},{1,0},{8,10},{10,12},{12... | collective-permute-start | bytes 884744 | tf_op jit(solution)/shard_map/ppermute | solution.py:34
  6.6 2.0 %collective-permute-start.3 = (f32[4,32,256]{2,1,0:T(8,128)S(1)}, f32[4,32,256]{2,1,0:T(8,128)S(1)}, u32[]{:S(2)}, u32[]{:S(2)}) collective-permute-start(f32[4,32,256]{2,1,0:T(8,128)S(1)} %bitcast.23), channel_id=1, source_target_pairs={{2,0},{4,2},{6,4},{7,6},{5,7},{3,5},{1,3},{0,1},{10,8},{12,10},{14... | collective-permute-start | bytes 393224 | tf_op jit(solution)/shard_map/ppermute | solution.py:37
  8.8 4.7 %collective-permute-done.refs_0_.refs_1_ = f32[9,32,256]{2,1,0:T(8,128)S(1)} collective-permute-done((f32[9,32,256]{2,1,0:T(8,128)S(1)}, f32[9,32,256]{2,1,0:T(8,128)S(1)}, u32[]{:S(2)}, u32[]{:S(2)}) %collective-permute-start) | collective-permute-done | bytes 294944 | tf_op jit(solution)/shard_map/ppermute | solution.py:34
  13.4 2.1 %collective-permute-start.4 = (f32[9,32,256]{2,1,0:T(8,128)S(1)}, f32[9,32,256]{2,1,0:T(8,128)S(1)}, u32[]{:S(2)}, u32[]{:S(2)}) collective-permute-start(f32[9,32,256]{2,1,0:T(8,128)S(1)} %collective-permute-done.refs_0_.refs_1_), channel_id=1, source_target_pairs={{0,2},{2,4},{4,6},{6,7},{7,5},{5,3},{3,1},{1,0},{8,10},{10,12},{12... | collective-permute-start | bytes 884744 | tf_op jit(solution)/shard_map/ppermute | solution.py:34
  15.9 1.1 collective-permute-done.3.refs_3_.refs_2_
  17.0 1.2 %copy-done.1 = f32[1,1,512,512]{3,2,1,0:T(8,128)S(1)} copy-done((f32[1,1,512,512]{3,2,1,0:T(8,128)S(1)}, f32[1,1,512,512]{3,2,1,0:T(8,128)}, u32[]{:S(2)}) %copy-start.1) | copy-done | bytes 1048600
  18.2 0.9 copy-done.2
  19.1 5.1 %shard_map.104 = (f32[128,512]{1,0:T(8,128)S(1)}, f32[128,640]{1,0:T(8,128)}, bf16[512,512]{1,0:T(8,128)(2,1)S(1)}, bf16[512,512]{1,0:T(8,128)(2,1)S(1)}, bf16[5...) custom-call(f32[512,128]{1,0:T(8,128)S(1)} %bitcast.27, f32[3,32,128]{2,1,0:T(8,128)S(1)} %copy-done.3, ...), custom_call_target="tpu_custom_call" | custom-call | flops 805306368 | bytes 6012928 | tf_op jit(solution)/shard_map/pallas_call | solution.py:45
  28.1 5.7 %all-to-all-start = ((f32[8,16,640]{2,1,0:T(8,128)}), f32[8,16,640]{2,1,0:T(8,128)S(1)}, u32[]{:S(2)}, u32[]{:S(2)}) async-start(f32[8,16,640]{2,1,0:T(8,128)} %bitcast.11), calls=%async_computation | async-start | bytes 655360 | tf_op jit(solution)/shard_map/all_to_all | solution.py:224
  33.8 2.0 %collective-permute-start.5 = (f32[9,32,256]{2,1,0:T(8,128)S(1)}, f32[9,32,256]{2,1,0:T(8,128)S(1)}, u32[]{:S(2)}, u32[]{:S(2)}) collective-permute-start(f32[9,32,256]{2,1,0:T(8,128)S(1)} %collective-permute-done.1.refs_1_.refs_2_), channel_id=1, source_target_pairs={{2,0},{4,2},{6,4},{7,6},{5,7},{3,5},{1,3},{0,1},{10,8},{12,10},{14... | collective-permute-start | bytes 884744 | tf_op jit(solution)/shard_map/ppermute | solution.py:37
  35.9 2.0 %collective-permute-start.18 = (f32[4,32,256]{2,1,0:T(8,128)S(1)}, f32[4,32,256]{2,1,0:T(8,128)S(1)}, u32[]{:S(2)}, u32[]{:S(2)}) collective-permute-start(f32[4,32,256]{2,1,0:T(8,128)S(1)} %collective-permute-done.3.refs_3_.refs_2_), channel_id=1, source_target_pairs={{2,0},{4,2},{6,4},{7,6},{5,7},{3,5},{1,3},{0,1},{10,8},{12,10},{14... | collective-permute-start | bytes 393224 | tf_op jit(solution)/shard_map/ppermute | solution.py:37
  37.9 10.6 %collective-permute-done.18.refs_4_ = f32[4,32,256]{2,1,0:T(8,128)S(1)} collective-permute-done((f32[4,32,256]{2,1,0:T(8,128)S(1)}, f32[4,32,256]{2,1,0:T(8,128)S(1)}, u32[]{:S(2)}, u32[]{:S(2)}) %collective-permute-start.18) | collective-permute-done | bytes 131104 | tf_op jit(solution)/shard_map/ppermute | solution.py:37
  48.6 2.8 %collective-permute-start.7 = (f32[9,32,256]{2,1,0:T(8,128)S(1)}, f32[9,32,256]{2,1,0:T(8,128)S(1)}, u32[]{:S(2)}, u32[]{:S(2)}) collective-permute-start(f32[9,32,256]{2,1,0:T(8,128)S(1)} %collective-permute-done.5.refs_4_), channel_id=1, source_target_pairs={{2,0},{4,2},{6,4},{7,6},{5,7},{3,5},{1,3},{0,1},{10,8},{12,10},{14... | collective-permute-start | bytes 884744 | tf_op jit(solution)/shard_map/ppermute | solution.py:37
  52.0 2.0 %collective-permute-start.19 = (f32[4,32,256]{2,1,0:T(8,128)S(1)}, f32[4,32,256]{2,1,0:T(8,128)}, u32[]{:S(2)}, u32[]{:S(2)}) collective-permute-start(f32[4,32,256]{2,1,0:T(8,128)S(1)} %collective-permute-done.17.refs_3_), channel_id=1, source_target_pairs={{0,2},{2,4},{4,6},{6,7},{7,5},{5,3},{3,1},{1,0},{8,10},{10,12},{12... | collective-permute-start | bytes 393224 | tf_op jit(solution)/shard_map/ppermute | solution.py:34
  54.0 2.2 %collective-permute-done.20.refs_6_ = f32[4,32,256]{2,1,0:T(8,128)S(1)} collective-permute-done((f32[4,32,256]{2,1,0:T(8,128)S(1)}, f32[4,32,256]{2,1,0:T(8,128)S(1)}, u32[]{:S(2)}, u32[]{:S(2)}) %collective-permute-start.20) | collective-permute-done | bytes 131104 | tf_op jit(solution)/shard_map/ppermute | solution.py:37
  57.2 4.4 %collective-permute-done.7.refs_6_ = f32[9,32,256]{2,1,0:T(8,128)S(1)} collective-permute-done((f32[9,32,256]{2,1,0:T(8,128)S(1)}, f32[9,32,256]{2,1,0:T(8,128)S(1)}, u32[]{:S(2)}, u32[]{:S(2)}) %collective-permute-start.7) | collective-permute-done | bytes 294944 | tf_op jit(solution)/shard_map/ppermute | solution.py:37
  61.5 1.5 %collective-permute-start.11 = (f32[16,256]{1,0:T(8,128)S(1)}, f32[16,256]{1,0:T(8,128)S(1)}, u32[]{:S(2)}, u32[]{:S(2)}) collective-permute-start(f32[16,256]{1,0:T(8,128)S(1)} %get-tuple-element.45.refs_4_.refs_7_.refs_9_), channel_id=1, source_target_pairs={{0,16},{8,24},{16,0},{24,8},{1,17},{9,25},{17,1},{25,9},{2,18},{10... | collective-permute-start | bytes 49160 | tf_op jit(solution)/shard_map/ppermute | solution.py:17
  63.0 1.2 %shard_map.106 = (bf16[1,256,256]{2,1,0:T(8,128)(2,1)S(1)}, bf16[1,256,256]{2,1,0:T(8,128)(2,1)S(1)}, bf16[2,256,256]{2,1,0:T(8,128)(2,1)S(1)}, bf16[2,256,256]{...) custom-call(s32[2]{0:T(128)S(1)} %pad_add_fusion.ids_ref, ...), custom_call_target="tpu_custom_call" | custom-call | bytes 4718592 | tf_op jit(solution)/shard_map/pallas_call | solution.py:45
  71.2 1.0 collective-permute-start.16
  72.1 2.1 %shard_map.111 = (bf16[4,256,256]{2,1,0:T(8,128)(2,1)S(1)}, bf16[4,256,256]{2,1,0:T(8,128)(2,1)S(1)}) custom-call(s32[2]{0:T(128)S(1)} %pad_add_fusion.ids_ref, f32[4,32,256]{2,1,0:T(8,128)S(1)} %bitcast.25, f32[4,32,256]{2,1,0:T(8,128)S(1)} %collective-permute-done.2.refs_2_.refs_1_, f32[4,32,256]{2,1,0:T(8,128)S(1)} %collective-permute-done.3.refs_3_.refs_2_, ...), custom_call_target="tpu_custom_call" | custom-call | bytes 2097152 | tf_op jit(solution)/shard_map/pallas_call | solution.py:45
  74.5 1.0 shard_map.112.refs_0_
  75.5 1.2 %collective-permute-start.24 = (f32[4,16,256]{2,1,0:T(8,128)S(1)}, f32[4,16,256]{2,1,0:T(8,128)S(1)}, u32[]{:S(2)}, u32[]{:S(2)}) collective-permute-start(f32[4,16,256]{2,1,0:T(8,128)S(1)} %shard_map.112.refs_0_), channel_id=1, source_target_pairs={{0,24},{8,16},{16,8},{24,0},{1,25},{9,17},{17,9},{25,1},{2,26},{10... | collective-permute-start | bytes 196616 | tf_op jit(solution)/shard_map/ppermute | solution.py:17
  77.6 1.9 %collective-permute-done.24.refs_3_ = f32[4,16,256]{2,1,0:T(8,128)S(1)} collective-permute-done((f32[4,16,256]{2,1,0:T(8,128)S(1)}, f32[4,16,256]{2,1,0:T(8,128)S(1)}, u32[]{:S(2)}, u32[]{:S(2)}) %collective-permute-start.24) | collective-permute-done | bytes 65568 | tf_op jit(solution)/shard_map/ppermute | solution.py:17
  79.5 1.9 %collective-permute-done.23.refs_2_ = f32[4,16,256]{2,1,0:T(8,128)S(1)} collective-permute-done((f32[4,16,256]{2,1,0:T(8,128)S(1)}, f32[4,16,256]{2,1,0:T(8,128)S(1)}, u32[]{:S(2)}, u32[]{:S(2)}) %collective-permute-start.23) | collective-permute-done | bytes 65568 | tf_op jit(solution)/shard_map/ppermute | solution.py:17
  84.1 1.4 %collective-permute-done.27.refs_3_.refs_5_ = f32[16,256]{1,0:T(8,128)S(1)} collective-permute-done((f32[16,256]{1,0:T(8,128)S(1)}, f32[16,256]{1,0:T(8,128)S(1)}, u32[]{:S(2)}, u32[]{:S(2)}) %collective-permute-start.27) | collective-permute-done | bytes 16416 | tf_op jit(solution)/shard_map/ppermute | solution.py:17
  85.5 1.2 %collective-permute-done.26.refs_2_.refs_4_ = f32[16,256]{1,0:T(8,128)S(1)} collective-permute-done((f32[16,256]{1,0:T(8,128)S(1)}, f32[16,256]{1,0:T(8,128)S(1)}, u32[]{:S(2)}, u32[]{:S(2)}) %collective-permute-start.26) | collective-permute-done | bytes 16416 | tf_op jit(solution)/shard_map/ppermute | solution.py:17
  87.6 1.2 %collective-permute-done.28.refs_1_ = f32[16,256]{1,0:T(8,128)S(1)} collective-permute-done((f32[16,256]{1,0:T(8,128)S(1)}, f32[16,256]{1,0:T(8,128)S(1)}, u32[]{:S(2)}, u32[]{:S(2)}) %collective-permute-start.28) | collective-permute-done | bytes 16416 | tf_op jit(solution)/shard_map/ppermute | solution.py:17
  89.7 1.0 collective-permute-done.29.refs_1_
  90.7 1.1 shard_map.116
  91.8 15.1 %all_to_all.10 = f32[8,16,640]{2,1,0:T(8,128)S(1)} all-to-all(f32[8,16,640]{2,1,0:T(8,128)S(1)} %shard_map.116), channel_id=1, replica_groups=mesh['leaf'=4,'row'=8] {'row'}, dimensions={0} | all-to-all | bytes 655360 | tf_op jit(solution)/shard_map/all_to_all | solution.py:455
  107.6 2.0 %shard_map.117 = (f32[512,128]{1,0:T(8,128)}, f32[3,32,128]{2,1,0:T(8,128)}) custom-call(f32[128,640]{1,0:T(8,128)S(1)} %bitcast.26, f32[128,512]{1,0:T(8,128)S(1)} %copy-done.13, f32[1,512]{1,0:T(1,128)S(1)} %bitcast.31, bf16[512,512]{1,0:T(8,128)(2,1)S(1)} %copy-done.5, bf16[512,512]{1,0:T(8,128)(2,1)S(1)} %copy-done.7, bf16[512,512]{1,0:T(8,128)(2,1)S(1)} %copy-done.9, ...), custom_call_target="tpu_custom_call" | custom-call | flops 805306368 | bytes 3000320 | tf_op jit(solution)/shard_map/pallas_call | solution.py:45
  (88 shorter events, 21.1 us)
Async XLA Ops:
  2.6 10.9 %collective-permute-start = (f32[9,32,256]{2,1,0:T(8,128)S(1)}, f32[9,32,256]{2,1,0:T(8,128)S(1)}, u32[]{:S(2)}, u32[]{:S(2)}) collective-permute-start(f32[9,32,256]{2,1,0:T(8,128)S(1)} %bitcast.18), channel_id=1, source_target_pairs={{0,2},{2,4},{4,6},{6,7},{7,5},{5,3},{3,1},{1,0},{8,10},{10,12},{12... | collective-permute-start | bytes 884744 | tf_op jit(solution)/shard_map/ppermute | solution.py:34
  5.7 11.3 %collective-permute-start.1 = (f32[9,32,256]{2,1,0:T(8,128)S(1)}, f32[9,32,256]{2,1,0:T(8,128)S(1)}, u32[]{:S(2)}, u32[]{:S(2)}) collective-permute-start(f32[9,32,256]{2,1,0:T(8,128)S(1)} %bitcast.19), channel_id=1, source_target_pairs={{2,0},{4,2},{6,4},{7,6},{5,7},{3,5},{1,3},{0,1},{10,8},{12,10},{14... | collective-permute-start | bytes 884744 | tf_op jit(solution)/shard_map/ppermute | solution.py:37
  6.6 10.3 %collective-permute-start.3 = (f32[4,32,256]{2,1,0:T(8,128)S(1)}, f32[4,32,256]{2,1,0:T(8,128)S(1)}, u32[]{:S(2)}, u32[]{:S(2)}) collective-permute-start(f32[4,32,256]{2,1,0:T(8,128)S(1)} %bitcast.23), channel_id=1, source_target_pairs={{2,0},{4,2},{6,4},{7,6},{5,7},{3,5},{1,3},{0,1},{10,8},{12,10},{14... | collective-permute-start | bytes 393224 | tf_op jit(solution)/shard_map/ppermute | solution.py:37
  8.6 8.3 %collective-permute-start.2 = (f32[4,32,256]{2,1,0:T(8,128)S(1)}, f32[4,32,256]{2,1,0:T(8,128)S(1)}, u32[]{:S(2)}, u32[]{:S(2)}) collective-permute-start(f32[4,32,256]{2,1,0:T(8,128)S(1)} %bitcast.24), channel_id=1, source_target_pairs={{0,2},{2,4},{4,6},{6,7},{7,5},{5,3},{3,1},{1,0},{8,10},{10,12},{12... | collective-permute-start | bytes 393224 | tf_op jit(solution)/shard_map/ppermute | solution.py:34
  13.4 22.4 %collective-permute-start.4 = (f32[9,32,256]{2,1,0:T(8,128)S(1)}, f32[9,32,256]{2,1,0:T(8,128)S(1)}, u32[]{:S(2)}, u32[]{:S(2)}) collective-permute-start(f32[9,32,256]{2,1,0:T(8,128)S(1)} %collective-permute-done.refs_0_.refs_1_), channel_id=1, source_target_pairs={{0,2},{2,4},{4,6},{6,7},{7,5},{5,3},{3,1},{1,0},{8,10},{10,12},{12... | collective-permute-start | bytes 884744 | tf_op jit(solution)/shard_map/ppermute | solution.py:34
  28.1 28.1 %all-to-all-start = ((f32[8,16,640]{2,1,0:T(8,128)}), f32[8,16,640]{2,1,0:T(8,128)S(1)}, u32[]{:S(2)}, u32[]{:S(2)}) async-start(f32[8,16,640]{2,1,0:T(8,128)} %bitcast.11), calls=%async_computation | async-start | bytes 655360 | tf_op jit(solution)/shard_map/all_to_all | solution.py:224
  33.8 14.7 %collective-permute-start.5 = (f32[9,32,256]{2,1,0:T(8,128)S(1)}, f32[9,32,256]{2,1,0:T(8,128)S(1)}, u32[]{:S(2)}, u32[]{:S(2)}) collective-permute-start(f32[9,32,256]{2,1,0:T(8,128)S(1)} %collective-permute-done.1.refs_1_.refs_2_), channel_id=1, source_target_pairs={{2,0},{4,2},{6,4},{7,6},{5,7},{3,5},{1,3},{0,1},{10,8},{12,10},{14... | collective-permute-start | bytes 884744 | tf_op jit(solution)/shard_map/ppermute | solution.py:37
  35.8 15.5 %collective-permute-start.6 = (f32[9,32,256]{2,1,0:T(8,128)S(1)}, f32[9,32,256]{2,1,0:T(8,128)S(1)}, u32[]{:S(2)}, u32[]{:S(2)}) collective-permute-start(f32[9,32,256]{2,1,0:T(8,128)S(1)} %collective-permute-done.4.refs_3_), channel_id=1, source_target_pairs={{0,2},{2,4},{4,6},{6,7},{7,5},{5,3},{3,1},{1,0},{8,10},{10,12},{12... | collective-permute-start | bytes 884744 | tf_op jit(solution)/shard_map/ppermute | solution.py:34
  35.9 12.6 %collective-permute-start.18 = (f32[4,32,256]{2,1,0:T(8,128)S(1)}, f32[4,32,256]{2,1,0:T(8,128)S(1)}, u32[]{:S(2)}, u32[]{:S(2)}) collective-permute-start(f32[4,32,256]{2,1,0:T(8,128)S(1)} %collective-permute-done.3.refs_3_.refs_2_), channel_id=1, source_target_pairs={{2,0},{4,2},{6,4},{7,6},{5,7},{3,5},{1,3},{0,1},{10,8},{12,10},{14... | collective-permute-start | bytes 393224 | tf_op jit(solution)/shard_map/ppermute | solution.py:37
  37.9 14.1 %collective-permute-start.17 = (f32[4,32,256]{2,1,0:T(8,128)S(1)}, f32[4,32,256]{2,1,0:T(8,128)S(1)}, u32[]{:S(2)}, u32[]{:S(2)}) collective-permute-start(f32[4,32,256]{2,1,0:T(8,128)S(1)} %collective-permute-done.2.refs_2_.refs_1_), channel_id=1, source_target_pairs={{0,2},{2,4},{4,6},{6,7},{7,5},{5,3},{3,1},{1,0},{8,10},{10,12},{12... | collective-permute-start | bytes 393224 | tf_op jit(solution)/shard_map/ppermute | solution.py:34
  48.6 7.7 %collective-permute-start.20 = (f32[4,32,256]{2,1,0:T(8,128)S(1)}, f32[4,32,256]{2,1,0:T(8,128)S(1)}, u32[]{:S(2)}, u32[]{:S(2)}) collective-permute-start(f32[4,32,256]{2,1,0:T(8,128)S(1)} %collective-permute-done.18.refs_4_), channel_id=1, source_target_pairs={{2,0},{4,2},{6,4},{7,6},{5,7},{3,5},{1,3},{0,1},{10,8},{12,10},{14... | collective-permute-start | bytes 393224 | tf_op jit(solution)/shard_map/ppermute | solution.py:37
  48.6 13.0 %collective-permute-start.7 = (f32[9,32,256]{2,1,0:T(8,128)S(1)}, f32[9,32,256]{2,1,0:T(8,128)S(1)}, u32[]{:S(2)}, u32[]{:S(2)}) collective-permute-start(f32[9,32,256]{2,1,0:T(8,128)S(1)} %collective-permute-done.5.refs_4_), channel_id=1, source_target_pairs={{2,0},{4,2},{6,4},{7,6},{5,7},{3,5},{1,3},{0,1},{10,8},{12,10},{14... | collective-permute-start | bytes 884744 | tf_op jit(solution)/shard_map/ppermute | solution.py:37
  51.3 11.7 %collective-permute-start.8 = (f32[9,32,256]{2,1,0:T(8,128)S(1)}, f32[9,32,256]{2,1,0:T(8,128)S(1)}, u32[]{:S(2)}, u32[]{:S(2)}) collective-permute-start(f32[9,32,256]{2,1,0:T(8,128)S(1)} %collective-permute-done.6.refs_5_), channel_id=1, source_target_pairs={{0,2},{2,4},{4,6},{6,7},{7,5},{5,3},{3,1},{1,0},{8,10},{10,12},{12... | collective-permute-start | bytes 884744 | tf_op jit(solution)/shard_map/ppermute | solution.py:34
  52.0 20.2 %collective-permute-start.19 = (f32[4,32,256]{2,1,0:T(8,128)S(1)}, f32[4,32,256]{2,1,0:T(8,128)}, u32[]{:S(2)}, u32[]{:S(2)}) collective-permute-start(f32[4,32,256]{2,1,0:T(8,128)S(1)} %collective-permute-done.17.refs_3_), channel_id=1, source_target_pairs={{0,2},{2,4},{4,6},{6,7},{7,5},{5,3},{3,1},{1,0},{8,10},{10,12},{12... | collective-permute-start | bytes 393224 | tf_op jit(solution)/shard_map/ppermute | solution.py:34
  56.2 15.9 %collective-permute-start.21 = (f32[4,32,256]{2,1,0:T(8,128)S(1)}, f32[4,32,256]{2,1,0:T(8,128)}, u32[]{:S(2)}, u32[]{:S(2)}) collective-permute-start(f32[4,32,256]{2,1,0:T(8,128)S(1)} %collective-permute-done.20.refs_6_), channel_id=1, source_target_pairs={{2,0},{4,2},{6,4},{7,6},{5,7},{3,5},{1,3},{0,1},{10,8},{12,10},{14... | collective-permute-start | bytes 393224 | tf_op jit(solution)/shard_map/ppermute | solution.py:37
  57.1 8.7 %collective-permute-start.12 = (f32[16,256]{1,0:T(8,128)S(1)}, f32[16,256]{1,0:T(8,128)S(1)}, u32[]{:S(2)}, u32[]{:S(2)}) collective-permute-start(f32[16,256]{1,0:T(8,128)S(1)} %get-tuple-element.45.refs_4_.refs_7_.refs_9_), channel_id=1, source_target_pairs={{0,24},{8,16},{16,8},{24,0},{1,25},{9,17},{17,9},{25,1},{2,26},{10... | collective-permute-start | bytes 49160 | tf_op jit(solution)/shard_map/ppermute | solution.py:17
  61.5 4.9 %collective-permute-start.11 = (f32[16,256]{1,0:T(8,128)S(1)}, f32[16,256]{1,0:T(8,128)S(1)}, u32[]{:S(2)}, u32[]{:S(2)}) collective-permute-start(f32[16,256]{1,0:T(8,128)S(1)} %get-tuple-element.45.refs_4_.refs_7_.refs_9_), channel_id=1, source_target_pairs={{0,16},{8,24},{16,0},{24,8},{1,17},{9,25},{17,1},{25,9},{2,18},{10... | collective-permute-start | bytes 49160 | tf_op jit(solution)/shard_map/ppermute | solution.py:17
  63.0 3.4 %collective-permute-start.10 = (f32[16,256]{1,0:T(8,128)S(1)}, f32[16,256]{1,0:T(8,128)S(1)}, u32[]{:S(2)}, u32[]{:S(2)}) collective-permute-start(f32[16,256]{1,0:T(8,128)S(1)} %get-tuple-element.45.refs_4_.refs_7_.refs_9_), channel_id=1, source_target_pairs={{0,8},{8,0},{16,24},{24,16},{1,9},{9,1},{17,25},{25,17},{2,10},{10... | collective-permute-start | bytes 49160 | tf_op jit(solution)/shard_map/ppermute | solution.py:17
  65.8 1.4 %collective-permute-start.9 = (f32[16,256]{1,0:T(8,128)S(1)}, f32[16,256]{1,0:T(8,128)S(1)}, u32[]{:S(2)}, u32[]{:S(2)}) collective-permute-start(f32[16,256]{1,0:T(8,128)S(1)} %get-tuple-element.42), channel_id=1, source_target_pairs={{0,8},{8,0},{16,24},{24,16},{1,9},{9,1},{17,25},{25,17},{2,10},{10... | collective-permute-start | bytes 49160 | tf_op jit(solution)/shard_map/ppermute | solution.py:17
  68.0 1.2 %collective-permute-start.13 = (f32[16,256]{1,0:T(8,128)S(1)}, f32[16,256]{1,0:T(8,128)S(1)}, u32[]{:S(2)}, u32[]{:S(2)}) collective-permute-start(f32[16,256]{1,0:T(8,128)S(1)} %get-tuple-element.47), channel_id=1, source_target_pairs={{0,8},{8,0},{16,24},{24,16},{1,9},{9,1},{17,25},{25,17},{2,10},{10... | collective-permute-start | bytes 49160 | tf_op jit(solution)/shard_map/ppermute | solution.py:17
  70.2 4.0 %collective-permute-start.14 = (f32[16,256]{1,0:T(8,128)S(1)}, f32[16,256]{1,0:T(8,128)S(1)}, u32[]{:S(2)}, u32[]{:S(2)}) collective-permute-start(f32[16,256]{1,0:T(8,128)S(1)} %get-tuple-element.52), channel_id=1, source_target_pairs={{0,8},{8,0},{16,24},{24,16},{1,9},{9,1},{17,25},{25,17},{2,10},{10... | collective-permute-start | bytes 49160 | tf_op jit(solution)/shard_map/ppermute | solution.py:17
  70.6 3.9 %collective-permute-start.15 = (f32[16,256]{1,0:T(8,128)S(1)}, f32[16,256]{1,0:T(8,128)S(1)}, u32[]{:S(2)}, u32[]{:S(2)}) collective-permute-start(f32[16,256]{1,0:T(8,128)S(1)} %get-tuple-element.53), channel_id=1, source_target_pairs={{0,16},{8,24},{16,0},{24,8},{1,17},{9,25},{17,1},{25,9},{2,18},{10... | collective-permute-start | bytes 49160 | tf_op jit(solution)/shard_map/ppermute | solution.py:17
  71.2 3.3 %collective-permute-start.16 = (f32[16,256]{1,0:T(8,128)S(1)}, f32[16,256]{1,0:T(8,128)S(1)}, u32[]{:S(2)}, u32[]{:S(2)}) collective-permute-start(f32[16,256]{1,0:T(8,128)S(1)} %get-tuple-element.54), channel_id=1, source_target_pairs={{0,24},{8,16},{16,8},{24,0},{1,25},{9,17},{17,9},{25,1},{2,26},{10... | collective-permute-start | bytes 49160 | tf_op jit(solution)/shard_map/ppermute | solution.py:17
  75.5 4.0 %collective-permute-start.24 = (f32[4,16,256]{2,1,0:T(8,128)S(1)}, f32[4,16,256]{2,1,0:T(8,128)S(1)}, u32[]{:S(2)}, u32[]{:S(2)}) collective-permute-start(f32[4,16,256]{2,1,0:T(8,128)S(1)} %shard_map.112.refs_0_), channel_id=1, source_target_pairs={{0,24},{8,16},{16,8},{24,0},{1,25},{9,17},{17,9},{25,1},{2,26},{10... | collective-permute-start | bytes 196616 | tf_op jit(solution)/shard_map/ppermute | solution.py:17
  76.7 4.7 %collective-permute-start.23 = (f32[4,16,256]{2,1,0:T(8,128)S(1)}, f32[4,16,256]{2,1,0:T(8,128)S(1)}, u32[]{:S(2)}, u32[]{:S(2)}) collective-permute-start(f32[4,16,256]{2,1,0:T(8,128)S(1)} %shard_map.112.refs_0_), channel_id=1, source_target_pairs={{0,16},{8,24},{16,0},{24,8},{1,17},{9,25},{17,1},{25,9},{2,18},{10... | collective-permute-start | bytes 196616 | tf_op jit(solution)/shard_map/ppermute | solution.py:17
  77.6 3.8 %collective-permute-start.22 = (f32[4,16,256]{2,1,0:T(8,128)S(1)}, f32[4,16,256]{2,1,0:T(8,128)S(1)}, u32[]{:S(2)}, u32[]{:S(2)}) collective-permute-start(f32[4,16,256]{2,1,0:T(8,128)S(1)} %shard_map.112.refs_0_), channel_id=1, source_target_pairs={{0,8},{8,0},{16,24},{24,16},{1,9},{9,1},{17,25},{25,17},{2,10},{10... | collective-permute-start | bytes 196616 | tf_op jit(solution)/shard_map/ppermute | solution.py:17
  82.2 3.3 %collective-permute-start.27 = (f32[16,256]{1,0:T(8,128)S(1)}, f32[16,256]{1,0:T(8,128)S(1)}, u32[]{:S(2)}, u32[]{:S(2)}) collective-permute-start(f32[16,256]{1,0:T(8,128)S(1)} %shard_map.113.refs_0_.refs_2_), channel_id=1, source_target_pairs={{0,24},{8,16},{16,8},{24,0},{1,25},{9,17},{17,9},{25,1},{2,26},{10... | collective-permute-start | bytes 49160 | tf_op jit(solution)/shard_map/ppermute | solution.py:17
  83.0 3.7 %collective-permute-start.26 = (f32[16,256]{1,0:T(8,128)S(1)}, f32[16,256]{1,0:T(8,128)S(1)}, u32[]{:S(2)}, u32[]{:S(2)}) collective-permute-start(f32[16,256]{1,0:T(8,128)S(1)} %shard_map.113.refs_0_.refs_2_), channel_id=1, source_target_pairs={{0,16},{8,24},{16,0},{24,8},{1,17},{9,25},{17,1},{25,9},{2,18},{10... | collective-permute-start | bytes 49160 | tf_op jit(solution)/shard_map/ppermute | solution.py:17
  83.6 3.1 %collective-permute-start.25 = (f32[16,256]{1,0:T(8,128)S(1)}, f32[16,256]{1,0:T(8,128)S(1)}, u32[]{:S(2)}, u32[]{:S(2)}) collective-permute-start(f32[16,256]{1,0:T(8,128)S(1)} %shard_map.113.refs_0_.refs_2_), channel_id=1, source_target_pairs={{0,8},{8,0},{16,24},{24,16},{1,9},{9,1},{17,25},{25,17},{2,10},{10... | collective-permute-start | bytes 49160 | tf_op jit(solution)/shard_map/ppermute | solution.py:17
  87.6 1.2 %collective-permute-start.28 = (f32[16,256]{1,0:T(8,128)S(1)}, f32[16,256]{1,0:T(8,128)S(1)}, u32[]{:S(2)}, u32[]{:S(2)}) collective-permute-start(f32[16,256]{1,0:T(8,128)S(1)} %shard_map.114.refs_0_), channel_id=1, source_target_pairs={{0,8},{8,0},{16,24},{24,16},{1,9},{9,1},{17,25},{25,17},{2,10},{10... | collective-permute-start | bytes 49160 | tf_op jit(solution)/shard_map/ppermute | solution.py:17
  88.8 18.1 %copy-start.11 = (bf16[512,512]{1,0:T(8,128)(2,1)S(1)}, bf16[512,512]{1,0:T(8,128)(2,1)}, u32[]{:S(2)}) copy-start(bf16[512,512]{1,0:T(8,128)(2,1)} %copy-done.10) | copy-start | bytes 1572868
  89.5 1.2 %collective-permute-start.29 = (f32[16,256]{1,0:T(8,128)S(1)}, f32[16,256]{1,0:T(8,128)S(1)}, u32[]{:S(2)}, u32[]{:S(2)}) collective-permute-start(f32[16,256]{1,0:T(8,128)S(1)} %shard_map.115.refs_0_), channel_id=1, source_target_pairs={{0,8},{8,0},{16,24},{24,16},{1,9},{9,1},{17,25},{25,17},{2,10},{10... | collective-permute-start | bytes 49160 | tf_op jit(solution)/shard_map/ppermute | solution.py:17
  (16 other events, 116.9 us)

commit v7 on v6

--- a/solution.py
+++ b/solution.py
@@ -21,21 +21,20 @@
     return list(range(0, count, 2)) + list(range(count - 1, 0, -2))
 
 
-def ring_gather(groups, count):
+def ring_gather(block, count):
     order = ring_order(count)
     right = [(order[i], order[(i + 1) % count]) for i in range(count)]
     left = [(target, source) for source, target in right]
-    parts = [[(0, block)] for block in groups]
-    moving = [[block, block] for block in groups]
+    parts = [(0, 0, block)]
+    forward = backward = block
+    middle = block.shape[0] // 2
     for step in range(1, count // 2 + 1):
-        for index in range(len(groups)):
-            last = 2 * step == count
-            if not last or index % 2 == 0:
-                moving[index][0] = lax.ppermute(moving[index][0], "row", right)
-                parts[index].append((-step, moving[index][0]))
-            if not last or index % 2 == 1:
-                moving[index][1] = lax.ppermute(moving[index][1], "row", left)
-                parts[index].append((step, moving[index][1]))
+        first = 0
+        if 2 * step == count:
+            forward, backward, first = forward[:middle], backward[middle:], middle
+        forward = lax.ppermute(forward, "row", right)
+        backward = lax.ppermute(backward, "row", left)
+        parts += [(-step, 0, forward), (step, first, backward)]
     return parts
 
 
@@ -116,21 +115,45 @@
         place = (place + step + ranks) % ranks
         return jnp.where(2 * place < ranks, 2 * place, 2 * (ranks - 1 - place) + 1)
 
-    def assemble(parts, names):
-        spans = [2**level if kind == "A" else 2 ** (level + 1) for kind, level in names]
-        steps = [step for step, _ in parts]
-        parts = [part for _, part in parts]
+    def width(name):
+        return 2 ** name[1] if name[0] == "A" else 2 ** (name[1] + 1)
+
+    all_names = [("A", level) for level in range(levels)] + [("B", level) for level in range(top)]
+
+    def runs(names):
+        found, slot, place = [], 0, 0
+        for name in all_names:
+            if name in names:
+                if found and found[-1][1] == slot:
+                    found[-1][1] += width(name)
+                else:
+                    found.append([slot, slot + width(name), place])
+                place += width(name)
+            slot += width(name)
+        return found
+
+    def assemble(names):
+        names = [name for name in all_names if name in names]
+        spans = [width(name) for name in names]
+        moves = []
+        for index, (step, before, part) in enumerate(parts):
+            for first, end, place in runs(names):
+                low, high = max(first, before), min(end, before + part.shape[0])
+                if low < high:
+                    moves.append((index, step, low - before, high - before, place + low - first))
 
         def body(ids_ref, *refs):
-            parts_refs, outs = refs[:ranks], refs[ranks:-2]
+            parts_refs, outs = refs[: len(parts)], refs[len(parts) : -2]
             natural, done = refs[-2:]
             group = ids_ref[0]
             copies = []
-            for index, ref in enumerate(parts_refs):
-                start = pl.multiple_of(source_row(ids_ref[1], steps[index]) * piece, 8)
+            for number, (index, step, low, high, place) in enumerate(moves):
+                start = pl.multiple_of(source_row(ids_ref[1], step) * piece, 8)
                 copies.append(
                     pltpu.make_async_copy(
-                        ref, natural.at[:, pl.ds(start, piece), :], done.at[index]
+                        parts_refs[index].at[low:high],
+                        natural.at[place : place + high - low, pl.ds(start, piece), :],
+                        done.at[number],
                     )
                 )
             for copy in copies:
@@ -155,23 +178,17 @@
         made = call(
             body,
             outs,
-            parts,
+            [part for _, _, part in parts],
             (ids,),
-            [pltpu.VMEM((sum(spans), base, base), F32), pltpu.SemaphoreType.DMA((ranks,))],
-            remote=ranks,
+            [pltpu.VMEM((sum(spans), base, base), F32), pltpu.SemaphoreType.DMA((len(moves),))],
+            remote=len(parts),
             room=24,
         )
         return {name: made[2 * i : 2 * i + 2] for i, name in enumerate(names)}
 
-    lower_names = [("A", level) for level in range(top)]
-    lower_names += [("B", level) for level in range(top)]
-    upper_names = [("A", top)]
-    below = (2**top - 1) * piece
-    own_blocks = [
-        jnp.concatenate([win_inverse[0, :below], win_coupling[0]], 0).reshape(-1, piece, base),
-        win_inverse[0, below:].reshape(-1, piece, base),
-    ]
-    lower_parts, upper_parts = ring_gather(own_blocks, ranks)
+    parts = ring_gather(
+        jnp.concatenate([win_inverse[0], win_coupling[0]], 0).reshape(-1, piece, base), ranks
+    )
 
     start = levels * piece
     beside = start + piece + tiles <= TILE
@@ -182,12 +199,11 @@
     aux = jnp.tile(aux, (ranks, 1))
     packed = tiles * TILE + TILE
 
-    firsts = [part for parts in (lower_parts, upper_parts) for step, part in parts if step in (1, -1)]
+    firsts = [part for step, _, part in parts if step in (1, -1)]
 
     def local_forward(rhs_ref, window_ref, aux_ref, inverse_any, coupling_any, *refs):
         refs = refs[len(firsts) :]
-        solved_ref, terms_ref, split_refs = refs[0], refs[1], refs[2:6]
-        held, inverse_ref, coupling_ref, done = refs[6:]
+        solved_ref, terms_ref, held, inverse_ref, coupling_ref, done = refs
         first = pltpu.make_async_copy(inverse_any, inverse_ref, done.at[0])
         second = pltpu.make_async_copy(coupling_any, coupling_ref, done.at[1])
         first.start()
@@ -203,13 +219,10 @@
         solved_ref[...] = solved.T
         second.wait()
         terms_ref[:, : tiles * TILE] = jnp.dot(coupling_ref[...], solved, precision=EXACT).T
-        for part_ref, part in zip(split_refs, split(coupling_ref[...]) + split(strict)):
-            part_ref[...] = part.astype(BF16)
-
-    square = [((tiles * TILE, local), BF16)] * 2 + [((local, local), BF16)] * 2
-    solved_loc, terms, *local_parts = call(
+
+    solved_loc, terms = call(
         local_forward,
-        [((columns, local), F32), ((columns, packed), F32)] + square,
+        [((columns, local), F32), ((columns, packed), F32)],
         (loc_rhs[0, 0], win_rhs, aux, loc_inverse[0, 0], loc_coupling[0, 0], *firsts),
         remote=2 + len(firsts),
         scratch=[
@@ -225,8 +238,8 @@
     number_lane += tiles * TILE
     known = terms[:, number_row, number_lane : number_lane + tiles].astype(jnp.int32)
 
-    lower = assemble(lower_parts, lower_names)
-    upper = assemble(upper_parts, upper_names)
+    lower = assemble([name for name in all_names if name != ("A", top)])
+    upper = assemble([("A", top)])
     blocks = {**lower, **upper}
 
     def scatter(ids_ref, known_ref, terms_ref, *refs):
@@ -454,32 +467,34 @@
     )
     back = lax.all_to_all(replies[0], "row", 0, 0, tiled=True).reshape(columns, packed)
 
-    def local_backward(back, solved_ref, pivot_ref, *refs):
-        sources, (out, window_ref), held, done = refs[:4], refs[4:6], refs[6:10], refs[10]
-        copies = [
-            pltpu.make_async_copy(source, target, done.at[index])
-            for index, (source, target) in enumerate(zip(sources, held))
-        ]
-        for copy in copies:
-            copy.start()
+    def local_backward(back, solved_ref, pivot_ref, inverse_any, coupling_any, *refs):
+        out, window_ref, inverse_ref, coupling_ref, done = refs
+        first = pltpu.make_async_copy(coupling_any, coupling_ref, done.at[0])
+        second = pltpu.make_async_copy(inverse_any, inverse_ref, done.at[1])
+        first.start()
+        second.start()
         final = back[:, tiles * TILE :].T
         for level in range(levels):
             window_ref[level] = final[level * piece : (level + 1) * piece]
         scaled = solved_ref[...] / pivot_ref[...]
-        copies[0].wait()
-        copies[1].wait()
-        remainder = scaled - times(back[:, : tiles * TILE], held[0][...], held[1][...], 0)
-        copies[2].wait()
-        copies[3].wait()
-        answer = remainder + times(remainder, held[2][...], held[3][...], 0)
+        first.wait()
+        high, low = split(coupling_ref[...])
+        remainder = scaled - times(back[:, : tiles * TILE], high.astype(BF16), low.astype(BF16), 0)
+        second.wait()
+        high, low = split(strict_lower(inverse_ref[...]))
+        answer = remainder + times(remainder, high.astype(BF16), low.astype(BF16), 0)
         out[...] = answer.T
 
     answer, window = call(
         local_backward,
         [((local, columns), F32), ((levels, piece, columns), F32)],
-        (back, solved_loc, loc_pivots[0], *local_parts),
-        scratch=[pltpu.VMEM(*part) for part in square] + [pltpu.SemaphoreType.DMA((4,))],
-        remote=4,
+        (back, solved_loc, loc_pivots[0], loc_inverse[0, 0], loc_coupling[0, 0]),
+        scratch=[
+            pltpu.VMEM((local, local), F32),
+            pltpu.VMEM((tiles * TILE, local), F32),
+            pltpu.SemaphoreType.DMA((2,)),
+        ],
+        remote=2,
         work=24 * local * local * columns,
         room=24,
     )

time: 110 us -> 104 us (0.945)
  starting transfers between devices: 31.1 us -> 25 us
  local copies, waits for them, and re-layouts: 8.99 us -> 5.53 us
  blocking collectives: 15.1 us -> 16.3 us
    ppermute x14 -> x8, starting transfers between devices: 16.8 us -> 10.5 us  [the longest x4 6.72 us: ring_gather(): backward = lax.ppermute(backward, 'row', left)]
    unnamed x34 -> x22, local copies, waits for them, and re-layouts: 6.75 us -> 3.84 us
    all_to_all x1, blocking collectives: 15.1 us -> 16.3 us  [shards(): lax.all_to_all(replies[0], 'row', 0, 0, tiled=True).reshape(columns, packed)]
    ppermute x14 -> x8, waiting for transfers between devices: 23 us -> 23.5 us  [the longest x4 23 us: ring_gather(): backward = lax.ppermute(backward, 'row', left)]
  transfers between devices with their start and end apart: 31 -> 25, of which waited for: 14 -> 12; matrix products, arithmetic and copies ran while one was open for 1% -> 2% of each run, Pallas kernels for 11% -> 11%
where the time goes in v7:
time: 104 us; the launch traced here: 103 us
  waiting for transfers between devices  34.6 us (33%)
  starting transfers between devices  25 us (24%)
  Pallas kernels  19.8 us (19%)
  blocking collectives  16.3 us (16%)
  local copies, waits for them, and re-layouts  5.53 us (5%)
  other arithmetic  1.26 us (1%)
    ppermute x4, waiting for transfers between devices, ring_gather(): backward = lax.ppermute(backward, 'row', left)  23 us
    pallas_call x14, Pallas kernels, call(): pl.pallas_call(body, out_shape=[jax.ShapeDtypeStruct(*o) for o in outs],...  19.8 us
    all_to_all x1, blocking collectives, shards(): lax.all_to_all(replies[0], 'row', 0, 0, tiled=True).reshape(columns, packed)  16.3 us
    ppermute x16, waiting for transfers between devices, swap(): return lax.ppermute(value, axis, [(i, i ^ offset) for i in range(count)])  11.2 us
    ppermute x16, starting transfers between devices, swap(): return lax.ppermute(value, axis, [(i, i ^ offset) for i in range(count)])  8.47 us
    ppermute x4, starting transfers between devices, ring_gather(): backward = lax.ppermute(backward, 'row', left)  6.72 us
    all_to_all x1, starting transfers between devices, shards(): lax.all_to_all(terms.reshape(ranks, share, packed), 'row', 0, 0, tiled=True)  6 us
    unnamed x22, local copies, waits for them, and re-layouts  3.84 us
  transfers between devices with their start and end apart: 25, of which 12 were waited for; matrix products, arithmetic and copies ran while one was open for 2% of the time, Pallas kernels for 11%

profile of v7, /device:TPU:0, one launch (start us, length us, event | category | flops | bytes accessed | tf_op | source)
XLA Modules:
  0.0 103.5 jit_solution(17639968987956512361)
XLA Ops:
  0.7 1.1 %pad_maximum_fusion = f32[416,256]{1,0:T(8,128)S(1)} fusion(f32[192,256]{1,0:T(8,128)} %bitcast.31, f32[224,256]{1,0:T(8,128)} %bitcast.30), kind=kLoop, calls=%fused_computation | loop fusion | flops 106496 | bytes 851968 | tf_op jit(solution)/shard_map/concatenate | solution.py:190
  1.8 3.0 %collective-permute-start.1 = (f32[13,32,256]{2,1,0:T(8,128)S(1)}, f32[13,32,256]{2,1,0:T(8,128)S(1)}, u32[]{:S(2)}, u32[]{:S(2)}) collective-permute-start(f32[13,32,256]{2,1,0:T(8,128)S(1)} %bitcast.16), channel_id=1, source_target_pairs={{2,0},{4,2},{6,4},{7,6},{5,7},{3,5},{1,3},{0,1},{10,8},{12,10},{14... | collective-permute-start | bytes 1277960 | tf_op jit(solution)/shard_map/ppermute | solution.py:36
  4.9 9.8 %collective-permute-done.1.refs_1_.refs_2_ = f32[13,32,256]{2,1,0:T(8,128)S(1)} collective-permute-done((f32[13,32,256]{2,1,0:T(8,128)S(1)}, f32[13,32,256]{2,1,0:T(8,128)S(1)}, u32[]{:S(2)}, u32[]{:S(2)}) %collective-permute-start.1) | collective-permute-done | bytes 426016 | tf_op jit(solution)/shard_map/ppermute | solution.py:36
  14.7 1.7 %collective-permute-start.3 = (f32[13,32,256]{2,1,0:T(8,128)S(1)}, f32[13,32,256]{2,1,0:T(8,128)S(1)}, u32[]{:S(2)}, u32[]{:S(2)}) collective-permute-start(f32[13,32,256]{2,1,0:T(8,128)S(1)} %collective-permute-done.1.refs_1_.refs_2_), channel_id=1, source_target_pairs={{2,0},{4,2},{6,4},{7,6},{5,7},{3,5},{1,3},{0,1},{10,8},{12,10},{14... | collective-permute-start | bytes 1277960 | tf_op jit(solution)/shard_map/ppermute | solution.py:36
  17.0 1.2 %copy-done = f32[1,1,512,512]{3,2,1,0:T(8,128)S(1)} copy-done((f32[1,1,512,512]{3,2,1,0:T(8,128)S(1)}, f32[1,1,512,512]{3,2,1,0:T(8,128)}, u32[]{:S(2)}) %copy-start) | copy-done | bytes 1048600
  18.2 1.2 %copy-done.2 = f32[1,1,512,512]{3,2,1,0:T(8,128)S(1)} copy-done((f32[1,1,512,512]{3,2,1,0:T(8,128)S(1)}, f32[1,1,512,512]{3,2,1,0:T(8,128)}, u32[]{:S(2)}) %copy-start.2) | copy-done | bytes 1048600
  19.5 4.7 %shard_map.104 = (f32[128,512]{1,0:T(8,128)S(1)}, f32[128,640]{1,0:T(8,128)}) custom-call(f32[512,128]{1,0:T(8,128)S(1)} %bitcast.25, f32[3,32,128]{2,1,0:T(8,128)S(1)} %copy-done.5, f32[128,128]{1,0:T(8,128)S(1)} %bitcast.26, f32[512,512]{1,0:T(8,128)S(1)} %bitcast.20, f32[512,512]{1,0:T(8,128)S(1)} %bitcast.22, ...), custom_call_target="tpu_custom_call" | custom-call | flops 805306368 | bytes 3915776 | tf_op jit(solution)/shard_map/pallas_call | solution.py:44
  24.8 6.0 %all-to-all-start = ((f32[8,16,640]{2,1,0:T(8,128)}), f32[8,16,640]{2,1,0:T(8,128)S(1)}, u32[]{:S(2)}, u32[]{:S(2)}) async-start(f32[8,16,640]{2,1,0:T(8,128)} %bitcast.10), calls=%async_computation | async-start | bytes 655360 | tf_op jit(solution)/shard_map/all_to_all | solution.py:237
  30.8 2.0 %collective-permute-start.5 = (f32[13,32,256]{2,1,0:T(8,128)S(1)}, f32[13,32,256]{2,1,0:T(8,128)S(1)}, u32[]{:S(2)}, u32[]{:S(2)}) collective-permute-start(f32[13,32,256]{2,1,0:T(8,128)S(1)} %collective-permute-done.3.refs_4_), channel_id=1, source_target_pairs={{2,0},{4,2},{6,4},{7,6},{5,7},{3,5},{1,3},{0,1},{10,8},{12,10},{14... | collective-permute-start | bytes 1277960 | tf_op jit(solution)/shard_map/ppermute | solution.py:36
  32.9 13.2 %collective-permute-done.5.refs_6_ = f32[13,32,256]{2,1,0:T(8,128)S(1)} collective-permute-done((f32[13,32,256]{2,1,0:T(8,128)S(1)}, f32[13,32,256]{2,1,0:T(8,128)S(1)}, u32[]{:S(2)}, u32[]{:S(2)}) %collective-permute-start.5) | collective-permute-done | bytes 426016 | tf_op jit(solution)/shard_map/ppermute | solution.py:36
  47.6 3.3 %collective-permute-start.6 = (f32[6,32,256]{2,1,0:T(8,128)}, f32[6,32,256]{2,1,0:T(8,128)}, u32[]{:S(2)}, u32[]{:S(2)}) collective-permute-start(f32[6,32,256]{2,1,0:T(8,128)} %slice.13), channel_id=1, source_target_pairs={{0,2},{2,4},{4,6},{6,7},{7,5},{5,3},{3,1},{1,0},{8,10},{10,12},{12... | collective-permute-start | bytes 589832 | tf_op jit(solution)/shard_map/ppermute | solution.py:35
  51.8 1.6 %collective-permute-start.10 = (f32[16,256]{1,0:T(8,128)S(1)}, f32[16,256]{1,0:T(8,128)S(1)}, u32[]{:S(2)}, u32[]{:S(2)}) collective-permute-start(f32[16,256]{1,0:T(8,128)S(1)} %get-tuple-element.41.refs_4_.refs_7_.refs_9_), channel_id=1, source_target_pairs={{0,16},{8,24},{16,0},{24,8},{1,17},{9,25},{17,1},{25,9},{2,18},{10... | collective-permute-start | bytes 49160 | tf_op jit(solution)/shard_map/ppermute | solution.py:17
  54.5 2.6 %shard_map.106 = (bf16[1,256,256]{2,1,0:T(8,128)(2,1)S(1)}, bf16[1,256,256]{2,1,0:T(8,128)(2,1)S(1)}, bf16[2,256,256]{2,1,0:T(8,128)(2,1)S(1)}, bf16[2,256,256]{...) custom-call(s32[2]{0:T(128)S(1)} %pad_add_fusion.ids_ref, ...), custom_call_target="tpu_custom_call" | custom-call | bytes 5767168 | tf_op jit(solution)/shard_map/pallas_call | solution.py:44
  57.8 0.8 shard_map.108
  58.7 1.2 %collective-permute-done.8.refs_1_ = f32[16,256]{1,0:T(8,128)S(1)} collective-permute-done((f32[16,256]{1,0:T(8,128)S(1)}, f32[16,256]{1,0:T(8,128)S(1)}, u32[]{:S(2)}, u32[]{:S(2)}) %collective-permute-start.8) | collective-permute-done | bytes 16416 | tf_op jit(solution)/shard_map/ppermute | solution.py:17
  60.9 1.0 collective-permute-done.12.refs_1_
  61.9 0.9 shard_map.110
  63.1 1.5 %collective-permute-start.14 = (f32[16,256]{1,0:T(8,128)S(1)}, f32[16,256]{1,0:T(8,128)S(1)}, u32[]{:S(2)}, u32[]{:S(2)}) collective-permute-start(f32[16,256]{1,0:T(8,128)S(1)} %get-tuple-element.49), channel_id=1, source_target_pairs={{0,16},{8,24},{16,0},{24,8},{1,17},{9,25},{17,1},{25,9},{2,18},{10... | collective-permute-start | bytes 49160 | tf_op jit(solution)/shard_map/ppermute | solution.py:17
  64.8 2.1 %shard_map.111 = (bf16[4,256,256]{2,1,0:T(8,128)(2,1)S(1)}, bf16[4,256,256]{2,1,0:T(8,128)(2,1)S(1)}) custom-call(s32[2]{0:T(128)S(1)} %pad_add_fusion.ids_ref, f32[13,32,256]{2,1,0:T(8,128)S(1)} %bitcast.19, f32[13,32,256]{2,1,0:T(8,128)S(1)} %collective-permute-done.refs_0_.refs_1_, f32[13,32,256]{2,1,0:T(8,128)S(1)} %collective-permute-done.1.refs_1_.refs_2_, ...), custom_call_target="tpu_custom_call" | custom-call | bytes 4456448 | tf_op jit(solution)/shard_map/pallas_call | solution.py:44
  66.9 0.8 collective-permute-done.15.refs_3_
  67.7 1.0 shard_map.112.refs_0_
  68.9 1.0 collective-permute-start.17
  70.6 3.0 %collective-permute-done.17.refs_2_ = f32[4,16,256]{2,1,0:T(8,128)S(1)} collective-permute-done((f32[4,16,256]{2,1,0:T(8,128)S(1)}, f32[4,16,256]{2,1,0:T(8,128)S(1)}, u32[]{:S(2)}, u32[]{:S(2)}) %collective-permute-start.17) | collective-permute-done | bytes 65568 | tf_op jit(solution)/shard_map/ppermute | solution.py:17
  74.2 0.8 shard_map.113.refs_0_.refs_2_
  75.3 0.9 collective-permute-start.20
  77.0 2.1 %collective-permute-done.20.refs_2_.refs_4_ = f32[16,256]{1,0:T(8,128)S(1)} collective-permute-done((f32[16,256]{1,0:T(8,128)S(1)}, f32[16,256]{1,0:T(8,128)S(1)}, u32[]{:S(2)}, u32[]{:S(2)}) %collective-permute-start.20) | collective-permute-done | bytes 16416 | tf_op jit(solution)/shard_map/ppermute | solution.py:17
  79.4 0.8 shard_map.114.refs_0_
  80.3 1.1 %collective-permute-done.22.refs_1_ = f32[16,256]{1,0:T(8,128)S(1)} collective-permute-done((f32[16,256]{1,0:T(8,128)S(1)}, f32[16,256]{1,0:T(8,128)S(1)}, u32[]{:S(2)}, u32[]{:S(2)}) %collective-permute-start.22) | collective-permute-done | bytes 16416 | tf_op jit(solution)/shard_map/ppermute | solution.py:17
  82.3 1.0 collective-permute-done.23.refs_1_
  83.3 1.1 %shard_map.116 = f32[8,16,640]{2,1,0:T(8,128)S(1)} custom-call(s32[2]{0:T(128)S(1)} %pad_add_fusion.ids_ref, s32[8,4]{1,0:T(8,128)S(1)} %bitcast.28, f32[16,256]{1,0:T(8,128)S(1)} %shard_map.115.refs_0_, f32[16,256]{1,0:T(8,128)S(1)} %collective-permute-done.23.refs_1_, f32[16,256]{1,0:T(8,128)S(1)} %shard_map.113.refs_0_.refs_2_, ...), custom_call_target="tpu_custom_call" | custom-call | bytes 1245184 | tf_op jit(solution)/shard_map/pallas_call | solution.py:44
  84.4 16.3 %all_to_all.10 = f32[8,16,640]{2,1,0:T(8,128)S(1)} all-to-all(f32[8,16,640]{2,1,0:T(8,128)S(1)} %shard_map.116), channel_id=1, replica_groups=mesh['leaf'=4,'row'=8] {'row'}, dimensions={0} | all-to-all | bytes 655360 | tf_op jit(solution)/shard_map/all_to_all | solution.py:468
  101.5 2.0 %shard_map.117 = (f32[512,128]{1,0:T(8,128)}, f32[3,32,128]{2,1,0:T(8,128)}) custom-call(f32[128,640]{1,0:T(8,128)S(1)} %bitcast.24, f32[128,512]{1,0:T(8,128)S(1)} %copy-done.7, f32[1,512]{1,0:T(1,128)S(1)} %bitcast.29, f32[512,512]{1,0:T(8,128)S(1)} %bitcast.21, f32[512,512]{1,0:T(8,128)S(1)} %bitcast.23), custom_call_target="tpu_custom_call" | custom-call | flops 805306368 | bytes 3000320 | tf_op jit(solution)/shard_map/pallas_call | solution.py:44
  (64 shorter events, 11.7 us)
Async XLA Ops:
  0.6 15.7 %copy-start.9 = (f32[3,32]{1,0:T(4,128)S(1)}, f32[3,32]{1,0:T(4,128)}, u32[]{:S(2)}) copy-start(f32[3,32]{1,0:T(4,128)} %param.15) | copy-start | bytes 1156
  0.6 16.1 %copy-start.10 = (s32[1,1,4]{2,1,0:T(1,128)S(1)}, s32[1,1,4]{2,1,0:T(1,128)}, u32[]{:S(2)}) copy-start(s32[1,1,4]{2,1,0:T(1,128)} %param.13) | copy-start | bytes 52
  0.7 16.4 %copy-start.4 = (f32[1,1,512,128]{3,2,1,0:T(8,128)S(1)}, f32[1,1,512,128]{3,2,1,0:T(8,128)}, u32[]{:S(2)}) copy-start(f32[1,1,512,128]{3,2,1,0:T(8,128)} %param.9) | copy-start | bytes 786436
  1.8 15.2 %copy-start.5 = (f32[3,32,128]{2,1,0:T(8,128)S(1)}, f32[3,32,128]{2,1,0:T(8,128)}, u32[]{:S(2)}) copy-start(f32[3,32,128]{2,1,0:T(8,128)} %window_ref.1) | copy-start | bytes 147460
  1.8 12.9 %collective-permute-start.1 = (f32[13,32,256]{2,1,0:T(8,128)S(1)}, f32[13,32,256]{2,1,0:T(8,128)S(1)}, u32[]{:S(2)}, u32[]{:S(2)}) collective-permute-start(f32[13,32,256]{2,1,0:T(8,128)S(1)} %bitcast.16), channel_id=1, source_target_pairs={{2,0},{4,2},{6,4},{7,6},{5,7},{3,5},{1,3},{0,1},{10,8},{12,10},{14... | collective-permute-start | bytes 1277960 | tf_op jit(solution)/shard_map/ppermute | solution.py:36
  4.8 11.6 %collective-permute-start = (f32[13,32,256]{2,1,0:T(8,128)S(1)}, f32[13,32,256]{2,1,0:T(8,128)S(1)}, u32[]{:S(2)}, u32[]{:S(2)}) collective-permute-start(f32[13,32,256]{2,1,0:T(8,128)S(1)} %bitcast.17), channel_id=1, source_target_pairs={{0,2},{2,4},{4,6},{6,7},{7,5},{5,3},{3,1},{1,0},{8,10},{10,12},{12... | collective-permute-start | bytes 1277960 | tf_op jit(solution)/shard_map/ppermute | solution.py:35
  14.7 16.2 %collective-permute-start.3 = (f32[13,32,256]{2,1,0:T(8,128)S(1)}, f32[13,32,256]{2,1,0:T(8,128)S(1)}, u32[]{:S(2)}, u32[]{:S(2)}) collective-permute-start(f32[13,32,256]{2,1,0:T(8,128)S(1)} %collective-permute-done.1.refs_1_.refs_2_), channel_id=1, source_target_pairs={{2,0},{4,2},{6,4},{7,6},{5,7},{3,5},{1,3},{0,1},{10,8},{12,10},{14... | collective-permute-start | bytes 1277960 | tf_op jit(solution)/shard_map/ppermute | solution.py:36
  16.4 16.4 %collective-permute-start.2 = (f32[13,32,256]{2,1,0:T(8,128)S(1)}, f32[13,32,256]{2,1,0:T(8,128)S(1)}, u32[]{:S(2)}, u32[]{:S(2)}) collective-permute-start(f32[13,32,256]{2,1,0:T(8,128)S(1)} %collective-permute-done.refs_0_.refs_1_), channel_id=1, source_target_pairs={{0,2},{2,4},{4,6},{6,7},{7,5},{5,3},{3,1},{1,0},{8,10},{10,12},{12... | collective-permute-start | bytes 1277960 | tf_op jit(solution)/shard_map/ppermute | solution.py:35
  24.8 26.1 %all-to-all-start = ((f32[8,16,640]{2,1,0:T(8,128)}), f32[8,16,640]{2,1,0:T(8,128)S(1)}, u32[]{:S(2)}, u32[]{:S(2)}) async-start(f32[8,16,640]{2,1,0:T(8,128)} %bitcast.10), calls=%async_computation | async-start | bytes 655360 | tf_op jit(solution)/shard_map/all_to_all | solution.py:237
  30.8 15.3 %collective-permute-start.5 = (f32[13,32,256]{2,1,0:T(8,128)S(1)}, f32[13,32,256]{2,1,0:T(8,128)S(1)}, u32[]{:S(2)}, u32[]{:S(2)}) collective-permute-start(f32[13,32,256]{2,1,0:T(8,128)S(1)} %collective-permute-done.3.refs_4_), channel_id=1, source_target_pairs={{2,0},{4,2},{6,4},{7,6},{5,7},{3,5},{1,3},{0,1},{10,8},{12,10},{14... | collective-permute-start | bytes 1277960 | tf_op jit(solution)/shard_map/ppermute | solution.py:36
  32.9 14.1 %collective-permute-start.4 = (f32[13,32,256]{2,1,0:T(8,128)S(1)}, f32[13,32,256]{2,1,0:T(8,128)S(1)}, u32[]{:S(2)}, u32[]{:S(2)}) collective-permute-start(f32[13,32,256]{2,1,0:T(8,128)S(1)} %collective-permute-done.2.refs_3_), channel_id=1, source_target_pairs={{0,2},{2,4},{4,6},{6,7},{7,5},{5,3},{3,1},{1,0},{8,10},{10,12},{12... | collective-permute-start | bytes 1277960 | tf_op jit(solution)/shard_map/ppermute | solution.py:35
  46.9 7.6 %collective-permute-start.7 = (f32[7,32,256]{2,1,0:T(8,128)}, f32[7,32,256]{2,1,0:T(8,128)S(1)}, u32[]{:S(2)}, u32[]{:S(2)}) collective-permute-start(f32[7,32,256]{2,1,0:T(8,128)} %slice.14), channel_id=1, source_target_pairs={{2,0},{4,2},{6,4},{7,6},{5,7},{3,5},{1,3},{0,1},{10,8},{12,10},{14... | collective-permute-start | bytes 688136 | tf_op jit(solution)/shard_map/ppermute | solution.py:36
  47.6 6.8 %collective-permute-start.6 = (f32[6,32,256]{2,1,0:T(8,128)}, f32[6,32,256]{2,1,0:T(8,128)}, u32[]{:S(2)}, u32[]{:S(2)}) collective-permute-start(f32[6,32,256]{2,1,0:T(8,128)} %slice.13), channel_id=1, source_target_pairs={{0,2},{2,4},{4,6},{6,7},{7,5},{5,3},{3,1},{1,0},{8,10},{10,12},{12... | collective-permute-start | bytes 589832 | tf_op jit(solution)/shard_map/ppermute | solution.py:35
  51.8 6.9 %collective-permute-start.10 = (f32[16,256]{1,0:T(8,128)S(1)}, f32[16,256]{1,0:T(8,128)S(1)}, u32[]{:S(2)}, u32[]{:S(2)}) collective-permute-start(f32[16,256]{1,0:T(8,128)S(1)} %get-tuple-element.41.refs_4_.refs_7_.refs_9_), channel_id=1, source_target_pairs={{0,16},{8,24},{16,0},{24,8},{1,17},{9,25},{17,1},{25,9},{2,18},{10... | collective-permute-start | bytes 49160 | tf_op jit(solution)/shard_map/ppermute | solution.py:17
  53.3 5.3 %collective-permute-start.11 = (f32[16,256]{1,0:T(8,128)S(1)}, f32[16,256]{1,0:T(8,128)S(1)}, u32[]{:S(2)}, u32[]{:S(2)}) collective-permute-start(f32[16,256]{1,0:T(8,128)S(1)} %get-tuple-element.41.refs_4_.refs_7_.refs_9_), channel_id=1, source_target_pairs={{0,24},{8,16},{16,8},{24,0},{1,25},{9,17},{17,9},{25,1},{2,26},{10... | collective-permute-start | bytes 49160 | tf_op jit(solution)/shard_map/ppermute | solution.py:17
  53.3 5.4 %collective-permute-start.9 = (f32[16,256]{1,0:T(8,128)S(1)}, f32[16,256]{1,0:T(8,128)S(1)}, u32[]{:S(2)}, u32[]{:S(2)}) collective-permute-start(f32[16,256]{1,0:T(8,128)S(1)} %get-tuple-element.41.refs_4_.refs_7_.refs_9_), channel_id=1, source_target_pairs={{0,8},{8,0},{16,24},{24,16},{1,9},{9,1},{17,25},{25,17},{2,10},{10... | collective-permute-start | bytes 49160 | tf_op jit(solution)/shard_map/ppermute | solution.py:17
  58.6 1.2 %collective-permute-start.8 = (f32[16,256]{1,0:T(8,128)S(1)}, f32[16,256]{1,0:T(8,128)S(1)}, u32[]{:S(2)}, u32[]{:S(2)}) collective-permute-start(f32[16,256]{1,0:T(8,128)S(1)} %get-tuple-element.38), channel_id=1, source_target_pairs={{0,8},{8,0},{16,24},{24,16},{1,9},{9,1},{17,25},{25,17},{2,10},{10... | collective-permute-start | bytes 49160 | tf_op jit(solution)/shard_map/ppermute | solution.py:17
  60.6 1.2 %collective-permute-start.12 = (f32[16,256]{1,0:T(8,128)S(1)}, f32[16,256]{1,0:T(8,128)S(1)}, u32[]{:S(2)}, u32[]{:S(2)}) collective-permute-start(f32[16,256]{1,0:T(8,128)S(1)} %get-tuple-element.43), channel_id=1, source_target_pairs={{0,8},{8,0},{16,24},{24,16},{1,9},{9,1},{17,25},{25,17},{2,10},{10... | collective-permute-start | bytes 49160 | tf_op jit(solution)/shard_map/ppermute | solution.py:17
  62.8 4.0 %collective-permute-start.13 = (f32[16,256]{1,0:T(8,128)S(1)}, f32[16,256]{1,0:T(8,128)S(1)}, u32[]{:S(2)}, u32[]{:S(2)}) collective-permute-start(f32[16,256]{1,0:T(8,128)S(1)} %get-tuple-element.48), channel_id=1, source_target_pairs={{0,8},{8,0},{16,24},{24,16},{1,9},{9,1},{17,25},{25,17},{2,10},{10... | collective-permute-start | bytes 49160 | tf_op jit(solution)/shard_map/ppermute | solution.py:17
  63.1 3.8 %collective-permute-start.14 = (f32[16,256]{1,0:T(8,128)S(1)}, f32[16,256]{1,0:T(8,128)S(1)}, u32[]{:S(2)}, u32[]{:S(2)}) collective-permute-start(f32[16,256]{1,0:T(8,128)S(1)} %get-tuple-element.49), channel_id=1, source_target_pairs={{0,16},{8,24},{16,0},{24,8},{1,17},{9,25},{17,1},{25,9},{2,18},{10... | collective-permute-start | bytes 49160 | tf_op jit(solution)/shard_map/ppermute | solution.py:17
  64.5 3.2 %collective-permute-start.15 = (f32[16,256]{1,0:T(8,128)S(1)}, f32[16,256]{1,0:T(8,128)S(1)}, u32[]{:S(2)}, u32[]{:S(2)}) collective-permute-start(f32[16,256]{1,0:T(8,128)S(1)} %get-tuple-element.50), channel_id=1, source_target_pairs={{0,24},{8,16},{16,8},{24,0},{1,25},{9,17},{17,9},{25,1},{2,26},{10... | collective-permute-start | bytes 49160 | tf_op jit(solution)/shard_map/ppermute | solution.py:17
  68.7 1.9 %collective-permute-start.16 = (f32[4,16,256]{2,1,0:T(8,128)S(1)}, f32[4,16,256]{2,1,0:T(8,128)S(1)}, u32[]{:S(2)}, u32[]{:S(2)}) collective-permute-start(f32[4,16,256]{2,1,0:T(8,128)S(1)} %shard_map.112.refs_0_), channel_id=1, source_target_pairs={{0,8},{8,0},{16,24},{24,16},{1,9},{9,1},{17,25},{25,17},{2,10},{10... | collective-permute-start | bytes 196616 | tf_op jit(solution)/shard_map/ppermute | solution.py:17
  68.9 4.8 %collective-permute-start.17 = (f32[4,16,256]{2,1,0:T(8,128)S(1)}, f32[4,16,256]{2,1,0:T(8,128)S(1)}, u32[]{:S(2)}, u32[]{:S(2)}) collective-permute-start(f32[4,16,256]{2,1,0:T(8,128)S(1)} %shard_map.112.refs_0_), channel_id=1, source_target_pairs={{0,16},{8,24},{16,0},{24,8},{1,17},{9,25},{17,1},{25,9},{2,18},{10... | collective-permute-start | bytes 196616 | tf_op jit(solution)/shard_map/ppermute | solution.py:17
  69.9 4.4 %collective-permute-start.18 = (f32[4,16,256]{2,1,0:T(8,128)S(1)}, f32[4,16,256]{2,1,0:T(8,128)S(1)}, u32[]{:S(2)}, u32[]{:S(2)}) collective-permute-start(f32[4,16,256]{2,1,0:T(8,128)S(1)} %shard_map.112.refs_0_), channel_id=1, source_target_pairs={{0,24},{8,16},{16,8},{24,0},{1,25},{9,17},{17,9},{25,1},{2,26},{10... | collective-permute-start | bytes 196616 | tf_op jit(solution)/shard_map/ppermute | solution.py:17
  75.1 1.9 %collective-permute-start.19 = (f32[16,256]{1,0:T(8,128)S(1)}, f32[16,256]{1,0:T(8,128)S(1)}, u32[]{:S(2)}, u32[]{:S(2)}) collective-permute-start(f32[16,256]{1,0:T(8,128)S(1)} %shard_map.113.refs_0_.refs_2_), channel_id=1, source_target_pairs={{0,8},{8,0},{16,24},{24,16},{1,9},{9,1},{17,25},{25,17},{2,10},{10... | collective-permute-start | bytes 49160 | tf_op jit(solution)/shard_map/ppermute | solution.py:17
  75.3 3.7 %collective-permute-start.20 = (f32[16,256]{1,0:T(8,128)S(1)}, f32[16,256]{1,0:T(8,128)S(1)}, u32[]{:S(2)}, u32[]{:S(2)}) collective-permute-start(f32[16,256]{1,0:T(8,128)S(1)} %shard_map.113.refs_0_.refs_2_), channel_id=1, source_target_pairs={{0,16},{8,24},{16,0},{24,8},{1,17},{9,25},{17,1},{25,9},{2,18},{10... | collective-permute-start | bytes 49160 | tf_op jit(solution)/shard_map/ppermute | solution.py:17
  76.2 3.2 %collective-permute-start.21 = (f32[16,256]{1,0:T(8,128)S(1)}, f32[16,256]{1,0:T(8,128)S(1)}, u32[]{:S(2)}, u32[]{:S(2)}) collective-permute-start(f32[16,256]{1,0:T(8,128)S(1)} %shard_map.113.refs_0_.refs_2_), channel_id=1, source_target_pairs={{0,24},{8,16},{16,8},{24,0},{1,25},{9,17},{17,9},{25,1},{2,26},{10... | collective-permute-start | bytes 49160 | tf_op jit(solution)/shard_map/ppermute | solution.py:17
  80.2 1.2 %collective-permute-start.22 = (f32[16,256]{1,0:T(8,128)S(1)}, f32[16,256]{1,0:T(8,128)S(1)}, u32[]{:S(2)}, u32[]{:S(2)}) collective-permute-start(f32[16,256]{1,0:T(8,128)S(1)} %shard_map.114.refs_0_), channel_id=1, source_target_pairs={{0,8},{8,0},{16,24},{24,16},{1,9},{9,1},{17,25},{25,17},{2,10},{10... | collective-permute-start | bytes 49160 | tf_op jit(solution)/shard_map/ppermute | solution.py:17
  81.4 19.4 %copy-start.3 = (f32[1,1,512,512]{3,2,1,0:T(8,128)S(1)}, f32[1,1,512,512]{3,2,1,0:T(8,128)}, u32[]{:S(2)}) copy-start(f32[1,1,512,512]{3,2,1,0:T(8,128)} %param.11) | copy-start | bytes 3145732
  82.1 18.6 %copy-start.1 = (f32[1,1,512,512]{3,2,1,0:T(8,128)S(1)}, f32[1,1,512,512]{3,2,1,0:T(8,128)}, u32[]{:S(2)}) copy-start(f32[1,1,512,512]{3,2,1,0:T(8,128)} %param.10) | copy-start | bytes 3145732
  82.1 1.2 %collective-permute-start.23 = (f32[16,256]{1,0:T(8,128)S(1)}, f32[16,256]{1,0:T(8,128)S(1)}, u32[]{:S(2)}, u32[]{:S(2)}) collective-permute-start(f32[16,256]{1,0:T(8,128)S(1)} %shard_map.115.refs_0_), channel_id=1, source_target_pairs={{0,8},{8,0},{16,24},{24,16},{1,9},{9,1},{17,25},{25,17},{2,10},{10... | collective-permute-start | bytes 49160 | tf_op jit(solution)/shard_map/ppermute | solution.py:17
  84.4 16.4 %copy-start.7 = (f32[128,512]{1,0:T(8,128)S(1)}, f32[128,512]{1,0:T(8,128)}, u32[]{:S(2)}) copy-start(f32[128,512]{1,0:T(8,128)} %copy-done.6) | copy-start | bytes 786436
  (4 other events, 3.8 us)

commit v8 on v7

--- a/solution.py
+++ b/solution.py
@@ -8,7 +8,6 @@
 from jax.sharding import PartitionSpec as P
 
 TILE = 128
-EXACT = lax.Precision.HIGHEST
 F32 = jnp.float32
 BF16 = jnp.bfloat16
 
@@ -21,7 +20,7 @@
     return list(range(0, count, 2)) + list(range(count - 1, 0, -2))
 
 
-def ring_gather(block, count):
+def ring_gather(block, count, ahead):
     order = ring_order(count)
     right = [(order[i], order[(i + 1) % count]) for i in range(count)]
     left = [(target, source) for source, target in right]
@@ -34,6 +33,8 @@
             forward, backward, first = forward[:middle], backward[middle:], middle
         forward = lax.ppermute(forward, "row", right)
         backward = lax.ppermute(backward, "row", left)
+        if step == 1:
+            forward, backward, _ = lax.optimization_barrier((forward, backward, ahead))
         parts += [(-step, 0, forward), (step, first, backward)]
     return parts
 
@@ -73,6 +74,15 @@
         return product(first.astype(BF16)) + product(second.astype(BF16))
     both = product(jnp.concatenate([first, second], 0).astype(BF16))
     return both[:rows] + both[rows:]
+
+
+def times_left(block, value):
+    columns = value.shape[1]
+    both = jnp.concatenate(split(value), 1).astype(BF16)
+    product = sum(
+        jnp.dot(part.astype(BF16), both, preferred_element_type=F32) for part in split(block)
+    )
+    return product[:, :columns] + product[:, columns:]
 
 
 def strict_lower(block):
@@ -186,10 +196,6 @@
         )
         return {name: made[2 * i : 2 * i + 2] for i, name in enumerate(names)}
 
-    parts = ring_gather(
-        jnp.concatenate([win_inverse[0], win_coupling[0]], 0).reshape(-1, piece, base), ranks
-    )
-
     start = levels * piece
     beside = start + piece + tiles <= TILE
     number_row, number_lane = (0, start + piece) if beside else (levels, start)
@@ -199,10 +205,7 @@
     aux = jnp.tile(aux, (ranks, 1))
     packed = tiles * TILE + TILE
 
-    firsts = [part for step, _, part in parts if step in (1, -1)]
-
     def local_forward(rhs_ref, window_ref, aux_ref, inverse_any, coupling_any, *refs):
-        refs = refs[len(firsts) :]
         solved_ref, terms_ref, held, inverse_ref, coupling_ref, done = refs
         first = pltpu.make_async_copy(inverse_any, inverse_ref, done.at[0])
         second = pltpu.make_async_copy(coupling_any, coupling_ref, done.at[1])
@@ -214,17 +217,16 @@
             held[level * piece : (level + 1) * piece, :] = window_ref[level]
         terms_ref[:, tiles * TILE :] = held[...].T + aux_ref[...]
         first.wait()
-        strict = strict_lower(inverse_ref[...])
-        solved = rhs + jnp.dot(strict, rhs, precision=EXACT)
+        solved = rhs + times_left(strict_lower(inverse_ref[...]), rhs)
         solved_ref[...] = solved.T
         second.wait()
-        terms_ref[:, : tiles * TILE] = jnp.dot(coupling_ref[...], solved, precision=EXACT).T
+        terms_ref[:, : tiles * TILE] = times_left(coupling_ref[...], solved).T
 
     solved_loc, terms = call(
         local_forward,
         [((columns, local), F32), ((columns, packed), F32)],
-        (loc_rhs[0, 0], win_rhs, aux, loc_inverse[0, 0], loc_coupling[0, 0], *firsts),
-        remote=2 + len(firsts),
+        (loc_rhs[0, 0], win_rhs, aux, loc_inverse[0, 0], loc_coupling[0, 0]),
+        remote=2,
         scratch=[
             pltpu.VMEM((TILE, columns), F32),
             pltpu.VMEM((local, local), F32),
@@ -233,6 +235,11 @@
         ],
         work=24 * local * local * columns,
         room=24,
+    )
+    parts = ring_gather(
+        jnp.concatenate([win_inverse[0], win_coupling[0]], 0).reshape(-1, piece, base),
+        ranks,
+        terms,
     )
     terms = lax.all_to_all(terms.reshape(ranks, share, packed), "row", 0, 0, tiled=True)
     number_lane += tiles * TILE
@@ -320,12 +327,16 @@
     def link(level, chunks):
         span, above = 2**level, 2 ** (level + 1)
         high, low = blocks["B", level]
+        lowest = () if level else blocks["A", 0]
 
         def body(ids_ref, *refs):
-            chunk_refs = refs[:span]
-            high_ref, low_ref, rest_ref, solved_ref = refs[span : span + 4]
-            outs, parts = refs[span + 4 : -1], refs[-1]
+            chunk_refs, refs = refs[:span], refs[span:]
             value = total(chunk_refs)
+            if lowest:
+                value = value + times(value, refs[0][0], refs[1][0], 1)
+                refs = refs[2:]
+            high_ref, low_ref, rest_ref, solved_ref = refs[:4]
+            outs, parts = refs[4:-1], refs[-1]
             solved_ref[...] = value
             for slot in range(above):
                 parts[slot] = rest_ref[slot] - times(value, high_ref[slot], low_ref[slot], 1)
@@ -336,7 +347,7 @@
         made = call(
             body,
             [(wide, F32)] * (above + 1),
-            (*chunks, high, low, rest[level + 1]),
+            (*chunks, *lowest, high, low, rest[level + 1]),
             (ids,),
             [pltpu.VMEM((above, *wide), F32)],
         )
@@ -345,7 +356,8 @@
     chunks = [rest[0]]
     solved = []
     for level in range(top):
-        chunks = leaf_swaps(diagonal(level, chunks, all_pivots if level == 1 else ()))
+        if level:
+            chunks = leaf_swaps(diagonal(level, chunks, all_pivots if level == 1 else ()))
         value, chunks = link(level, chunks)
         solved.append(value)
         chunks = leaf_swaps(chunks)

time: 104 us -> 98.2 us (0.944)
  Pallas kernels: 19.8 us -> 17 us
  waiting for transfers between devices: 34.6 us -> 32.4 us
    ppermute x4, starting transfers between devices: 3.8 us -> 10.8 us  [ring_gather(): forward = lax.ppermute(forward, 'row', right)]
    ppermute x4, starting transfers between devices: 6.72 us -> 0.3 us  [ring_gather(): backward = lax.ppermute(backward, 'row', left)]
    ppermute x4, waiting for transfers between devices: 23 us -> 16.8 us  [ring_gather(): backward = lax.ppermute(backward, 'row', left)]
    ppermute x4, waiting for transfers between devices: 0.49 us -> 4.53 us  [ring_gather(): forward = lax.ppermute(forward, 'row', right)]
    pallas_call x14 -> x13, Pallas kernels: 19.8 us -> 17 us  [call(): pl.pallas_call(body, out_shape=[jax.ShapeDtypeStruct(*o) for o in outs],...]
    all_to_all x1, starting transfers between devices: 6 us -> 4.82 us  [shards(): lax.all_to_all(terms.reshape(ranks, share, packed), 'row', 0, 0, tiled=True)]
  transfers between devices with their start and end apart: 25 -> 25, of which waited for: 12 -> 14; matrix products, arithmetic and copies ran while one was open for 2% -> 2% of each run, Pallas kernels for 11% -> 9%
where the time goes in v8:
time: 98.2 us; the launch traced here: 97.7 us
  waiting for transfers between devices  32.4 us (33%)
  starting transfers between devices  24.2 us (25%)
  Pallas kernels  17 us (17%)
  blocking collectives  16.4 us (17%)
  local copies, waits for them, and re-layouts  5.57 us (6%)
  other arithmetic  1.26 us (1%)
    pallas_call x13, Pallas kernels, call(): pl.pallas_call(body, out_shape=[jax.ShapeDtypeStruct(*o) for o in outs],...  17 us
    ppermute x4, waiting for transfers between devices, ring_gather(): backward = lax.ppermute(backward, 'row', left)  16.8 us
    all_to_all x1, blocking collectives, shards(): lax.all_to_all(replies[0], 'row', 0, 0, tiled=True).reshape(columns, packed)  16.4 us
    ppermute x16, waiting for transfers between devices, swap(): return lax.ppermute(value, axis, [(i, i ^ offset) for i in range(count)])  11.1 us
    ppermute x4, starting transfers between devices, ring_gather(): forward = lax.ppermute(forward, 'row', right)  10.8 us
    ppermute x16, starting transfers between devices, swap(): return lax.ppermute(value, axis, [(i, i ^ offset) for i in range(count)])  8.24 us
    all_to_all x1, starting transfers between devices, shards(): lax.all_to_all(terms.reshape(ranks, share, packed), 'row', 0, 0, tiled=True)  4.82 us
    ppermute x4, waiting for transfers between devices, ring_gather(): forward = lax.ppermute(forward, 'row', right)  4.53 us
  transfers between devices with their start and end apart: 25, of which 14 were waited for; matrix products, arithmetic and copies ran while one was open for 2% of the time, Pallas kernels for 9%

profile of v8, /device:TPU:0, one launch (start us, length us, event | category | flops | bytes accessed | tf_op | source)
XLA Modules:
  0.0 97.7 jit_solution(17993392414413913787)
XLA Ops:
  0.7 1.1 %pad_maximum_fusion = f32[416,256]{1,0:T(8,128)S(1)} fusion(f32[192,256]{1,0:T(8,128)} %bitcast.31, f32[224,256]{1,0:T(8,128)} %bitcast.30), kind=kLoop, calls=%fused_computation | loop fusion | flops 106496 | bytes 851968 | tf_op jit(solution)/shard_map/concatenate | solution.py:240
  1.8 3.1 %collective-permute-start = (f32[13,32,256]{2,1,0:T(8,128)S(1)}, f32[13,32,256]{2,1,0:T(8,128)S(1)}, u32[]{:S(2)}, u32[]{:S(2)}) collective-permute-start(f32[13,32,256]{2,1,0:T(8,128)S(1)} %bitcast.16), channel_id=1, source_target_pairs={{0,2},{2,4},{4,6},{6,7},{7,5},{5,3},{3,1},{1,0},{8,10},{10,12},{12... | collective-permute-start | bytes 1277960 | tf_op jit(solution)/shard_map/ppermute | solution.py:34
  5.2 1.2 %copy-done = f32[1,1,512,512]{3,2,1,0:T(8,128)S(1)} copy-done((f32[1,1,512,512]{3,2,1,0:T(8,128)S(1)}, f32[1,1,512,512]{3,2,1,0:T(8,128)}, u32[]{:S(2)}) %copy-start) | copy-done | bytes 1048600
  6.5 1.2 %copy-done.2 = f32[1,1,512,512]{3,2,1,0:T(8,128)S(1)} copy-done((f32[1,1,512,512]{3,2,1,0:T(8,128)S(1)}, f32[1,1,512,512]{3,2,1,0:T(8,128)}, u32[]{:S(2)}) %copy-start.2) | copy-done | bytes 1048600
  7.7 2.5 %shard_map.104 = (f32[128,512]{1,0:T(8,128)S(1)}, f32[128,640]{1,0:T(8,128)}) custom-call(f32[512,128]{1,0:T(8,128)S(1)} %bitcast.28, f32[3,32,128]{2,1,0:T(8,128)S(1)} %copy-done.5, f32[128,128]{1,0:T(8,128)S(1)} %bitcast.21, f32[512,512]{1,0:T(8,128)S(1)} %bitcast.24, f32[512,512]{1,0:T(8,128)S(1)} %bitcast.26), custom_call_target="tpu_custom_call" | custom-call | flops 805306368 | bytes 3063808 | tf_op jit(solution)/shard_map/pallas_call | solution.py:45
  10.9 3.7 %collective-permute-done.refs_1_ = f32[13,32,256]{2,1,0:T(8,128)S(1)} collective-permute-done((f32[13,32,256]{2,1,0:T(8,128)S(1)}, f32[13,32,256]{2,1,0:T(8,128)S(1)}, u32[]{:S(2)}, u32[]{:S(2)}) %collective-permute-start) | collective-permute-done | bytes 426016 | tf_op jit(solution)/shard_map/ppermute | solution.py:34
  14.6 1.5 %collective-permute-done.1.refs_2_ = f32[13,32,256]{2,1,0:T(8,128)S(1)} collective-permute-done((f32[13,32,256]{2,1,0:T(8,128)S(1)}, f32[13,32,256]{2,1,0:T(8,128)S(1)}, u32[]{:S(2)}, u32[]{:S(2)}) %collective-permute-start.1) | collective-permute-done | bytes 426016 | tf_op jit(solution)/shard_map/ppermute | solution.py:35
  16.4 1.7 %collective-permute-start.2 = (f32[13,32,256]{2,1,0:T(8,128)S(1)}, f32[13,32,256]{2,1,0:T(8,128)S(1)}, u32[]{:S(2)}, u32[]{:S(2)}) collective-permute-start(f32[13,32,256]{2,1,0:T(8,128)S(1)} %collective-permute-done.refs_1_), channel_id=1, source_target_pairs={{0,2},{2,4},{4,6},{6,7},{7,5},{5,3},{3,1},{1,0},{8,10},{10,12},{12... | collective-permute-start | bytes 1277960 | tf_op jit(solution)/shard_map/ppermute | solution.py:34
  18.2 4.8 %all-to-all-start = ((f32[8,16,640]{2,1,0:T(8,128)}), f32[8,16,640]{2,1,0:T(8,128)S(1)}, u32[]{:S(2)}, u32[]{:S(2)}) async-start(f32[8,16,640]{2,1,0:T(8,128)} %bitcast.7), calls=%async_computation | async-start | bytes 655360 | tf_op jit(solution)/shard_map/all_to_all | solution.py:244
  23.0 6.6 %collective-permute-done.3.refs_4_ = f32[13,32,256]{2,1,0:T(8,128)S(1)} collective-permute-done((f32[13,32,256]{2,1,0:T(8,128)S(1)}, f32[13,32,256]{2,1,0:T(8,128)S(1)}, u32[]{:S(2)}, u32[]{:S(2)}) %collective-permute-start.3) | collective-permute-done | bytes 426016 | tf_op jit(solution)/shard_map/ppermute | solution.py:35
  29.6 2.6 %collective-permute-start.4 = (f32[13,32,256]{2,1,0:T(8,128)S(1)}, f32[13,32,256]{2,1,0:T(8,128)S(1)}, u32[]{:S(2)}, u32[]{:S(2)}) collective-permute-start(f32[13,32,256]{2,1,0:T(8,128)S(1)} %collective-permute-done.2.refs_3_), channel_id=1, source_target_pairs={{0,2},{2,4},{4,6},{6,7},{7,5},{5,3},{3,1},{1,0},{8,10},{10,12},{12... | collective-permute-start | bytes 1277960 | tf_op jit(solution)/shard_map/ppermute | solution.py:34
  32.3 8.6 %collective-permute-done.5.refs_6_ = f32[13,32,256]{2,1,0:T(8,128)S(1)} collective-permute-done((f32[13,32,256]{2,1,0:T(8,128)S(1)}, f32[13,32,256]{2,1,0:T(8,128)S(1)}, u32[]{:S(2)}, u32[]{:S(2)}) %collective-permute-start.5) | collective-permute-done | bytes 426016 | tf_op jit(solution)/shard_map/ppermute | solution.py:35
  42.4 3.3 %collective-permute-start.6 = (f32[6,32,256]{2,1,0:T(8,128)}, f32[6,32,256]{2,1,0:T(8,128)}, u32[]{:S(2)}, u32[]{:S(2)}) collective-permute-start(f32[6,32,256]{2,1,0:T(8,128)} %slice.13), channel_id=1, source_target_pairs={{0,2},{2,4},{4,6},{6,7},{7,5},{5,3},{3,1},{1,0},{8,10},{10,12},{12... | collective-permute-start | bytes 589832 | tf_op jit(solution)/shard_map/ppermute | solution.py:34
  46.6 1.6 %collective-permute-start.10 = (f32[16,256]{1,0:T(8,128)S(1)}, f32[16,256]{1,0:T(8,128)S(1)}, u32[]{:S(2)}, u32[]{:S(2)}) collective-permute-start(f32[16,256]{1,0:T(8,128)S(1)} %get-tuple-element.45.refs_4_.refs_7_.refs_9_), channel_id=1, source_target_pairs={{0,16},{8,24},{16,0},{24,8},{1,17},{9,25},{17,1},{25,9},{2,18},{10... | collective-permute-start | bytes 49160 | tf_op jit(solution)/shard_map/ppermute | solution.py:16
  49.3 2.6 %shard_map.106 = (bf16[1,256,256]{2,1,0:T(8,128)(2,1)S(1)}, bf16[1,256,256]{2,1,0:T(8,128)(2,1)S(1)}, bf16[2,256,256]{2,1,0:T(8,128)(2,1)S(1)}, bf16[2,256,256]{...) custom-call(s32[2]{0:T(128)S(1)} %pad_add_fusion.ids_ref, ...), custom_call_target="tpu_custom_call" | custom-call | bytes 5767168 | tf_op jit(solution)/shard_map/pallas_call | solution.py:45
  52.0 0.9 shard_map.107
  53.0 1.2 %collective-permute-done.8.refs_1_ = f32[16,256]{1,0:T(8,128)S(1)} collective-permute-done((f32[16,256]{1,0:T(8,128)S(1)}, f32[16,256]{1,0:T(8,128)S(1)}, u32[]{:S(2)}, u32[]{:S(2)}) %collective-permute-start.8) | collective-permute-done | bytes 16416 | tf_op jit(solution)/shard_map/ppermute | solution.py:16
  55.1 1.0 %collective-permute-done.12.refs_1_ = f32[16,256]{1,0:T(8,128)S(1)} collective-permute-done((f32[16,256]{1,0:T(8,128)S(1)}, f32[16,256]{1,0:T(8,128)S(1)}, u32[]{:S(2)}, u32[]{:S(2)}) %collective-permute-start.12) | collective-permute-done | bytes 16416 | tf_op jit(solution)/shard_map/ppermute | solution.py:16
  56.1 0.9 shard_map.109
  57.3 1.5 %collective-permute-start.14 = (f32[16,256]{1,0:T(8,128)S(1)}, f32[16,256]{1,0:T(8,128)S(1)}, u32[]{:S(2)}, u32[]{:S(2)}) collective-permute-start(f32[16,256]{1,0:T(8,128)S(1)} %get-tuple-element.53), channel_id=1, source_target_pairs={{0,16},{8,24},{16,0},{24,8},{1,17},{9,25},{17,1},{25,9},{2,18},{10... | collective-permute-start | bytes 49160 | tf_op jit(solution)/shard_map/ppermute | solution.py:16
  59.0 2.1 %shard_map.110 = (bf16[4,256,256]{2,1,0:T(8,128)(2,1)S(1)}, bf16[4,256,256]{2,1,0:T(8,128)(2,1)S(1)}) custom-call(s32[2]{0:T(128)S(1)} %pad_add_fusion.ids_ref, f32[13,32,256]{2,1,0:T(8,128)S(1)} %bitcast.19, f32[13,32,256]{2,1,0:T(8,128)S(1)} %collective-permute-done.refs_1_, f32[13,32,256]{2,1,0:T(8,128)S(1)} %collective-permute-done.1.refs_2_, ...), custom_call_target="tpu_custom_call" | custom-call | bytes 4456448 | tf_op jit(solution)/shard_map/pallas_call | solution.py:45
  61.1 0.8 collective-permute-done.15.refs_3_
  62.0 1.0 shard_map.111.refs_0_
  63.1 1.0 %collective-permute-start.17 = (f32[4,16,256]{2,1,0:T(8,128)S(1)}, f32[4,16,256]{2,1,0:T(8,128)S(1)}, u32[]{:S(2)}, u32[]{:S(2)}) collective-permute-start(f32[4,16,256]{2,1,0:T(8,128)S(1)} %shard_map.111.refs_0_), channel_id=1, source_target_pairs={{0,16},{8,24},{16,0},{24,8},{1,17},{9,25},{17,1},{25,9},{2,18},{10... | collective-permute-start | bytes 196616 | tf_op jit(solution)/shard_map/ppermute | solution.py:16
  64.9 3.1 %collective-permute-done.17.refs_2_ = f32[4,16,256]{2,1,0:T(8,128)S(1)} collective-permute-done((f32[4,16,256]{2,1,0:T(8,128)S(1)}, f32[4,16,256]{2,1,0:T(8,128)S(1)}, u32[]{:S(2)}, u32[]{:S(2)}) %collective-permute-start.17) | collective-permute-done | bytes 65568 | tf_op jit(solution)/shard_map/ppermute | solution.py:16
  69.6 0.9 collective-permute-start.20
  71.2 2.1 %collective-permute-done.20.refs_2_.refs_4_ = f32[16,256]{1,0:T(8,128)S(1)} collective-permute-done((f32[16,256]{1,0:T(8,128)S(1)}, f32[16,256]{1,0:T(8,128)S(1)}, u32[]{:S(2)}, u32[]{:S(2)}) %collective-permute-start.20) | collective-permute-done | bytes 16416 | tf_op jit(solution)/shard_map/ppermute | solution.py:16
  74.6 1.1 %collective-permute-done.22.refs_1_ = f32[16,256]{1,0:T(8,128)S(1)} collective-permute-done((f32[16,256]{1,0:T(8,128)S(1)}, f32[16,256]{1,0:T(8,128)S(1)}, u32[]{:S(2)}, u32[]{:S(2)}) %collective-permute-start.22) | collective-permute-done | bytes 16416 | tf_op jit(solution)/shard_map/ppermute | solution.py:16
  76.6 1.0 %collective-permute-done.23.refs_1_ = f32[16,256]{1,0:T(8,128)S(1)} collective-permute-done((f32[16,256]{1,0:T(8,128)S(1)}, f32[16,256]{1,0:T(8,128)S(1)}, u32[]{:S(2)}, u32[]{:S(2)}) %collective-permute-start.23) | collective-permute-done | bytes 16416 | tf_op jit(solution)/shard_map/ppermute | solution.py:16
  77.6 1.1 %shard_map.115 = f32[8,16,640]{2,1,0:T(8,128)S(1)} custom-call(s32[2]{0:T(128)S(1)} %pad_add_fusion.ids_ref, s32[8,4]{1,0:T(8,128)S(1)} %bitcast.23, f32[16,256]{1,0:T(8,128)S(1)} %shard_map.114.refs_0_, f32[16,256]{1,0:T(8,128)S(1)} %collective-permute-done.23.refs_1_, f32[16,256]{1,0:T(8,128)S(1)} %shard_map.112.refs_0_.refs_2_, ...), custom_call_target="tpu_custom_call" | custom-call | bytes 1245184 | tf_op jit(solution)/shard_map/pallas_call | solution.py:45
  78.7 16.4 %all_to_all.10 = f32[8,16,640]{2,1,0:T(8,128)S(1)} all-to-all(f32[8,16,640]{2,1,0:T(8,128)S(1)} %shard_map.115), channel_id=1, replica_groups=mesh['leaf'=4,'row'=8] {'row'}, dimensions={0} | all-to-all | bytes 655360 | tf_op jit(solution)/shard_map/all_to_all | solution.py:480
  95.7 2.0 %shard_map.116 = (f32[512,128]{1,0:T(8,128)}, f32[3,32,128]{2,1,0:T(8,128)}) custom-call(f32[128,640]{1,0:T(8,128)S(1)} %bitcast.20, f32[128,512]{1,0:T(8,128)S(1)} %copy-done.8, f32[1,512]{1,0:T(1,128)S(1)} %bitcast.29, f32[512,512]{1,0:T(8,128)S(1)} %bitcast.25, f32[512,512]{1,0:T(8,128)S(1)} %bitcast.27), custom_call_target="tpu_custom_call" | custom-call | flops 805306368 | bytes 3000320 | tf_op jit(solution)/shard_map/pallas_call | solution.py:45
  (63 shorter events, 12.5 us)
Async XLA Ops:
  0.6 4.2 %copy-start.9 = (f32[3,32]{1,0:T(4,128)S(1)}, f32[3,32]{1,0:T(4,128)}, u32[]{:S(2)}) copy-start(f32[3,32]{1,0:T(4,128)} %param.15) | copy-start | bytes 1156
  0.6 4.3 %copy-start.10 = (s32[1,1,4]{2,1,0:T(1,128)S(1)}, s32[1,1,4]{2,1,0:T(1,128)}, u32[]{:S(2)}) copy-start(s32[1,1,4]{2,1,0:T(1,128)} %param.13) | copy-start | bytes 52
  0.7 4.6 %copy-start.4 = (f32[1,1,512,128]{3,2,1,0:T(8,128)S(1)}, f32[1,1,512,128]{3,2,1,0:T(8,128)}, u32[]{:S(2)}) copy-start(f32[1,1,512,128]{3,2,1,0:T(8,128)} %param.9) | copy-start | bytes 786436
  1.8 3.4 %copy-start.5 = (f32[3,32,128]{2,1,0:T(8,128)S(1)}, f32[3,32,128]{2,1,0:T(8,128)}, u32[]{:S(2)}) copy-start(f32[3,32,128]{2,1,0:T(8,128)} %window_ref.1) | copy-start | bytes 147460
  1.8 12.8 %collective-permute-start = (f32[13,32,256]{2,1,0:T(8,128)S(1)}, f32[13,32,256]{2,1,0:T(8,128)S(1)}, u32[]{:S(2)}, u32[]{:S(2)}) collective-permute-start(f32[13,32,256]{2,1,0:T(8,128)S(1)} %bitcast.16), channel_id=1, source_target_pairs={{0,2},{2,4},{4,6},{6,7},{7,5},{5,3},{3,1},{1,0},{8,10},{10,12},{12... | collective-permute-start | bytes 1277960 | tf_op jit(solution)/shard_map/ppermute | solution.py:34
  4.9 11.3 %collective-permute-start.1 = (f32[13,32,256]{2,1,0:T(8,128)S(1)}, f32[13,32,256]{2,1,0:T(8,128)S(1)}, u32[]{:S(2)}, u32[]{:S(2)}) collective-permute-start(f32[13,32,256]{2,1,0:T(8,128)S(1)} %bitcast.17), channel_id=1, source_target_pairs={{2,0},{4,2},{6,4},{7,6},{5,7},{3,5},{1,3},{0,1},{10,8},{12,10},{14... | collective-permute-start | bytes 1277960 | tf_op jit(solution)/shard_map/ppermute | solution.py:35
  16.1 13.5 %collective-permute-start.3 = (f32[13,32,256]{2,1,0:T(8,128)S(1)}, f32[13,32,256]{2,1,0:T(8,128)S(1)}, u32[]{:S(2)}, u32[]{:S(2)}) collective-permute-start(f32[13,32,256]{2,1,0:T(8,128)S(1)} %collective-permute-done.1.refs_2_), channel_id=1, source_target_pairs={{2,0},{4,2},{6,4},{7,6},{5,7},{3,5},{1,3},{0,1},{10,8},{12,10},{14... | collective-permute-start | bytes 1277960 | tf_op jit(solution)/shard_map/ppermute | solution.py:35
  16.4 13.2 %collective-permute-start.2 = (f32[13,32,256]{2,1,0:T(8,128)S(1)}, f32[13,32,256]{2,1,0:T(8,128)S(1)}, u32[]{:S(2)}, u32[]{:S(2)}) collective-permute-start(f32[13,32,256]{2,1,0:T(8,128)S(1)} %collective-permute-done.refs_1_), channel_id=1, source_target_pairs={{0,2},{2,4},{4,6},{6,7},{7,5},{5,3},{3,1},{1,0},{8,10},{10,12},{12... | collective-permute-start | bytes 1277960 | tf_op jit(solution)/shard_map/ppermute | solution.py:34
  18.2 27.6 %all-to-all-start = ((f32[8,16,640]{2,1,0:T(8,128)}), f32[8,16,640]{2,1,0:T(8,128)S(1)}, u32[]{:S(2)}, u32[]{:S(2)}) async-start(f32[8,16,640]{2,1,0:T(8,128)} %bitcast.7), calls=%async_computation | async-start | bytes 655360 | tf_op jit(solution)/shard_map/all_to_all | solution.py:244
  29.6 11.3 %collective-permute-start.5 = (f32[13,32,256]{2,1,0:T(8,128)S(1)}, f32[13,32,256]{2,1,0:T(8,128)S(1)}, u32[]{:S(2)}, u32[]{:S(2)}) collective-permute-start(f32[13,32,256]{2,1,0:T(8,128)S(1)} %collective-permute-done.3.refs_4_), channel_id=1, source_target_pairs={{2,0},{4,2},{6,4},{7,6},{5,7},{3,5},{1,3},{0,1},{10,8},{12,10},{14... | collective-permute-start | bytes 1277960 | tf_op jit(solution)/shard_map/ppermute | solution.py:35
  29.6 12.1 %collective-permute-start.4 = (f32[13,32,256]{2,1,0:T(8,128)S(1)}, f32[13,32,256]{2,1,0:T(8,128)S(1)}, u32[]{:S(2)}, u32[]{:S(2)}) collective-permute-start(f32[13,32,256]{2,1,0:T(8,128)S(1)} %collective-permute-done.2.refs_3_), channel_id=1, source_target_pairs={{0,2},{2,4},{4,6},{6,7},{7,5},{5,3},{3,1},{1,0},{8,10},{10,12},{12... | collective-permute-start | bytes 1277960 | tf_op jit(solution)/shard_map/ppermute | solution.py:34
  41.6 7.7 %collective-permute-start.7 = (f32[7,32,256]{2,1,0:T(8,128)}, f32[7,32,256]{2,1,0:T(8,128)S(1)}, u32[]{:S(2)}, u32[]{:S(2)}) collective-permute-start(f32[7,32,256]{2,1,0:T(8,128)} %slice.14), channel_id=1, source_target_pairs={{2,0},{4,2},{6,4},{7,6},{5,7},{3,5},{1,3},{0,1},{10,8},{12,10},{14... | collective-permute-start | bytes 688136 | tf_op jit(solution)/shard_map/ppermute | solution.py:35
  42.4 6.9 %collective-permute-start.6 = (f32[6,32,256]{2,1,0:T(8,128)}, f32[6,32,256]{2,1,0:T(8,128)}, u32[]{:S(2)}, u32[]{:S(2)}) collective-permute-start(f32[6,32,256]{2,1,0:T(8,128)} %slice.13), channel_id=1, source_target_pairs={{0,2},{2,4},{4,6},{6,7},{7,5},{5,3},{3,1},{1,0},{8,10},{10,12},{12... | collective-permute-start | bytes 589832 | tf_op jit(solution)/shard_map/ppermute | solution.py:34
  46.6 6.4 %collective-permute-start.9 = (f32[16,256]{1,0:T(8,128)S(1)}, f32[16,256]{1,0:T(8,128)S(1)}, u32[]{:S(2)}, u32[]{:S(2)}) collective-permute-start(f32[16,256]{1,0:T(8,128)S(1)} %get-tuple-element.45.refs_4_.refs_7_.refs_9_), channel_id=1, source_target_pairs={{0,8},{8,0},{16,24},{24,16},{1,9},{9,1},{17,25},{25,17},{2,10},{10... | collective-permute-start | bytes 49160 | tf_op jit(solution)/shard_map/ppermute | solution.py:16
  46.6 6.3 %collective-permute-start.10 = (f32[16,256]{1,0:T(8,128)S(1)}, f32[16,256]{1,0:T(8,128)S(1)}, u32[]{:S(2)}, u32[]{:S(2)}) collective-permute-start(f32[16,256]{1,0:T(8,128)S(1)} %get-tuple-element.45.refs_4_.refs_7_.refs_9_), channel_id=1, source_target_pairs={{0,16},{8,24},{16,0},{24,8},{1,17},{9,25},{17,1},{25,9},{2,18},{10... | collective-permute-start | bytes 49160 | tf_op jit(solution)/shard_map/ppermute | solution.py:16
  48.2 4.7 %collective-permute-start.11 = (f32[16,256]{1,0:T(8,128)S(1)}, f32[16,256]{1,0:T(8,128)S(1)}, u32[]{:S(2)}, u32[]{:S(2)}) collective-permute-start(f32[16,256]{1,0:T(8,128)S(1)} %get-tuple-element.45.refs_4_.refs_7_.refs_9_), channel_id=1, source_target_pairs={{0,24},{8,16},{16,8},{24,0},{1,25},{9,17},{17,9},{25,1},{2,26},{10... | collective-permute-start | bytes 49160 | tf_op jit(solution)/shard_map/ppermute | solution.py:16
  52.9 1.2 %collective-permute-start.8 = (f32[16,256]{1,0:T(8,128)S(1)}, f32[16,256]{1,0:T(8,128)S(1)}, u32[]{:S(2)}, u32[]{:S(2)}) collective-permute-start(f32[16,256]{1,0:T(8,128)S(1)} %get-tuple-element.42), channel_id=1, source_target_pairs={{0,8},{8,0},{16,24},{24,16},{1,9},{9,1},{17,25},{25,17},{2,10},{10... | collective-permute-start | bytes 49160 | tf_op jit(solution)/shard_map/ppermute | solution.py:16
  54.9 1.2 %collective-permute-start.12 = (f32[16,256]{1,0:T(8,128)S(1)}, f32[16,256]{1,0:T(8,128)S(1)}, u32[]{:S(2)}, u32[]{:S(2)}) collective-permute-start(f32[16,256]{1,0:T(8,128)S(1)} %get-tuple-element.47), channel_id=1, source_target_pairs={{0,8},{8,0},{16,24},{24,16},{1,9},{9,1},{17,25},{25,17},{2,10},{10... | collective-permute-start | bytes 49160 | tf_op jit(solution)/shard_map/ppermute | solution.py:16
  57.1 4.0 %collective-permute-start.13 = (f32[16,256]{1,0:T(8,128)S(1)}, f32[16,256]{1,0:T(8,128)S(1)}, u32[]{:S(2)}, u32[]{:S(2)}) collective-permute-start(f32[16,256]{1,0:T(8,128)S(1)} %get-tuple-element.52), channel_id=1, source_target_pairs={{0,8},{8,0},{16,24},{24,16},{1,9},{9,1},{17,25},{25,17},{2,10},{10... | collective-permute-start | bytes 49160 | tf_op jit(solution)/shard_map/ppermute | solution.py:16
  57.3 3.8 %collective-permute-start.14 = (f32[16,256]{1,0:T(8,128)S(1)}, f32[16,256]{1,0:T(8,128)S(1)}, u32[]{:S(2)}, u32[]{:S(2)}) collective-permute-start(f32[16,256]{1,0:T(8,128)S(1)} %get-tuple-element.53), channel_id=1, source_target_pairs={{0,16},{8,24},{16,0},{24,8},{1,17},{9,25},{17,1},{25,9},{2,18},{10... | collective-permute-start | bytes 49160 | tf_op jit(solution)/shard_map/ppermute | solution.py:16
  58.8 3.2 %collective-permute-start.15 = (f32[16,256]{1,0:T(8,128)S(1)}, f32[16,256]{1,0:T(8,128)S(1)}, u32[]{:S(2)}, u32[]{:S(2)}) collective-permute-start(f32[16,256]{1,0:T(8,128)S(1)} %get-tuple-element.54), channel_id=1, source_target_pairs={{0,24},{8,16},{16,8},{24,0},{1,25},{9,17},{17,9},{25,1},{2,26},{10... | collective-permute-start | bytes 49160 | tf_op jit(solution)/shard_map/ppermute | solution.py:16
  62.9 2.0 %collective-permute-start.16 = (f32[4,16,256]{2,1,0:T(8,128)S(1)}, f32[4,16,256]{2,1,0:T(8,128)S(1)}, u32[]{:S(2)}, u32[]{:S(2)}) collective-permute-start(f32[4,16,256]{2,1,0:T(8,128)S(1)} %shard_map.111.refs_0_), channel_id=1, source_target_pairs={{0,8},{8,0},{16,24},{24,16},{1,9},{9,1},{17,25},{25,17},{2,10},{10... | collective-permute-start | bytes 196616 | tf_op jit(solution)/shard_map/ppermute | solution.py:16
  63.1 4.9 %collective-permute-start.17 = (f32[4,16,256]{2,1,0:T(8,128)S(1)}, f32[4,16,256]{2,1,0:T(8,128)S(1)}, u32[]{:S(2)}, u32[]{:S(2)}) collective-permute-start(f32[4,16,256]{2,1,0:T(8,128)S(1)} %shard_map.111.refs_0_), channel_id=1, source_target_pairs={{0,16},{8,24},{16,0},{24,8},{1,17},{9,25},{17,1},{25,9},{2,18},{10... | collective-permute-start | bytes 196616 | tf_op jit(solution)/shard_map/ppermute | solution.py:16
  64.1 4.4 %collective-permute-start.18 = (f32[4,16,256]{2,1,0:T(8,128)S(1)}, f32[4,16,256]{2,1,0:T(8,128)S(1)}, u32[]{:S(2)}, u32[]{:S(2)}) collective-permute-start(f32[4,16,256]{2,1,0:T(8,128)S(1)} %shard_map.111.refs_0_), channel_id=1, source_target_pairs={{0,24},{8,16},{16,8},{24,0},{1,25},{9,17},{17,9},{25,1},{2,26},{10... | collective-permute-start | bytes 196616 | tf_op jit(solution)/shard_map/ppermute | solution.py:16
  69.3 1.9 %collective-permute-start.19 = (f32[16,256]{1,0:T(8,128)S(1)}, f32[16,256]{1,0:T(8,128)S(1)}, u32[]{:S(2)}, u32[]{:S(2)}) collective-permute-start(f32[16,256]{1,0:T(8,128)S(1)} %shard_map.112.refs_0_.refs_2_), channel_id=1, source_target_pairs={{0,8},{8,0},{16,24},{24,16},{1,9},{9,1},{17,25},{25,17},{2,10},{10... | collective-permute-start | bytes 49160 | tf_op jit(solution)/shard_map/ppermute | solution.py:16
  69.6 3.7 %collective-permute-start.20 = (f32[16,256]{1,0:T(8,128)S(1)}, f32[16,256]{1,0:T(8,128)S(1)}, u32[]{:S(2)}, u32[]{:S(2)}) collective-permute-start(f32[16,256]{1,0:T(8,128)S(1)} %shard_map.112.refs_0_.refs_2_), channel_id=1, source_target_pairs={{0,16},{8,24},{16,0},{24,8},{1,17},{9,25},{17,1},{25,9},{2,18},{10... | collective-permute-start | bytes 49160 | tf_op jit(solution)/shard_map/ppermute | solution.py:16
  70.5 3.2 %collective-permute-start.21 = (f32[16,256]{1,0:T(8,128)S(1)}, f32[16,256]{1,0:T(8,128)S(1)}, u32[]{:S(2)}, u32[]{:S(2)}) collective-permute-start(f32[16,256]{1,0:T(8,128)S(1)} %shard_map.112.refs_0_.refs_2_), channel_id=1, source_target_pairs={{0,24},{8,16},{16,8},{24,0},{1,25},{9,17},{17,9},{25,1},{2,26},{10... | collective-permute-start | bytes 49160 | tf_op jit(solution)/shard_map/ppermute | solution.py:16
  74.4 1.2 %collective-permute-start.22 = (f32[16,256]{1,0:T(8,128)S(1)}, f32[16,256]{1,0:T(8,128)S(1)}, u32[]{:S(2)}, u32[]{:S(2)}) collective-permute-start(f32[16,256]{1,0:T(8,128)S(1)} %shard_map.113.refs_0_), channel_id=1, source_target_pairs={{0,8},{8,0},{16,24},{24,16},{1,9},{9,1},{17,25},{25,17},{2,10},{10... | collective-permute-start | bytes 49160 | tf_op jit(solution)/shard_map/ppermute | solution.py:16
  75.6 19.4 %copy-start.3 = (f32[1,1,512,512]{3,2,1,0:T(8,128)S(1)}, f32[1,1,512,512]{3,2,1,0:T(8,128)}, u32[]{:S(2)}) copy-start(f32[1,1,512,512]{3,2,1,0:T(8,128)} %param.11) | copy-start | bytes 3145732
  76.4 18.7 %copy-start.1 = (f32[1,1,512,512]{3,2,1,0:T(8,128)S(1)}, f32[1,1,512,512]{3,2,1,0:T(8,128)}, u32[]{:S(2)}) copy-start(f32[1,1,512,512]{3,2,1,0:T(8,128)} %param.10) | copy-start | bytes 3145732
  76.4 1.2 %collective-permute-start.23 = (f32[16,256]{1,0:T(8,128)S(1)}, f32[16,256]{1,0:T(8,128)S(1)}, u32[]{:S(2)}, u32[]{:S(2)}) collective-permute-start(f32[16,256]{1,0:T(8,128)S(1)} %shard_map.114.refs_0_), channel_id=1, source_target_pairs={{0,8},{8,0},{16,24},{24,16},{1,9},{9,1},{17,25},{25,17},{2,10},{10... | collective-permute-start | bytes 49160 | tf_op jit(solution)/shard_map/ppermute | solution.py:16
  78.7 16.4 %copy-start.8 = (f32[128,512]{1,0:T(8,128)S(1)}, f32[128,512]{1,0:T(8,128)}, u32[]{:S(2)}) copy-start(f32[128,512]{1,0:T(8,128)} %copy-done.7) | copy-start | bytes 786436
  (4 other events, 3.8 us)

commit v9 on v8

--- a/solution.py
+++ b/solution.py
@@ -20,23 +20,28 @@
     return list(range(0, count, 2)) + list(range(count - 1, 0, -2))
 
 
-def ring_gather(block, count, ahead):
+def ring_gather(blocks, count, ahead):
     order = ring_order(count)
     right = [(order[i], order[(i + 1) % count]) for i in range(count)]
     left = [(target, source) for source, target in right]
-    parts = [(0, 0, block)]
-    forward = backward = block
-    middle = block.shape[0] // 2
+    before = (0, blocks[0].shape[0])
+    parts = [(0, before[i], blocks[i]) for i in range(2)]
+    forward, backward = list(blocks), list(blocks)
     for step in range(1, count // 2 + 1):
-        first = 0
-        if 2 * step == count:
-            forward, backward, first = forward[:middle], backward[middle:], middle
-        forward = lax.ppermute(forward, "row", right)
-        backward = lax.ppermute(backward, "row", left)
+        last = 2 * step == count
+        for i in range(2):
+            if not last or i == 0:
+                forward[i] = lax.ppermute(forward[i], "row", right)
+            if not last or i == 1:
+                backward[i] = lax.ppermute(backward[i], "row", left)
         if step == 1:
-            forward, backward, _ = lax.optimization_barrier((forward, backward, ahead))
-        parts += [(-step, 0, forward), (step, first, backward)]
-    return parts
+            forward, backward, ahead = lax.optimization_barrier((forward, backward, ahead))
+        for i in range(2):
+            if not last or i == 0:
+                parts.append((-step, before[i], forward[i]))
+            if not last or i == 1:
+                parts.append((step, before[i], backward[i]))
+    return parts, ahead
 
 
 def call(body, outs, arrays, scalars=(), scratch=(), work=0, remote=0, room=16):
@@ -236,8 +241,8 @@
         work=24 * local * local * columns,
         room=24,
     )
-    parts = ring_gather(
-        jnp.concatenate([win_inverse[0], win_coupling[0]], 0).reshape(-1, piece, base),
+    parts, terms = ring_gather(
+        [win_inverse[0].reshape(-1, piece, base), win_coupling[0].reshape(-1, piece, base)],
         ranks,
         terms,
     )

time: 98.2 us -> 102 us (1.039)
  starting transfers between devices: 24.2 us -> 35.3 us
  waiting for transfers between devices: 32.4 us -> 27 us
  other arithmetic: 1.26 us -> 0.16 us
    ppermute x8 -> x14, starting transfers between devices: 11.1 us -> 21.7 us  [the longest x7 17.8 us: ring_gather(): forward[i] = lax.ppermute(forward[i], 'row', right)]
    ppermute x8 -> x14, waiting for transfers between devices: 21.3 us -> 15.4 us  [the longest x7 12.8 us: ring_gather(): forward[i] = lax.ppermute(forward[i], 'row', right)]
    slice x2 -> x0, local copies, waits for them, and re-layouts: 1.4 us -> none  [ring_gather(): forward, backward, first = (forward[:middle], backward[middle:], middle)]
    concatenate x1 -> x0, other arithmetic: 1.11 us -> none  [shards(): jnp.concatenate([win_inverse[0], win_coupling[0]], 0)]
    unnamed x22 -> x26, local copies, waits for them, and re-layouts: 3.84 us -> 4.8 us
  transfers between devices with their start and end apart: 25 -> 31, of which waited for: 14 -> 17; matrix products, arithmetic and copies ran while one was open for 2% -> 0% of each run, Pallas kernels for 9% -> 8%
where the time goes in v9:
time: 102 us
  starting transfers between devices  35.3 us (35%)
  waiting for transfers between devices  27 us (26%)
  blocking collectives  16.7 us (16%)
  Pallas kernels  16.3 us (16%)
  local copies, waits for them, and re-layouts  5.12 us (5%)
    ppermute x7, starting transfers between devices, ring_gather(): forward[i] = lax.ppermute(forward[i], 'row', right)  17.8 us
    all_to_all x1, blocking collectives, shards(): lax.all_to_all(replies[0], 'row', 0, 0, tiled=True).reshape(columns, packed)  16.7 us
    pallas_call x13, Pallas kernels, call(): pl.pallas_call(body, out_shape=[jax.ShapeDtypeStruct(*o) for o in outs],...  16.3 us
    ppermute x7, waiting for transfers between devices, ring_gather(): forward[i] = lax.ppermute(forward[i], 'row', right)  12.8 us
    ppermute x16, waiting for transfers between devices, swap(): return lax.ppermute(value, axis, [(i, i ^ offset) for i in range(count)])  11.6 us
    ppermute x16, starting transfers between devices, swap(): return lax.ppermute(value, axis, [(i, i ^ offset) for i in range(count)])  8.68 us
    all_to_all x1, starting transfers between devices, shards(): lax.all_to_all(terms.reshape(ranks, share, packed), 'row', 0, 0, tiled=True)  4.97 us
    unnamed x26, local copies, waits for them, and re-layouts  4.8 us
  transfers between devices with their start and end apart: 31, of which 17 were waited for; matrix products, arithmetic and copies ran while one was open for 0% of the time, Pallas kernels for 8%

profile of v9, /device:TPU:0, one launch (start us, length us, event | category | flops | bytes accessed | tf_op | source)
XLA Modules:
  0.0 101.5 jit_solution(12466414592628314027)
XLA Ops:
  0.7 3.1 %collective-permute-start = (f32[7,32,256]{2,1,0:T(8,128)}, f32[7,32,256]{2,1,0:T(8,128)S(1)}, u32[]{:S(2)}, u32[]{:S(2)}) collective-permute-start(f32[7,32,256]{2,1,0:T(8,128)} %bitcast.15), channel_id=1, source_target_pairs={{0,2},{2,4},{4,6},{6,7},{7,5},{5,3},{3,1},{1,0},{8,10},{10,12},{12... | collective-permute-start | bytes 688136 | tf_op jit(solution)/shard_map/ppermute | solution.py:34
  3.7 2.0 %collective-permute-start.1 = (f32[6,32,256]{2,1,0:T(8,128)}, f32[6,32,256]{2,1,0:T(8,128)S(1)}, u32[]{:S(2)}, u32[]{:S(2)}) collective-permute-start(f32[6,32,256]{2,1,0:T(8,128)} %bitcast.19), channel_id=1, source_target_pairs={{0,2},{2,4},{4,6},{6,7},{7,5},{5,3},{3,1},{1,0},{8,10},{10,12},{12... | collective-permute-start | bytes 589832 | tf_op jit(solution)/shard_map/ppermute | solution.py:34
  6.1 1.2 %copy-done.2 = f32[1,1,512,512]{3,2,1,0:T(8,128)S(1)} copy-done((f32[1,1,512,512]{3,2,1,0:T(8,128)S(1)}, f32[1,1,512,512]{3,2,1,0:T(8,128)}, u32[]{:S(2)}) %copy-start.2) | copy-done | bytes 1048600
  7.4 1.2 %copy-done.4 = f32[1,1,512,512]{3,2,1,0:T(8,128)S(1)} copy-done((f32[1,1,512,512]{3,2,1,0:T(8,128)S(1)}, f32[1,1,512,512]{3,2,1,0:T(8,128)}, u32[]{:S(2)}) %copy-start.4) | copy-done | bytes 1048600
  9.5 2.5 %shard_map.104 = (f32[128,512]{1,0:T(8,128)S(1)}, f32[128,640]{1,0:T(8,128)}) custom-call(f32[512,128]{1,0:T(8,128)S(1)} %bitcast.31, f32[3,32,128]{2,1,0:T(8,128)S(1)} %copy-done.7, f32[128,128]{1,0:T(8,128)S(1)} %bitcast.24, f32[512,512]{1,0:T(8,128)S(1)} %bitcast.27, f32[512,512]{1,0:T(8,128)S(1)} %bitcast.29), custom_call_target="tpu_custom_call" | custom-call | flops 805306368 | bytes 3063808 | tf_op jit(solution)/shard_map/pallas_call | solution.py:50
  13.7 1.5 %collective-permute-done.3.refs_5_ = f32[6,32,256]{2,1,0:T(8,128)S(1)} collective-permute-done((f32[6,32,256]{2,1,0:T(8,128)}, f32[6,32,256]{2,1,0:T(8,128)S(1)}, u32[]{:S(2)}, u32[]{:S(2)}) %collective-permute-start.3) | collective-permute-done | bytes 196640 | tf_op jit(solution)/shard_map/ppermute | solution.py:36
  15.2 5.0 %all-to-all-start = ((f32[8,16,640]{2,1,0:T(8,128)}), f32[8,16,640]{2,1,0:T(8,128)S(1)}, u32[]{:S(2)}, u32[]{:S(2)}) async-start(f32[8,16,640]{2,1,0:T(8,128)} %bitcast.9), calls=%async_computation | async-start | bytes 655360 | tf_op jit(solution)/shard_map/all_to_all | solution.py:249
  20.2 2.0 %collective-permute-start.4 = (f32[7,32,256]{2,1,0:T(8,128)S(1)}, f32[7,32,256]{2,1,0:T(8,128)S(1)}, u32[]{:S(2)}, u32[]{:S(2)}) collective-permute-start(f32[7,32,256]{2,1,0:T(8,128)S(1)} %collective-permute-done.refs_2_), channel_id=1, source_target_pairs={{0,2},{2,4},{4,6},{6,7},{7,5},{5,3},{3,1},{1,0},{8,10},{10,12},{12... | collective-permute-start | bytes 688136 | tf_op jit(solution)/shard_map/ppermute | solution.py:34
  22.3 2.0 %collective-permute-start.5 = (f32[7,32,256]{2,1,0:T(8,128)S(1)}, f32[7,32,256]{2,1,0:T(8,128)S(1)}, u32[]{:S(2)}, u32[]{:S(2)}) collective-permute-start(f32[7,32,256]{2,1,0:T(8,128)S(1)} %collective-permute-done.2.refs_3_), channel_id=1, source_target_pairs={{2,0},{4,2},{6,4},{7,6},{5,7},{3,5},{1,3},{0,1},{10,8},{12,10},{14... | collective-permute-start | bytes 688136 | tf_op jit(solution)/shard_map/ppermute | solution.py:36
  24.3 5.1 %collective-permute-done.4.refs_6_ = f32[7,32,256]{2,1,0:T(8,128)S(1)} collective-permute-done((f32[7,32,256]{2,1,0:T(8,128)S(1)}, f32[7,32,256]{2,1,0:T(8,128)S(1)}, u32[]{:S(2)}, u32[]{:S(2)}) %collective-permute-start.4) | collective-permute-done | bytes 229408 | tf_op jit(solution)/shard_map/ppermute | solution.py:34
  29.4 3.2 %collective-permute-start.8 = (f32[7,32,256]{2,1,0:T(8,128)S(1)}, f32[7,32,256]{2,1,0:T(8,128)S(1)}, u32[]{:S(2)}, u32[]{:S(2)}) collective-permute-start(f32[7,32,256]{2,1,0:T(8,128)S(1)} %collective-permute-done.4.refs_6_), channel_id=1, source_target_pairs={{0,2},{2,4},{4,6},{6,7},{7,5},{5,3},{3,1},{1,0},{8,10},{10,12},{12... | collective-permute-start | bytes 688136 | tf_op jit(solution)/shard_map/ppermute | solution.py:34
  32.6 2.5 %collective-permute-start.6 = (f32[6,32,256]{2,1,0:T(8,128)S(1)}, f32[6,32,256]{2,1,0:T(8,128)S(1)}, u32[]{:S(2)}, u32[]{:S(2)}) collective-permute-start(f32[6,32,256]{2,1,0:T(8,128)S(1)} %collective-permute-done.1.refs_4_), channel_id=1, source_target_pairs={{0,2},{2,4},{4,6},{6,7},{7,5},{5,3},{3,1},{1,0},{8,10},{10,12},{12... | collective-permute-start | bytes 589832 | tf_op jit(solution)/shard_map/ppermute | solution.py:34
  35.1 1.1 %collective-permute-done.5.refs_7_ = f32[7,32,256]{2,1,0:T(8,128)S(1)} collective-permute-done((f32[7,32,256]{2,1,0:T(8,128)S(1)}, f32[7,32,256]{2,1,0:T(8,128)S(1)}, u32[]{:S(2)}, u32[]{:S(2)}) %collective-permute-start.5) | collective-permute-done | bytes 229408 | tf_op jit(solution)/shard_map/ppermute | solution.py:36
  36.4 2.3 %collective-permute-done.8.refs_10_ = f32[7,32,256]{2,1,0:T(8,128)S(1)} collective-permute-done((f32[7,32,256]{2,1,0:T(8,128)S(1)}, f32[7,32,256]{2,1,0:T(8,128)S(1)}, u32[]{:S(2)}, u32[]{:S(2)}) %collective-permute-start.8) | collective-permute-done | bytes 229408 | tf_op jit(solution)/shard_map/ppermute | solution.py:34
  38.7 2.5 %collective-permute-start.12 = (f32[7,32,256]{2,1,0:T(8,128)S(1)}, f32[7,32,256]{2,1,0:T(8,128)S(1)}, u32[]{:S(2)}, u32[]{:S(2)}) collective-permute-start(f32[7,32,256]{2,1,0:T(8,128)S(1)} %collective-permute-done.8.refs_10_), channel_id=1, source_target_pairs={{0,2},{2,4},{4,6},{6,7},{7,5},{5,3},{3,1},{1,0},{8,10},{10,12},{12... | collective-permute-start | bytes 688136 | tf_op jit(solution)/shard_map/ppermute | solution.py:34
  41.2 1.7 %collective-permute-done.6.refs_8_ = f32[6,32,256]{2,1,0:T(8,128)S(1)} collective-permute-done((f32[6,32,256]{2,1,0:T(8,128)S(1)}, f32[6,32,256]{2,1,0:T(8,128)S(1)}, u32[]{:S(2)}, u32[]{:S(2)}) %collective-permute-start.6) | collective-permute-done | bytes 196640 | tf_op jit(solution)/shard_map/ppermute | solution.py:34
  42.9 2.5 %collective-permute-start.10 = (f32[6,32,256]{2,1,0:T(8,128)S(1)}, f32[6,32,256]{2,1,0:T(8,128)S(1)}, u32[]{:S(2)}, u32[]{:S(2)}) collective-permute-start(f32[6,32,256]{2,1,0:T(8,128)S(1)} %collective-permute-done.6.refs_8_), channel_id=1, source_target_pairs={{0,2},{2,4},{4,6},{6,7},{7,5},{5,3},{3,1},{1,0},{8,10},{10,12},{12... | collective-permute-start | bytes 589832 | tf_op jit(solution)/shard_map/ppermute | solution.py:34
  45.4 1.7 %collective-permute-start.13 = (f32[6,32,256]{2,1,0:T(8,128)S(1)}, f32[6,32,256]{2,1,0:T(8,128)}, u32[]{:S(2)}, u32[]{:S(2)}) collective-permute-start(f32[6,32,256]{2,1,0:T(8,128)S(1)} %collective-permute-done.11.refs_13_), channel_id=1, source_target_pairs={{2,0},{4,2},{6,4},{7,6},{5,7},{3,5},{1,3},{0,1},{10,8},{12,10},{14... | collective-permute-start | bytes 589832 | tf_op jit(solution)/shard_map/ppermute | solution.py:36
  48.0 2.7 %collective-permute-done.10.refs_12_ = f32[6,32,256]{2,1,0:T(8,128)S(1)} collective-permute-done((f32[6,32,256]{2,1,0:T(8,128)S(1)}, f32[6,32,256]{2,1,0:T(8,128)S(1)}, u32[]{:S(2)}, u32[]{:S(2)}) %collective-permute-start.10) | collective-permute-done | bytes 196640 | tf_op jit(solution)/shard_map/ppermute | solution.py:34
  50.7 1.5 %collective-permute-start.16 = (f32[16,256]{1,0:T(8,128)S(1)}, f32[16,256]{1,0:T(8,128)S(1)}, u32[]{:S(2)}, u32[]{:S(2)}) collective-permute-start(f32[16,256]{1,0:T(8,128)S(1)} %get-tuple-element.51.refs_4_.refs_7_.refs_9_), channel_id=1, source_target_pairs={{0,16},{8,24},{16,0},{24,8},{1,17},{9,25},{17,1},{25,9},{2,18},{10... | collective-permute-start | bytes 49160 | tf_op jit(solution)/shard_map/ppermute | solution.py:16
  52.2 2.8 %shard_map.106 = (bf16[1,256,256]{2,1,0:T(8,128)(2,1)S(1)}, bf16[1,256,256]{2,1,0:T(8,128)(2,1)S(1)}, bf16[2,256,256]{2,1,0:T(8,128)(2,1)S(1)}, bf16[2,256,256]{...) custom-call(s32[2]{0:T(128)S(1)} %pad_add_fusion.ids_ref, ...), custom_call_target="tpu_custom_call" | custom-call | bytes 5767168 | tf_op jit(solution)/shard_map/pallas_call | solution.py:50
  60.8 1.5 %collective-permute-start.20 = (f32[16,256]{1,0:T(8,128)S(1)}, f32[16,256]{1,0:T(8,128)S(1)}, u32[]{:S(2)}, u32[]{:S(2)}) collective-permute-start(f32[16,256]{1,0:T(8,128)S(1)} %get-tuple-element.59), channel_id=1, source_target_pairs={{0,16},{8,24},{16,0},{24,8},{1,17},{9,25},{17,1},{25,9},{2,18},{10... | collective-permute-start | bytes 49160 | tf_op jit(solution)/shard_map/ppermute | solution.py:16
  62.4 1.3 %shard_map.110 = (bf16[4,256,256]{2,1,0:T(8,128)(2,1)S(1)}, bf16[4,256,256]{2,1,0:T(8,128)(2,1)S(1)}) custom-call(s32[2]{0:T(128)S(1)} %pad_add_fusion.ids_ref, f32[7,32,256]{2,1,0:T(8,128)S(1)} %bitcast.18, f32[6,32,256]{2,1,0:T(8,128)S(1)} %bitcast.22, f32[7,32,256]{2,1,0:T(8,128)S(1)} %collective-permute-done.refs_2_, ...), custom_call_target="tpu_custom_call" | custom-call | bytes 4456448 | tf_op jit(solution)/shard_map/pallas_call | solution.py:50
  64.6 1.0 %collective-permute-done.21.refs_3_ = f32[16,256]{1,0:T(8,128)S(1)} collective-permute-done((f32[16,256]{1,0:T(8,128)S(1)}, f32[16,256]{1,0:T(8,128)S(1)}, u32[]{:S(2)}, u32[]{:S(2)}) %collective-permute-start.21) | collective-permute-done | bytes 16416 | tf_op jit(solution)/shard_map/ppermute | solution.py:16
  67.3 1.1 %collective-permute-start.24 = (f32[4,16,256]{2,1,0:T(8,128)S(1)}, f32[4,16,256]{2,1,0:T(8,128)S(1)}, u32[]{:S(2)}, u32[]{:S(2)}) collective-permute-start(f32[4,16,256]{2,1,0:T(8,128)S(1)} %shard_map.111.refs_0_), channel_id=1, source_target_pairs={{0,24},{8,16},{16,8},{24,0},{1,25},{9,17},{17,9},{25,1},{2,26},{10... | collective-permute-start | bytes 196616 | tf_op jit(solution)/shard_map/ppermute | solution.py:16
  68.5 3.2 %collective-permute-done.23.refs_2_ = f32[4,16,256]{2,1,0:T(8,128)S(1)} collective-permute-done((f32[4,16,256]{2,1,0:T(8,128)S(1)}, f32[4,16,256]{2,1,0:T(8,128)S(1)}, u32[]{:S(2)}, u32[]{:S(2)}) %collective-permute-start.23) | collective-permute-done | bytes 65568 | tf_op jit(solution)/shard_map/ppermute | solution.py:16
  74.7 2.3 %collective-permute-done.26.refs_2_.refs_4_ = f32[16,256]{1,0:T(8,128)S(1)} collective-permute-done((f32[16,256]{1,0:T(8,128)S(1)}, f32[16,256]{1,0:T(8,128)S(1)}, u32[]{:S(2)}, u32[]{:S(2)}) %collective-permute-start.26) | collective-permute-done | bytes 16416 | tf_op jit(solution)/shard_map/ppermute | solution.py:16
  78.1 1.1 %collective-permute-done.28.refs_1_ = f32[16,256]{1,0:T(8,128)S(1)} collective-permute-done((f32[16,256]{1,0:T(8,128)S(1)}, f32[16,256]{1,0:T(8,128)S(1)}, u32[]{:S(2)}, u32[]{:S(2)}) %collective-permute-start.28) | collective-permute-done | bytes 16416 | tf_op jit(solution)/shard_map/ppermute | solution.py:16
  80.0 1.0 %collective-permute-done.29.refs_1_ = f32[16,256]{1,0:T(8,128)S(1)} collective-permute-done((f32[16,256]{1,0:T(8,128)S(1)}, f32[16,256]{1,0:T(8,128)S(1)}, u32[]{:S(2)}, u32[]{:S(2)}) %collective-permute-start.29) | collective-permute-done | bytes 16416 | tf_op jit(solution)/shard_map/ppermute | solution.py:16
  81.1 1.1 %shard_map.115 = f32[8,16,640]{2,1,0:T(8,128)S(1)} custom-call(s32[2]{0:T(128)S(1)} %pad_add_fusion.ids_ref, s32[8,4]{1,0:T(8,128)S(1)} %bitcast.26, f32[16,256]{1,0:T(8,128)S(1)} %shard_map.114.refs_0_, f32[16,256]{1,0:T(8,128)S(1)} %collective-permute-done.29.refs_1_, f32[16,256]{1,0:T(8,128)S(1)} %shard_map.112.refs_0_.refs_2_, ...), custom_call_target="tpu_custom_call" | custom-call | bytes 1245184 | tf_op jit(solution)/shard_map/pallas_call | solution.py:50
  82.1 16.7 %all_to_all.10 = f32[8,16,640]{2,1,0:T(8,128)S(1)} all-to-all(f32[8,16,640]{2,1,0:T(8,128)S(1)} %shard_map.115), channel_id=1, replica_groups=mesh['leaf'=4,'row'=8] {'row'}, dimensions={0} | all-to-all | bytes 655360 | tf_op jit(solution)/shard_map/all_to_all | solution.py:485
  99.5 2.0 %shard_map.116 = (f32[512,128]{1,0:T(8,128)}, f32[3,32,128]{2,1,0:T(8,128)}) custom-call(f32[128,640]{1,0:T(8,128)S(1)} %bitcast.23, f32[128,512]{1,0:T(8,128)S(1)} %copy-done.10, f32[1,512]{1,0:T(1,128)S(1)} %bitcast.32, f32[512,512]{1,0:T(8,128)S(1)} %bitcast.28, f32[512,512]{1,0:T(8,128)S(1)} %bitcast.30), custom_call_target="tpu_custom_call" | custom-call | flops 805306368 | bytes 3000320 | tf_op jit(solution)/shard_map/pallas_call | solution.py:50
  (76 shorter events, 18.4 us)
Async XLA Ops:
  0.7 14.6 %collective-permute-start = (f32[7,32,256]{2,1,0:T(8,128)}, f32[7,32,256]{2,1,0:T(8,128)S(1)}, u32[]{:S(2)}, u32[]{:S(2)}) collective-permute-start(f32[7,32,256]{2,1,0:T(8,128)} %bitcast.15), channel_id=1, source_target_pairs={{0,2},{2,4},{4,6},{6,7},{7,5},{5,3},{3,1},{1,0},{8,10},{10,12},{12... | collective-permute-start | bytes 688136 | tf_op jit(solution)/shard_map/ppermute | solution.py:34
  3.7 11.5 %collective-permute-start.2 = (f32[7,32,256]{2,1,0:T(8,128)}, f32[7,32,256]{2,1,0:T(8,128)S(1)}, u32[]{:S(2)}, u32[]{:S(2)}) collective-permute-start(f32[7,32,256]{2,1,0:T(8,128)} %bitcast.16), channel_id=1, source_target_pairs={{2,0},{4,2},{6,4},{7,6},{5,7},{3,5},{1,3},{0,1},{10,8},{12,10},{14... | collective-permute-start | bytes 688136 | tf_op jit(solution)/shard_map/ppermute | solution.py:36
  3.7 10.0 %collective-permute-start.1 = (f32[6,32,256]{2,1,0:T(8,128)}, f32[6,32,256]{2,1,0:T(8,128)S(1)}, u32[]{:S(2)}, u32[]{:S(2)}) collective-permute-start(f32[6,32,256]{2,1,0:T(8,128)} %bitcast.19), channel_id=1, source_target_pairs={{0,2},{2,4},{4,6},{6,7},{7,5},{5,3},{3,1},{1,0},{8,10},{10,12},{12... | collective-permute-start | bytes 589832 | tf_op jit(solution)/shard_map/ppermute | solution.py:34
  5.8 9.5 %collective-permute-start.3 = (f32[6,32,256]{2,1,0:T(8,128)}, f32[6,32,256]{2,1,0:T(8,128)S(1)}, u32[]{:S(2)}, u32[]{:S(2)}) collective-permute-start(f32[6,32,256]{2,1,0:T(8,128)} %bitcast.20), channel_id=1, source_target_pairs={{2,0},{4,2},{6,4},{7,6},{5,7},{3,5},{1,3},{0,1},{10,8},{12,10},{14... | collective-permute-start | bytes 589832 | tf_op jit(solution)/shard_map/ppermute | solution.py:36
  15.2 37.0 %copy-start.1 = (f32[1,192,256]{2,1,0:T(8,128)S(1)}, f32[1,192,256]{2,1,0:T(8,128)}, u32[]{:S(2)}) copy-start(f32[1,192,256]{2,1,0:T(8,128)} %param.17) | copy-start | bytes 589828
  15.2 31.8 %all-to-all-start = ((f32[8,16,640]{2,1,0:T(8,128)}), f32[8,16,640]{2,1,0:T(8,128)S(1)}, u32[]{:S(2)}, u32[]{:S(2)}) async-start(f32[8,16,640]{2,1,0:T(8,128)} %bitcast.9), calls=%async_computation | async-start | bytes 655360 | tf_op jit(solution)/shard_map/all_to_all | solution.py:249
  20.2 9.2 %collective-permute-start.4 = (f32[7,32,256]{2,1,0:T(8,128)S(1)}, f32[7,32,256]{2,1,0:T(8,128)S(1)}, u32[]{:S(2)}, u32[]{:S(2)}) collective-permute-start(f32[7,32,256]{2,1,0:T(8,128)S(1)} %collective-permute-done.refs_2_), channel_id=1, source_target_pairs={{0,2},{2,4},{4,6},{6,7},{7,5},{5,3},{3,1},{1,0},{8,10},{10,12},{12... | collective-permute-start | bytes 688136 | tf_op jit(solution)/shard_map/ppermute | solution.py:34
  22.2 12.9 %collective-permute-start.7 = (f32[6,32,256]{2,1,0:T(8,128)S(1)}, f32[6,32,256]{2,1,0:T(8,128)S(1)}, u32[]{:S(2)}, u32[]{:S(2)}) collective-permute-start(f32[6,32,256]{2,1,0:T(8,128)S(1)} %collective-permute-done.3.refs_5_), channel_id=1, source_target_pairs={{2,0},{4,2},{6,4},{7,6},{5,7},{3,5},{1,3},{0,1},{10,8},{12,10},{14... | collective-permute-start | bytes 589832 | tf_op jit(solution)/shard_map/ppermute | solution.py:36
  22.3 13.9 %collective-permute-start.5 = (f32[7,32,256]{2,1,0:T(8,128)S(1)}, f32[7,32,256]{2,1,0:T(8,128)S(1)}, u32[]{:S(2)}, u32[]{:S(2)}) collective-permute-start(f32[7,32,256]{2,1,0:T(8,128)S(1)} %collective-permute-done.2.refs_3_), channel_id=1, source_target_pairs={{2,0},{4,2},{6,4},{7,6},{5,7},{3,5},{1,3},{0,1},{10,8},{12,10},{14... | collective-permute-start | bytes 688136 | tf_op jit(solution)/shard_map/ppermute | solution.py:36
  29.4 9.3 %collective-permute-start.8 = (f32[7,32,256]{2,1,0:T(8,128)S(1)}, f32[7,32,256]{2,1,0:T(8,128)S(1)}, u32[]{:S(2)}, u32[]{:S(2)}) collective-permute-start(f32[7,32,256]{2,1,0:T(8,128)S(1)} %collective-permute-done.4.refs_6_), channel_id=1, source_target_pairs={{0,2},{2,4},{4,6},{6,7},{7,5},{5,3},{3,1},{1,0},{8,10},{10,12},{12... | collective-permute-start | bytes 688136 | tf_op jit(solution)/shard_map/ppermute | solution.py:34
  32.6 10.3 %collective-permute-start.6 = (f32[6,32,256]{2,1,0:T(8,128)S(1)}, f32[6,32,256]{2,1,0:T(8,128)S(1)}, u32[]{:S(2)}, u32[]{:S(2)}) collective-permute-start(f32[6,32,256]{2,1,0:T(8,128)S(1)} %collective-permute-done.1.refs_4_), channel_id=1, source_target_pairs={{0,2},{2,4},{4,6},{6,7},{7,5},{5,3},{3,1},{1,0},{8,10},{10,12},{12... | collective-permute-start | bytes 589832 | tf_op jit(solution)/shard_map/ppermute | solution.py:34
  35.1 10.3 %collective-permute-start.11 = (f32[6,32,256]{2,1,0:T(8,128)S(1)}, f32[6,32,256]{2,1,0:T(8,128)S(1)}, u32[]{:S(2)}, u32[]{:S(2)}) collective-permute-start(f32[6,32,256]{2,1,0:T(8,128)S(1)} %collective-permute-done.7.refs_9_), channel_id=1, source_target_pairs={{2,0},{4,2},{6,4},{7,6},{5,7},{3,5},{1,3},{0,1},{10,8},{12,10},{14... | collective-permute-start | bytes 589832 | tf_op jit(solution)/shard_map/ppermute | solution.py:36
  36.2 16.0 %collective-permute-start.9 = (f32[7,32,256]{2,1,0:T(8,128)S(1)}, f32[7,32,256]{2,1,0:T(8,128)S(1)}, u32[]{:S(2)}, u32[]{:S(2)}) collective-permute-start(f32[7,32,256]{2,1,0:T(8,128)S(1)} %collective-permute-done.5.refs_7_), channel_id=1, source_target_pairs={{2,0},{4,2},{6,4},{7,6},{5,7},{3,5},{1,3},{0,1},{10,8},{12,10},{14... | collective-permute-start | bytes 688136 | tf_op jit(solution)/shard_map/ppermute | solution.py:36
  38.7 13.5 %collective-permute-start.12 = (f32[7,32,256]{2,1,0:T(8,128)S(1)}, f32[7,32,256]{2,1,0:T(8,128)S(1)}, u32[]{:S(2)}, u32[]{:S(2)}) collective-permute-start(f32[7,32,256]{2,1,0:T(8,128)S(1)} %collective-permute-done.8.refs_10_), channel_id=1, source_target_pairs={{0,2},{2,4},{4,6},{6,7},{7,5},{5,3},{3,1},{1,0},{8,10},{10,12},{12... | collective-permute-start | bytes 688136 | tf_op jit(solution)/shard_map/ppermute | solution.py:34
  42.9 7.8 %collective-permute-start.10 = (f32[6,32,256]{2,1,0:T(8,128)S(1)}, f32[6,32,256]{2,1,0:T(8,128)S(1)}, u32[]{:S(2)}, u32[]{:S(2)}) collective-permute-start(f32[6,32,256]{2,1,0:T(8,128)S(1)} %collective-permute-done.6.refs_8_), channel_id=1, source_target_pairs={{0,2},{2,4},{4,6},{6,7},{7,5},{5,3},{3,1},{1,0},{8,10},{10,12},{12... | collective-permute-start | bytes 589832 | tf_op jit(solution)/shard_map/ppermute | solution.py:34
  45.4 6.8 %collective-permute-start.13 = (f32[6,32,256]{2,1,0:T(8,128)S(1)}, f32[6,32,256]{2,1,0:T(8,128)}, u32[]{:S(2)}, u32[]{:S(2)}) collective-permute-start(f32[6,32,256]{2,1,0:T(8,128)S(1)} %collective-permute-done.11.refs_13_), channel_id=1, source_target_pairs={{2,0},{4,2},{6,4},{7,6},{5,7},{3,5},{1,3},{0,1},{10,8},{12,10},{14... | collective-permute-start | bytes 589832 | tf_op jit(solution)/shard_map/ppermute | solution.py:36
  47.9 8.7 %collective-permute-start.15 = (f32[16,256]{1,0:T(8,128)S(1)}, f32[16,256]{1,0:T(8,128)S(1)}, u32[]{:S(2)}, u32[]{:S(2)}) collective-permute-start(f32[16,256]{1,0:T(8,128)S(1)} %get-tuple-element.51.refs_4_.refs_7_.refs_9_), channel_id=1, source_target_pairs={{0,8},{8,0},{16,24},{24,16},{1,9},{9,1},{17,25},{25,17},{2,10},{10... | collective-permute-start | bytes 49160 | tf_op jit(solution)/shard_map/ppermute | solution.py:16
  50.7 5.9 %collective-permute-start.16 = (f32[16,256]{1,0:T(8,128)S(1)}, f32[16,256]{1,0:T(8,128)S(1)}, u32[]{:S(2)}, u32[]{:S(2)}) collective-permute-start(f32[16,256]{1,0:T(8,128)S(1)} %get-tuple-element.51.refs_4_.refs_7_.refs_9_), channel_id=1, source_target_pairs={{0,16},{8,24},{16,0},{24,8},{1,17},{9,25},{17,1},{25,9},{2,18},{10... | collective-permute-start | bytes 49160 | tf_op jit(solution)/shard_map/ppermute | solution.py:16
  52.2 4.4 %collective-permute-start.17 = (f32[16,256]{1,0:T(8,128)S(1)}, f32[16,256]{1,0:T(8,128)S(1)}, u32[]{:S(2)}, u32[]{:S(2)}) collective-permute-start(f32[16,256]{1,0:T(8,128)S(1)} %get-tuple-element.51.refs_4_.refs_7_.refs_9_), channel_id=1, source_target_pairs={{0,24},{8,16},{16,8},{24,0},{1,25},{9,17},{17,9},{25,1},{2,26},{10... | collective-permute-start | bytes 49160 | tf_op jit(solution)/shard_map/ppermute | solution.py:16
  55.9 1.5 %collective-permute-start.14 = (f32[16,256]{1,0:T(8,128)S(1)}, f32[16,256]{1,0:T(8,128)S(1)}, u32[]{:S(2)}, u32[]{:S(2)}) collective-permute-start(f32[16,256]{1,0:T(8,128)S(1)} %get-tuple-element.48), channel_id=1, source_target_pairs={{0,8},{8,0},{16,24},{24,16},{1,9},{9,1},{17,25},{25,17},{2,10},{10... | collective-permute-start | bytes 49160 | tf_op jit(solution)/shard_map/ppermute | solution.py:16
  58.2 1.2 %collective-permute-start.18 = (f32[16,256]{1,0:T(8,128)S(1)}, f32[16,256]{1,0:T(8,128)S(1)}, u32[]{:S(2)}, u32[]{:S(2)}) collective-permute-start(f32[16,256]{1,0:T(8,128)S(1)} %get-tuple-element.53), channel_id=1, source_target_pairs={{0,8},{8,0},{16,24},{24,16},{1,9},{9,1},{17,25},{25,17},{2,10},{10... | collective-permute-start | bytes 49160 | tf_op jit(solution)/shard_map/ppermute | solution.py:16
  60.4 3.2 %collective-permute-start.19 = (f32[16,256]{1,0:T(8,128)S(1)}, f32[16,256]{1,0:T(8,128)S(1)}, u32[]{:S(2)}, u32[]{:S(2)}) collective-permute-start(f32[16,256]{1,0:T(8,128)S(1)} %get-tuple-element.58), channel_id=1, source_target_pairs={{0,8},{8,0},{16,24},{24,16},{1,9},{9,1},{17,25},{25,17},{2,10},{10... | collective-permute-start | bytes 49160 | tf_op jit(solution)/shard_map/ppermute | solution.py:16
  60.8 3.7 %collective-permute-start.20 = (f32[16,256]{1,0:T(8,128)S(1)}, f32[16,256]{1,0:T(8,128)S(1)}, u32[]{:S(2)}, u32[]{:S(2)}) collective-permute-start(f32[16,256]{1,0:T(8,128)S(1)} %get-tuple-element.59), channel_id=1, source_target_pairs={{0,16},{8,24},{16,0},{24,8},{1,17},{9,25},{17,1},{25,9},{2,18},{10... | collective-permute-start | bytes 49160 | tf_op jit(solution)/shard_map/ppermute | solution.py:16
  62.3 3.3 %collective-permute-start.21 = (f32[16,256]{1,0:T(8,128)S(1)}, f32[16,256]{1,0:T(8,128)S(1)}, u32[]{:S(2)}, u32[]{:S(2)}) collective-permute-start(f32[16,256]{1,0:T(8,128)S(1)} %get-tuple-element.60), channel_id=1, source_target_pairs={{0,24},{8,16},{16,8},{24,0},{1,25},{9,17},{17,9},{25,1},{2,26},{10... | collective-permute-start | bytes 49160 | tf_op jit(solution)/shard_map/ppermute | solution.py:16
  66.6 1.9 %collective-permute-start.22 = (f32[4,16,256]{2,1,0:T(8,128)S(1)}, f32[4,16,256]{2,1,0:T(8,128)S(1)}, u32[]{:S(2)}, u32[]{:S(2)}) collective-permute-start(f32[4,16,256]{2,1,0:T(8,128)S(1)} %shard_map.111.refs_0_), channel_id=1, source_target_pairs={{0,8},{8,0},{16,24},{24,16},{1,9},{9,1},{17,25},{25,17},{2,10},{10... | collective-permute-start | bytes 196616 | tf_op jit(solution)/shard_map/ppermute | solution.py:16
  66.7 4.9 %collective-permute-start.23 = (f32[4,16,256]{2,1,0:T(8,128)S(1)}, f32[4,16,256]{2,1,0:T(8,128)S(1)}, u32[]{:S(2)}, u32[]{:S(2)}) collective-permute-start(f32[4,16,256]{2,1,0:T(8,128)S(1)} %shard_map.111.refs_0_), channel_id=1, source_target_pairs={{0,16},{8,24},{16,0},{24,8},{1,17},{9,25},{17,1},{25,9},{2,18},{10... | collective-permute-start | bytes 196616 | tf_op jit(solution)/shard_map/ppermute | solution.py:16
  67.3 4.6 %collective-permute-start.24 = (f32[4,16,256]{2,1,0:T(8,128)S(1)}, f32[4,16,256]{2,1,0:T(8,128)S(1)}, u32[]{:S(2)}, u32[]{:S(2)}) collective-permute-start(f32[4,16,256]{2,1,0:T(8,128)S(1)} %shard_map.111.refs_0_), channel_id=1, source_target_pairs={{0,24},{8,16},{16,8},{24,0},{1,25},{9,17},{17,9},{25,1},{2,26},{10... | collective-permute-start | bytes 196616 | tf_op jit(solution)/shard_map/ppermute | solution.py:16
  72.8 1.9 %collective-permute-start.25 = (f32[16,256]{1,0:T(8,128)S(1)}, f32[16,256]{1,0:T(8,128)S(1)}, u32[]{:S(2)}, u32[]{:S(2)}) collective-permute-start(f32[16,256]{1,0:T(8,128)S(1)} %shard_map.112.refs_0_.refs_2_), channel_id=1, source_target_pairs={{0,8},{8,0},{16,24},{24,16},{1,9},{9,1},{17,25},{25,17},{2,10},{10... | collective-permute-start | bytes 49160 | tf_op jit(solution)/shard_map/ppermute | solution.py:16
  73.2 3.8 %collective-permute-start.26 = (f32[16,256]{1,0:T(8,128)S(1)}, f32[16,256]{1,0:T(8,128)S(1)}, u32[]{:S(2)}, u32[]{:S(2)}) collective-permute-start(f32[16,256]{1,0:T(8,128)S(1)} %shard_map.112.refs_0_.refs_2_), channel_id=1, source_target_pairs={{0,16},{8,24},{16,0},{24,8},{1,17},{9,25},{17,1},{25,9},{2,18},{10... | collective-permute-start | bytes 49160 | tf_op jit(solution)/shard_map/ppermute | solution.py:16
  73.9 3.2 %collective-permute-start.27 = (f32[16,256]{1,0:T(8,128)S(1)}, f32[16,256]{1,0:T(8,128)S(1)}, u32[]{:S(2)}, u32[]{:S(2)}) collective-permute-start(f32[16,256]{1,0:T(8,128)S(1)} %shard_map.112.refs_0_.refs_2_), channel_id=1, source_target_pairs={{0,24},{8,16},{16,8},{24,0},{1,25},{9,17},{17,9},{25,1},{2,26},{10... | collective-permute-start | bytes 49160 | tf_op jit(solution)/shard_map/ppermute | solution.py:16
  77.9 1.2 %collective-permute-start.28 = (f32[16,256]{1,0:T(8,128)S(1)}, f32[16,256]{1,0:T(8,128)S(1)}, u32[]{:S(2)}, u32[]{:S(2)}) collective-permute-start(f32[16,256]{1,0:T(8,128)S(1)} %shard_map.113.refs_0_), channel_id=1, source_target_pairs={{0,8},{8,0},{16,24},{24,16},{1,9},{9,1},{17,25},{25,17},{2,10},{10... | collective-permute-start | bytes 49160 | tf_op jit(solution)/shard_map/ppermute | solution.py:16
  79.9 1.2 %collective-permute-start.29 = (f32[16,256]{1,0:T(8,128)S(1)}, f32[16,256]{1,0:T(8,128)S(1)}, u32[]{:S(2)}, u32[]{:S(2)}) collective-permute-start(f32[16,256]{1,0:T(8,128)S(1)} %shard_map.114.refs_0_), channel_id=1, source_target_pairs={{0,8},{8,0},{16,24},{24,16},{1,9},{9,1},{17,25},{25,17},{2,10},{10... | collective-permute-start | bytes 49160 | tf_op jit(solution)/shard_map/ppermute | solution.py:16
  (12 other events, 108.1 us)

commit v10 on v8

--- a/solution.py
+++ b/solution.py
@@ -245,9 +245,10 @@
     number_lane += tiles * TILE
     known = terms[:, number_row, number_lane : number_lane + tiles].astype(jnp.int32)
 
-    lower = assemble([name for name in all_names if name != ("A", top)])
-    upper = assemble([("A", top)])
-    blocks = {**lower, **upper}
+    blocks = assemble([("A", 0), ("B", 0)])
+    for name in all_names:
+        if name not in blocks:
+            blocks.update(assemble([name]))
 
     def scatter(ids_ref, known_ref, terms_ref, *refs):
         outs, pivots_ref, path = refs[:-2], refs[-2], refs[-1]

time: 98.2 us -> 97.5 us (level)
  waiting for transfers between devices: 32.4 us -> 30.4 us
    ppermute x16, waiting for transfers between devices: 11.1 us -> 9.93 us  [swap(): return lax.ppermute(value, axis, [(i, i ^ offset) for i in range(count)])]
    pallas_call x13 -> x15, Pallas kernels: 17 us -> 17.9 us  [call(): pl.pallas_call(body, out_shape=[jax.ShapeDtypeStruct(*o) for o in outs],...]
  transfers between devices with their start and end apart: 25 -> 25, of which waited for: 14 -> 12; matrix products, arithmetic and copies ran while one was open for 2% -> 3% of each run, Pallas kernels for 9% -> 10%
where the time goes in v10:
time: 97.5 us; the launch traced here: 97 us
  waiting for transfers between devices  30.4 us (31%)
  starting transfers between devices  24.5 us (25%)
  Pallas kernels  17.9 us (18%)
  blocking collectives  15.7 us (16%)
  local copies, waits for them, and re-layouts  5.58 us (6%)
  other arithmetic  2.02 us (2%)
    pallas_call x15, Pallas kernels, call(): pl.pallas_call(body, out_shape=[jax.ShapeDtypeStruct(*o) for o in outs],...  17.9 us
    ppermute x4, waiting for transfers between devices, ring_gather(): backward = lax.ppermute(backward, 'row', left)  16.8 us
    all_to_all x1, blocking collectives, shards(): lax.all_to_all(replies[0], 'row', 0, 0, tiled=True).reshape(columns, packed)  15.7 us
    ppermute x4, starting transfers between devices, ring_gather(): forward = lax.ppermute(forward, 'row', right)  10.8 us
    ppermute x16, waiting for transfers between devices, swap(): return lax.ppermute(value, axis, [(i, i ^ offset) for i in range(count)])  9.93 us
    ppermute x16, starting transfers between devices, swap(): return lax.ppermute(value, axis, [(i, i ^ offset) for i in range(count)])  8.58 us
    all_to_all x1, starting transfers between devices, shards(): lax.all_to_all(terms.reshape(ranks, share, packed), 'row', 0, 0, tiled=True)  4.82 us
    unnamed x22, local copies, waits for them, and re-layouts  3.84 us
  transfers between devices with their start and end apart: 25, of which 12 were waited for; matrix products, arithmetic and copies ran while one was open for 3% of the time, Pallas kernels for 10%

profile of v10, /device:TPU:0, one launch (start us, length us, event | category | flops | bytes accessed | tf_op | source)
XLA Modules:
  0.0 97.0 jit_solution(4608118374343666234)
XLA Ops:
  0.7 1.1 %pad_maximum_fusion = f32[416,256]{1,0:T(8,128)S(1)} fusion(f32[192,256]{1,0:T(8,128)} %bitcast.33, f32[224,256]{1,0:T(8,128)} %bitcast.32), kind=kLoop, calls=%fused_computation | loop fusion | flops 106496 | bytes 851968 | tf_op jit(solution)/shard_map/concatenate | solution.py:240
  1.8 3.1 %collective-permute-start = (f32[13,32,256]{2,1,0:T(8,128)S(1)}, f32[13,32,256]{2,1,0:T(8,128)S(1)}, u32[]{:S(2)}, u32[]{:S(2)}) collective-permute-start(f32[13,32,256]{2,1,0:T(8,128)S(1)} %bitcast.16), channel_id=1, source_target_pairs={{0,2},{2,4},{4,6},{6,7},{7,5},{5,3},{3,1},{1,0},{8,10},{10,12},{12... | collective-permute-start | bytes 1277960 | tf_op jit(solution)/shard_map/ppermute | solution.py:34
  5.2 1.2 %copy-done = f32[1,1,512,512]{3,2,1,0:T(8,128)S(1)} copy-done((f32[1,1,512,512]{3,2,1,0:T(8,128)S(1)}, f32[1,1,512,512]{3,2,1,0:T(8,128)}, u32[]{:S(2)}) %copy-start) | copy-done | bytes 1048600
  6.5 1.2 %copy-done.2 = f32[1,1,512,512]{3,2,1,0:T(8,128)S(1)} copy-done((f32[1,1,512,512]{3,2,1,0:T(8,128)S(1)}, f32[1,1,512,512]{3,2,1,0:T(8,128)}, u32[]{:S(2)}) %copy-start.2) | copy-done | bytes 1048600
  7.7 2.5 %shard_map.104 = (f32[128,512]{1,0:T(8,128)S(1)}, f32[128,640]{1,0:T(8,128)}) custom-call(f32[512,128]{1,0:T(8,128)S(1)} %bitcast.30, f32[3,32,128]{2,1,0:T(8,128)S(1)} %copy-done.5, f32[128,128]{1,0:T(8,128)S(1)} %bitcast.23, f32[512,512]{1,0:T(8,128)S(1)} %bitcast.26, f32[512,512]{1,0:T(8,128)S(1)} %bitcast.28), custom_call_target="tpu_custom_call" | custom-call | flops 805306368 | bytes 3063808 | tf_op jit(solution)/shard_map/pallas_call | solution.py:45
  10.9 3.7 %collective-permute-done.refs_1_ = f32[13,32,256]{2,1,0:T(8,128)S(1)} collective-permute-done((f32[13,32,256]{2,1,0:T(8,128)S(1)}, f32[13,32,256]{2,1,0:T(8,128)S(1)}, u32[]{:S(2)}, u32[]{:S(2)}) %collective-permute-start) | collective-permute-done | bytes 426016 | tf_op jit(solution)/shard_map/ppermute | solution.py:34
  14.6 1.5 %collective-permute-done.1.refs_2_ = f32[13,32,256]{2,1,0:T(8,128)S(1)} collective-permute-done((f32[13,32,256]{2,1,0:T(8,128)S(1)}, f32[13,32,256]{2,1,0:T(8,128)S(1)}, u32[]{:S(2)}, u32[]{:S(2)}) %collective-permute-start.1) | collective-permute-done | bytes 426016 | tf_op jit(solution)/shard_map/ppermute | solution.py:35
  16.4 1.7 %collective-permute-start.2 = (f32[13,32,256]{2,1,0:T(8,128)S(1)}, f32[13,32,256]{2,1,0:T(8,128)S(1)}, u32[]{:S(2)}, u32[]{:S(2)}) collective-permute-start(f32[13,32,256]{2,1,0:T(8,128)S(1)} %collective-permute-done.refs_1_), channel_id=1, source_target_pairs={{0,2},{2,4},{4,6},{6,7},{7,5},{5,3},{3,1},{1,0},{8,10},{10,12},{12... | collective-permute-start | bytes 1277960 | tf_op jit(solution)/shard_map/ppermute | solution.py:34
  18.2 4.8 %all-to-all-start = ((f32[8,16,640]{2,1,0:T(8,128)}), f32[8,16,640]{2,1,0:T(8,128)}, u32[]{:S(2)}, u32[]{:S(2)}) async-start(f32[8,16,640]{2,1,0:T(8,128)} %bitcast.7), calls=%async_computation | async-start | bytes 655360 | tf_op jit(solution)/shard_map/all_to_all | solution.py:244
  23.0 6.6 %collective-permute-done.3.refs_4_ = f32[13,32,256]{2,1,0:T(8,128)S(1)} collective-permute-done((f32[13,32,256]{2,1,0:T(8,128)S(1)}, f32[13,32,256]{2,1,0:T(8,128)S(1)}, u32[]{:S(2)}, u32[]{:S(2)}) %collective-permute-start.3) | collective-permute-done | bytes 426016 | tf_op jit(solution)/shard_map/ppermute | solution.py:35
  29.6 2.6 %collective-permute-start.4 = (f32[13,32,256]{2,1,0:T(8,128)S(1)}, f32[13,32,256]{2,1,0:T(8,128)S(1)}, u32[]{:S(2)}, u32[]{:S(2)}) collective-permute-start(f32[13,32,256]{2,1,0:T(8,128)S(1)} %collective-permute-done.2.refs_3_), channel_id=1, source_target_pairs={{0,2},{2,4},{4,6},{6,7},{7,5},{5,3},{3,1},{1,0},{8,10},{10,12},{12... | collective-permute-start | bytes 1277960 | tf_op jit(solution)/shard_map/ppermute | solution.py:34
  32.3 8.6 %collective-permute-done.5.refs_6_ = f32[13,32,256]{2,1,0:T(8,128)S(1)} collective-permute-done((f32[13,32,256]{2,1,0:T(8,128)S(1)}, f32[13,32,256]{2,1,0:T(8,128)S(1)}, u32[]{:S(2)}, u32[]{:S(2)}) %collective-permute-start.5) | collective-permute-done | bytes 426016 | tf_op jit(solution)/shard_map/ppermute | solution.py:35
  42.4 3.3 %collective-permute-start.6 = (f32[6,32,256]{2,1,0:T(8,128)}, f32[6,32,256]{2,1,0:T(8,128)S(1)}, u32[]{:S(2)}, u32[]{:S(2)}) collective-permute-start(f32[6,32,256]{2,1,0:T(8,128)} %slice.13), channel_id=1, source_target_pairs={{0,2},{2,4},{4,6},{6,7},{7,5},{5,3},{3,1},{1,0},{8,10},{10,12},{12... | collective-permute-start | bytes 589832 | tf_op jit(solution)/shard_map/ppermute | solution.py:34
  46.6 1.1 %shard_map.105 = (f32[1,16,256]{2,1,0:T(8,128)S(1)}, f32[2,16,256]{2,1,0:T(8,128)S(1)}, f32[4,16,256]{2,1,0:T(8,128)S(1)}, f32[16,256]{1,0:T(8,128)S(1)}) custom-call(s32[2]{0:T(128)S(1)} %pad_add_fusion.ids_ref, s32[8,4]{1,0:T(8,128)S(1)} %bitcast.24, f32[8,16,640]{2,1,0:T(8,128)} %all-to-all-done.terms_ref), custom_call_target="tpu_custom_call" | custom-call | bytes 458752 | tf_op jit(solution)/shard_map/pallas_call | solution.py:45
  47.8 1.6 %collective-permute-start.10 = (f32[16,256]{1,0:T(8,128)S(1)}, f32[16,256]{1,0:T(8,128)S(1)}, u32[]{:S(2)}, u32[]{:S(2)}) collective-permute-start(f32[16,256]{1,0:T(8,128)S(1)} %get-tuple-element.45.refs_4_.refs_7_.refs_9_), channel_id=1, source_target_pairs={{0,16},{8,24},{16,0},{24,8},{1,17},{9,25},{17,1},{25,9},{2,18},{10... | collective-permute-start | bytes 49160 | tf_op jit(solution)/shard_map/ppermute | solution.py:16
  49.7 1.6 %shard_map.106 = (bf16[1,256,256]{2,1,0:T(8,128)(2,1)S(1)}, bf16[1,256,256]{2,1,0:T(8,128)(2,1)S(1)}, bf16[2,256,256]{2,1,0:T(8,128)(2,1)S(1)}, bf16[2,256,256]{2,1,0:T(8,128)(2,1)S(1)}) custom-call(s32[2]{0:T(128)S(1)} %pad_add_fusion.ids_ref, f32[13,32,256]{2,1,0:T(8,128)S(1)} %bitcast.18, f32[13,32,256]{2,1,0:T(8,128)S(1)} %collective-permute-done.refs_1_, ...), custom_call_target="tpu_custom_call" | custom-call | bytes 4194304 | tf_op jit(solution)/shard_map/pallas_call | solution.py:45
  51.2 0.9 shard_map.107
  52.5 1.1 %shard_map.108 = (bf16[2,256,256]{2,1,0:T(8,128)(2,1)S(1)}, bf16[2,256,256]{2,1,0:T(8,128)(2,1)S(1)}) custom-call(s32[2]{0:T(128)S(1)} %pad_add_fusion.ids_ref, f32[13,32,256]{2,1,0:T(8,128)S(1)} %bitcast.19, f32[13,32,256]{2,1,0:T(8,128)S(1)} %collective-permute-done.refs_1_, f32[13,32,256]{2,1,0:T(8,128)S(1)} %collective-permute-done.1.refs_2_, ...), custom_call_target="tpu_custom_call" | custom-call | bytes 3932160 | tf_op jit(solution)/shard_map/pallas_call | solution.py:45
  54.7 1.2 %shard_map.110 = (bf16[4,256,256]{2,1,0:T(8,128)(2,1)S(1)}, bf16[4,256,256]{2,1,0:T(8,128)(2,1)S(1)}) custom-call(s32[2]{0:T(128)S(1)} %pad_add_fusion.ids_ref, f32[13,32,256]{2,1,0:T(8,128)S(1)} %bitcast.20, f32[13,32,256]{2,1,0:T(8,128)S(1)} %collective-permute-done.refs_1_, f32[13,32,256]{2,1,0:T(8,128)S(1)} %collective-permute-done.1.refs_2_, ...), custom_call_target="tpu_custom_call" | custom-call | bytes 4456448 | tf_op jit(solution)/shard_map/pallas_call | solution.py:45
  55.9 0.9 shard_map.111
  57.3 1.5 %collective-permute-start.14 = (f32[16,256]{1,0:T(8,128)S(1)}, f32[16,256]{1,0:T(8,128)S(1)}, u32[]{:S(2)}, u32[]{:S(2)}) collective-permute-start(f32[16,256]{1,0:T(8,128)S(1)} %get-tuple-element.53), channel_id=1, source_target_pairs={{0,16},{8,24},{16,0},{24,8},{1,17},{9,25},{17,1},{25,9},{2,18},{10... | collective-permute-start | bytes 49160 | tf_op jit(solution)/shard_map/ppermute | solution.py:16
  58.8 1.3 %shard_map.112 = (bf16[4,256,256]{2,1,0:T(8,128)(2,1)S(1)}, bf16[4,256,256]{2,1,0:T(8,128)(2,1)S(1)}) custom-call(s32[2]{0:T(128)S(1)} %pad_add_fusion.ids_ref, f32[13,32,256]{2,1,0:T(8,128)S(1)} %bitcast.21, f32[13,32,256]{2,1,0:T(8,128)S(1)} %collective-permute-done.refs_1_, f32[13,32,256]{2,1,0:T(8,128)S(1)} %collective-permute-done.1.refs_2_, ...), custom_call_target="tpu_custom_call" | custom-call | bytes 4456448 | tf_op jit(solution)/shard_map/pallas_call | solution.py:45
  61.0 1.0 %collective-permute-done.15.refs_3_ = f32[16,256]{1,0:T(8,128)S(1)} collective-permute-done((f32[16,256]{1,0:T(8,128)S(1)}, f32[16,256]{1,0:T(8,128)S(1)}, u32[]{:S(2)}, u32[]{:S(2)}) %collective-permute-start.15) | collective-permute-done | bytes 16416 | tf_op jit(solution)/shard_map/ppermute | solution.py:16
  62.1 1.0 shard_map.113.refs_0_
  63.8 1.1 %collective-permute-start.18 = (f32[4,16,256]{2,1,0:T(8,128)S(1)}, f32[4,16,256]{2,1,0:T(8,128)S(1)}, u32[]{:S(2)}, u32[]{:S(2)}) collective-permute-start(f32[4,16,256]{2,1,0:T(8,128)S(1)} %shard_map.113.refs_0_), channel_id=1, source_target_pairs={{0,24},{8,16},{16,8},{24,0},{1,25},{9,17},{17,9},{25,1},{2,26},{10... | collective-permute-start | bytes 196616 | tf_op jit(solution)/shard_map/ppermute | solution.py:16
  65.0 3.2 %collective-permute-done.17.refs_2_ = f32[4,16,256]{2,1,0:T(8,128)S(1)} collective-permute-done((f32[4,16,256]{2,1,0:T(8,128)S(1)}, f32[4,16,256]{2,1,0:T(8,128)S(1)}, u32[]{:S(2)}, u32[]{:S(2)}) %collective-permute-start.17) | collective-permute-done | bytes 65568 | tf_op jit(solution)/shard_map/ppermute | solution.py:16
  71.2 2.3 %collective-permute-done.20.refs_2_.refs_4_ = f32[16,256]{1,0:T(8,128)S(1)} collective-permute-done((f32[16,256]{1,0:T(8,128)S(1)}, f32[16,256]{1,0:T(8,128)S(1)}, u32[]{:S(2)}, u32[]{:S(2)}) %collective-permute-start.20) | collective-permute-done | bytes 16416 | tf_op jit(solution)/shard_map/ppermute | solution.py:16
  74.5 1.1 %collective-permute-done.22.refs_1_ = f32[16,256]{1,0:T(8,128)S(1)} collective-permute-done((f32[16,256]{1,0:T(8,128)S(1)}, f32[16,256]{1,0:T(8,128)S(1)}, u32[]{:S(2)}, u32[]{:S(2)}) %collective-permute-start.22) | collective-permute-done | bytes 16416 | tf_op jit(solution)/shard_map/ppermute | solution.py:16
  76.5 1.0 %collective-permute-done.23.refs_1_ = f32[16,256]{1,0:T(8,128)S(1)} collective-permute-done((f32[16,256]{1,0:T(8,128)S(1)}, f32[16,256]{1,0:T(8,128)S(1)}, u32[]{:S(2)}, u32[]{:S(2)}) %collective-permute-start.23) | collective-permute-done | bytes 16416 | tf_op jit(solution)/shard_map/ppermute | solution.py:16
  77.5 1.1 %shard_map.117 = f32[8,16,640]{2,1,0:T(8,128)S(1)} custom-call(s32[2]{0:T(128)S(1)} %pad_add_fusion.ids_ref, s32[8,4]{1,0:T(8,128)S(1)} %bitcast.25, f32[16,256]{1,0:T(8,128)S(1)} %shard_map.116.refs_0_, f32[16,256]{1,0:T(8,128)S(1)} %collective-permute-done.23.refs_1_, f32[16,256]{1,0:T(8,128)S(1)} %shard_map.114.refs_0_.refs_2_, ...), custom_call_target="tpu_custom_call" | custom-call | bytes 1245184 | tf_op jit(solution)/shard_map/pallas_call | solution.py:45
  78.6 15.7 %all_to_all.10 = f32[8,16,640]{2,1,0:T(8,128)S(1)} all-to-all(f32[8,16,640]{2,1,0:T(8,128)S(1)} %shard_map.117), channel_id=1, replica_groups=mesh['leaf'=4,'row'=8] {'row'}, dimensions={0} | all-to-all | bytes 655360 | tf_op jit(solution)/shard_map/all_to_all | solution.py:481
  95.0 2.0 %shard_map.118 = (f32[512,128]{1,0:T(8,128)}, f32[3,32,128]{2,1,0:T(8,128)}) custom-call(f32[128,640]{1,0:T(8,128)S(1)} %bitcast.22, f32[128,512]{1,0:T(8,128)S(1)} %copy-done.8, f32[1,512]{1,0:T(1,128)S(1)} %bitcast.31, f32[512,512]{1,0:T(8,128)S(1)} %bitcast.27, f32[512,512]{1,0:T(8,128)S(1)} %bitcast.29), custom_call_target="tpu_custom_call" | custom-call | flops 805306368 | bytes 3000320 | tf_op jit(solution)/shard_map/pallas_call | solution.py:45
  (65 shorter events, 13.3 us)
Async XLA Ops:
  0.6 4.2 %copy-start.9 = (f32[3,32]{1,0:T(4,128)S(1)}, f32[3,32]{1,0:T(4,128)}, u32[]{:S(2)}) copy-start(f32[3,32]{1,0:T(4,128)} %param.15) | copy-start | bytes 1156
  0.6 4.3 %copy-start.10 = (s32[1,1,4]{2,1,0:T(1,128)S(1)}, s32[1,1,4]{2,1,0:T(1,128)}, u32[]{:S(2)}) copy-start(s32[1,1,4]{2,1,0:T(1,128)} %param.13) | copy-start | bytes 52
  0.7 4.6 %copy-start.4 = (f32[1,1,512,128]{3,2,1,0:T(8,128)S(1)}, f32[1,1,512,128]{3,2,1,0:T(8,128)}, u32[]{:S(2)}) copy-start(f32[1,1,512,128]{3,2,1,0:T(8,128)} %param.9) | copy-start | bytes 786436
  1.8 3.4 %copy-start.5 = (f32[3,32,128]{2,1,0:T(8,128)S(1)}, f32[3,32,128]{2,1,0:T(8,128)}, u32[]{:S(2)}) copy-start(f32[3,32,128]{2,1,0:T(8,128)} %window_ref.1) | copy-start | bytes 147460
  1.8 12.8 %collective-permute-start = (f32[13,32,256]{2,1,0:T(8,128)S(1)}, f32[13,32,256]{2,1,0:T(8,128)S(1)}, u32[]{:S(2)}, u32[]{:S(2)}) collective-permute-start(f32[13,32,256]{2,1,0:T(8,128)S(1)} %bitcast.16), channel_id=1, source_target_pairs={{0,2},{2,4},{4,6},{6,7},{7,5},{5,3},{3,1},{1,0},{8,10},{10,12},{12... | collective-permute-start | bytes 1277960 | tf_op jit(solution)/shard_map/ppermute | solution.py:34
  4.9 11.3 %collective-permute-start.1 = (f32[13,32,256]{2,1,0:T(8,128)S(1)}, f32[13,32,256]{2,1,0:T(8,128)S(1)}, u32[]{:S(2)}, u32[]{:S(2)}) collective-permute-start(f32[13,32,256]{2,1,0:T(8,128)S(1)} %bitcast.17), channel_id=1, source_target_pairs={{2,0},{4,2},{6,4},{7,6},{5,7},{3,5},{1,3},{0,1},{10,8},{12,10},{14... | collective-permute-start | bytes 1277960 | tf_op jit(solution)/shard_map/ppermute | solution.py:35
  16.1 13.5 %collective-permute-start.3 = (f32[13,32,256]{2,1,0:T(8,128)S(1)}, f32[13,32,256]{2,1,0:T(8,128)S(1)}, u32[]{:S(2)}, u32[]{:S(2)}) collective-permute-start(f32[13,32,256]{2,1,0:T(8,128)S(1)} %collective-permute-done.1.refs_2_), channel_id=1, source_target_pairs={{2,0},{4,2},{6,4},{7,6},{5,7},{3,5},{1,3},{0,1},{10,8},{12,10},{14... | collective-permute-start | bytes 1277960 | tf_op jit(solution)/shard_map/ppermute | solution.py:35
  16.4 13.2 %collective-permute-start.2 = (f32[13,32,256]{2,1,0:T(8,128)S(1)}, f32[13,32,256]{2,1,0:T(8,128)S(1)}, u32[]{:S(2)}, u32[]{:S(2)}) collective-permute-start(f32[13,32,256]{2,1,0:T(8,128)S(1)} %collective-permute-done.refs_1_), channel_id=1, source_target_pairs={{0,2},{2,4},{4,6},{6,7},{7,5},{5,3},{3,1},{1,0},{8,10},{10,12},{12... | collective-permute-start | bytes 1277960 | tf_op jit(solution)/shard_map/ppermute | solution.py:34
  18.2 27.6 %all-to-all-start = ((f32[8,16,640]{2,1,0:T(8,128)}), f32[8,16,640]{2,1,0:T(8,128)}, u32[]{:S(2)}, u32[]{:S(2)}) async-start(f32[8,16,640]{2,1,0:T(8,128)} %bitcast.7), calls=%async_computation | async-start | bytes 655360 | tf_op jit(solution)/shard_map/all_to_all | solution.py:244
  29.6 11.3 %collective-permute-start.5 = (f32[13,32,256]{2,1,0:T(8,128)S(1)}, f32[13,32,256]{2,1,0:T(8,128)S(1)}, u32[]{:S(2)}, u32[]{:S(2)}) collective-permute-start(f32[13,32,256]{2,1,0:T(8,128)S(1)} %collective-permute-done.3.refs_4_), channel_id=1, source_target_pairs={{2,0},{4,2},{6,4},{7,6},{5,7},{3,5},{1,3},{0,1},{10,8},{12,10},{14... | collective-permute-start | bytes 1277960 | tf_op jit(solution)/shard_map/ppermute | solution.py:35
  29.6 12.1 %collective-permute-start.4 = (f32[13,32,256]{2,1,0:T(8,128)S(1)}, f32[13,32,256]{2,1,0:T(8,128)S(1)}, u32[]{:S(2)}, u32[]{:S(2)}) collective-permute-start(f32[13,32,256]{2,1,0:T(8,128)S(1)} %collective-permute-done.2.refs_3_), channel_id=1, source_target_pairs={{0,2},{2,4},{4,6},{6,7},{7,5},{5,3},{3,1},{1,0},{8,10},{10,12},{12... | collective-permute-start | bytes 1277960 | tf_op jit(solution)/shard_map/ppermute | solution.py:34
  41.6 8.0 %collective-permute-start.7 = (f32[7,32,256]{2,1,0:T(8,128)}, f32[7,32,256]{2,1,0:T(8,128)S(1)}, u32[]{:S(2)}, u32[]{:S(2)}) collective-permute-start(f32[7,32,256]{2,1,0:T(8,128)} %slice.14), channel_id=1, source_target_pairs={{2,0},{4,2},{6,4},{7,6},{5,7},{3,5},{1,3},{0,1},{10,8},{12,10},{14... | collective-permute-start | bytes 688136 | tf_op jit(solution)/shard_map/ppermute | solution.py:35
  42.4 7.3 %collective-permute-start.6 = (f32[6,32,256]{2,1,0:T(8,128)}, f32[6,32,256]{2,1,0:T(8,128)S(1)}, u32[]{:S(2)}, u32[]{:S(2)}) collective-permute-start(f32[6,32,256]{2,1,0:T(8,128)} %slice.13), channel_id=1, source_target_pairs={{0,2},{2,4},{4,6},{6,7},{7,5},{5,3},{3,1},{1,0},{8,10},{10,12},{12... | collective-permute-start | bytes 589832 | tf_op jit(solution)/shard_map/ppermute | solution.py:34
  47.7 6.0 %collective-permute-start.9 = (f32[16,256]{1,0:T(8,128)S(1)}, f32[16,256]{1,0:T(8,128)S(1)}, u32[]{:S(2)}, u32[]{:S(2)}) collective-permute-start(f32[16,256]{1,0:T(8,128)S(1)} %get-tuple-element.45.refs_4_.refs_7_.refs_9_), channel_id=1, source_target_pairs={{0,8},{8,0},{16,24},{24,16},{1,9},{9,1},{17,25},{25,17},{2,10},{10... | collective-permute-start | bytes 49160 | tf_op jit(solution)/shard_map/ppermute | solution.py:16
  47.8 5.9 %collective-permute-start.10 = (f32[16,256]{1,0:T(8,128)S(1)}, f32[16,256]{1,0:T(8,128)S(1)}, u32[]{:S(2)}, u32[]{:S(2)}) collective-permute-start(f32[16,256]{1,0:T(8,128)S(1)} %get-tuple-element.45.refs_4_.refs_7_.refs_9_), channel_id=1, source_target_pairs={{0,16},{8,24},{16,0},{24,8},{1,17},{9,25},{17,1},{25,9},{2,18},{10... | collective-permute-start | bytes 49160 | tf_op jit(solution)/shard_map/ppermute | solution.py:16
  49.3 4.3 %collective-permute-start.11 = (f32[16,256]{1,0:T(8,128)S(1)}, f32[16,256]{1,0:T(8,128)S(1)}, u32[]{:S(2)}, u32[]{:S(2)}) collective-permute-start(f32[16,256]{1,0:T(8,128)S(1)} %get-tuple-element.45.refs_4_.refs_7_.refs_9_), channel_id=1, source_target_pairs={{0,24},{8,16},{16,8},{24,0},{1,25},{9,17},{17,9},{25,1},{2,26},{10... | collective-permute-start | bytes 49160 | tf_op jit(solution)/shard_map/ppermute | solution.py:16
  52.1 1.6 %collective-permute-start.8 = (f32[16,256]{1,0:T(8,128)S(1)}, f32[16,256]{1,0:T(8,128)S(1)}, u32[]{:S(2)}, u32[]{:S(2)}) collective-permute-start(f32[16,256]{1,0:T(8,128)S(1)} %get-tuple-element.42), channel_id=1, source_target_pairs={{0,8},{8,0},{16,24},{24,16},{1,9},{9,1},{17,25},{25,17},{2,10},{10... | collective-permute-start | bytes 49160 | tf_op jit(solution)/shard_map/ppermute | solution.py:16
  54.5 1.4 %collective-permute-start.12 = (f32[16,256]{1,0:T(8,128)S(1)}, f32[16,256]{1,0:T(8,128)S(1)}, u32[]{:S(2)}, u32[]{:S(2)}) collective-permute-start(f32[16,256]{1,0:T(8,128)S(1)} %get-tuple-element.47), channel_id=1, source_target_pairs={{0,8},{8,0},{16,24},{24,16},{1,9},{9,1},{17,25},{25,17},{2,10},{10... | collective-permute-start | bytes 49160 | tf_op jit(solution)/shard_map/ppermute | solution.py:16
  56.9 3.3 %collective-permute-start.13 = (f32[16,256]{1,0:T(8,128)S(1)}, f32[16,256]{1,0:T(8,128)S(1)}, u32[]{:S(2)}, u32[]{:S(2)}) collective-permute-start(f32[16,256]{1,0:T(8,128)S(1)} %get-tuple-element.52), channel_id=1, source_target_pairs={{0,8},{8,0},{16,24},{24,16},{1,9},{9,1},{17,25},{25,17},{2,10},{10... | collective-permute-start | bytes 49160 | tf_op jit(solution)/shard_map/ppermute | solution.py:16
  57.3 3.7 %collective-permute-start.14 = (f32[16,256]{1,0:T(8,128)S(1)}, f32[16,256]{1,0:T(8,128)S(1)}, u32[]{:S(2)}, u32[]{:S(2)}) collective-permute-start(f32[16,256]{1,0:T(8,128)S(1)} %get-tuple-element.53), channel_id=1, source_target_pairs={{0,16},{8,24},{16,0},{24,8},{1,17},{9,25},{17,1},{25,9},{2,18},{10... | collective-permute-start | bytes 49160 | tf_op jit(solution)/shard_map/ppermute | solution.py:16
  58.8 3.3 %collective-permute-start.15 = (f32[16,256]{1,0:T(8,128)S(1)}, f32[16,256]{1,0:T(8,128)S(1)}, u32[]{:S(2)}, u32[]{:S(2)}) collective-permute-start(f32[16,256]{1,0:T(8,128)S(1)} %get-tuple-element.54), channel_id=1, source_target_pairs={{0,24},{8,16},{16,8},{24,0},{1,25},{9,17},{17,9},{25,1},{2,26},{10... | collective-permute-start | bytes 49160 | tf_op jit(solution)/shard_map/ppermute | solution.py:16
  63.0 1.9 %collective-permute-start.16 = (f32[4,16,256]{2,1,0:T(8,128)S(1)}, f32[4,16,256]{2,1,0:T(8,128)S(1)}, u32[]{:S(2)}, u32[]{:S(2)}) collective-permute-start(f32[4,16,256]{2,1,0:T(8,128)S(1)} %shard_map.113.refs_0_), channel_id=1, source_target_pairs={{0,8},{8,0},{16,24},{24,16},{1,9},{9,1},{17,25},{25,17},{2,10},{10... | collective-permute-start | bytes 196616 | tf_op jit(solution)/shard_map/ppermute | solution.py:16
  63.2 4.9 %collective-permute-start.17 = (f32[4,16,256]{2,1,0:T(8,128)S(1)}, f32[4,16,256]{2,1,0:T(8,128)S(1)}, u32[]{:S(2)}, u32[]{:S(2)}) collective-permute-start(f32[4,16,256]{2,1,0:T(8,128)S(1)} %shard_map.113.refs_0_), channel_id=1, source_target_pairs={{0,16},{8,24},{16,0},{24,8},{1,17},{9,25},{17,1},{25,9},{2,18},{10... | collective-permute-start | bytes 196616 | tf_op jit(solution)/shard_map/ppermute | solution.py:16
  63.8 4.6 %collective-permute-start.18 = (f32[4,16,256]{2,1,0:T(8,128)S(1)}, f32[4,16,256]{2,1,0:T(8,128)S(1)}, u32[]{:S(2)}, u32[]{:S(2)}) collective-permute-start(f32[4,16,256]{2,1,0:T(8,128)S(1)} %shard_map.113.refs_0_), channel_id=1, source_target_pairs={{0,24},{8,16},{16,8},{24,0},{1,25},{9,17},{17,9},{25,1},{2,26},{10... | collective-permute-start | bytes 196616 | tf_op jit(solution)/shard_map/ppermute | solution.py:16
  69.3 1.9 %collective-permute-start.19 = (f32[16,256]{1,0:T(8,128)S(1)}, f32[16,256]{1,0:T(8,128)S(1)}, u32[]{:S(2)}, u32[]{:S(2)}) collective-permute-start(f32[16,256]{1,0:T(8,128)S(1)} %shard_map.114.refs_0_.refs_2_), channel_id=1, source_target_pairs={{0,8},{8,0},{16,24},{24,16},{1,9},{9,1},{17,25},{25,17},{2,10},{10... | collective-permute-start | bytes 49160 | tf_op jit(solution)/shard_map/ppermute | solution.py:16
  69.7 3.8 %collective-permute-start.20 = (f32[16,256]{1,0:T(8,128)S(1)}, f32[16,256]{1,0:T(8,128)S(1)}, u32[]{:S(2)}, u32[]{:S(2)}) collective-permute-start(f32[16,256]{1,0:T(8,128)S(1)} %shard_map.114.refs_0_.refs_2_), channel_id=1, source_target_pairs={{0,16},{8,24},{16,0},{24,8},{1,17},{9,25},{17,1},{25,9},{2,18},{10... | collective-permute-start | bytes 49160 | tf_op jit(solution)/shard_map/ppermute | solution.py:16
  70.4 3.2 %collective-permute-start.21 = (f32[16,256]{1,0:T(8,128)S(1)}, f32[16,256]{1,0:T(8,128)S(1)}, u32[]{:S(2)}, u32[]{:S(2)}) collective-permute-start(f32[16,256]{1,0:T(8,128)S(1)} %shard_map.114.refs_0_.refs_2_), channel_id=1, source_target_pairs={{0,24},{8,16},{16,8},{24,0},{1,25},{9,17},{17,9},{25,1},{2,26},{10... | collective-permute-start | bytes 49160 | tf_op jit(solution)/shard_map/ppermute | solution.py:16
  74.4 1.2 %collective-permute-start.22 = (f32[16,256]{1,0:T(8,128)S(1)}, f32[16,256]{1,0:T(8,128)S(1)}, u32[]{:S(2)}, u32[]{:S(2)}) collective-permute-start(f32[16,256]{1,0:T(8,128)S(1)} %shard_map.115.refs_0_), channel_id=1, source_target_pairs={{0,8},{8,0},{16,24},{24,16},{1,9},{9,1},{17,25},{25,17},{2,10},{10... | collective-permute-start | bytes 49160 | tf_op jit(solution)/shard_map/ppermute | solution.py:16
  75.6 18.8 %copy-start.3 = (f32[1,1,512,512]{3,2,1,0:T(8,128)S(1)}, f32[1,1,512,512]{3,2,1,0:T(8,128)}, u32[]{:S(2)}) copy-start(f32[1,1,512,512]{3,2,1,0:T(8,128)} %param.11) | copy-start | bytes 3145732
  76.3 18.0 %copy-start.1 = (f32[1,1,512,512]{3,2,1,0:T(8,128)S(1)}, f32[1,1,512,512]{3,2,1,0:T(8,128)}, u32[]{:S(2)}) copy-start(f32[1,1,512,512]{3,2,1,0:T(8,128)} %param.10) | copy-start | bytes 3145732
  76.3 1.2 %collective-permute-start.23 = (f32[16,256]{1,0:T(8,128)S(1)}, f32[16,256]{1,0:T(8,128)S(1)}, u32[]{:S(2)}, u32[]{:S(2)}) collective-permute-start(f32[16,256]{1,0:T(8,128)S(1)} %shard_map.116.refs_0_), channel_id=1, source_target_pairs={{0,8},{8,0},{16,24},{24,16},{1,9},{9,1},{17,25},{25,17},{2,10},{10... | collective-permute-start | bytes 49160 | tf_op jit(solution)/shard_map/ppermute | solution.py:16
  78.6 15.7 %copy-start.8 = (f32[128,512]{1,0:T(8,128)S(1)}, f32[128,512]{1,0:T(8,128)}, u32[]{:S(2)}) copy-start(f32[128,512]{1,0:T(8,128)} %copy-done.7) | copy-start | bytes 786436
  (4 other events, 3.8 us)

commit v11 on v10

--- a/solution.py
+++ b/solution.py
@@ -20,7 +20,7 @@
     return list(range(0, count, 2)) + list(range(count - 1, 0, -2))
 
 
-def ring_gather(block, count, ahead):
+def ring_gather(block, count, ahead, use):
     order = ring_order(count)
     right = [(order[i], order[(i + 1) % count]) for i in range(count)]
     left = [(target, source) for source, target in right]
@@ -30,13 +30,15 @@
     for step in range(1, count // 2 + 1):
         first = 0
         if 2 * step == count:
+            forward, backward, used = lax.optimization_barrier((forward, backward, used))
             forward, backward, first = forward[:middle], backward[middle:], middle
         forward = lax.ppermute(forward, "row", right)
         backward = lax.ppermute(backward, "row", left)
         if step == 1:
-            forward, backward, _ = lax.optimization_barrier((forward, backward, ahead))
+            forward, backward, ahead = lax.optimization_barrier((forward, backward, ahead))
+            used = use(ahead)
         parts += [(-step, 0, forward), (step, first, backward)]
-    return parts
+    return parts, used
 
 
 def call(body, outs, arrays, scalars=(), scratch=(), work=0, remote=0, room=16):
@@ -236,59 +238,61 @@
         work=24 * local * local * columns,
         room=24,
     )
-    parts = ring_gather(
+    def place_terms(terms):
+        terms = lax.all_to_all(terms.reshape(ranks, share, packed), "row", 0, 0, tiled=True)
+        known = terms[:, number_row, tiles * TILE + number_lane :][:, :tiles].astype(jnp.int32)
+
+        def scatter(ids_ref, known_ref, terms_ref, *refs):
+            outs, pivots_ref, path = refs[:-2], refs[-2], refs[-1]
+            lane = lax.broadcasted_iota(jnp.int32, (share, TILE), 1)
+            path[...] = jnp.zeros_like(path)
+            for source in range(ranks):
+                for tile in range(tiles):
+                    place = known_ref[source, tile]
+                    path[place] = path[place] - terms_ref[source, :, tile * TILE : (tile + 1) * TILE]
+
+            def spread(first):
+                rows = []
+                for half in range(halves):
+                    row = jnp.zeros((share, TILE), F32)
+                    for source in range(half * TILE // piece, (half + 1) * TILE // piece):
+                        place = source * piece % TILE
+                        shift = (TILE + place - first) % TILE
+                        turned = pltpu.roll(terms_ref[source, :, tiles * TILE :], shift, 1)
+                        row = jnp.where((lane >= place) & (lane < place + piece), turned, row)
+                    rows.append(row)
+                return jnp.concatenate(rows, 1)
+
+            pivots_ref[...] = spread(levels * piece)
+            for level in range(levels):
+                span = 2**level
+                filled = outs[level]
+                for slot in range(span):
+                    first = (span - 1 + slot) * halves
+                    for half in range(halves):
+                        filled[slot, :, half * TILE : (half + 1) * TILE] = path[first + half]
+                own = ids_ref[0] % span
+                filled[own] = filled[own] + spread(level * piece)
+
+        *rest, pivots = call(
+            scatter,
+            [((2**level, *wide), F32) for level in range(levels)] + [(wide, F32)],
+            (terms,),
+            (ids, known),
+            [pltpu.VMEM((path_tiles, share, TILE), F32)],
+        )
+        return known, rest, pivots
+
+    parts, (known, rest, pivots) = ring_gather(
         jnp.concatenate([win_inverse[0], win_coupling[0]], 0).reshape(-1, piece, base),
         ranks,
         terms,
-    )
-    terms = lax.all_to_all(terms.reshape(ranks, share, packed), "row", 0, 0, tiled=True)
-    number_lane += tiles * TILE
-    known = terms[:, number_row, number_lane : number_lane + tiles].astype(jnp.int32)
-
+        place_terms,
+    )
     blocks = assemble([("A", 0), ("B", 0)])
     for name in all_names:
         if name not in blocks:
             blocks.update(assemble([name]))
-
-    def scatter(ids_ref, known_ref, terms_ref, *refs):
-        outs, pivots_ref, path = refs[:-2], refs[-2], refs[-1]
-        lane = lax.broadcasted_iota(jnp.int32, (share, TILE), 1)
-        path[...] = jnp.zeros_like(path)
-        for source in range(ranks):
-            for tile in range(tiles):
-                place = known_ref[source, tile]
-                path[place] = path[place] - terms_ref[source, :, tile * TILE : (tile + 1) * TILE]
-
-        def spread(first):
-            rows = []
-            for half in range(halves):
-                row = jnp.zeros((share, TILE), F32)
-                for source in range(half * TILE // piece, (half + 1) * TILE // piece):
-                    place = source * piece % TILE
-                    shift = (TILE + place - first) % TILE
-                    turned = pltpu.roll(terms_ref[source, :, tiles * TILE :], shift, 1)
-                    row = jnp.where((lane >= place) & (lane < place + piece), turned, row)
-                rows.append(row)
-            return jnp.concatenate(rows, 1)
-
-        pivots_ref[...] = spread(levels * piece)
-        for level in range(levels):
-            span = 2**level
-            filled = outs[level]
-            for slot in range(span):
-                first = (span - 1 + slot) * halves
-                for half in range(halves):
-                    filled[slot, :, half * TILE : (half + 1) * TILE] = path[first + half]
-            own = ids_ref[0] % span
-            filled[own] = filled[own] + spread(level * piece)
-
-    *rest, pivots = call(
-        scatter,
-        [((2**level, *wide), F32) for level in range(levels)] + [(wide, F32)],
-        (terms,),
-        (ids, known),
-        [pltpu.VMEM((path_tiles, share, TILE), F32)],
-    )
 
     all_pivots = leaf_swaps([pivots] * leaves)
 

time: 97.5 us -> 97 us (level)
  waiting for transfers between devices: 30.4 us -> 31.9 us
  local copies, waits for them, and re-layouts: 5.58 us -> 4.27 us
    ppermute x4, waiting for transfers between devices: 16.8 us -> 4.44 us  [ring_gather(): backward = lax.ppermute(backward, 'row', left)]
    ppermute x4, waiting for transfers between devices: 3.73 us -> 11.2 us  [ring_gather(): forward = lax.ppermute(forward, 'row', right)]
    all_to_all x1, waiting for transfers between devices: 0.01 us -> 6.62 us  [place_terms(): lax.all_to_all(terms.reshape(ranks, share, packed), 'row', 0, 0, tiled=True)]
    slice x2, local copies, waits for them, and re-layouts: 1.42 us -> 0.03 us  [ring_gather(): forward, backward, first = (forward[:middle], backward[middle:], middle)]
  transfers between devices with their start and end apart: 25 -> 25, of which waited for: 12 -> 16; matrix products, arithmetic and copies ran while one was open for 3% -> 1% of each run, Pallas kernels for 10% -> 10%
where the time goes in v11:
time: 97 us; the launch traced here: 96.7 us
  waiting for transfers between devices  31.9 us (33%)
  starting transfers between devices  25.2 us (26%)
  Pallas kernels  17.5 us (18%)
  blocking collectives  15.7 us (16%)
  local copies, waits for them, and re-layouts  4.27 us (4%)
  other arithmetic  1.19 us (1%)
    pallas_call x15, Pallas kernels, call(): pl.pallas_call(body, out_shape=[jax.ShapeDtypeStruct(*o) for o in outs],...  17.5 us
    all_to_all x1, blocking collectives, shards(): lax.all_to_all(replies[0], 'row', 0, 0, tiled=True).reshape(columns, packed)  15.7 us
    ppermute x4, waiting for transfers between devices, ring_gather(): forward = lax.ppermute(forward, 'row', right)  11.2 us
    ppermute x4, starting transfers between devices, ring_gather(): forward = lax.ppermute(forward, 'row', right)  11.1 us
    ppermute x16, waiting for transfers between devices, swap(): return lax.ppermute(value, axis, [(i, i ^ offset) for i in range(count)])  9.7 us
    ppermute x16, starting transfers between devices, swap(): return lax.ppermute(value, axis, [(i, i ^ offset) for i in range(count)])  8.77 us
    all_to_all x1, waiting for transfers between devices, place_terms(): lax.all_to_all(terms.reshape(ranks, share, packed), 'row', 0, 0, tiled=True)  6.62 us
    all_to_all x1, starting transfers between devices, place_terms(): lax.all_to_all(terms.reshape(ranks, share, packed), 'row', 0, 0, tiled=True)  4.82 us
  transfers between devices with their start and end apart: 25, of which 16 were waited for; matrix products, arithmetic and copies ran while one was open for 1% of the time, Pallas kernels for 10%

profile of v11, /device:TPU:0, one launch (start us, length us, event | category | flops | bytes accessed | tf_op | source)
XLA Modules:
  0.0 96.7 jit_solution(1855217791665422965)
XLA Ops:
  0.7 1.1 %pad_maximum_fusion = f32[416,256]{1,0:T(8,128)S(1)} fusion(f32[192,256]{1,0:T(8,128)} %bitcast.33, f32[224,256]{1,0:T(8,128)} %bitcast.32), kind=kLoop, calls=%fused_computation | loop fusion | flops 106496 | bytes 851968 | tf_op jit(solution)/shard_map/concatenate | solution.py:287
  1.8 3.1 %collective-permute-start = (f32[13,32,256]{2,1,0:T(8,128)S(1)}, f32[13,32,256]{2,1,0:T(8,128)S(1)}, u32[]{:S(2)}, u32[]{:S(2)}) collective-permute-start(f32[13,32,256]{2,1,0:T(8,128)S(1)} %bitcast.18), channel_id=1, source_target_pairs={{0,2},{2,4},{4,6},{6,7},{7,5},{5,3},{3,1},{1,0},{8,10},{10,12},{12... | collective-permute-start | bytes 1277960 | tf_op jit(solution)/shard_map/ppermute | solution.py:35
  5.2 1.2 %copy-done = f32[1,1,512,512]{3,2,1,0:T(8,128)S(1)} copy-done((f32[1,1,512,512]{3,2,1,0:T(8,128)S(1)}, f32[1,1,512,512]{3,2,1,0:T(8,128)}, u32[]{:S(2)}) %copy-start) | copy-done | bytes 1048600
  6.5 1.2 %copy-done.2 = f32[1,1,512,512]{3,2,1,0:T(8,128)S(1)} copy-done((f32[1,1,512,512]{3,2,1,0:T(8,128)S(1)}, f32[1,1,512,512]{3,2,1,0:T(8,128)}, u32[]{:S(2)}) %copy-start.2) | copy-done | bytes 1048600
  7.7 2.5 %shard_map.104 = (f32[128,512]{1,0:T(8,128)S(1)}, f32[128,640]{1,0:T(8,128)}) custom-call(f32[512,128]{1,0:T(8,128)S(1)} %bitcast.30, f32[3,32,128]{2,1,0:T(8,128)S(1)} %copy-done.5, f32[128,128]{1,0:T(8,128)S(1)} %bitcast.25, f32[512,512]{1,0:T(8,128)S(1)} %bitcast.26, f32[512,512]{1,0:T(8,128)S(1)} %bitcast.28), custom_call_target="tpu_custom_call" | custom-call | flops 805306368 | bytes 3063808 | tf_op jit(solution)/shard_map/pallas_call | solution.py:47
  10.9 3.7 %collective-permute-done.refs_1_ = f32[13,32,256]{2,1,0:T(8,128)S(1)} collective-permute-done((f32[13,32,256]{2,1,0:T(8,128)S(1)}, f32[13,32,256]{2,1,0:T(8,128)S(1)}, u32[]{:S(2)}, u32[]{:S(2)}) %collective-permute-start) | collective-permute-done | bytes 426016 | tf_op jit(solution)/shard_map/ppermute | solution.py:35
  14.6 1.5 %collective-permute-done.1.refs_2_ = f32[13,32,256]{2,1,0:T(8,128)S(1)} collective-permute-done((f32[13,32,256]{2,1,0:T(8,128)S(1)}, f32[13,32,256]{2,1,0:T(8,128)S(1)}, u32[]{:S(2)}, u32[]{:S(2)}) %collective-permute-start.1) | collective-permute-done | bytes 426016 | tf_op jit(solution)/shard_map/ppermute | solution.py:36
  16.1 1.6 %collective-permute-start.2 = (f32[13,32,256]{2,1,0:T(8,128)S(1)}, f32[13,32,256]{2,1,0:T(8,128)S(1)}, u32[]{:S(2)}, u32[]{:S(2)}) collective-permute-start(f32[13,32,256]{2,1,0:T(8,128)S(1)} %collective-permute-done.refs_1_), channel_id=1, source_target_pairs={{0,2},{2,4},{4,6},{6,7},{7,5},{5,3},{3,1},{1,0},{8,10},{10,12},{12... | collective-permute-start | bytes 1277960 | tf_op jit(solution)/shard_map/ppermute | solution.py:35
  18.2 4.8 %all-to-all-start = ((f32[8,16,640]{2,1,0:T(8,128)}), f32[8,16,640]{2,1,0:T(8,128)S(1)}, u32[]{:S(2)}, u32[]{:S(2)}) async-start(f32[8,16,640]{2,1,0:T(8,128)} %bitcast.10), calls=%async_computation | async-start | bytes 655360 | tf_op jit(solution)/shard_map/all_to_all | solution.py:242
  23.0 5.8 %collective-permute-done.2.refs_3_ = f32[13,32,256]{2,1,0:T(8,128)S(1)} collective-permute-done((f32[13,32,256]{2,1,0:T(8,128)S(1)}, f32[13,32,256]{2,1,0:T(8,128)S(1)}, u32[]{:S(2)}, u32[]{:S(2)}) %collective-permute-start.2) | collective-permute-done | bytes 426016 | tf_op jit(solution)/shard_map/ppermute | solution.py:35
  28.8 3.1 %collective-permute-start.3 = (f32[13,32,256]{2,1,0:T(8,128)S(1)}, f32[13,32,256]{2,1,0:T(8,128)S(1)}, u32[]{:S(2)}, u32[]{:S(2)}) collective-permute-start(f32[13,32,256]{2,1,0:T(8,128)S(1)} %collective-permute-done.2.refs_3_), channel_id=1, source_target_pairs={{0,2},{2,4},{4,6},{6,7},{7,5},{5,3},{3,1},{1,0},{8,10},{10,12},{12... | collective-permute-start | bytes 1277960 | tf_op jit(solution)/shard_map/ppermute | solution.py:35
  31.9 6.6 %all-to-all-done.terms_ref = f32[8,16,640]{2,1,0:T(8,128)S(1)} async-done(((f32[8,16,640]{2,1,0:T(8,128)}), f32[8,16,640]{2,1,0:T(8,128)S(1)}, u32[]{:S(2)}, u32[]{:S(2)}) %all-to-all-start) | async-done | bytes 327712 | tf_op jit(solution)/shard_map/all_to_all | solution.py:242
  40.0 2.2 %collective-permute-done.5.refs_6_ = f32[13,32,256]{2,1,0:T(8,128)S(1)} collective-permute-done((f32[13,32,256]{2,1,0:T(8,128)S(1)}, f32[13,32,256]{2,1,0:T(8,128)S(1)}, u32[]{:S(2)}, u32[]{:S(2)}) %collective-permute-start.5) | collective-permute-done | bytes 426016 | tf_op jit(solution)/shard_map/ppermute | solution.py:36
  42.3 3.4 %collective-permute-start.6 = (f32[6,32,256]{2,1,0:T(8,128)S(1)}, f32[6,32,256]{2,1,0:T(8,128)S(1)}, u32[]{:S(2)}, u32[]{:S(2)}) collective-permute-start(f32[6,32,256]{2,1,0:T(8,128)S(1)} %slice.14), channel_id=1, source_target_pairs={{0,2},{2,4},{4,6},{6,7},{7,5},{5,3},{3,1},{1,0},{8,10},{10,12},{12... | collective-permute-start | bytes 589832 | tf_op jit(solution)/shard_map/ppermute | solution.py:35
  45.7 1.5 %collective-permute-start.10 = (f32[16,256]{1,0:T(8,128)S(1)}, f32[16,256]{1,0:T(8,128)S(1)}, u32[]{:S(2)}, u32[]{:S(2)}) collective-permute-start(f32[16,256]{1,0:T(8,128)S(1)} %get-tuple-element.61.refs_4_.refs_7_.refs_9_), channel_id=1, source_target_pairs={{0,16},{8,24},{16,0},{24,8},{1,17},{9,25},{17,1},{25,9},{2,18},{10... | collective-permute-start | bytes 49160 | tf_op jit(solution)/shard_map/ppermute | solution.py:16
  47.8 1.0 %collective-permute-done.6.refs_7_ = f32[6,32,256]{2,1,0:T(8,128)S(1)} collective-permute-done((f32[6,32,256]{2,1,0:T(8,128)S(1)}, f32[6,32,256]{2,1,0:T(8,128)S(1)}, u32[]{:S(2)}, u32[]{:S(2)}) %collective-permute-start.6) | collective-permute-done | bytes 196640 | tf_op jit(solution)/shard_map/ppermute | solution.py:35
  49.6 1.6 %shard_map.106 = (bf16[1,256,256]{2,1,0:T(8,128)(2,1)S(1)}, bf16[1,256,256]{2,1,0:T(8,128)(2,1)S(1)}, bf16[2,256,256]{2,1,0:T(8,128)(2,1)S(1)}, bf16[2,256,256]{2,1,0:T(8,128)(2,1)S(1)}) custom-call(s32[2]{0:T(128)S(1)} %pad_add_fusion.ids_ref, f32[13,32,256]{2,1,0:T(8,128)S(1)} %bitcast.20, f32[13,32,256]{2,1,0:T(8,128)S(1)} %collective-permute-done.refs_1_, ...), custom_call_target="tpu_custom_call" | custom-call | bytes 4194304 | tf_op jit(solution)/shard_map/pallas_call | solution.py:47
  52.1 1.1 %shard_map.108 = (bf16[2,256,256]{2,1,0:T(8,128)(2,1)S(1)}, bf16[2,256,256]{2,1,0:T(8,128)(2,1)S(1)}) custom-call(s32[2]{0:T(128)S(1)} %pad_add_fusion.ids_ref, f32[13,32,256]{2,1,0:T(8,128)S(1)} %bitcast.21, f32[13,32,256]{2,1,0:T(8,128)S(1)} %collective-permute-done.refs_1_, f32[13,32,256]{2,1,0:T(8,128)S(1)} %collective-permute-done.1.refs_2_, ...), custom_call_target="tpu_custom_call" | custom-call | bytes 3932160 | tf_op jit(solution)/shard_map/pallas_call | solution.py:47
  54.7 1.2 %shard_map.110 = (bf16[4,256,256]{2,1,0:T(8,128)(2,1)S(1)}, bf16[4,256,256]{2,1,0:T(8,128)(2,1)S(1)}) custom-call(s32[2]{0:T(128)S(1)} %pad_add_fusion.ids_ref, f32[13,32,256]{2,1,0:T(8,128)S(1)} %bitcast.22, f32[13,32,256]{2,1,0:T(8,128)S(1)} %collective-permute-done.refs_1_, f32[13,32,256]{2,1,0:T(8,128)S(1)} %collective-permute-done.1.refs_2_, ...), custom_call_target="tpu_custom_call" | custom-call | bytes 4456448 | tf_op jit(solution)/shard_map/pallas_call | solution.py:47
  55.9 0.9 shard_map.111
  56.9 1.5 %collective-permute-start.14 = (f32[16,256]{1,0:T(8,128)S(1)}, f32[16,256]{1,0:T(8,128)S(1)}, u32[]{:S(2)}, u32[]{:S(2)}) collective-permute-start(f32[16,256]{1,0:T(8,128)S(1)} %get-tuple-element.69), channel_id=1, source_target_pairs={{0,16},{8,24},{16,0},{24,8},{1,17},{9,25},{17,1},{25,9},{2,18},{10... | collective-permute-start | bytes 49160 | tf_op jit(solution)/shard_map/ppermute | solution.py:16
  58.8 1.3 %shard_map.112 = (bf16[4,256,256]{2,1,0:T(8,128)(2,1)S(1)}, bf16[4,256,256]{2,1,0:T(8,128)(2,1)S(1)}) custom-call(s32[2]{0:T(128)S(1)} %pad_add_fusion.ids_ref, f32[13,32,256]{2,1,0:T(8,128)S(1)} %bitcast.23, f32[13,32,256]{2,1,0:T(8,128)S(1)} %collective-permute-done.refs_1_, f32[13,32,256]{2,1,0:T(8,128)S(1)} %collective-permute-done.1.refs_2_, ...), custom_call_target="tpu_custom_call" | custom-call | bytes 4456448 | tf_op jit(solution)/shard_map/pallas_call | solution.py:47
  60.7 0.9 collective-permute-done.15.refs_3_
  61.6 1.0 shard_map.113.refs_0_
  63.5 1.0 %collective-permute-start.18 = (f32[4,16,256]{2,1,0:T(8,128)S(1)}, f32[4,16,256]{2,1,0:T(8,128)S(1)}, u32[]{:S(2)}, u32[]{:S(2)}) collective-permute-start(f32[4,16,256]{2,1,0:T(8,128)S(1)} %shard_map.113.refs_0_), channel_id=1, source_target_pairs={{0,24},{8,16},{16,8},{24,0},{1,25},{9,17},{17,9},{25,1},{2,26},{10... | collective-permute-start | bytes 196616 | tf_op jit(solution)/shard_map/ppermute | solution.py:16
  64.5 3.2 %collective-permute-done.17.refs_2_ = f32[4,16,256]{2,1,0:T(8,128)S(1)} collective-permute-done((f32[4,16,256]{2,1,0:T(8,128)S(1)}, f32[4,16,256]{2,1,0:T(8,128)S(1)}, u32[]{:S(2)}, u32[]{:S(2)}) %collective-permute-start.17) | collective-permute-done | bytes 65568 | tf_op jit(solution)/shard_map/ppermute | solution.py:16
  70.7 2.3 %collective-permute-done.20.refs_2_.refs_4_ = f32[16,256]{1,0:T(8,128)S(1)} collective-permute-done((f32[16,256]{1,0:T(8,128)S(1)}, f32[16,256]{1,0:T(8,128)S(1)}, u32[]{:S(2)}, u32[]{:S(2)}) %collective-permute-start.20) | collective-permute-done | bytes 16416 | tf_op jit(solution)/shard_map/ppermute | solution.py:16
  74.2 1.1 %collective-permute-done.22.refs_1_ = f32[16,256]{1,0:T(8,128)S(1)} collective-permute-done((f32[16,256]{1,0:T(8,128)S(1)}, f32[16,256]{1,0:T(8,128)S(1)}, u32[]{:S(2)}, u32[]{:S(2)}) %collective-permute-start.22) | collective-permute-done | bytes 16416 | tf_op jit(solution)/shard_map/ppermute | solution.py:16
  76.2 1.0 %collective-permute-done.23.refs_1_ = f32[16,256]{1,0:T(8,128)S(1)} collective-permute-done((f32[16,256]{1,0:T(8,128)S(1)}, f32[16,256]{1,0:T(8,128)S(1)}, u32[]{:S(2)}, u32[]{:S(2)}) %collective-permute-start.23) | collective-permute-done | bytes 16416 | tf_op jit(solution)/shard_map/ppermute | solution.py:16
  77.2 1.1 %shard_map.117 = f32[8,16,640]{2,1,0:T(8,128)S(1)} custom-call(s32[2]{0:T(128)S(1)} %pad_add_fusion.ids_ref, s32[8,4]{1,0:T(8,128)S(1)} %slice_convert_fusion.known_ref, f32[16,256]{1,0:T(8,128)S(1)} %shard_map.116.refs_0_, f32[16,256]{1,0:T(8,128)S(1)} %collective-permute-done.23.refs_1_, f32[16,256]{1,0:T(8,128)S(1)} %shard_map.114.refs_0_.refs_2_, ...), custom_call_target="tpu_custom_call" | custom-call | bytes 1245184 | tf_op jit(solution)/shard_map/pallas_call | solution.py:47
  78.3 15.7 %all_to_all.10 = f32[8,16,640]{2,1,0:T(8,128)S(1)} all-to-all(f32[8,16,640]{2,1,0:T(8,128)S(1)} %shard_map.117), channel_id=1, replica_groups=mesh['leaf'=4,'row'=8] {'row'}, dimensions={0} | all-to-all | bytes 655360 | tf_op jit(solution)/shard_map/all_to_all | solution.py:485
  94.7 2.0 %shard_map.118 = (f32[512,128]{1,0:T(8,128)}, f32[3,32,128]{2,1,0:T(8,128)}) custom-call(f32[128,640]{1,0:T(8,128)S(1)} %bitcast.24, f32[128,512]{1,0:T(8,128)S(1)} %copy-done.8, f32[1,512]{1,0:T(1,128)S(1)} %bitcast.31, f32[512,512]{1,0:T(8,128)S(1)} %bitcast.27, f32[512,512]{1,0:T(8,128)S(1)} %bitcast.29), custom_call_target="tpu_custom_call" | custom-call | flops 805306368 | bytes 3000320 | tf_op jit(solution)/shard_map/pallas_call | solution.py:47
  (66 shorter events, 14.5 us)
Async XLA Ops:
  0.6 4.2 %copy-start.9 = (f32[3,32]{1,0:T(4,128)S(1)}, f32[3,32]{1,0:T(4,128)}, u32[]{:S(2)}) copy-start(f32[3,32]{1,0:T(4,128)} %param.15) | copy-start | bytes 1156
  0.6 4.3 %copy-start.10 = (s32[1,1,4]{2,1,0:T(1,128)S(1)}, s32[1,1,4]{2,1,0:T(1,128)}, u32[]{:S(2)}) copy-start(s32[1,1,4]{2,1,0:T(1,128)} %param.13) | copy-start | bytes 52
  0.7 4.6 %copy-start.4 = (f32[1,1,512,128]{3,2,1,0:T(8,128)S(1)}, f32[1,1,512,128]{3,2,1,0:T(8,128)}, u32[]{:S(2)}) copy-start(f32[1,1,512,128]{3,2,1,0:T(8,128)} %param.9) | copy-start | bytes 786436
  1.8 3.4 %copy-start.5 = (f32[3,32,128]{2,1,0:T(8,128)S(1)}, f32[3,32,128]{2,1,0:T(8,128)}, u32[]{:S(2)}) copy-start(f32[3,32,128]{2,1,0:T(8,128)} %window_ref.1) | copy-start | bytes 147460
  1.8 12.8 %collective-permute-start = (f32[13,32,256]{2,1,0:T(8,128)S(1)}, f32[13,32,256]{2,1,0:T(8,128)S(1)}, u32[]{:S(2)}, u32[]{:S(2)}) collective-permute-start(f32[13,32,256]{2,1,0:T(8,128)S(1)} %bitcast.18), channel_id=1, source_target_pairs={{0,2},{2,4},{4,6},{6,7},{7,5},{5,3},{3,1},{1,0},{8,10},{10,12},{12... | collective-permute-start | bytes 1277960 | tf_op jit(solution)/shard_map/ppermute | solution.py:35
  4.9 11.3 %collective-permute-start.1 = (f32[13,32,256]{2,1,0:T(8,128)S(1)}, f32[13,32,256]{2,1,0:T(8,128)S(1)}, u32[]{:S(2)}, u32[]{:S(2)}) collective-permute-start(f32[13,32,256]{2,1,0:T(8,128)S(1)} %bitcast.19), channel_id=1, source_target_pairs={{2,0},{4,2},{6,4},{7,6},{5,7},{3,5},{1,3},{0,1},{10,8},{12,10},{14... | collective-permute-start | bytes 1277960 | tf_op jit(solution)/shard_map/ppermute | solution.py:36
  16.1 12.6 %collective-permute-start.2 = (f32[13,32,256]{2,1,0:T(8,128)S(1)}, f32[13,32,256]{2,1,0:T(8,128)S(1)}, u32[]{:S(2)}, u32[]{:S(2)}) collective-permute-start(f32[13,32,256]{2,1,0:T(8,128)S(1)} %collective-permute-done.refs_1_), channel_id=1, source_target_pairs={{0,2},{2,4},{4,6},{6,7},{7,5},{5,3},{3,1},{1,0},{8,10},{10,12},{12... | collective-permute-start | bytes 1277960 | tf_op jit(solution)/shard_map/ppermute | solution.py:35
  17.7 14.1 %collective-permute-start.4 = (f32[13,32,256]{2,1,0:T(8,128)S(1)}, f32[13,32,256]{2,1,0:T(8,128)S(1)}, u32[]{:S(2)}, u32[]{:S(2)}) collective-permute-start(f32[13,32,256]{2,1,0:T(8,128)S(1)} %collective-permute-done.1.refs_2_), channel_id=1, source_target_pairs={{2,0},{4,2},{6,4},{7,6},{5,7},{3,5},{1,3},{0,1},{10,8},{12,10},{14... | collective-permute-start | bytes 1277960 | tf_op jit(solution)/shard_map/ppermute | solution.py:36
  18.2 20.3 %all-to-all-start = ((f32[8,16,640]{2,1,0:T(8,128)}), f32[8,16,640]{2,1,0:T(8,128)S(1)}, u32[]{:S(2)}, u32[]{:S(2)}) async-start(f32[8,16,640]{2,1,0:T(8,128)} %bitcast.10), calls=%async_computation | async-start | bytes 655360 | tf_op jit(solution)/shard_map/all_to_all | solution.py:242
  28.8 11.2 %collective-permute-start.3 = (f32[13,32,256]{2,1,0:T(8,128)S(1)}, f32[13,32,256]{2,1,0:T(8,128)S(1)}, u32[]{:S(2)}, u32[]{:S(2)}) collective-permute-start(f32[13,32,256]{2,1,0:T(8,128)S(1)} %collective-permute-done.2.refs_3_), channel_id=1, source_target_pairs={{0,2},{2,4},{4,6},{6,7},{7,5},{5,3},{3,1},{1,0},{8,10},{10,12},{12... | collective-permute-start | bytes 1277960 | tf_op jit(solution)/shard_map/ppermute | solution.py:35
  31.8 10.4 %collective-permute-start.5 = (f32[13,32,256]{2,1,0:T(8,128)S(1)}, f32[13,32,256]{2,1,0:T(8,128)S(1)}, u32[]{:S(2)}, u32[]{:S(2)}) collective-permute-start(f32[13,32,256]{2,1,0:T(8,128)S(1)} %collective-permute-done.4.refs_4_), channel_id=1, source_target_pairs={{2,0},{4,2},{6,4},{7,6},{5,7},{3,5},{1,3},{0,1},{10,8},{12,10},{14... | collective-permute-start | bytes 1277960 | tf_op jit(solution)/shard_map/ppermute | solution.py:36
  42.2 7.4 %collective-permute-start.7 = (f32[7,32,256]{2,1,0:T(8,128)S(1)}, f32[7,32,256]{2,1,0:T(8,128)S(1)}, u32[]{:S(2)}, u32[]{:S(2)}) collective-permute-start(f32[7,32,256]{2,1,0:T(8,128)S(1)} %slice.15), channel_id=1, source_target_pairs={{2,0},{4,2},{6,4},{7,6},{5,7},{3,5},{1,3},{0,1},{10,8},{12,10},{14... | collective-permute-start | bytes 688136 | tf_op jit(solution)/shard_map/ppermute | solution.py:36
  42.3 6.6 %collective-permute-start.6 = (f32[6,32,256]{2,1,0:T(8,128)S(1)}, f32[6,32,256]{2,1,0:T(8,128)S(1)}, u32[]{:S(2)}, u32[]{:S(2)}) collective-permute-start(f32[6,32,256]{2,1,0:T(8,128)S(1)} %slice.14), channel_id=1, source_target_pairs={{0,2},{2,4},{4,6},{6,7},{7,5},{5,3},{3,1},{1,0},{8,10},{10,12},{12... | collective-permute-start | bytes 589832 | tf_op jit(solution)/shard_map/ppermute | solution.py:35
  45.7 7.6 %collective-permute-start.10 = (f32[16,256]{1,0:T(8,128)S(1)}, f32[16,256]{1,0:T(8,128)S(1)}, u32[]{:S(2)}, u32[]{:S(2)}) collective-permute-start(f32[16,256]{1,0:T(8,128)S(1)} %get-tuple-element.61.refs_4_.refs_7_.refs_9_), channel_id=1, source_target_pairs={{0,16},{8,24},{16,0},{24,8},{1,17},{9,25},{17,1},{25,9},{2,18},{10... | collective-permute-start | bytes 49160 | tf_op jit(solution)/shard_map/ppermute | solution.py:16
  47.2 6.1 %collective-permute-start.11 = (f32[16,256]{1,0:T(8,128)S(1)}, f32[16,256]{1,0:T(8,128)S(1)}, u32[]{:S(2)}, u32[]{:S(2)}) collective-permute-start(f32[16,256]{1,0:T(8,128)S(1)} %get-tuple-element.61.refs_4_.refs_7_.refs_9_), channel_id=1, source_target_pairs={{0,24},{8,16},{16,8},{24,0},{1,25},{9,17},{17,9},{25,1},{2,26},{10... | collective-permute-start | bytes 49160 | tf_op jit(solution)/shard_map/ppermute | solution.py:16
  47.2 6.1 %collective-permute-start.9 = (f32[16,256]{1,0:T(8,128)S(1)}, f32[16,256]{1,0:T(8,128)S(1)}, u32[]{:S(2)}, u32[]{:S(2)}) collective-permute-start(f32[16,256]{1,0:T(8,128)S(1)} %get-tuple-element.61.refs_4_.refs_7_.refs_9_), channel_id=1, source_target_pairs={{0,8},{8,0},{16,24},{24,16},{1,9},{9,1},{17,25},{25,17},{2,10},{10... | collective-permute-start | bytes 49160 | tf_op jit(solution)/shard_map/ppermute | solution.py:16
  52.1 1.2 %collective-permute-start.8 = (f32[16,256]{1,0:T(8,128)S(1)}, f32[16,256]{1,0:T(8,128)S(1)}, u32[]{:S(2)}, u32[]{:S(2)}) collective-permute-start(f32[16,256]{1,0:T(8,128)S(1)} %get-tuple-element.58), channel_id=1, source_target_pairs={{0,8},{8,0},{16,24},{24,16},{1,9},{9,1},{17,25},{25,17},{2,10},{10... | collective-permute-start | bytes 49160 | tf_op jit(solution)/shard_map/ppermute | solution.py:16
  54.1 1.7 %collective-permute-start.12 = (f32[16,256]{1,0:T(8,128)S(1)}, f32[16,256]{1,0:T(8,128)S(1)}, u32[]{:S(2)}, u32[]{:S(2)}) collective-permute-start(f32[16,256]{1,0:T(8,128)S(1)} %get-tuple-element.63), channel_id=1, source_target_pairs={{0,8},{8,0},{16,24},{24,16},{1,9},{9,1},{17,25},{25,17},{2,10},{10... | collective-permute-start | bytes 49160 | tf_op jit(solution)/shard_map/ppermute | solution.py:16
  56.8 3.3 %collective-permute-start.13 = (f32[16,256]{1,0:T(8,128)S(1)}, f32[16,256]{1,0:T(8,128)S(1)}, u32[]{:S(2)}, u32[]{:S(2)}) collective-permute-start(f32[16,256]{1,0:T(8,128)S(1)} %get-tuple-element.68), channel_id=1, source_target_pairs={{0,8},{8,0},{16,24},{24,16},{1,9},{9,1},{17,25},{25,17},{2,10},{10... | collective-permute-start | bytes 49160 | tf_op jit(solution)/shard_map/ppermute | solution.py:16
  56.9 3.8 %collective-permute-start.14 = (f32[16,256]{1,0:T(8,128)S(1)}, f32[16,256]{1,0:T(8,128)S(1)}, u32[]{:S(2)}, u32[]{:S(2)}) collective-permute-start(f32[16,256]{1,0:T(8,128)S(1)} %get-tuple-element.69), channel_id=1, source_target_pairs={{0,16},{8,24},{16,0},{24,8},{1,17},{9,25},{17,1},{25,9},{2,18},{10... | collective-permute-start | bytes 49160 | tf_op jit(solution)/shard_map/ppermute | solution.py:16
  58.5 3.2 %collective-permute-start.15 = (f32[16,256]{1,0:T(8,128)S(1)}, f32[16,256]{1,0:T(8,128)S(1)}, u32[]{:S(2)}, u32[]{:S(2)}) collective-permute-start(f32[16,256]{1,0:T(8,128)S(1)} %get-tuple-element.70), channel_id=1, source_target_pairs={{0,24},{8,16},{16,8},{24,0},{1,25},{9,17},{17,9},{25,1},{2,26},{10... | collective-permute-start | bytes 49160 | tf_op jit(solution)/shard_map/ppermute | solution.py:16
  62.6 1.9 %collective-permute-start.16 = (f32[4,16,256]{2,1,0:T(8,128)S(1)}, f32[4,16,256]{2,1,0:T(8,128)S(1)}, u32[]{:S(2)}, u32[]{:S(2)}) collective-permute-start(f32[4,16,256]{2,1,0:T(8,128)S(1)} %shard_map.113.refs_0_), channel_id=1, source_target_pairs={{0,8},{8,0},{16,24},{24,16},{1,9},{9,1},{17,25},{25,17},{2,10},{10... | collective-permute-start | bytes 196616 | tf_op jit(solution)/shard_map/ppermute | solution.py:16
  62.8 4.9 %collective-permute-start.17 = (f32[4,16,256]{2,1,0:T(8,128)S(1)}, f32[4,16,256]{2,1,0:T(8,128)S(1)}, u32[]{:S(2)}, u32[]{:S(2)}) collective-permute-start(f32[4,16,256]{2,1,0:T(8,128)S(1)} %shard_map.113.refs_0_), channel_id=1, source_target_pairs={{0,16},{8,24},{16,0},{24,8},{1,17},{9,25},{17,1},{25,9},{2,18},{10... | collective-permute-start | bytes 196616 | tf_op jit(solution)/shard_map/ppermute | solution.py:16
  63.5 4.5 %collective-permute-start.18 = (f32[4,16,256]{2,1,0:T(8,128)S(1)}, f32[4,16,256]{2,1,0:T(8,128)S(1)}, u32[]{:S(2)}, u32[]{:S(2)}) collective-permute-start(f32[4,16,256]{2,1,0:T(8,128)S(1)} %shard_map.113.refs_0_), channel_id=1, source_target_pairs={{0,24},{8,16},{16,8},{24,0},{1,25},{9,17},{17,9},{25,1},{2,26},{10... | collective-permute-start | bytes 196616 | tf_op jit(solution)/shard_map/ppermute | solution.py:16
  68.8 1.9 %collective-permute-start.19 = (f32[16,256]{1,0:T(8,128)S(1)}, f32[16,256]{1,0:T(8,128)S(1)}, u32[]{:S(2)}, u32[]{:S(2)}) collective-permute-start(f32[16,256]{1,0:T(8,128)S(1)} %shard_map.114.refs_0_.refs_2_), channel_id=1, source_target_pairs={{0,8},{8,0},{16,24},{24,16},{1,9},{9,1},{17,25},{25,17},{2,10},{10... | collective-permute-start | bytes 49160 | tf_op jit(solution)/shard_map/ppermute | solution.py:16
  69.2 3.7 %collective-permute-start.20 = (f32[16,256]{1,0:T(8,128)S(1)}, f32[16,256]{1,0:T(8,128)S(1)}, u32[]{:S(2)}, u32[]{:S(2)}) collective-permute-start(f32[16,256]{1,0:T(8,128)S(1)} %shard_map.114.refs_0_.refs_2_), channel_id=1, source_target_pairs={{0,16},{8,24},{16,0},{24,8},{1,17},{9,25},{17,1},{25,9},{2,18},{10... | collective-permute-start | bytes 49160 | tf_op jit(solution)/shard_map/ppermute | solution.py:16
  70.1 3.2 %collective-permute-start.21 = (f32[16,256]{1,0:T(8,128)S(1)}, f32[16,256]{1,0:T(8,128)S(1)}, u32[]{:S(2)}, u32[]{:S(2)}) collective-permute-start(f32[16,256]{1,0:T(8,128)S(1)} %shard_map.114.refs_0_.refs_2_), channel_id=1, source_target_pairs={{0,24},{8,16},{16,8},{24,0},{1,25},{9,17},{17,9},{25,1},{2,26},{10... | collective-permute-start | bytes 49160 | tf_op jit(solution)/shard_map/ppermute | solution.py:16
  74.1 1.2 %collective-permute-start.22 = (f32[16,256]{1,0:T(8,128)S(1)}, f32[16,256]{1,0:T(8,128)S(1)}, u32[]{:S(2)}, u32[]{:S(2)}) collective-permute-start(f32[16,256]{1,0:T(8,128)S(1)} %shard_map.115.refs_0_), channel_id=1, source_target_pairs={{0,8},{8,0},{16,24},{24,16},{1,9},{9,1},{17,25},{25,17},{2,10},{10... | collective-permute-start | bytes 49160 | tf_op jit(solution)/shard_map/ppermute | solution.py:16
  75.3 18.7 %copy-start.3 = (f32[1,1,512,512]{3,2,1,0:T(8,128)S(1)}, f32[1,1,512,512]{3,2,1,0:T(8,128)}, u32[]{:S(2)}) copy-start(f32[1,1,512,512]{3,2,1,0:T(8,128)} %param.11) | copy-start | bytes 3145732
  76.0 17.9 %copy-start.1 = (f32[1,1,512,512]{3,2,1,0:T(8,128)S(1)}, f32[1,1,512,512]{3,2,1,0:T(8,128)}, u32[]{:S(2)}) copy-start(f32[1,1,512,512]{3,2,1,0:T(8,128)} %param.10) | copy-start | bytes 3145732
  76.0 1.2 %collective-permute-start.23 = (f32[16,256]{1,0:T(8,128)S(1)}, f32[16,256]{1,0:T(8,128)S(1)}, u32[]{:S(2)}, u32[]{:S(2)}) collective-permute-start(f32[16,256]{1,0:T(8,128)S(1)} %shard_map.116.refs_0_), channel_id=1, source_target_pairs={{0,8},{8,0},{16,24},{24,16},{1,9},{9,1},{17,25},{25,17},{2,10},{10... | collective-permute-start | bytes 49160 | tf_op jit(solution)/shard_map/ppermute | solution.py:16
  78.3 15.7 %copy-start.8 = (f32[128,512]{1,0:T(8,128)S(1)}, f32[128,512]{1,0:T(8,128)}, u32[]{:S(2)}) copy-start(f32[128,512]{1,0:T(8,128)} %copy-done.7) | copy-start | bytes 786436
  (4 other events, 3.8 us)

commit v12 on v11

--- a/solution.py
+++ b/solution.py
@@ -281,9 +281,9 @@
             (ids, known),
             [pltpu.VMEM((path_tiles, share, TILE), F32)],
         )
-        return known, rest, pivots
-
-    parts, (known, rest, pivots) = ring_gather(
+        return known, rest, leaf_swaps([pivots] * leaves)
+
+    parts, (known, rest, all_pivots) = ring_gather(
         jnp.concatenate([win_inverse[0], win_coupling[0]], 0).reshape(-1, piece, base),
         ranks,
         terms,
@@ -294,7 +294,7 @@
         if name not in blocks:
             blocks.update(assemble([name]))
 
-    all_pivots = leaf_swaps([pivots] * leaves)
+    pivots = all_pivots[0]
 
     def total(refs):
         value = refs[0][0] if len(refs[0].shape) > len(wide) and len(refs) == 1 else refs[0][...]

time: 97 us -> 97.5 us (level)
  waiting for transfers between devices: 31.9 us -> 35.6 us
  blocking collectives: 15.7 us -> 14 us
  starting transfers between devices: 25.2 us -> 23.7 us
    ppermute x4, waiting for transfers between devices: 11.2 us -> 14.7 us  [ring_gather(): forward = lax.ppermute(forward, 'row', right)]
    ppermute x16, waiting for transfers between devices: 9.7 us -> 12.4 us  [swap(): return lax.ppermute(value, axis, [(i, i ^ offset) for i in range(count)])]
    ppermute x4, waiting for transfers between devices: 4.44 us -> 1.94 us  [ring_gather(): backward = lax.ppermute(backward, 'row', left)]
    ppermute x4, starting transfers between devices: 11.1 us -> 9.28 us  [ring_gather(): forward = lax.ppermute(forward, 'row', right)]
    all_to_all x1, blocking collectives: 15.7 us -> 14 us  [shards(): lax.all_to_all(replies[0], 'row', 0, 0, tiled=True).reshape(columns, packed)]
  transfers between devices with their start and end apart: 25 -> 25, of which waited for: 16 -> 16; matrix products, arithmetic and copies ran while one was open for 1% -> 1% of each run, Pallas kernels for 10% -> 7%
where the time goes in v12:
time: 97.5 us; the launch traced here: 97.1 us
  waiting for transfers between devices  35.6 us (37%)
  starting transfers between devices  23.7 us (24%)
  Pallas kernels  17.5 us (18%)
  blocking collectives  14 us (14%)
  local copies, waits for them, and re-layouts  4.27 us (4%)
  other arithmetic  1.19 us (1%)
    pallas_call x15, Pallas kernels, call(): pl.pallas_call(body, out_shape=[jax.ShapeDtypeStruct(*o) for o in outs],...  17.5 us
    ppermute x4, waiting for transfers between devices, ring_gather(): forward = lax.ppermute(forward, 'row', right)  14.7 us
    all_to_all x1, blocking collectives, shards(): lax.all_to_all(replies[0], 'row', 0, 0, tiled=True).reshape(columns, packed)  14 us
    ppermute x16, waiting for transfers between devices, swap(): return lax.ppermute(value, axis, [(i, i ^ offset) for i in range(count)])  12.4 us
    ppermute x4, starting transfers between devices, ring_gather(): forward = lax.ppermute(forward, 'row', right)  9.28 us
    ppermute x16, starting transfers between devices, swap(): return lax.ppermute(value, axis, [(i, i ^ offset) for i in range(count)])  8.54 us
    all_to_all x1, waiting for transfers between devices, place_terms(): lax.all_to_all(terms.reshape(ranks, share, packed), 'row', 0, 0, tiled=True)  6.62 us
    all_to_all x1, starting transfers between devices, place_terms(): lax.all_to_all(terms.reshape(ranks, share, packed), 'row', 0, 0, tiled=True)  4.82 us
  transfers between devices with their start and end apart: 25, of which 16 were waited for; matrix products, arithmetic and copies ran while one was open for 1% of the time, Pallas kernels for 7%

profile of v12, /device:TPU:0, one launch (start us, length us, event | category | flops | bytes accessed | tf_op | source)
XLA Modules:
  0.0 97.1 jit_solution(2074015402937392795)
XLA Ops:
  0.7 1.1 %pad_maximum_fusion = f32[416,256]{1,0:T(8,128)S(1)} fusion(f32[192,256]{1,0:T(8,128)} %bitcast.33, f32[224,256]{1,0:T(8,128)} %bitcast.32), kind=kLoop, calls=%fused_computation | loop fusion | flops 106496 | bytes 851968 | tf_op jit(solution)/shard_map/concatenate | solution.py:287
  1.8 3.1 %collective-permute-start = (f32[13,32,256]{2,1,0:T(8,128)S(1)}, f32[13,32,256]{2,1,0:T(8,128)S(1)}, u32[]{:S(2)}, u32[]{:S(2)}) collective-permute-start(f32[13,32,256]{2,1,0:T(8,128)S(1)} %bitcast.18), channel_id=1, source_target_pairs={{0,2},{2,4},{4,6},{6,7},{7,5},{5,3},{3,1},{1,0},{8,10},{10,12},{12... | collective-permute-start | bytes 1277960 | tf_op jit(solution)/shard_map/ppermute | solution.py:35
  5.2 1.2 %copy-done = f32[1,1,512,512]{3,2,1,0:T(8,128)S(1)} copy-done((f32[1,1,512,512]{3,2,1,0:T(8,128)S(1)}, f32[1,1,512,512]{3,2,1,0:T(8,128)}, u32[]{:S(2)}) %copy-start) | copy-done | bytes 1048600
  6.5 1.2 %copy-done.2 = f32[1,1,512,512]{3,2,1,0:T(8,128)S(1)} copy-done((f32[1,1,512,512]{3,2,1,0:T(8,128)S(1)}, f32[1,1,512,512]{3,2,1,0:T(8,128)}, u32[]{:S(2)}) %copy-start.2) | copy-done | bytes 1048600
  7.7 2.5 %shard_map.104 = (f32[128,512]{1,0:T(8,128)S(1)}, f32[128,640]{1,0:T(8,128)}) custom-call(f32[512,128]{1,0:T(8,128)S(1)} %bitcast.30, f32[3,32,128]{2,1,0:T(8,128)S(1)} %copy-done.5, f32[128,128]{1,0:T(8,128)S(1)} %bitcast.25, f32[512,512]{1,0:T(8,128)S(1)} %bitcast.26, f32[512,512]{1,0:T(8,128)S(1)} %bitcast.28), custom_call_target="tpu_custom_call" | custom-call | flops 805306368 | bytes 3063808 | tf_op jit(solution)/shard_map/pallas_call | solution.py:47
  10.9 3.7 %collective-permute-done.refs_1_ = f32[13,32,256]{2,1,0:T(8,128)S(1)} collective-permute-done((f32[13,32,256]{2,1,0:T(8,128)S(1)}, f32[13,32,256]{2,1,0:T(8,128)S(1)}, u32[]{:S(2)}, u32[]{:S(2)}) %collective-permute-start) | collective-permute-done | bytes 426016 | tf_op jit(solution)/shard_map/ppermute | solution.py:35
  14.6 1.5 %collective-permute-done.1.refs_2_ = f32[13,32,256]{2,1,0:T(8,128)S(1)} collective-permute-done((f32[13,32,256]{2,1,0:T(8,128)S(1)}, f32[13,32,256]{2,1,0:T(8,128)S(1)}, u32[]{:S(2)}, u32[]{:S(2)}) %collective-permute-start.1) | collective-permute-done | bytes 426016 | tf_op jit(solution)/shard_map/ppermute | solution.py:36
  16.1 1.6 %collective-permute-start.2 = (f32[13,32,256]{2,1,0:T(8,128)S(1)}, f32[13,32,256]{2,1,0:T(8,128)S(1)}, u32[]{:S(2)}, u32[]{:S(2)}) collective-permute-start(f32[13,32,256]{2,1,0:T(8,128)S(1)} %collective-permute-done.refs_1_), channel_id=1, source_target_pairs={{0,2},{2,4},{4,6},{6,7},{7,5},{5,3},{3,1},{1,0},{8,10},{10,12},{12... | collective-permute-start | bytes 1277960 | tf_op jit(solution)/shard_map/ppermute | solution.py:35
  18.2 4.8 %all-to-all-start = ((f32[8,16,640]{2,1,0:T(8,128)}), f32[8,16,640]{2,1,0:T(8,128)S(1)}, u32[]{:S(2)}, u32[]{:S(2)}) async-start(f32[8,16,640]{2,1,0:T(8,128)} %bitcast.10), calls=%async_computation | async-start | bytes 655360 | tf_op jit(solution)/shard_map/all_to_all | solution.py:242
  23.0 5.8 %collective-permute-done.2.refs_3_ = f32[13,32,256]{2,1,0:T(8,128)S(1)} collective-permute-done((f32[13,32,256]{2,1,0:T(8,128)S(1)}, f32[13,32,256]{2,1,0:T(8,128)S(1)}, u32[]{:S(2)}, u32[]{:S(2)}) %collective-permute-start.2) | collective-permute-done | bytes 426016 | tf_op jit(solution)/shard_map/ppermute | solution.py:35
  28.8 3.1 %collective-permute-start.3 = (f32[13,32,256]{2,1,0:T(8,128)S(1)}, f32[13,32,256]{2,1,0:T(8,128)S(1)}, u32[]{:S(2)}, u32[]{:S(2)}) collective-permute-start(f32[13,32,256]{2,1,0:T(8,128)S(1)} %collective-permute-done.2.refs_3_), channel_id=1, source_target_pairs={{0,2},{2,4},{4,6},{6,7},{7,5},{5,3},{3,1},{1,0},{8,10},{10,12},{12... | collective-permute-start | bytes 1277960 | tf_op jit(solution)/shard_map/ppermute | solution.py:35
  31.9 6.6 %all-to-all-done.terms_ref = f32[8,16,640]{2,1,0:T(8,128)S(1)} async-done(((f32[8,16,640]{2,1,0:T(8,128)}), f32[8,16,640]{2,1,0:T(8,128)S(1)}, u32[]{:S(2)}, u32[]{:S(2)}) %all-to-all-start) | async-done | bytes 327712 | tf_op jit(solution)/shard_map/all_to_all | solution.py:242
  39.4 1.6 %collective-permute-start.7 = (f32[16,256]{1,0:T(8,128)S(1)}, f32[16,256]{1,0:T(8,128)S(1)}, u32[]{:S(2)}, u32[]{:S(2)}) collective-permute-start(f32[16,256]{1,0:T(8,128)S(1)} %get-tuple-element.64.refs_4_.refs_7_.refs_9_), channel_id=1, source_target_pairs={{0,16},{8,24},{16,0},{24,8},{1,17},{9,25},{17,1},{25,9},{2,18},{10... | collective-permute-start | bytes 49160 | tf_op jit(solution)/shard_map/ppermute | solution.py:16
  41.3 1.9 %collective-permute-done.7.refs_6_ = f32[16,256]{1,0:T(8,128)S(1)} collective-permute-done((f32[16,256]{1,0:T(8,128)S(1)}, f32[16,256]{1,0:T(8,128)S(1)}, u32[]{:S(2)}, u32[]{:S(2)}) %collective-permute-start.7) | collective-permute-done | bytes 16416 | tf_op jit(solution)/shard_map/ppermute | solution.py:16
  44.7 1.6 %collective-permute-start.9 = (f32[6,32,256]{2,1,0:T(8,128)S(1)}, f32[6,32,256]{2,1,0:T(8,128)S(1)}, u32[]{:S(2)}, u32[]{:S(2)}) collective-permute-start(f32[6,32,256]{2,1,0:T(8,128)S(1)} %slice.14), channel_id=1, source_target_pairs={{0,2},{2,4},{4,6},{6,7},{7,5},{5,3},{3,1},{1,0},{8,10},{10,12},{12... | collective-permute-start | bytes 589832 | tf_op jit(solution)/shard_map/ppermute | solution.py:35
  46.3 5.2 %collective-permute-done.9.refs_7_ = f32[6,32,256]{2,1,0:T(8,128)S(1)} collective-permute-done((f32[6,32,256]{2,1,0:T(8,128)S(1)}, f32[6,32,256]{2,1,0:T(8,128)S(1)}, u32[]{:S(2)}, u32[]{:S(2)}) %collective-permute-start.9) | collective-permute-done | bytes 196640 | tf_op jit(solution)/shard_map/ppermute | solution.py:35
  51.9 1.6 %shard_map.106 = (bf16[1,256,256]{2,1,0:T(8,128)(2,1)S(1)}, bf16[1,256,256]{2,1,0:T(8,128)(2,1)S(1)}, bf16[2,256,256]{2,1,0:T(8,128)(2,1)S(1)}, bf16[2,256,256]{2,1,0:T(8,128)(2,1)S(1)}) custom-call(s32[2]{0:T(128)S(1)} %pad_add_fusion.ids_ref, f32[13,32,256]{2,1,0:T(8,128)S(1)} %bitcast.20, f32[13,32,256]{2,1,0:T(8,128)S(1)} %collective-permute-done.refs_1_, ...), custom_call_target="tpu_custom_call" | custom-call | bytes 4194304 | tf_op jit(solution)/shard_map/pallas_call | solution.py:47
  54.4 1.1 %shard_map.108 = (bf16[2,256,256]{2,1,0:T(8,128)(2,1)S(1)}, bf16[2,256,256]{2,1,0:T(8,128)(2,1)S(1)}) custom-call(s32[2]{0:T(128)S(1)} %pad_add_fusion.ids_ref, f32[13,32,256]{2,1,0:T(8,128)S(1)} %bitcast.21, f32[13,32,256]{2,1,0:T(8,128)S(1)} %collective-permute-done.refs_1_, f32[13,32,256]{2,1,0:T(8,128)S(1)} %collective-permute-done.1.refs_2_, ...), custom_call_target="tpu_custom_call" | custom-call | bytes 3932160 | tf_op jit(solution)/shard_map/pallas_call | solution.py:47
  56.9 1.2 %shard_map.110 = (bf16[4,256,256]{2,1,0:T(8,128)(2,1)S(1)}, bf16[4,256,256]{2,1,0:T(8,128)(2,1)S(1)}) custom-call(s32[2]{0:T(128)S(1)} %pad_add_fusion.ids_ref, f32[13,32,256]{2,1,0:T(8,128)S(1)} %bitcast.22, f32[13,32,256]{2,1,0:T(8,128)S(1)} %collective-permute-done.refs_1_, f32[13,32,256]{2,1,0:T(8,128)S(1)} %collective-permute-done.1.refs_2_, ...), custom_call_target="tpu_custom_call" | custom-call | bytes 4456448 | tf_op jit(solution)/shard_map/pallas_call | solution.py:47
  59.9 1.1 %collective-permute-start.15 = (f32[16,256]{1,0:T(8,128)S(1)}, f32[16,256]{1,0:T(8,128)S(1)}, u32[]{:S(2)}, u32[]{:S(2)}) collective-permute-start(f32[16,256]{1,0:T(8,128)S(1)} %get-tuple-element.76), channel_id=1, source_target_pairs={{0,24},{8,16},{16,8},{24,0},{1,25},{9,17},{17,9},{25,1},{2,26},{10... | collective-permute-start | bytes 49160 | tf_op jit(solution)/shard_map/ppermute | solution.py:16
  61.0 1.3 %shard_map.112 = (bf16[4,256,256]{2,1,0:T(8,128)(2,1)S(1)}, bf16[4,256,256]{2,1,0:T(8,128)(2,1)S(1)}) custom-call(s32[2]{0:T(128)S(1)} %pad_add_fusion.ids_ref, f32[13,32,256]{2,1,0:T(8,128)S(1)} %bitcast.23, f32[13,32,256]{2,1,0:T(8,128)S(1)} %collective-permute-done.refs_1_, f32[13,32,256]{2,1,0:T(8,128)S(1)} %collective-permute-done.1.refs_2_, ...), custom_call_target="tpu_custom_call" | custom-call | bytes 4456448 | tf_op jit(solution)/shard_map/pallas_call | solution.py:47
  63.2 1.0 shard_map.113.refs_0_
  64.3 1.3 %collective-permute-start.17 = (f32[4,16,256]{2,1,0:T(8,128)S(1)}, f32[4,16,256]{2,1,0:T(8,128)S(1)}, u32[]{:S(2)}, u32[]{:S(2)}) collective-permute-start(f32[4,16,256]{2,1,0:T(8,128)S(1)} %shard_map.113.refs_0_), channel_id=1, source_target_pairs={{0,16},{8,24},{16,0},{24,8},{1,17},{9,25},{17,1},{25,9},{2,18},{10... | collective-permute-start | bytes 196616 | tf_op jit(solution)/shard_map/ppermute | solution.py:16
  66.0 2.8 %collective-permute-done.17.refs_2_ = f32[4,16,256]{2,1,0:T(8,128)S(1)} collective-permute-done((f32[4,16,256]{2,1,0:T(8,128)S(1)}, f32[4,16,256]{2,1,0:T(8,128)S(1)}, u32[]{:S(2)}, u32[]{:S(2)}) %collective-permute-start.17) | collective-permute-done | bytes 65568 | tf_op jit(solution)/shard_map/ppermute | solution.py:16
  68.8 1.1 %collective-permute-done.18.refs_3_ = f32[4,16,256]{2,1,0:T(8,128)S(1)} collective-permute-done((f32[4,16,256]{2,1,0:T(8,128)S(1)}, f32[4,16,256]{2,1,0:T(8,128)S(1)}, u32[]{:S(2)}, u32[]{:S(2)}) %collective-permute-start.18) | collective-permute-done | bytes 65568 | tf_op jit(solution)/shard_map/ppermute | solution.py:16
  70.9 1.2 %collective-permute-start.20 = (f32[16,256]{1,0:T(8,128)S(1)}, f32[16,256]{1,0:T(8,128)S(1)}, u32[]{:S(2)}, u32[]{:S(2)}) collective-permute-start(f32[16,256]{1,0:T(8,128)S(1)} %shard_map.114.refs_0_.refs_2_), channel_id=1, source_target_pairs={{0,16},{8,24},{16,0},{24,8},{1,17},{9,25},{17,1},{25,9},{2,18},{10... | collective-permute-start | bytes 49160 | tf_op jit(solution)/shard_map/ppermute | solution.py:16
  72.6 2.0 %collective-permute-done.20.refs_2_.refs_4_ = f32[16,256]{1,0:T(8,128)S(1)} collective-permute-done((f32[16,256]{1,0:T(8,128)S(1)}, f32[16,256]{1,0:T(8,128)S(1)}, u32[]{:S(2)}, u32[]{:S(2)}) %collective-permute-start.20) | collective-permute-done | bytes 16416 | tf_op jit(solution)/shard_map/ppermute | solution.py:16
  76.3 1.1 %collective-permute-done.22.refs_1_ = f32[16,256]{1,0:T(8,128)S(1)} collective-permute-done((f32[16,256]{1,0:T(8,128)S(1)}, f32[16,256]{1,0:T(8,128)S(1)}, u32[]{:S(2)}, u32[]{:S(2)}) %collective-permute-start.22) | collective-permute-done | bytes 16416 | tf_op jit(solution)/shard_map/ppermute | solution.py:16
  78.3 1.0 %collective-permute-done.23.refs_1_ = f32[16,256]{1,0:T(8,128)S(1)} collective-permute-done((f32[16,256]{1,0:T(8,128)S(1)}, f32[16,256]{1,0:T(8,128)S(1)}, u32[]{:S(2)}, u32[]{:S(2)}) %collective-permute-start.23) | collective-permute-done | bytes 16416 | tf_op jit(solution)/shard_map/ppermute | solution.py:16
  79.3 1.1 %shard_map.117 = f32[8,16,640]{2,1,0:T(8,128)S(1)} custom-call(s32[2]{0:T(128)S(1)} %pad_add_fusion.ids_ref, s32[8,4]{1,0:T(8,128)S(1)} %slice_convert_fusion.known_ref, f32[16,256]{1,0:T(8,128)S(1)} %shard_map.116.refs_0_, f32[16,256]{1,0:T(8,128)S(1)} %collective-permute-done.23.refs_1_, f32[16,256]{1,0:T(8,128)S(1)} %shard_map.114.refs_0_.refs_2_, ...), custom_call_target="tpu_custom_call" | custom-call | bytes 1245184 | tf_op jit(solution)/shard_map/pallas_call | solution.py:47
  80.4 14.0 %all_to_all.10 = f32[8,16,640]{2,1,0:T(8,128)S(1)} all-to-all(f32[8,16,640]{2,1,0:T(8,128)S(1)} %shard_map.117), channel_id=1, replica_groups=mesh['leaf'=4,'row'=8] {'row'}, dimensions={0} | all-to-all | bytes 655360 | tf_op jit(solution)/shard_map/all_to_all | solution.py:485
  95.1 2.0 %shard_map.118 = (f32[512,128]{1,0:T(8,128)}, f32[3,32,128]{2,1,0:T(8,128)}) custom-call(f32[128,640]{1,0:T(8,128)S(1)} %bitcast.24, f32[128,512]{1,0:T(8,128)S(1)} %copy-done.8, f32[1,512]{1,0:T(1,128)S(1)} %bitcast.31, f32[512,512]{1,0:T(8,128)S(1)} %bitcast.27, f32[512,512]{1,0:T(8,128)S(1)} %bitcast.29), custom_call_target="tpu_custom_call" | custom-call | flops 805306368 | bytes 3000320 | tf_op jit(solution)/shard_map/pallas_call | solution.py:47
  (66 shorter events, 14.9 us)
Async XLA Ops:
  0.6 4.2 %copy-start.9 = (f32[3,32]{1,0:T(4,128)S(1)}, f32[3,32]{1,0:T(4,128)}, u32[]{:S(2)}) copy-start(f32[3,32]{1,0:T(4,128)} %param.15) | copy-start | bytes 1156
  0.6 4.3 %copy-start.10 = (s32[1,1,4]{2,1,0:T(1,128)S(1)}, s32[1,1,4]{2,1,0:T(1,128)}, u32[]{:S(2)}) copy-start(s32[1,1,4]{2,1,0:T(1,128)} %param.13) | copy-start | bytes 52
  0.7 4.6 %copy-start.4 = (f32[1,1,512,128]{3,2,1,0:T(8,128)S(1)}, f32[1,1,512,128]{3,2,1,0:T(8,128)}, u32[]{:S(2)}) copy-start(f32[1,1,512,128]{3,2,1,0:T(8,128)} %param.9) | copy-start | bytes 786436
  1.8 3.4 %copy-start.5 = (f32[3,32,128]{2,1,0:T(8,128)S(1)}, f32[3,32,128]{2,1,0:T(8,128)}, u32[]{:S(2)}) copy-start(f32[3,32,128]{2,1,0:T(8,128)} %window_ref.1) | copy-start | bytes 147460
  1.8 12.8 %collective-permute-start = (f32[13,32,256]{2,1,0:T(8,128)S(1)}, f32[13,32,256]{2,1,0:T(8,128)S(1)}, u32[]{:S(2)}, u32[]{:S(2)}) collective-permute-start(f32[13,32,256]{2,1,0:T(8,128)S(1)} %bitcast.18), channel_id=1, source_target_pairs={{0,2},{2,4},{4,6},{6,7},{7,5},{5,3},{3,1},{1,0},{8,10},{10,12},{12... | collective-permute-start | bytes 1277960 | tf_op jit(solution)/shard_map/ppermute | solution.py:35
  4.9 11.3 %collective-permute-start.1 = (f32[13,32,256]{2,1,0:T(8,128)S(1)}, f32[13,32,256]{2,1,0:T(8,128)S(1)}, u32[]{:S(2)}, u32[]{:S(2)}) collective-permute-start(f32[13,32,256]{2,1,0:T(8,128)S(1)} %bitcast.19), channel_id=1, source_target_pairs={{2,0},{4,2},{6,4},{7,6},{5,7},{3,5},{1,3},{0,1},{10,8},{12,10},{14... | collective-permute-start | bytes 1277960 | tf_op jit(solution)/shard_map/ppermute | solution.py:36
  16.1 12.6 %collective-permute-start.2 = (f32[13,32,256]{2,1,0:T(8,128)S(1)}, f32[13,32,256]{2,1,0:T(8,128)S(1)}, u32[]{:S(2)}, u32[]{:S(2)}) collective-permute-start(f32[13,32,256]{2,1,0:T(8,128)S(1)} %collective-permute-done.refs_1_), channel_id=1, source_target_pairs={{0,2},{2,4},{4,6},{6,7},{7,5},{5,3},{3,1},{1,0},{8,10},{10,12},{12... | collective-permute-start | bytes 1277960 | tf_op jit(solution)/shard_map/ppermute | solution.py:35
  17.7 14.1 %collective-permute-start.4 = (f32[13,32,256]{2,1,0:T(8,128)S(1)}, f32[13,32,256]{2,1,0:T(8,128)S(1)}, u32[]{:S(2)}, u32[]{:S(2)}) collective-permute-start(f32[13,32,256]{2,1,0:T(8,128)S(1)} %collective-permute-done.1.refs_2_), channel_id=1, source_target_pairs={{2,0},{4,2},{6,4},{7,6},{5,7},{3,5},{1,3},{0,1},{10,8},{12,10},{14... | collective-permute-start | bytes 1277960 | tf_op jit(solution)/shard_map/ppermute | solution.py:36
  18.2 20.3 %all-to-all-start = ((f32[8,16,640]{2,1,0:T(8,128)}), f32[8,16,640]{2,1,0:T(8,128)S(1)}, u32[]{:S(2)}, u32[]{:S(2)}) async-start(f32[8,16,640]{2,1,0:T(8,128)} %bitcast.10), calls=%async_computation | async-start | bytes 655360 | tf_op jit(solution)/shard_map/all_to_all | solution.py:242
  28.8 15.4 %collective-permute-start.3 = (f32[13,32,256]{2,1,0:T(8,128)S(1)}, f32[13,32,256]{2,1,0:T(8,128)S(1)}, u32[]{:S(2)}, u32[]{:S(2)}) collective-permute-start(f32[13,32,256]{2,1,0:T(8,128)S(1)} %collective-permute-done.2.refs_3_), channel_id=1, source_target_pairs={{0,2},{2,4},{4,6},{6,7},{7,5},{5,3},{3,1},{1,0},{8,10},{10,12},{12... | collective-permute-start | bytes 1277960 | tf_op jit(solution)/shard_map/ppermute | solution.py:35
  31.8 12.3 %collective-permute-start.5 = (f32[13,32,256]{2,1,0:T(8,128)S(1)}, f32[13,32,256]{2,1,0:T(8,128)S(1)}, u32[]{:S(2)}, u32[]{:S(2)}) collective-permute-start(f32[13,32,256]{2,1,0:T(8,128)S(1)} %collective-permute-done.4.refs_4_), channel_id=1, source_target_pairs={{2,0},{4,2},{6,4},{7,6},{5,7},{3,5},{1,3},{0,1},{10,8},{12,10},{14... | collective-permute-start | bytes 1277960 | tf_op jit(solution)/shard_map/ppermute | solution.py:36
  39.3 1.9 %collective-permute-start.6 = (f32[16,256]{1,0:T(8,128)S(1)}, f32[16,256]{1,0:T(8,128)S(1)}, u32[]{:S(2)}, u32[]{:S(2)}) collective-permute-start(f32[16,256]{1,0:T(8,128)S(1)} %get-tuple-element.64.refs_4_.refs_7_.refs_9_), channel_id=1, source_target_pairs={{0,8},{8,0},{16,24},{24,16},{1,9},{9,1},{17,25},{25,17},{2,10},{10... | collective-permute-start | bytes 49160 | tf_op jit(solution)/shard_map/ppermute | solution.py:16
  39.4 3.8 %collective-permute-start.7 = (f32[16,256]{1,0:T(8,128)S(1)}, f32[16,256]{1,0:T(8,128)S(1)}, u32[]{:S(2)}, u32[]{:S(2)}) collective-permute-start(f32[16,256]{1,0:T(8,128)S(1)} %get-tuple-element.64.refs_4_.refs_7_.refs_9_), channel_id=1, source_target_pairs={{0,16},{8,24},{16,0},{24,8},{1,17},{9,25},{17,1},{25,9},{2,18},{10... | collective-permute-start | bytes 49160 | tf_op jit(solution)/shard_map/ppermute | solution.py:16
  41.0 3.2 %collective-permute-start.8 = (f32[16,256]{1,0:T(8,128)S(1)}, f32[16,256]{1,0:T(8,128)S(1)}, u32[]{:S(2)}, u32[]{:S(2)}) collective-permute-start(f32[16,256]{1,0:T(8,128)S(1)} %get-tuple-element.64.refs_4_.refs_7_.refs_9_), channel_id=1, source_target_pairs={{0,24},{8,16},{16,8},{24,0},{1,25},{9,17},{17,9},{25,1},{2,26},{10... | collective-permute-start | bytes 49160 | tf_op jit(solution)/shard_map/ppermute | solution.py:16
  44.2 7.7 %collective-permute-start.10 = (f32[7,32,256]{2,1,0:T(8,128)S(1)}, f32[7,32,256]{2,1,0:T(8,128)S(1)}, u32[]{:S(2)}, u32[]{:S(2)}) collective-permute-start(f32[7,32,256]{2,1,0:T(8,128)S(1)} %slice.15), channel_id=1, source_target_pairs={{2,0},{4,2},{6,4},{7,6},{5,7},{3,5},{1,3},{0,1},{10,8},{12,10},{14... | collective-permute-start | bytes 688136 | tf_op jit(solution)/shard_map/ppermute | solution.py:36
  44.7 6.7 %collective-permute-start.9 = (f32[6,32,256]{2,1,0:T(8,128)S(1)}, f32[6,32,256]{2,1,0:T(8,128)S(1)}, u32[]{:S(2)}, u32[]{:S(2)}) collective-permute-start(f32[6,32,256]{2,1,0:T(8,128)S(1)} %slice.14), channel_id=1, source_target_pairs={{0,2},{2,4},{4,6},{6,7},{7,5},{5,3},{3,1},{1,0},{8,10},{10,12},{12... | collective-permute-start | bytes 589832 | tf_op jit(solution)/shard_map/ppermute | solution.py:35
  54.4 1.2 %collective-permute-start.11 = (f32[16,256]{1,0:T(8,128)S(1)}, f32[16,256]{1,0:T(8,128)S(1)}, u32[]{:S(2)}, u32[]{:S(2)}) collective-permute-start(f32[16,256]{1,0:T(8,128)S(1)} %get-tuple-element.61), channel_id=1, source_target_pairs={{0,8},{8,0},{16,24},{24,16},{1,9},{9,1},{17,25},{25,17},{2,10},{10... | collective-permute-start | bytes 49160 | tf_op jit(solution)/shard_map/ppermute | solution.py:16
  56.4 1.7 %collective-permute-start.12 = (f32[16,256]{1,0:T(8,128)S(1)}, f32[16,256]{1,0:T(8,128)S(1)}, u32[]{:S(2)}, u32[]{:S(2)}) collective-permute-start(f32[16,256]{1,0:T(8,128)S(1)} %get-tuple-element.69), channel_id=1, source_target_pairs={{0,8},{8,0},{16,24},{24,16},{1,9},{9,1},{17,25},{25,17},{2,10},{10... | collective-permute-start | bytes 49160 | tf_op jit(solution)/shard_map/ppermute | solution.py:16
  59.1 3.3 %collective-permute-start.13 = (f32[16,256]{1,0:T(8,128)S(1)}, f32[16,256]{1,0:T(8,128)S(1)}, u32[]{:S(2)}, u32[]{:S(2)}) collective-permute-start(f32[16,256]{1,0:T(8,128)S(1)} %get-tuple-element.74), channel_id=1, source_target_pairs={{0,8},{8,0},{16,24},{24,16},{1,9},{9,1},{17,25},{25,17},{2,10},{10... | collective-permute-start | bytes 49160 | tf_op jit(solution)/shard_map/ppermute | solution.py:16
  59.2 3.9 %collective-permute-start.14 = (f32[16,256]{1,0:T(8,128)S(1)}, f32[16,256]{1,0:T(8,128)S(1)}, u32[]{:S(2)}, u32[]{:S(2)}) collective-permute-start(f32[16,256]{1,0:T(8,128)S(1)} %get-tuple-element.75), channel_id=1, source_target_pairs={{0,16},{8,24},{16,0},{24,8},{1,17},{9,25},{17,1},{25,9},{2,18},{10... | collective-permute-start | bytes 49160 | tf_op jit(solution)/shard_map/ppermute | solution.py:16
  59.9 3.3 %collective-permute-start.15 = (f32[16,256]{1,0:T(8,128)S(1)}, f32[16,256]{1,0:T(8,128)S(1)}, u32[]{:S(2)}, u32[]{:S(2)}) collective-permute-start(f32[16,256]{1,0:T(8,128)S(1)} %get-tuple-element.76), channel_id=1, source_target_pairs={{0,24},{8,16},{16,8},{24,0},{1,25},{9,17},{17,9},{25,1},{2,26},{10... | collective-permute-start | bytes 49160 | tf_op jit(solution)/shard_map/ppermute | solution.py:16
  64.1 1.9 %collective-permute-start.16 = (f32[4,16,256]{2,1,0:T(8,128)S(1)}, f32[4,16,256]{2,1,0:T(8,128)S(1)}, u32[]{:S(2)}, u32[]{:S(2)}) collective-permute-start(f32[4,16,256]{2,1,0:T(8,128)S(1)} %shard_map.113.refs_0_), channel_id=1, source_target_pairs={{0,8},{8,0},{16,24},{24,16},{1,9},{9,1},{17,25},{25,17},{2,10},{10... | collective-permute-start | bytes 196616 | tf_op jit(solution)/shard_map/ppermute | solution.py:16
  64.3 4.5 %collective-permute-start.17 = (f32[4,16,256]{2,1,0:T(8,128)S(1)}, f32[4,16,256]{2,1,0:T(8,128)S(1)}, u32[]{:S(2)}, u32[]{:S(2)}) collective-permute-start(f32[4,16,256]{2,1,0:T(8,128)S(1)} %shard_map.113.refs_0_), channel_id=1, source_target_pairs={{0,16},{8,24},{16,0},{24,8},{1,17},{9,25},{17,1},{25,9},{2,18},{10... | collective-permute-start | bytes 196616 | tf_op jit(solution)/shard_map/ppermute | solution.py:16
  65.6 4.3 %collective-permute-start.18 = (f32[4,16,256]{2,1,0:T(8,128)S(1)}, f32[4,16,256]{2,1,0:T(8,128)S(1)}, u32[]{:S(2)}, u32[]{:S(2)}) collective-permute-start(f32[4,16,256]{2,1,0:T(8,128)S(1)} %shard_map.113.refs_0_), channel_id=1, source_target_pairs={{0,24},{8,16},{16,8},{24,0},{1,25},{9,17},{17,9},{25,1},{2,26},{10... | collective-permute-start | bytes 196616 | tf_op jit(solution)/shard_map/ppermute | solution.py:16
  70.8 1.9 %collective-permute-start.19 = (f32[16,256]{1,0:T(8,128)S(1)}, f32[16,256]{1,0:T(8,128)S(1)}, u32[]{:S(2)}, u32[]{:S(2)}) collective-permute-start(f32[16,256]{1,0:T(8,128)S(1)} %shard_map.114.refs_0_.refs_2_), channel_id=1, source_target_pairs={{0,8},{8,0},{16,24},{24,16},{1,9},{9,1},{17,25},{25,17},{2,10},{10... | collective-permute-start | bytes 49160 | tf_op jit(solution)/shard_map/ppermute | solution.py:16
  70.9 3.8 %collective-permute-start.20 = (f32[16,256]{1,0:T(8,128)S(1)}, f32[16,256]{1,0:T(8,128)S(1)}, u32[]{:S(2)}, u32[]{:S(2)}) collective-permute-start(f32[16,256]{1,0:T(8,128)S(1)} %shard_map.114.refs_0_.refs_2_), channel_id=1, source_target_pairs={{0,16},{8,24},{16,0},{24,8},{1,17},{9,25},{17,1},{25,9},{2,18},{10... | collective-permute-start | bytes 49160 | tf_op jit(solution)/shard_map/ppermute | solution.py:16
  72.0 3.3 %collective-permute-start.21 = (f32[16,256]{1,0:T(8,128)S(1)}, f32[16,256]{1,0:T(8,128)S(1)}, u32[]{:S(2)}, u32[]{:S(2)}) collective-permute-start(f32[16,256]{1,0:T(8,128)S(1)} %shard_map.114.refs_0_.refs_2_), channel_id=1, source_target_pairs={{0,24},{8,16},{16,8},{24,0},{1,25},{9,17},{17,9},{25,1},{2,26},{10... | collective-permute-start | bytes 49160 | tf_op jit(solution)/shard_map/ppermute | solution.py:16
  76.2 1.2 %collective-permute-start.22 = (f32[16,256]{1,0:T(8,128)S(1)}, f32[16,256]{1,0:T(8,128)S(1)}, u32[]{:S(2)}, u32[]{:S(2)}) collective-permute-start(f32[16,256]{1,0:T(8,128)S(1)} %shard_map.115.refs_0_), channel_id=1, source_target_pairs={{0,8},{8,0},{16,24},{24,16},{1,9},{9,1},{17,25},{25,17},{2,10},{10... | collective-permute-start | bytes 49160 | tf_op jit(solution)/shard_map/ppermute | solution.py:16
  77.4 17.1 %copy-start.3 = (f32[1,1,512,512]{3,2,1,0:T(8,128)S(1)}, f32[1,1,512,512]{3,2,1,0:T(8,128)}, u32[]{:S(2)}) copy-start(f32[1,1,512,512]{3,2,1,0:T(8,128)} %param.11) | copy-start | bytes 3145732
  78.1 16.3 %copy-start.1 = (f32[1,1,512,512]{3,2,1,0:T(8,128)S(1)}, f32[1,1,512,512]{3,2,1,0:T(8,128)}, u32[]{:S(2)}) copy-start(f32[1,1,512,512]{3,2,1,0:T(8,128)} %param.10) | copy-start | bytes 3145732
  78.1 1.2 %collective-permute-start.23 = (f32[16,256]{1,0:T(8,128)S(1)}, f32[16,256]{1,0:T(8,128)S(1)}, u32[]{:S(2)}, u32[]{:S(2)}) collective-permute-start(f32[16,256]{1,0:T(8,128)S(1)} %shard_map.116.refs_0_), channel_id=1, source_target_pairs={{0,8},{8,0},{16,24},{24,16},{1,9},{9,1},{17,25},{25,17},{2,10},{10... | collective-permute-start | bytes 49160 | tf_op jit(solution)/shard_map/ppermute | solution.py:16
  80.4 14.1 %copy-start.8 = (f32[128,512]{1,0:T(8,128)S(1)}, f32[128,512]{1,0:T(8,128)}, u32[]{:S(2)}) copy-start(f32[128,512]{1,0:T(8,128)} %copy-done.7) | copy-start | bytes 786436
  (4 other events, 3.8 us)
